TPU v7x, 32 devices: a whole 2x2x4 slice. The times are simulated.
32 devices in a mesh: tab: 8 (over z, y), rep: 4 (over x, core).
Axes of the slice: x: 2, y: 2, z: 4, core: 2. Of those that a mesh axis runs over, the one named last changes fastest.
Arguments:
- ids: int32 [16384, 26], P(('tab', 'rep')), may hold values from 0 to 32767
- table_rows: int32 [26], replicated, may hold values from 4096 to 32768, as said below
- table_place: int32 [26], replicated, may hold values from 0 to 39, as said below
- dense_in: bfloat16 [16384, 13], P(('tab', 'rep')), may hold values from -6 to 6
- labels: int32 [16384], P(('tab', 'rep')), may hold values 0 or 1
- tables: bfloat16 [40, 39, 32768], P('tab'), may hold values from -6 to 6
- cross_w: bfloat16 [3, 1027, 1027], replicated, may hold values from -0.1875 to 0.1875
- cross_b: bfloat16 [3, 1027], replicated, may hold values from -3 to 3
- tower1_w: bfloat16 [1024, 1027], replicated, may hold values from -0.1875 to 0.1875
- tower1_b: bfloat16 [1024], replicated, may hold values from -3 to 3
- tower2_w: bfloat16 [1024, 1024], replicated, may hold values from -0.1875 to 0.1875
- tower2_b: bfloat16 [1024], replicated, may hold values from -3 to 3
- out_w: bfloat16 [2051], replicated, may hold values from -0.125 to 0.125
- out_b: bfloat16 [], replicated, may hold values from -2 to 2
Outputs:
- loss: float32 [], replicated
- logits: float32 [16384], P(('tab', 'rep'))
- dense_grad: float32 [16384, 13], P(('tab', 'rep'))
- cross_w_grad: float32 [3, 1027, 1027], replicated
- cross_b_grad: float32 [3, 1027], replicated
- tower1_w_grad: float32 [1024, 1027], replicated
- tower1_b_grad: float32 [1024], replicated
- tower2_w_grad: float32 [1024, 1024], replicated
- tower2_b_grad: float32 [1024], replicated
- out_w_grad: float32 [2051], replicated
- out_b_grad: float32 [], replicated
- table_grad: float32 [40, 39, 32768], P('tab', None, 'rep')
Inputs may be any that keep to these rules, and one draw needn't show every extreme that they name: `table_rows`: every table has at least 4096 rows, and one table has exactly 32768. `table_place`: distinct slots; slot s lies on the device of index s // 5 along tab. Some device holds 5 tables.
All inputs are finite; a program needn't handle non-finite values. No bound on the sum of `labels` on one device may be relied on, other than what follows from the above.
Results may differ from a plain program's by a relative error of at most 0.0044.
Values may be sent and summed in bfloat16 or wider, within the bound.
No kernel may reach another device: no remote copies, remote signals or barrier semaphores. Data moves between devices by JAX's collectives and lax.ppermute only.
A program may use at most 1.0625 GiB of HBM per device.

v0:
```python
import jax
import jax.numpy as jnp
from jax import lax
from jax.sharding import PartitionSpec as P

HIGH = lax.Precision.HIGHEST


def swish_slope(preact):
    sigmoid_val = jax.nn.sigmoid(preact)
    return sigmoid_val * (1.0 + preact * (1.0 - sigmoid_val))


def contract_rows(left_op, right_op):
    return lax.dot_general(
        left_op, right_op, (((0,), (0,)), ((), ())), preferred_element_type=jnp.float32
    )


def contract_cols(left_op, right_op):
    return lax.dot_general(
        left_op, right_op, (((1,), (1,)), ((), ())), preferred_element_type=jnp.float32
    )


def lookup(slot_table, slot_ids):
    return jnp.take(slot_table, slot_ids, axis=1)


def on_device(
    ids,
    table_rows,
    table_place,
    dense_in,
    labels,
    tables,
    cross_w,
    cross_b,
    tower1_w,
    tower1_b,
    tower2_w,
    tower2_b,
    out_w,
    out_b,
):
    tab_count = lax.axis_size("tab")
    device_count = tab_count * lax.axis_size("rep")
    slot_count = tables.shape[0]
    embed_dim = tables.shape[1]
    table_len = tables.shape[2]
    row_count = dense_in.shape[0]
    dense_width = dense_in.shape[1]
    field_count = ids.shape[1]
    model_width = cross_w.shape[1]
    layer_count = cross_w.shape[0]
    all_slots = slot_count * tab_count
    effective = ids % table_rows[None, :]
    slot_iota = jnp.arange(all_slots, dtype=jnp.int32)
    matches = table_place[:, None] == slot_iota[None, :]
    field_iota = jnp.arange(field_count, dtype=jnp.int32)
    slot_field = jnp.sum(jnp.where(matches, field_iota[:, None], 0), axis=0)
    slot_used = jnp.any(matches, axis=0)
    gathered = lax.all_gather(effective, "tab", axis=0, tiled=True)
    first_slot = lax.axis_index("tab") * slot_count
    own_field = lax.dynamic_slice_in_dim(slot_field, first_slot, slot_count)
    own_used = lax.dynamic_slice_in_dim(slot_used, first_slot, slot_count)
    wanted = jnp.where(own_used[:, None], jnp.take(gathered.T, own_field, axis=0), 0)
    looked = jax.vmap(lookup)(tables, wanted)
    arrived = lax.all_to_all(looked, "tab", split_axis=2, concat_axis=0, tiled=True)
    picked = jnp.take(arrived, table_place, axis=0)
    embedded = jnp.transpose(picked, (2, 0, 1)).reshape(row_count, field_count * embed_dim)
    anchor = jnp.concatenate([dense_in, embedded], axis=1)
    anchor_f = anchor.astype(jnp.float32)
    current = anchor_f
    kept_low = []
    kept_update = []
    for layer_at in range(layer_count):
        current_low = current.astype(jnp.bfloat16)
        update = jnp.dot(
            current_low, cross_w[layer_at], preferred_element_type=jnp.float32
        ) + cross_b[layer_at].astype(jnp.float32)
        kept_low.append(current_low)
        kept_update.append(update)
        current = anchor_f * update + current
    first_pre = contract_cols(anchor, tower1_w) + tower1_b.astype(jnp.float32)
    first_low = jax.nn.silu(first_pre).astype(jnp.bfloat16)
    second_pre = jnp.dot(first_low, tower2_w, preferred_element_type=jnp.float32) + tower2_b.astype(
        jnp.float32
    )
    second_act = jax.nn.silu(second_pre)
    out_weight = out_w.astype(jnp.float32)
    logits = (
        jnp.dot(current, out_weight[:model_width], precision=HIGH)
        + jnp.dot(second_act, out_weight[model_width:], precision=HIGH)
        + out_b.astype(jnp.float32)
    )
    target = labels.astype(jnp.float32)
    loss_part = jnp.sum(jax.nn.softplus(logits) - target * logits)
    residue = jax.nn.sigmoid(logits) - target
    out_w_part = jnp.concatenate(
        [jnp.dot(residue, current, precision=HIGH), jnp.dot(residue, second_act, precision=HIGH)]
    )
    out_b_part = jnp.sum(residue)
    grad_current = residue[:, None] * out_weight[None, :model_width]
    grad_second = (
        residue[:, None] * out_weight[None, model_width:] * swish_slope(second_pre)
    ).astype(jnp.bfloat16)
    tower2_w_part = contract_rows(first_low, grad_second)
    tower2_b_part = jnp.sum(grad_second.astype(jnp.float32), axis=0)
    grad_first_act = contract_cols(grad_second, tower2_w)
    grad_first = (grad_first_act * swish_slope(first_pre)).astype(jnp.bfloat16)
    tower1_b_part = jnp.sum(grad_first.astype(jnp.float32), axis=0)
    grad_anchor = jnp.dot(grad_first, tower1_w, preferred_element_type=jnp.float32)
    weight_parts = [None] * layer_count
    bias_parts = [None] * layer_count
    for layer_at in reversed(range(layer_count)):
        grad_update = (anchor_f * grad_current).astype(jnp.bfloat16)
        weight_part = contract_rows(kept_low[layer_at], grad_update)
        bias_part = jnp.sum(grad_update.astype(jnp.float32), axis=0)
        weight_parts[layer_at] = weight_part
        bias_parts[layer_at] = bias_part
        grad_anchor = grad_anchor + grad_current * kept_update[layer_at]
        grad_current = grad_current + contract_cols(grad_update, cross_w[layer_at])
    grad_anchor = grad_anchor + grad_current
    grad_embed = (
        grad_anchor[:, dense_width:].astype(jnp.bfloat16).reshape(row_count, field_count, embed_dim)
    )
    grad_fields = jnp.transpose(grad_embed, (1, 2, 0))
    grad_slots = (
        jnp.zeros((all_slots, embed_dim, row_count), jnp.bfloat16).at[table_place].set(grad_fields)
    )
    returned = lax.all_to_all(grad_slots, "tab", split_axis=0, concat_axis=2, tiled=True)

    def accumulate(slot_grads, slot_ids):
        return (
            jnp.zeros((embed_dim, table_len), jnp.float32)
            .at[:, slot_ids]
            .add(slot_grads.astype(jnp.float32))
        )

    local_tables = jax.vmap(accumulate)(returned, wanted)
    table_grad = lax.psum_scatter(local_tables, "rep", scatter_dimension=2, tiled=True)
    tower_share = lax.psum_scatter(
        contract_rows(grad_first, anchor), ("tab", "rep"), scatter_dimension=0, tiled=True
    )
    tower1_w_grad = lax.all_gather(tower_share, ("tab", "rep"), axis=0, tiled=True)
    weight_stack = jnp.stack(weight_parts)
    bias_stack = jnp.stack(bias_parts)
    (
        cross_w_grad,
        cross_b_grad,
        tower2_w_grad,
        tower2_b_grad,
        tower1_b_grad,
        out_w_grad,
        out_b_grad,
        loss_total,
    ) = lax.psum(
        (
            weight_stack,
            bias_stack,
            tower2_w_part,
            tower2_b_part,
            tower1_b_part,
            out_w_part,
            out_b_part,
            loss_part,
        ),
        ("tab", "rep"),
    )
    loss = loss_total / (row_count * device_count)
    dense_grad = grad_anchor[:, :dense_width]
    return (
        loss,
        logits,
        dense_grad,
        cross_w_grad,
        cross_b_grad,
        tower1_w_grad,
        tower1_b_grad,
        tower2_w_grad,
        tower2_b_grad,
        out_w_grad,
        out_b_grad,
        table_grad,
    )


def solution(mesh):
    placed = (
        P(("tab", "rep"), None),
        P(),
        P(),
        P(("tab", "rep"), None),
        P(("tab", "rep")),
        P("tab", None, None),
        P(),
        P(),
        P(),
        P(),
        P(),
        P(),
        P(),
        P(),
    )
    return jax.shard_map(
        on_device,
        mesh=mesh,
        in_specs=placed,
        out_specs=(
            P(),
            P(("tab", "rep")),
            P(("tab", "rep"), None),
            P(),
            P(),
            P(),
            P(),
            P(),
            P(),
            P(),
            P(),
            P("tab", None, "rep"),
        ),
        check_vma=False,
    )
```

profile of v0, /device:TPU:0, one launch (start us, length us, event | category | flops | bytes accessed | tf_op | source)
XLA Modules:
  0.0 4393.1 jit_solution(12355363237856381763)
XLA Ops:
  12.7 33.0 all_gather.6
  46.6 34.6 copy.53
  82.1 337.7 %gather_fusion.2 = bf16[20480,39]{1,0:T(8,128)(2,1)} fusion(bf16[5,39,32768]{1,2,0:T(8,128)(2,1)} %copy.53, s32[20480]{0:T(1024)S(1)} %reshape.165), kind=kCustom, calls=%fused_computation.2 | custom fusion | bytes 3358720 | tf_op jit(solution)/shard_map/vmap(jit(_take))/gather | solution.py:27
  419.8 27.5 fusion.47
  447.3 11.4 reshape.200
  458.7 508.9 %all-to-all-start = ((bf16[8,2,49920]{2,1,0:T(2,128)(2,1)}), bf16[8,2,49920]{2,1,0:T(2,128)(2,1)}, u32[]{:S(2)}, u32[]{:S(2)}) async-start(bf16[8,2,49920]{2,1,0:T(2,128)(2,1)} %reshape.200), calls=%async_computation | async-start | bytes 3194880 | tf_op jit(solution)/shard_map/all_to_all | solution.py:69
  968.7 30.9 all-to-all-done
  999.6 11.1 reshape.201
  1010.7 8.9 copy.56
  1026.4 4.0 convolution_add_fusion.5
  1050.5 106.2 %reduce-scatter.3.cloned.1.call-done = f32[32,1027]{1,0:T(8,128)} async-done(((f32[1024,1027]{1,0:T(8,128)}), f32[32,1027]{1,0:T(8,128)}) %reduce-scatter.3.cloned.1.call-update) | async-done | bytes 131472 | tf_op jit(solution)/shard_map/reduce_scatter | solution.py:143
  1160.0 4.6 convert_reduce_fusion.2
  1164.7 4.1 convolution_add_fusion
  1174.5 4.8 scatter_fusion
  1179.3 4.7 all-to-all-start.1
  1184.4 55.3 %all-to-all-done.1 = bf16[40,39,512]{2,1,0:T(8,128)(2,1)S(1)} async-done(((bf16[40,39,512]{2,1,0:T(8,128)(2,1)}), bf16[40,39,512]{2,1,0:T(8,128)(2,1)S(1)}, u32[]{:S(2)}, u32[]{:S(2)}) %all-to-all-start.1) | async-done | bytes 1597472 | tf_op jit(solution)/shard_map/all_to_all | solution.py:132
  1242.0 4.4 reshape.147
  1246.4 7.5 copy.65
  1253.9 26.1 broadcast.159
  1280.0 2048.4 %scatter_fusion.1 = f32[163840,39]{1,0:T(8,128)} fusion(f32[163840,39]{1,0:T(8,128)} %broadcast.159, s32[20480]{0:T(1024)S(1)} %reshape.179, f32[20480,39]{1,0:T(8,128)} %bitcast.92), kind=kCustom, calls=%fused_computation.4 | custom fusion | flops 798720 | bytes 9666560
  3328.4 65.4 %copy.66 = f32[5,32768,39]{1,0,2:T(8,128)} copy(f32[5,32768,39]{2,1,0:T(8,128)} %bitcast.25) | data formatting | bytes 51118080
  3395.0 3.9 convolution_bitcast_fusion
  3398.9 3.8 convolution_bitcast_fusion.2
  3402.8 4.0 convolution_bitcast_fusion.1
  3410.1 11.4 pad_maximum_fusion
  3427.3 565.5 %all-reduce = (f32[]{:T(128)}, f32[3,1027]{1,0:T(4,128)}, f32[1024]{0:T(1024)}, f32[1024]{0:T(1024)}, f32[2051]{0:T(1024)}, /*index=5*/f32[]{:T(128)}) all-reduce(f32[]{:T(128)} %fusion.33, f32[3,1027]{1,0:T(4,128)S(1)} %pad_maximum_fusion.2, f32[1024]{0:T(1024)S(1)} %get-tuple-element.100, ...), channel_id=1, replica_groups=mesh['tab'=8,'rep'=4] {'tab','rep'}, use_global_device_ids=true, to_apply=%region_3.4 | all-reduce | flops 7182 | bytes 57456 | tf_op jit(solution)/shard_map/psum | solution.py:158
  3994.9 5.9 copy.61
  4000.8 230.1 %reduce-scatter.5.cloned.1.call-done = f32[5,39,8192]{2,0,1:T(8,128)} async-done(((f32[5,39,32768]{2,0,1:T(8,128)}), f32[5,39,8192]{2,0,1:T(8,128)}) %reduce-scatter.5.cloned.1.call-update) | async-done | bytes 6389776 | tf_op jit(solution)/shard_map/reduce_scatter | solution.py:142
  4230.9 10.4 copy.62
  4241.4 126.8 %all-reduce.4.cloned.1.call-done = (f32[3,1027,1027]{2,1,0:T(8,128)}, f32[1024,1024]{1,0:T(8,128)}) async-done(((f32[3,1027,1027]{2,1,0:T(8,128)}, f32[1024,1024]{1,0:T(8,128)}), (f32[3,1027,1027]{2,1,0:T(8,128)}, f32[1024,1024]{1,0:T(8,128)})) %all-reduce.4.cloned.1.call-update) | async-done | bytes 16851068 | tf_op jit(solution)/shard_map/psum | solution.py:158
  4368.1 11.5 copy.80
  4379.6 4.8 copy.81
  (153 shorter events, 56.5 us)
Async XLA Ops:
  8.0 1016.8 %copy-start = (bf16[1024,1027]{0,1:T(8,128)(2,1)S(1)}, bf16[1024,1027]{0,1:T(8,128)(2,1)}, u32[]{:S(2)}) copy-start(bf16[1024,1027]{0,1:T(8,128)(2,1)} %param.22) | copy-start | bytes 6309892
  458.7 509.0 %copy-start.26 = (bf16[2051]{0:T(1024)(128)(2,1)S(1)}, bf16[2051]{0:T(1024)(128)(2,1)}, u32[]{:S(2)}) copy-start(bf16[2051]{0:T(1024)(128)(2,1)} %param.26) | copy-start | bytes 12310
  458.7 509.2 %copy-start.34 = (bf16[1024]{0:T(1024)(128)(2,1)S(1)}, bf16[1024]{0:T(1024)(128)(2,1)}, u32[]{:S(2)}) copy-start(bf16[1024]{0:T(1024)(128)(2,1)} %param.23) | copy-start | bytes 6148
  458.7 509.2 %copy-start.35 = (bf16[1024]{0:T(1024)(128)(2,1)S(1)}, bf16[1024]{0:T(1024)(128)(2,1)}, u32[]{:S(2)}) copy-start(bf16[1024]{0:T(1024)(128)(2,1)} %param.25) | copy-start | bytes 6148
  458.7 509.9 %copy-start.39 = (s32[26]{0:T(128)S(1)}, s32[26]{0:T(128)}, u32[]{:S(2)}) copy-start(s32[26]{0:T(128)} %param.16) | copy-start | bytes 316
  458.7 509.9 %copy-start.27 = (bf16[3,1027]{1,0:T(4,128)(2,1)S(1)}, bf16[3,1027]{1,0:T(4,128)(2,1)}, u32[]{:S(2)}) copy-start(bf16[3,1027]{1,0:T(4,128)(2,1)} %param.21) | copy-start | bytes 18490
  458.7 540.9 %all-to-all-start = ((bf16[8,2,49920]{2,1,0:T(2,128)(2,1)}), bf16[8,2,49920]{2,1,0:T(2,128)(2,1)}, u32[]{:S(2)}, u32[]{:S(2)}) async-start(bf16[8,2,49920]{2,1,0:T(2,128)(2,1)} %reshape.200), calls=%async_computation | async-start | bytes 3194880 | tf_op jit(solution)/shard_map/all_to_all | solution.py:69
  967.7 189.0 %reduce-scatter.3.cloned.1.call-start = ((), (), s32[]{:S(2)}) async-start(), calls=%async_computation.4 | async-start | bytes 4866048 | tf_op jit(solution)/shard_map/reduce_scatter | solution.py:143
  967.9 74.3 %copy-start.29 = (f32[1024]{0:T(1024)}, f32[1024]{0:T(1024)S(1)}, u32[]{:S(2)}) copy-start(f32[1024]{0:T(1024)S(1)} %convert_element_type.82) | copy-start | bytes 12292
  1024.8 5.7 slice-start
  1026.4 17.3 copy-start.17
  1026.4 4.1 slice-start.1
  1035.8 3.7 copy-start.5
  1050.4 2944.5 %all-gather.2.cloned.1.call-start = ((), (), s32[]{:S(2)}) async-start(), calls=%async_computation.5 | async-start | bytes 4866048 | tf_op jit(solution)/shard_map/all_gather | solution.py:146
  1160.0 8.8 copy-start.7
  1164.6 4.2 copy-start.9
  1164.6 4.2 copy-start.3
  1164.7 4.2 copy-start.12
  1164.7 4.5 copy-start.13
  1164.7 4.7 copy-start.16
  1179.3 4.7 copy-start.37
  1179.3 4.8 copy-start.36
  1179.3 60.4 %all-to-all-start.1 = ((bf16[40,39,512]{2,1,0:T(8,128)(2,1)}), bf16[40,39,512]{2,1,0:T(8,128)(2,1)S(1)}, u32[]{:S(2)}, u32[]{:S(2)}) async-start(bf16[40,39,512]{2,1,0:T(8,128)(2,1)} %scatter_fusion), calls=%async_computation.2 | async-start | bytes 3276800 | tf_op jit(solution)/shard_map/all_to_all | solution.py:132
  1184.0 3047.0 %reduce-scatter.5.cloned.1.call-start = ((), (), s32[]{:S(2)}) async-start(), calls=%async_computation.6 | async-start | bytes 51118080 | tf_op jit(solution)/shard_map/reduce_scatter | solution.py:142
  3393.8 974.3 %all-reduce.4.cloned.1.call-start = ((), (), s32[]{:S(2)}) async-start(), calls=%async_computation.7 | async-start | bytes 36921344 | tf_op jit(solution)/shard_map/psum | solution.py:158
  3395.0 3.9 copy-start.10
  3398.9 3.8 copy-start.4
  3398.9 3.8 copy-start.8
  3402.7 4.0 copy-start.18
  3402.7 4.0 copy-start.24
  3421.6 3.4 copy-start.20
  4368.1 16.2 copy-start.1
  (16 other events, 34.4 us)
Sparse Core Ops, SparseCore 0:
  1050.5 106.0 reduce-scatter.2
  1160.0 82.1 all-gather.1
  3421.7 946.3 all-reduce.3
Sparse Core Ops, SparseCore 1:
  3393.9 837.0 reduce-scatter.4
where the time goes:
time: 4360 us; the launch traced here: 4390 us
  other arithmetic  2100 us (48%)
  blocking collectives  599 us (14%)
  local copies, waits for them, and re-layouts  563 us (13%)
  waiting for transfers between devices  549 us (13%)
  starting transfers between devices  514 us (12%)
  matrix products  52.6 us (1%)
    unnamed x6, other arithmetic  2080 us
    psum x1, blocking collectives, on_device(): lax.psum((weight_stack, bias_stack, tower2_w_part, tower2_b_part, tower1_...  566 us
    all_to_all x1, starting transfers between devices, on_device(): lax.all_to_all(looked, 'tab', split_axis=2, concat_axis=0, tiled=True)  509 us
    gather x3, local copies, waits for them, and re-layouts, lookup(): return jnp.take(slot_table, slot_ids, axis=1)  338 us
    reduce_scatter x1, waiting for transfers between devices, on_device(): lax.psum_scatter(local_tables, 'rep', scatter_dimension=2, tiled=True)  230 us
    unnamed x94, local copies, waits for them, and re-layouts  188 us
    psum x1, waiting for transfers between devices, on_device(): lax.psum((weight_stack, bias_stack, tower2_w_part, tower2_b_part, tower1_...  127 us
    reduce_scatter x1, waiting for transfers between devices, on_device(): lax.psum_scatter(contract_rows(grad_first, anchor), ('tab', 'rep'), scatt...  106 us
  transfers between devices with their start and end apart: 6, of which 5 were waited for; matrix products, arithmetic and copies ran while one was open for 51% of the time, Pallas kernels for 0%

commit v1 on v0

--- a/solution.py
+++ b/solution.py
@@ -1,9 +1,146 @@
+import functools
+
 import jax
 import jax.numpy as jnp
 from jax import lax
+from jax.experimental import pallas as pl
+from jax.experimental.pallas import tpu as pltpu
 from jax.sharding import PartitionSpec as P
 
 HIGH = lax.Precision.HIGHEST
+BF = jnp.bfloat16
+F32 = jnp.float32
+LOOK_LOW = 512
+LOOK_GROUP = 8
+LOOK_COLS = 1024
+ADD_LOW = 512
+ADD_COLS = 2048
+
+
+def round_up(size, unit):
+    return -(-size // unit) * unit
+
+
+def lookup_kernel(group_ref, ids_ref, table_ref, out_ref, stack):
+    slot = pl.program_id(0)
+    embed_dim = table_ref.shape[1]
+    block_count, pad_dim, low_count = stack.shape
+    cols = out_ref.shape[2]
+
+    @pl.when(pl.program_id(1) == 0)
+    def _():
+        for block in range(block_count):
+            stack[block, :embed_dim, :] = table_ref[0, :, block * low_count : (block + 1) * low_count]
+
+    picked = ids_ref[0]
+    high = lax.shift_right_arithmetic(picked, low_count.bit_length() - 1)
+    low = picked & (low_count - 1)
+    low_iota = lax.broadcasted_iota(jnp.int32, (low_count, cols), 0)
+    onehot = jnp.where(low_iota == low, 1.0, 0.0).astype(BF)
+
+    def step(group, total):
+        left = stack[pl.ds(group * LOOK_GROUP, LOOK_GROUP)].reshape(LOOK_GROUP * pad_dim, low_count)
+        partial = jnp.dot(left, onehot, preferred_element_type=F32)
+        for at in range(LOOK_GROUP):
+            rows = partial[at * pad_dim : at * pad_dim + total.shape[0]]
+            total = total + jnp.where(high == group * LOOK_GROUP + at, rows, 0.0)
+        return total
+
+    rows_kept = round_up(embed_dim, 8)
+    total = lax.fori_loop(0, group_ref[slot], step, jnp.zeros((rows_kept, cols), F32))
+    out_ref[0] = total[:embed_dim].astype(BF)
+
+
+def lookup(tables, wanted, own_rows):
+    slot_count, embed_dim, table_len = tables.shape
+    count = wanted.shape[1]
+    pad_dim = round_up(embed_dim, 16)
+    unit = LOOK_LOW * LOOK_GROUP
+    groups = (own_rows + unit - 1) // unit
+    return pl.pallas_call(
+        lookup_kernel,
+        grid_spec=pltpu.PrefetchScalarGridSpec(
+            num_scalar_prefetch=1,
+            grid=(slot_count, count // LOOK_COLS),
+            in_specs=[
+                pl.BlockSpec((1, 1, LOOK_COLS), lambda s, c, *_: (s, 0, c)),
+                pl.BlockSpec((1, embed_dim, table_len), lambda s, c, *_: (s, 0, 0)),
+            ],
+            out_specs=pl.BlockSpec((1, embed_dim, LOOK_COLS), lambda s, c, *_: (s, 0, c)),
+            scratch_shapes=[pltpu.VMEM((table_len // LOOK_LOW, pad_dim, LOOK_LOW), BF)],
+        ),
+        out_shape=jax.ShapeDtypeStruct((slot_count, embed_dim, count), BF),
+        compiler_params=pltpu.CompilerParams(vmem_limit_bytes=48 * 1024 * 1024),
+        cost_estimate=pl.CostEstimate(
+            flops=2 * slot_count * count * table_len * pad_dim,
+            bytes_accessed=2 * slot_count * embed_dim * (table_len + count),
+            transcendentals=0,
+        ),
+        name="lookup",
+    )(groups, wanted[:, None, :], tables)
+
+
+def add_kernel(base_ref, ids_ref, grad_ref, out_ref, total):
+    step = pl.program_id(1)
+    embed_dim = grad_ref.shape[2]
+    cols = grad_ref.shape[3]
+
+    @pl.when(step == 0)
+    def _():
+        total[...] = jnp.zeros_like(total)
+
+    local = ids_ref[0, 0] - base_ref[0]
+    high = lax.shift_right_arithmetic(local, ADD_LOW.bit_length() - 1)
+    low = local & (ADD_LOW - 1)
+    high_count = total.shape[1] // embed_dim
+    high_iota = lax.broadcasted_iota(jnp.int32, (high_count, cols), 0)
+    low_iota = lax.broadcasted_iota(jnp.int32, (ADD_LOW, cols), 0)
+    high_hot = jnp.where(high_iota == high, 1.0, 0.0)
+    low_hot = jnp.where(low_iota == low, 1.0, 0.0).astype(BF)
+    grads = grad_ref[0, 0].astype(F32)
+    left = (grads[:, None, :] * high_hot[None, :, :]).astype(BF).reshape(embed_dim * high_count, cols)
+    product = lax.dot_general(left, low_hot, (((1,), (1,)), ((), ())), preferred_element_type=F32)
+    for lane in range(ADD_LOW // 128):
+        total[lane] += product[:, lane * 128 : (lane + 1) * 128]
+
+    @pl.when(step == pl.num_programs(1) - 1)
+    def _():
+        for at in range(high_count):
+            for part in range(0, embed_dim, 8):
+                size = min(8, embed_dim - part)
+                for lane in range(ADD_LOW // 128):
+                    first = at * ADD_LOW + lane * 128
+                    out_ref[0, part : part + size, first : first + 128] = total[
+                        lane, pl.ds(part * high_count + at, size, stride=high_count), :
+                    ]
+
+
+def add_rows(grads, wanted, base, share):
+    part_count, slot_count, embed_dim, count = grads.shape
+    steps = count // ADD_COLS
+    return pl.pallas_call(
+        add_kernel,
+        grid_spec=pltpu.PrefetchScalarGridSpec(
+            num_scalar_prefetch=1,
+            grid=(slot_count, part_count * steps),
+            in_specs=[
+                pl.BlockSpec((1, 1, 1, ADD_COLS), lambda s, c, *_: (c // steps, s, 0, c % steps)),
+                pl.BlockSpec(
+                    (1, 1, embed_dim, ADD_COLS), lambda s, c, *_: (c // steps, s, 0, c % steps)
+                ),
+            ],
+            out_specs=pl.BlockSpec((1, embed_dim, share), lambda s, c, *_: (s, 0, 0)),
+            scratch_shapes=[pltpu.VMEM((ADD_LOW // 128, embed_dim * (share // ADD_LOW), 128), F32)],
+        ),
+        out_shape=jax.ShapeDtypeStruct((slot_count, embed_dim, share), F32),
+        compiler_params=pltpu.CompilerParams(vmem_limit_bytes=48 * 1024 * 1024),
+        cost_estimate=pl.CostEstimate(
+            flops=2 * part_count * slot_count * count * share * embed_dim,
+            bytes_accessed=2 * slot_count * embed_dim * (2 * share + part_count * count),
+            transcendentals=0,
+        ),
+        name="add_rows",
+    )(base, wanted[:, :, None, :], grads)
 
 
 def swish_slope(preact):
@@ -21,10 +158,6 @@
     return lax.dot_general(
         left_op, right_op, (((1,), (1,)), ((), ())), preferred_element_type=jnp.float32
     )
-
-
-def lookup(slot_table, slot_ids):
-    return jnp.take(slot_table, slot_ids, axis=1)
 
 
 def on_device(
@@ -65,7 +198,9 @@
     own_field = lax.dynamic_slice_in_dim(slot_field, first_slot, slot_count)
     own_used = lax.dynamic_slice_in_dim(slot_used, first_slot, slot_count)
     wanted = jnp.where(own_used[:, None], jnp.take(gathered.T, own_field, axis=0), 0)
-    looked = jax.vmap(lookup)(tables, wanted)
+    own_rows = jnp.where(own_used, jnp.take(table_rows, own_field), 1)
+    wanted_all = lax.all_gather(wanted, "rep", axis=0, tiled=False)
+    looked = lookup(tables, wanted, own_rows)
     arrived = lax.all_to_all(looked, "tab", split_axis=2, concat_axis=0, tiled=True)
     picked = jnp.take(arrived, table_place, axis=0)
     embedded = jnp.transpose(picked, (2, 0, 1)).reshape(row_count, field_count * embed_dim)
@@ -131,15 +266,10 @@
     )
     returned = lax.all_to_all(grad_slots, "tab", split_axis=0, concat_axis=2, tiled=True)
 
-    def accumulate(slot_grads, slot_ids):
-        return (
-            jnp.zeros((embed_dim, table_len), jnp.float32)
-            .at[:, slot_ids]
-            .add(slot_grads.astype(jnp.float32))
-        )
-
-    local_tables = jax.vmap(accumulate)(returned, wanted)
-    table_grad = lax.psum_scatter(local_tables, "rep", scatter_dimension=2, tiled=True)
+    returned_all = lax.all_gather(returned, "rep", axis=0, tiled=False)
+    share = table_len // lax.axis_size("rep")
+    base = (lax.axis_index("rep") * share).astype(jnp.int32).reshape(1)
+    table_grad = add_rows(returned_all, wanted_all, base, share)
     tower_share = lax.psum_scatter(
         contract_rows(grad_first, anchor), ("tab", "rep"), scatter_dimension=0, tiled=True
     )

time: 4360 us -> 742 us (0.17)
  other arithmetic: 2100 us -> 19.8 us
  starting transfers between devices: 514 us -> 18.9 us
  local copies, waits for them, and re-layouts: 563 us -> 84.2 us
  blocking collectives: 599 us -> 133 us
  waiting for transfers between devices: 549 us -> 269 us
  Pallas kernels: 0 us -> 141 us
    unnamed x6 -> x1, other arithmetic: 2080 us -> 0.01 us
    psum x1, blocking collectives: 566 us -> 42.1 us  [on_device(): lax.psum((weight_stack, bias_stack, tower2_w_part, tower2_b_part, tower1_...]
    all_to_all x1, starting transfers between devices: 509 us -> 18.3 us  [on_device(): lax.all_to_all(looked, 'tab', split_axis=2, concat_axis=0, tiled=True)]
    gather x3 -> x1, local copies, waits for them, and re-layouts: 338 us -> 1.3 us  [on_device(): own_rows = jnp.where(own_used, jnp.take(table_rows, own_field), 1)]
    reduce_scatter x1 -> x0, waiting for transfers between devices: 230 us -> none  [on_device(): lax.psum_scatter(local_tables, 'rep', scatter_dimension=2, tiled=True)]
    pallas_call x0 -> x2, Pallas kernels: none -> 141 us  [the longest x1 73.3 us: lookup(): pl.pallas_call(lookup_kernel, grid_spec=pltpu.PrefetchScalarGridSpec(num_...]
    unnamed x94 -> x85, local copies, waits for them, and re-layouts: 188 us -> 51.2 us
    all_to_all x1 -> x0, waiting for transfers between devices: 55.3 us -> none  [on_device(): lax.all_to_all(grad_slots, 'tab', split_axis=0, concat_axis=2, tiled=True)]
  transfers between devices with their start and end apart: 6 -> 5, of which waited for: 5 -> 3; matrix products, arithmetic and copies ran while one was open for 51% -> 8% of each run, Pallas kernels for 0% -> 9%
where the time goes in v1:
time: 742 us; the launch traced here: 743 us
  waiting for transfers between devices  269 us (36%)
  Pallas kernels  141 us (19%)
  blocking collectives  133 us (18%)
  local copies, waits for them, and re-layouts  84.2 us (11%)
  matrix products  57.3 us (8%)
  other arithmetic  19.8 us (3%)
  starting transfers between devices  18.9 us (3%)
  between operations  18.8 us (3%)
    psum x1, waiting for transfers between devices, on_device(): lax.psum((weight_stack, bias_stack, tower2_w_part, tower2_b_part, tower1_...  181 us
    pallas_call x1, Pallas kernels, lookup(): pl.pallas_call(lookup_kernel, grid_spec=pltpu.PrefetchScalarGridSpec(num_...  73.3 us
    pallas_call x1, Pallas kernels, add_rows(): pl.pallas_call(add_kernel, grid_spec=pltpu.PrefetchScalarGridSpec(num_sca...  68 us
    reduce_scatter x1, waiting for transfers between devices, on_device(): lax.psum_scatter(contract_rows(grad_first, anchor), ('tab', 'rep'), scatt...  55.6 us
    all_to_all x1, blocking collectives, on_device(): lax.all_to_all(grad_slots, 'tab', split_axis=0, concat_axis=2, tiled=True)  51.7 us
    unnamed x85, local copies, waits for them, and re-layouts  51.2 us
    psum x1, blocking collectives, on_device(): lax.psum((weight_stack, bias_stack, tower2_w_part, tower2_b_part, tower1_...  42.1 us
    all_gather x1, blocking collectives, on_device(): gathered = lax.all_gather(effective, 'tab', axis=0, tiled=True)  33 us
  transfers between devices with their start and end apart: 5, of which 3 were waited for; matrix products, arithmetic and copies ran while one was open for 8% of the time, Pallas kernels for 9%

profile of v1, /device:TPU:0, one launch (start us, length us, event | category | flops | bytes accessed | tf_op | source)
XLA Modules:
  0.0 743.0 jit_solution(14124422177560453826)
XLA Ops:
  14.0 33.0 %all_gather.16 = s32[4096,26]{0,1:T(8,128)S(1)} all-gather(s32[512,26]{0,1:T(8,128)S(1)} %add_select_fusion), channel_id=1, replica_groups=mesh['tab'=8,'rep'=4] {'tab'}, dimensions={0}, use_global_device_ids=true | all-gather | bytes 479232 | tf_op jit(solution)/shard_map/all_gather | solution.py:196
  47.8 73.3 %lookup.1 = bf16[5,39,4096]{2,1,0:T(8,128)(2,1)S(1)} custom-call(s32[5]{0:T(128)S(1)} %get-tuple-element.81.group_ref, s32[5,1,4096]{2,1,0:T(1,128)S(1)} %broadcast_select_fusion.1.ids_ref, bf16[5,39,32768]{2,1,0:T(8,128)(2,1)} %table_ref.1), custom_call_target="tpu_custom_call" | custom-call | flops 64424509440 | bytes 14376960 | tf_op jit(solution)/shard_map/lookup/pallas_call | solution.py:60
  122.3 8.6 %copy.39 = bf16[5,39,4096]{1,0,2:T(8,128)(2,1)} copy(bf16[5,39,4096]{2,1,0:T(8,128)(2,1)} %copy-done.2) | data formatting | bytes 3194880 | tf_op jit(solution)/shard_map/lookup/pallas_call | solution.py:60
  131.0 11.4 %reshape.195 = bf16[8,2,49920]{2,1,0:T(2,128)(2,1)} reshape(bf16[4096,5,39]{2,1,0:T(8,128)(2,1)} %bitcast.73) | data formatting | bytes 3194880
  142.4 18.3 %all-to-all-start = ((bf16[8,2,49920]{2,1,0:T(2,128)(2,1)}), bf16[8,2,49920]{2,1,0:T(2,128)(2,1)}, u32[]{:S(2)}, u32[]{:S(2)}) async-start(bf16[8,2,49920]{2,1,0:T(2,128)(2,1)} %reshape.195), calls=%async_computation | async-start | bytes 3194880 | tf_op jit(solution)/shard_map/all_to_all | solution.py:204
  161.7 32.6 %all-to-all-done = bf16[8,2,49920]{2,1,0:T(2,128)(2,1)} async-done(((bf16[8,2,49920]{2,1,0:T(2,128)(2,1)}), bf16[8,2,49920]{2,1,0:T(2,128)(2,1)}, u32[]{:S(2)}, u32[]{:S(2)}) %all-to-all-start) | async-done | bytes 1597472 | tf_op jit(solution)/shard_map/all_to_all | solution.py:204
  194.3 11.1 %reshape.196 = bf16[4096,5,39]{2,1,0:T(8,128)(2,1)} reshape(bf16[8,2,49920]{2,1,0:T(2,128)(2,1)} %all-to-all-done) | data formatting | bytes 3194880
  205.4 8.9 %copy.40 = bf16[5,39,8,512]{3,1,0,2:T(8,128)(2,1)} copy(bf16[5,39,8,512]{1,0,3,2:T(8,128)(2,1)} %bitcast.74) | data formatting | bytes 3194880 | tf_op jit(solution)/shard_map/all_to_all | solution.py:204
  220.8 4.0 convolution_add_fusion.5
  226.9 3.3 fusion.10
  240.0 3.8 fusion.43
  243.8 3.3 multiply_add_fusion
  247.2 4.7 convert_reduce_fusion.2
  251.9 4.1 convolution_add_fusion
  261.6 3.6 scatter_fusion
  265.2 51.7 %all_to_all.33 = bf16[40,39,512]{2,1,0:T(8,128)(2,1)S(1)} all-to-all(bf16[40,39,512]{2,1,0:T(8,128)(2,1)S(1)} %scatter_fusion), channel_id=1, replica_groups=mesh['tab'=8,'rep'=4] {'tab'}, dimensions={0} | all-to-all | bytes 3194880 | tf_op jit(solution)/shard_map/all_to_all | solution.py:267
  317.5 2.1 all_gather.19
  320.1 55.6 %reduce-scatter.2.cloned.1.call-done = f32[32,1027]{1,0:T(8,128)} async-done(((f32[1024,1027]{1,0:T(8,128)}), f32[32,1027]{1,0:T(8,128)}) %reduce-scatter.2.cloned.1.call-update) | async-done | bytes 131472 | tf_op jit(solution)/shard_map/reduce_scatter | solution.py:273
  375.8 5.3 convolution_bitcast_fusion
  381.0 3.8 convolution_bitcast_fusion.2
  384.9 4.0 convolution_bitcast_fusion.1
  388.9 3.4 fusion.41
  392.3 11.4 %pad_maximum_fusion = f32[3,1027,1027]{2,1,0:T(8,128)} fusion(f32[1,1027,1027]{2,1,0:T(8,128)} %convolution_bitcast_fusion, f32[1,1027,1027]{2,1,0:T(8,128)} %convolution_bitcast_fusion.1, f32[1,1027,1027]{2,1,0:T(8,128)} %convolution_bitcast_fusion.2), kind=kLoop, calls=%fused_computation.4 | loop fusion | flops 6328374 | bytes 25313496 | tf_op jit(solution)/shard_map/stack | solution.py:277
  404.7 6.5 all_gather.18
  411.6 3.4 convolution_reduce_fusion
  415.0 3.1 fusion.25
  418.9 42.1 %all-reduce = (f32[]{:T(128)}, f32[3,1027]{1,0:T(4,128)}, f32[1024]{0:T(1024)}, f32[1024]{0:T(1024)}, f32[2051]{0:T(1024)}, /*index=5*/f32[]{:T(128)}) all-reduce(f32[]{:T(128)} %fusion.32, f32[3,1027]{1,0:T(4,128)S(1)} %pad_maximum_fusion.2, f32[1024]{0:T(1024)S(1)} %get-tuple-element.88, ...), channel_id=1, replica_groups=mesh['tab'=8,'rep'=4] {'tab','rep'}, use_global_device_ids=true, to_apply=%region_3.4 | all-reduce | flops 7182 | bytes 57456 | tf_op jit(solution)/shard_map/psum | solution.py:288
  463.0 68.0 %add_rows.1 = f32[5,39,8192]{2,1,0:T(8,128)} custom-call(s32[1]{0:T(128)} %bitcast.16.base_ref, s32[4,5,1,4096]{3,2,1,0:T(1,128)S(1)} %copy.43.ids_ref, bf16[4,5,39,4096]{3,2,1,0:T(8,128)(2,1)} %all-gather.5.cloned.1.call-done.grad_ref), custom_call_target="tpu_custom_call" | custom-call | flops 52344913920 | bytes 12779520 | tf_op jit(solution)/shard_map/add_rows/pallas_call | solution.py:121
  531.0 5.9 copy.44
  536.9 181.1 %all-reduce.4.cloned.1.call-done = (f32[3,1027,1027]{2,1,0:T(8,128)}, f32[1024,1024]{1,0:T(8,128)}) async-done(((f32[3,1027,1027]{2,1,0:T(8,128)}, f32[1024,1024]{1,0:T(8,128)}), (f32[3,1027,1027]{2,1,0:T(8,128)}, f32[1024,1024]{1,0:T(8,128)})) %all-reduce.4.cloned.1.call-update) | async-done | bytes 16851068 | tf_op jit(solution)/shard_map/psum | solution.py:288
  718.0 11.5 %copy.51 = f32[3,1027,1027]{2,1,0:T(8,128)} copy(f32[3,1027,1027]{2,1,0:T(8,128)} %get-tuple-element.93) | data formatting | bytes 25313496
  729.5 4.8 copy.52
  (139 shorter events, 36.3 us)
Async XLA Ops:
  8.0 211.2 %copy-start = (bf16[1024,1027]{0,1:T(8,128)(2,1)S(1)}, bf16[1024,1027]{0,1:T(8,128)(2,1)}, u32[]{:S(2)}) copy-start(bf16[1024,1027]{0,1:T(8,128)(2,1)} %param.22) | copy-start | bytes 6309892
  11.1 110.1 %copy-start.30 = (pred[5]{0:T(512)(128)(4,1)}, pred[5]{0:T(512)(128)(4,1)S(1)}, u32[]{:S(2)}) copy-start(pred[5]{0:T(512)(128)(4,1)S(1)} %get-tuple-element.79) | copy-start | bytes 19
  47.6 73.6 %copy-start.20 = (s32[5,4096]{1,0:T(8,128)}, s32[5,4096]{1,0:T(8,128)S(1)}, u32[]{:S(2)}) copy-start(s32[5,4096]{1,0:T(8,128)S(1)} %gather_fusion.1) | copy-start | bytes 245764
  47.7 73.5 %copy-start.32 = (pred[5]{0:T(512)(128)(4,1)}, pred[5]{0:T(512)(128)(4,1)S(1)}, u32[]{:S(2)}) copy-start(pred[5]{0:T(512)(128)(4,1)S(1)} %get-tuple-element.82) | copy-start | bytes 19
  142.4 18.4 %copy-start.26 = (bf16[2051]{0:T(1024)(128)(2,1)S(1)}, bf16[2051]{0:T(1024)(128)(2,1)}, u32[]{:S(2)}) copy-start(bf16[2051]{0:T(1024)(128)(2,1)} %param.26) | copy-start | bytes 12310
  142.4 19.2 %copy-start.34 = (bf16[1024]{0:T(1024)(128)(2,1)S(1)}, bf16[1024]{0:T(1024)(128)(2,1)}, u32[]{:S(2)}) copy-start(bf16[1024]{0:T(1024)(128)(2,1)} %param.23) | copy-start | bytes 6148
  142.4 19.2 %copy-start.35 = (bf16[1024]{0:T(1024)(128)(2,1)S(1)}, bf16[1024]{0:T(1024)(128)(2,1)}, u32[]{:S(2)}) copy-start(bf16[1024]{0:T(1024)(128)(2,1)} %param.25) | copy-start | bytes 6148
  142.4 19.3 %copy-start.37 = (s32[26]{0:T(128)S(1)}, s32[26]{0:T(128)}, u32[]{:S(2)}) copy-start(s32[26]{0:T(128)} %param.16) | copy-start | bytes 316
  142.4 19.3 %copy-start.27 = (bf16[3,1027]{1,0:T(4,128)(2,1)S(1)}, bf16[3,1027]{1,0:T(4,128)(2,1)}, u32[]{:S(2)}) copy-start(bf16[3,1027]{1,0:T(4,128)(2,1)} %param.21) | copy-start | bytes 18490
  142.4 51.9 %all-to-all-start = ((bf16[8,2,49920]{2,1,0:T(2,128)(2,1)}), bf16[8,2,49920]{2,1,0:T(2,128)(2,1)}, u32[]{:S(2)}, u32[]{:S(2)}) async-start(bf16[8,2,49920]{2,1,0:T(2,128)(2,1)} %reshape.195), calls=%async_computation | async-start | bytes 3194880 | tf_op jit(solution)/shard_map/all_to_all | solution.py:204
  160.7 215.0 %reduce-scatter.2.cloned.1.call-start = ((), (), s32[]{:S(2)}) async-start(), calls=%async_computation.3 | async-start | bytes 4866048 | tf_op jit(solution)/shard_map/reduce_scatter | solution.py:273
  219.2 5.7 slice-start
  220.8 16.2 %copy-start.17 = (f32[512,1024]{1,0:T(8,128)}, f32[512,1024]{1,0:T(8,128)S(1)}, u32[]{:S(2)}) copy-start(f32[512,1024]{1,0:T(8,128)S(1)} %fusion.44) | copy-start | bytes 6291460
  220.8 4.1 slice-start.1
  226.9 3.4 copy-start.11
  230.3 3.7 copy-start.6
  236.1 182.1 %copy-start.29 = (f32[512]{0:T(512)}, f32[512]{0:T(512)S(1)}, u32[]{:S(2)}) copy-start(f32[512]{0:T(512)S(1)} %get-tuple-element.91) | copy-start | bytes 6148
  243.8 219.2 %all-gather.5.cloned.1.call-start = ((), (), s32[]{:S(2)}) async-start(), calls=%async_computation.5 | async-start | bytes 8192000 | tf_op jit(solution)/shard_map/all_gather | solution.py:269
  247.2 8.9 %copy-start.7 = (f32[512,1027]{0,1:T(8,128)}, f32[512,1027]{0,1:T(8,128)S(1)}, u32[]{:S(2)}) copy-start(f32[512,1027]{0,1:T(8,128)S(1)} %multiply_add_fusion) | copy-start | bytes 6309892
  251.8 4.2 copy-start.9
  251.8 4.2 copy-start.4
  251.9 4.2 copy-start.12
  251.9 4.5 copy-start.13
  251.9 4.8 copy-start.16
  319.7 211.4 %all-gather.3.cloned.1.call-start = ((), (), s32[]{:S(2)}) async-start(), calls=%async_computation.4 | async-start | bytes 4866048 | tf_op jit(solution)/shard_map/all_gather | solution.py:276
  375.7 342.3 %all-reduce.4.cloned.1.call-start = ((), (), s32[]{:S(2)}) async-start(), calls=%async_computation.6 | async-start | bytes 36921344 | tf_op jit(solution)/shard_map/psum | solution.py:288
  375.8 5.3 copy-start.10
  381.0 3.8 copy-start.5
  381.0 3.8 copy-start.8
  384.9 4.0 copy-start.18
  384.9 4.0 copy-start.24
  718.0 16.2 %copy-start.1 = (bf16[1024,1027]{0,1:T(8,128)(2,1)S(1)}, bf16[1024,1027]{0,1:T(8,128)(2,1)}, u32[]{:S(2)}) copy-start(bf16[1024,1027]{0,1:T(8,128)(2,1)} %param.22) | copy-start | bytes 6309892
  (13 other events, 22.4 us)
Sparse Core Ops, SparseCore 0:
  243.9 131.7 reduce-scatter.1
  403.8 314.1 all-reduce.3
Sparse Core Ops, SparseCore 1:
  319.7 46.5 all-gather.4
  375.8 83.1 all-gather.2

commit v2 on v1

v2 whole, which is shorter than its diff:
```python
import functools

import jax
import jax.numpy as jnp
from jax import lax
from jax.experimental import pallas as pl
from jax.experimental.pallas import tpu as pltpu
from jax.sharding import PartitionSpec as P

BF = jnp.bfloat16
F32 = jnp.float32
I32 = jnp.int32
LOOK_LOW = 512
LOOK_GROUP = 8
ADD_LOW = 512
MAIN = 1024
CHUNK = 384
PIECE = 32
MIB = 1024 * 1024
NT = (((1,), (1,)), ((), ()))
TN = (((0,), (0,)), ((), ()))


def round_up(size, unit):
    return -(-size // unit) * unit


def params(mib):
    return pltpu.CompilerParams(vmem_limit_bytes=mib * MIB)


def cost(flops, size):
    return pl.CostEstimate(flops=flops, bytes_accessed=size, transcendentals=0)


def swap(value, axis, mask):
    return lax.ppermute(value, axis, [(at, at ^ mask) for at in range(lax.axis_size(axis))])


def masks_of(axis):
    size = lax.axis_size(axis)
    return [1 << bit for bit in range(size.bit_length() - 1)]


def lookup_kernel(group_ref, ids_ref, table_ref, out_ref, stack):
    slot = pl.program_id(0)
    embed_dim = table_ref.shape[1]
    block_count, pad_dim, low_count = stack.shape
    cols = out_ref.shape[3]

    @pl.when(pl.program_id(1) == 0)
    def _():
        for block in range(block_count):
            stack[block, :embed_dim, :] = table_ref[0, :, block * low_count : (block + 1) * low_count]

    picked = ids_ref[0, 0]
    high = lax.shift_right_arithmetic(picked, low_count.bit_length() - 1)
    low = picked & (low_count - 1)
    low_iota = lax.broadcasted_iota(I32, (low_count, cols), 0)
    onehot = jnp.where(low_iota == low, 1.0, 0.0).astype(BF)
    rows_kept = round_up(embed_dim, 8)

    def step(group, total):
        left = stack[pl.ds(group * LOOK_GROUP, LOOK_GROUP)].reshape(LOOK_GROUP * pad_dim, low_count)
        partial = jnp.dot(left, onehot, preferred_element_type=F32)
        for at in range(LOOK_GROUP):
            rows = partial[at * pad_dim : at * pad_dim + rows_kept]
            total = total + jnp.where(high == group * LOOK_GROUP + at, rows, 0.0)
        return total

    total = lax.fori_loop(0, group_ref[slot], step, jnp.zeros((rows_kept, cols), F32))
    out_ref[0, 0] = total[:embed_dim].astype(BF)


def lookup(tables, wanted, own_rows):
    slot_count, embed_dim, table_len = tables.shape
    tab_count, _, count = wanted.shape
    pad_dim = round_up(embed_dim, 16)
    unit = LOOK_LOW * LOOK_GROUP
    groups = (own_rows + unit - 1) // unit
    return pl.pallas_call(
        lookup_kernel,
        grid_spec=pltpu.PrefetchScalarGridSpec(
            num_scalar_prefetch=1,
            grid=(slot_count, tab_count),
            in_specs=[
                pl.BlockSpec((1, 1, 1, count), lambda s, t, *_: (t, s, 0, 0)),
                pl.BlockSpec((1, embed_dim, table_len), lambda s, t, *_: (s, 0, 0)),
            ],
            out_specs=pl.BlockSpec((1, 1, embed_dim, count), lambda s, t, *_: (t, s, 0, 0)),
            scratch_shapes=[pltpu.VMEM((table_len // LOOK_LOW, pad_dim, LOOK_LOW), BF)],
        ),
        out_shape=jax.ShapeDtypeStruct((tab_count, slot_count, embed_dim, count), BF),
        compiler_params=params(48),
        cost_estimate=cost(
            2 * slot_count * tab_count * count * table_len * pad_dim,
            2 * slot_count * embed_dim * (table_len + tab_count * count),
        ),
        name="lookup",
    )(groups, wanted[:, :, None, :], tables)


def add_kernel(part_count, base_ref, *refs):
    ids_refs = refs[:part_count]
    grad_refs = refs[part_count : 2 * part_count]
    out_ref, total = refs[-2:]
    step = pl.program_id(0)
    embed_dim, cols = grad_refs[0].shape[2:]
    high_count = total.shape[1] // embed_dim

    @pl.when(step == 0)
    def _():
        total[...] = jnp.zeros_like(total)

    high_iota = lax.broadcasted_iota(I32, (high_count, cols), 0)
    low_iota = lax.broadcasted_iota(I32, (ADD_LOW, cols), 0)
    product = None
    for ids_ref, grad_ref in zip(ids_refs, grad_refs):
        local = ids_ref[0, 0] - base_ref[0]
        high = lax.shift_right_arithmetic(local, ADD_LOW.bit_length() - 1)
        low = local & (ADD_LOW - 1)
        high_hot = jnp.where(high_iota == high, 1.0, 0.0)
        low_hot = jnp.where(low_iota == low, 1.0, 0.0).astype(BF)
        grads = grad_ref[0, 0].astype(F32)
        left = (grads[:, None, :] * high_hot[None, :, :]).astype(BF)
        left = left.reshape(embed_dim * high_count, cols)
        term = lax.dot_general(left, low_hot, NT, preferred_element_type=F32)
        product = term if product is None else product + term
    for lane in range(ADD_LOW // 128):
        total[lane] += product[:, lane * 128 : (lane + 1) * 128]

    @pl.when(step == pl.num_programs(0) - 1)
    def _():
        for at in range(high_count):
            for part in range(0, embed_dim, 8):
                size = min(8, embed_dim - part)
                for lane in range(ADD_LOW // 128):
                    first = at * ADD_LOW + lane * 128
                    out_ref[0, part : part + size, first : first + 128] = total[
                        lane, pl.ds(part * high_count + at, size, stride=high_count), :
                    ]


def add_rows(grads, wanted, base, share, slot, so_far):
    tab_count, slot_count, embed_dim, count = grads[0].shape
    part_count = len(grads)
    whole = [] if so_far is None else [so_far]
    return pl.pallas_call(
        functools.partial(add_kernel, part_count),
        grid=(tab_count,),
        in_specs=[pl.BlockSpec(memory_space=pltpu.SMEM)]
        + [pl.BlockSpec((1, 1, 1, count), lambda t: (t, slot, 0, 0))] * part_count
        + [pl.BlockSpec((1, 1, embed_dim, count), lambda t: (t, slot, 0, 0))] * part_count
        + [pl.BlockSpec(memory_space=pl.ANY)] * len(whole),
        out_specs=pl.BlockSpec((1, embed_dim, share), lambda t: (slot, 0, 0)),
        scratch_shapes=[pltpu.VMEM((ADD_LOW // 128, embed_dim * (share // ADD_LOW), 128), F32)],
        out_shape=jax.ShapeDtypeStruct((slot_count, embed_dim, share), F32),
        input_output_aliases={} if so_far is None else {1 + 2 * part_count: 0},
        compiler_params=params(40),
        cost_estimate=cost(
            2 * part_count * tab_count * count * share * embed_dim,
            2 * embed_dim * (2 * share + part_count * tab_count * count),
        ),
        name="add_rows",
    )(base, *[part[:, :, None, :] for part in wanted], *grads, *whole)


def row_sums(value):
    part = value[:, :128]
    for first in range(128, value.shape[1], 128):
        part = part + value[:, first : first + 128]
    return jnp.sum(part.T, axis=0, keepdims=True)


def dense_kernel(
    dense_width,
    place_ref,
    bias_ref,
    arrived_ref,
    dense_ref,
    label_ref,
    weight_hbm,
    cols_ref,
    logits_ref,
    dense_grad_ref,
    slots_ref,
    left_ref,
    right_ref,
    sums_ref,
    weight,
    anchor,
    current,
    update,
    first_pre,
    second_pre,
    grad_anchor,
    grad_current,
    sems,
):
    layer_count = update.shape[0]
    tower1, tower2 = layer_count, layer_count + 1
    field_count = place_ref.shape[0]
    embed_dim = arrived_ref.shape[1]
    width = dense_width + field_count * embed_dim
    size, cols = anchor.shape
    spans = [pl.ds(first, CHUNK) for first in range(0, size, CHUNK)]
    copies = [
        pltpu.make_async_copy(weight_hbm.at[at], weight.at[at], sems.at[at])
        for at in range(layer_count + 2)
    ]
    for copy in copies:
        copy.start()

    def column(at, span):
        return cols_ref[span, at : at + 1]

    def times(at, span, operand):
        return jnp.dot(weight[at, span, :], operand[...], preferred_element_type=F32)

    def transposed_times(at, span, operand):
        return lax.dot_general(weight[at, :, span], operand[...], TN, preferred_element_type=F32)

    anchor[0:16] = dense_ref[...]
    tail = width // 8 * 8
    anchor[tail:] = jnp.zeros((size - tail, cols), F32)
    for field in range(field_count):
        first = dense_width + field * embed_dim
        anchor[first : first + embed_dim] = arrived_ref[place_ref[field]].astype(F32)
    for span in spans:
        left_ref[0, span] = anchor[span].astype(BF)
        right_ref[tower1, span] = anchor[span].astype(BF)
    for layer in range(layer_count):
        copies[layer].wait()
        for span in spans:
            value = transposed_times(layer, span, left_ref.at[layer]) + column(layer, span)
            update[layer, span] = value
            before = anchor if layer == 0 else current
            after = anchor[span] * value + before[span]
            current[span] = after
            if layer + 1 < layer_count:
                left_ref[layer + 1, span] = after.astype(BF)
    copies[tower1].wait()
    for span in spans:
        value = times(tower1, span, left_ref.at[0]) + column(tower1, span)
        first_pre[span] = value
        left_ref[tower2, span] = (value * jax.nn.sigmoid(value)).astype(BF)
    copies[tower2].wait()
    logits = jnp.full((1, cols), bias_ref[0], F32)
    for span in spans:
        value = transposed_times(tower2, span, left_ref.at[tower2]) + column(tower2, span)
        second_pre[span] = value
        act = value * jax.nn.sigmoid(value)
        terms = current[span] * column(layer_count + 2, span) + act * column(layer_count + 3, span)
        logits = logits + jnp.sum(terms, axis=0, keepdims=True)
    logits_ref[...] = logits
    target = label_ref[...]
    residue = jax.nn.sigmoid(logits) - target
    softplus = jnp.maximum(logits, 0.0) + jnp.log1p(jnp.exp(-jnp.abs(logits)))
    sums_ref[layer_count + 4 :, :] = jnp.zeros((sums_ref.shape[0] - layer_count - 4, size), F32)
    loss_row = jnp.sum(softplus - target * logits, axis=1, keepdims=True)
    bias_row = jnp.sum(residue, axis=1, keepdims=True)
    sums_ref[layer_count + 4 : layer_count + 5, 0:128] = jnp.broadcast_to(loss_row, (1, 128))
    sums_ref[layer_count + 4 : layer_count + 5, 128:256] = jnp.broadcast_to(bias_row, (1, 128))
    for span in spans:
        value = second_pre[span]
        sig = jax.nn.sigmoid(value)
        act = value * sig
        grad = residue * column(layer_count + 3, span) * (sig * (1.0 + value * (1.0 - sig)))
        low = grad.astype(BF)
        right_ref[tower2, span] = low
        sums_ref[tower2 : tower2 + 1, span] = row_sums(low.astype(F32))
        sums_ref[layer_count + 3 : layer_count + 4, span] = row_sums(residue * act)
        sums_ref[layer_count + 2 : layer_count + 3, span] = row_sums(residue * current[span])
        grad_current[span] = residue * column(layer_count + 2, span)
    for span in spans:
        value = first_pre[span]
        sig = jax.nn.sigmoid(value)
        grad = times(tower2, span, right_ref.at[tower2]) * (sig * (1.0 + value * (1.0 - sig)))
        low = grad.astype(BF)
        left_ref[tower1, span] = low
        sums_ref[tower1 : tower1 + 1, span] = row_sums(low.astype(F32))
    for span in spans:
        grad_anchor[span] = transposed_times(tower1, span, left_ref.at[tower1])
    for layer in reversed(range(layer_count)):
        for span in spans:
            grad = grad_current[span]
            low = (anchor[span] * grad).astype(BF)
            right_ref[layer, span] = low
            sums_ref[layer : layer + 1, span] = row_sums(low.astype(F32))
            grad_anchor[span] += grad * update[layer, span]
        for span in spans:
            grad_current[span] += times(layer, span, right_ref.at[layer])
    for span in spans:
        grad_anchor[span] += grad_current[span]
    dense_grad_ref[...] = grad_anchor[0:16]
    slots_ref[...] = jnp.zeros_like(slots_ref)
    for field in range(field_count):
        first = dense_width + field * embed_dim
        slots_ref[place_ref[field]] = grad_anchor[first : first + embed_dim].astype(BF)


def dense_step(arrived, place, dense_in, labels, weights, cols, out_b, layer_count):
    slot_count, embed_dim, count = arrived.shape
    dense_width = dense_in.shape[1]
    size = weights.shape[1]
    matrix_count = layer_count + 2
    dense_rows = jnp.pad(dense_in.T.astype(F32), ((0, 16 - dense_width), (0, 0)))
    vmem = pl.BlockSpec(memory_space=pltpu.VMEM)
    smem = pl.BlockSpec(memory_space=pltpu.SMEM)
    flat = pltpu.VMEM((size, count), F32)
    return pl.pallas_call(
        functools.partial(dense_kernel, dense_width),
        in_specs=[smem, smem, vmem, vmem, vmem, pl.BlockSpec(memory_space=pl.ANY), vmem],
        out_specs=[vmem] * 6,
        out_shape=[
            jax.ShapeDtypeStruct((1, count), F32),
            jax.ShapeDtypeStruct((16, count), F32),
            jax.ShapeDtypeStruct((slot_count, embed_dim, count), BF),
            jax.ShapeDtypeStruct((matrix_count, size, count), BF),
            jax.ShapeDtypeStruct((matrix_count, size, count), BF),
            jax.ShapeDtypeStruct((8, size), F32),
        ],
        scratch_shapes=[
            pltpu.VMEM(weights.shape, BF),
            flat,
            flat,
            pltpu.VMEM((layer_count, size, count), F32),
            flat,
            flat,
            flat,
            flat,
            pltpu.SemaphoreType.DMA((matrix_count,)),
        ],
        compiler_params=params(60),
        cost_estimate=cost(4 * matrix_count * size * size * count, 2 * weights.size + 30 * size * count),
        name="dense",
    )(
        place,
        out_b.astype(F32).reshape(1),
        arrived,
        dense_rows,
        labels.astype(F32).reshape(1, count),
        weights,
        cols,
    )


def weight_kernel(own_ref, left_ref, right_ref, keep_ref, send_ref, strip_ref, moved):
    pieces = MAIN // PIECE
    for at in range(pieces):
        first = pl.multiple_of((at ^ own_ref[0]) * PIECE, PIECE)
        moved[at * PIECE : (at + 1) * PIECE] = left_ref[0, pl.ds(first, PIECE), :]
    half = MAIN // 2
    right = right_ref[0, :MAIN, :]
    keep_ref[0] = lax.dot_general(moved[:half], right, NT, preferred_element_type=F32)
    send_ref[0] = lax.dot_general(moved[half:], right, NT, preferred_element_type=F32).astype(BF)
    below = lax.dot_general(left_ref[0, MAIN : MAIN + 16, :], right_ref[0], NT, preferred_element_type=F32)
    beside = lax.dot_general(right_ref[0, MAIN : MAIN + 16, :], left_ref[0], NT, preferred_element_type=F32)
    strip_ref[0, 0:3] = below[0:3]
    strip_ref[0, 3:6] = beside[0:3]
    strip_ref[0, 6:8] = jnp.zeros((2, strip_ref.shape[2]), F32)


def weight_parts(left, right, own):
    matrix_count, size, count = left.shape
    half = MAIN // 2
    return pl.pallas_call(
        weight_kernel,
        grid=(matrix_count,),
        in_specs=[
            pl.BlockSpec(memory_space=pltpu.SMEM),
            pl.BlockSpec((1, size, count), lambda m: (m, 0, 0)),
            pl.BlockSpec((1, size, count), lambda m: (m, 0, 0)),
        ],
        out_specs=[
            pl.BlockSpec((1, half, MAIN), lambda m: (m, 0, 0)),
            pl.BlockSpec((1, half, MAIN), lambda m: (m, 0, 0)),
            pl.BlockSpec((1, 8, size), lambda m: (m, 0, 0)),
        ],
        out_shape=[
            jax.ShapeDtypeStruct((matrix_count, half, MAIN), F32),
            jax.ShapeDtypeStruct((matrix_count, half, MAIN), BF),
            jax.ShapeDtypeStruct((matrix_count, 8, size), F32),
        ],
        scratch_shapes=[pltpu.VMEM((MAIN, count), BF)],
        compiler_params=params(40),
        cost_estimate=cost(2 * matrix_count * size * size * count, 10 * matrix_count * size * size),
        name="weight_parts",
    )(own, left, right)


def reduce_main(keep, send, swapped):
    total = keep + swap(send, "rep", 1).astype(F32)
    pair = [("rep", 2, 1), ("tab", 1, 2)]
    if swapped:
        pair = [pair[1], pair[0]]
    (axis, mask, dim) = pair[0]
    total = lax.index_in_dim(total, 0, dim, False) + swap(
        lax.index_in_dim(total, 1, dim, False).astype(BF), axis, mask
    ).astype(F32)
    (axis, mask, _) = pair[1]
    total = total[:, 0] + swap(total[:, 1].astype(BF), axis, mask).astype(F32)
    kept = total[:, 0, 0]
    for high, low in ((0, 1), (1, 0), (1, 1)):
        kept = kept + swap(total[:, high, low].astype(BF), "tab", 4 * high + 2 * low).astype(F32)
    piece = kept.astype(BF)
    for axis, known in (("rep", 2), ("tab", 3)):
        for mask in masks_of(axis)[known:]:
            piece = (piece.astype(F32) + swap(piece, axis, mask).astype(F32)).astype(BF)
    return piece


def gather_main(piece, swapped):
    low = jnp.stack([piece, swap(piece, "tab", 2)], axis=1)
    high = jnp.stack([swap(piece, "tab", 4), swap(piece, "tab", 6)], axis=1)
    value = jnp.stack([low, high], axis=1)
    pair = [("rep", 2, 1), ("tab", 1, 2)]
    if swapped:
        pair = [pair[1], pair[0]]
    (axis, mask, _) = pair[1]
    value = jnp.stack([value, swap(value, axis, mask)], axis=1)
    (axis, mask, dim) = pair[0]
    value = jnp.stack([value, swap(value, axis, mask)], axis=dim)
    value = value.reshape((value.shape[0], MAIN // PIECE // 2) + value.shape[-2:])
    return value, swap(value, "rep", 1)


def assemble_kernel(layer_count, chunk_count, own_ref, *refs):
    chunks = refs[: 2 * chunk_count]
    strip_ref, cross_ref, first_ref, second_ref = refs[2 * chunk_count :]
    matrix = pl.program_id(0)
    lanes_count = chunk_count // 2

    def fill(out_ref):
        for chunk in range(chunk_count):
            above, lane = divmod(chunk, lanes_count)
            for core in range(2):
                ref = chunks[2 * chunk + core]
                count, rows, lanes = ref.shape[1:]
                for at in range(count):
                    piece = (core * count + at) ^ own_ref[0]
                    first = pl.multiple_of(piece * PIECE + above * rows, rows)
                    out_ref[0, pl.ds(first, rows), lane * lanes : (lane + 1) * lanes] = ref[
                        0, at
                    ].astype(F32)
        height, width = out_ref.shape[1:]
        if width > MAIN:
            extra = width - MAIN
            for first in range(0, MAIN, 128):
                turned = strip_ref[0, :, first : first + 128].T
                out_ref[0, first : first + 128, MAIN:] = turned[:, 3 : 3 + extra]
        if height > MAIN:
            out_ref[0, MAIN:, :] = strip_ref[0, 0 : height - MAIN, :width]

    @pl.when(matrix < layer_count)
    def _():
        fill(cross_ref)

    @pl.when(matrix == layer_count)
    def _():
        fill(first_ref)

    @pl.when(matrix == layer_count + 1)
    def _():
        fill(second_ref)


def assemble(chunks, strips, own, layer_count, width, hidden):
    matrix_count = layer_count + 2
    size = strips.shape[2]
    specs = []
    for chunk in chunks:
        specs.append(pl.BlockSpec((1,) + chunk.shape[1:], lambda m: (m, 0, 0, 0)))
    return pl.pallas_call(
        functools.partial(assemble_kernel, layer_count, len(chunks) // 2),
        grid=(matrix_count,),
        in_specs=[pl.BlockSpec(memory_space=pltpu.SMEM)]
        + specs
        + [pl.BlockSpec((1, 8, size), lambda m: (m, 0, 0))],
        out_specs=[
            pl.BlockSpec((1, width, width), lambda m: (jnp.minimum(m, layer_count - 1), 0, 0)),
            pl.BlockSpec((1, hidden, width), lambda m: (0, 0, 0)),
            pl.BlockSpec((1, hidden, hidden), lambda m: (0, 0, 0)),
        ],
        out_shape=[
            jax.ShapeDtypeStruct((layer_count, width, width), F32),
            jax.ShapeDtypeStruct((1, hidden, width), F32),
            jax.ShapeDtypeStruct((1, hidden, hidden), F32),
        ],
        compiler_params=params(56),
        cost_estimate=cost(0, 6 * matrix_count * size * size),
        name="assemble",
    )(own, *chunks, strips)


def on_device(
    ids,
    table_rows,
    table_place,
    dense_in,
    labels,
    tables,
    cross_w,
    cross_b,
    tower1_w,
    tower1_b,
    tower2_w,
    tower2_b,
    out_w,
    out_b,
):
    tab_count = lax.axis_size("tab")
    rep_count = lax.axis_size("rep")
    slot_count, embed_dim, table_len = tables.shape
    row_count, dense_width = dense_in.shape
    field_count = ids.shape[1]
    layer_count, width = cross_w.shape[:2]
    hidden = tower1_w.shape[0]
    size = round_up(width, 128)
    all_slots = slot_count * tab_count
    tab_at = lax.axis_index("tab")
    rep_at = lax.axis_index("rep")

    matches = table_place[:, None] == jnp.arange(all_slots, dtype=I32)[None, :]
    effective = ids % table_rows[None, :]
    by_slot = jnp.sum(jnp.where(matches[:, :, None], effective.T[:, None, :], 0), axis=0)
    slot_rows = jnp.sum(jnp.where(matches, table_rows[:, None], 0), axis=0)
    own_rows = lax.dynamic_slice_in_dim(slot_rows, tab_at * slot_count, slot_count)
    wanted = lax.all_to_all(
        by_slot.reshape(tab_count, slot_count, row_count), "tab", split_axis=0, concat_axis=0, tiled=True
    )

    def padded(weight):
        return jnp.pad(weight, ((0, size - weight.shape[0]), (0, size - weight.shape[1])))

    weights = jnp.stack(
        [padded(cross_w[at]) for at in range(layer_count)] + [padded(tower1_w), padded(tower2_w)]
    )
    vectors = [cross_b[at] for at in range(layer_count)]
    vectors += [tower1_b, tower2_b, out_w[:width], out_w[width:], out_w[:0]]
    cols = jnp.stack([jnp.pad(v.astype(F32), (0, size - v.shape[0])) for v in vectors], axis=1)

    looked = lookup(tables, wanted, own_rows)
    arrived = lax.all_to_all(looked, "tab", split_axis=0, concat_axis=0, tiled=True)
    arrived = arrived.reshape(all_slots, embed_dim, row_count)
    logits, dense_grad, slots, left, right, sums = dense_step(
        arrived, table_place, dense_in, labels, weights, cols, out_b, layer_count
    )
    returned = lax.all_to_all(
        slots.reshape(tab_count, slot_count, embed_dim, row_count),
        "tab",
        split_axis=0,
        concat_axis=0,
        tiled=True,
    )

    def spread(own):
        parts = [own]
        for mask in reversed(masks_of("rep")):
            parts = parts + [swap(part, "rep", mask) for part in parts]
        return parts

    wanted_parts = spread(wanted)
    grad_parts = spread(returned)
    share = table_len // rep_count
    base = (rep_at * share).astype(I32).reshape(1)
    table_grad = None
    for slot in range(slot_count):
        table_grad = add_rows(grad_parts, wanted_parts, base, share, slot, table_grad)

    bits = [rep_at & 1, (rep_at >> 1) & 1, tab_at & 1, (tab_at >> 2) & 1, (tab_at >> 1) & 1]
    own = sum(bit << (4 - at) for at, bit in enumerate(bits)).astype(I32).reshape(1)
    keep, send, strips = weight_parts(left, right, own)
    matrix_count = layer_count + 2
    parts = (matrix_count, 2, 2, 2, 2, 2, PIECE // 2, 2, MAIN // 2)
    keep = keep.reshape(parts)
    send = send.reshape(parts)
    chunks = []
    for chunk in range(4):
        above, lane = divmod(chunk, 2)
        swapped = lane == 1
        piece = reduce_main(keep[..., above, :, lane, :], send[..., above, :, lane, :], swapped)
        chunks.extend(gather_main(piece, swapped))

    small = jnp.concatenate([strips.reshape(matrix_count * 8, size), sums], axis=0)
    for axis in ("rep", "tab"):
        for mask in masks_of(axis):
            small = small + swap(small, axis, mask)
    strips = small[:-8].reshape(matrix_count, 8, size)
    sums = small[-8:]
    cross_w_grad, tower1_w_grad, tower2_w_grad = assemble(
        chunks, strips, own, layer_count, width, hidden
    )
    scalars = sums[layer_count + 4]
    return (
        scalars[0] / (row_count * tab_count * rep_count),
        logits.reshape(row_count),
        dense_grad[:dense_width].T,
        cross_w_grad,
        sums[:layer_count, :width],
        tower1_w_grad[0],
        sums[layer_count, :hidden],
        tower2_w_grad[0],
        sums[layer_count + 1, :hidden],
        jnp.concatenate([sums[layer_count + 2, :width], sums[layer_count + 3, :hidden]]),
        scalars[128],
        table_grad,
    )


def solution(mesh):
    placed = (
        P(("tab", "rep"), None),
        P(),
        P(),
        P(("tab", "rep"), None),
        P(("tab", "rep")),
        P("tab", None, None),
        P(),
        P(),
        P(),
        P(),
        P(),
        P(),
        P(),
        P(),
    )
    return jax.shard_map(
        on_device,
        mesh=mesh,
        in_specs=placed,
        out_specs=(
            P(),
            P(("tab", "rep")),
            P(("tab", "rep"), None),
            P(),
            P(),
            P(),
            P(),
            P(),
            P(),
            P(),
            P(),
            P("tab", None, "rep"),
        ),
        check_vma=False,
    )
```

time: 742 us -> 565 us (0.76)
  waiting for transfers between devices: 269 us -> 126 us
  blocking collectives: 133 us -> 0 us
  starting transfers between devices: 18.9 us -> 122 us
  matrix products: 57.3 us -> 0 us
  Pallas kernels: 141 us -> 178 us
  local copies, waits for them, and re-layouts: 84.2 us -> 109 us
  between operations: 18.8 us -> 4.09 us
    psum x1 -> x0, waiting for transfers between devices: 181 us -> none  [on_device(): lax.psum((weight_stack, bias_stack, tower2_w_part, tower2_b_part, tower1_...]
    ppermute x0 -> x59, waiting for transfers between devices: none -> 106 us  [swap(): lax.ppermute(value, axis, [(at, at ^ mask) for at in range(lax.axis_size(...]
    ppermute x0 -> x59, starting transfers between devices: none -> 68 us  [swap(): lax.ppermute(value, axis, [(at, at ^ mask) for at in range(lax.axis_size(...]
    dot_general x19 -> x0, matrix products: 57.3 us -> none  [the longest x5 20.3 us: contract_rows(): lax.dot_general(left_op, right_op, (((0,), (0,)), ((), ())), preferred_el...]
    reduce_scatter x1 -> x0, waiting for transfers between devices: 55.6 us -> none  [on_device(): lax.psum_scatter(contract_rows(grad_first, anchor), ('tab', 'rep'), scatt...]
    pallas_call x1 -> x8, Pallas kernels: 68 us -> 122 us  [the longest x5 69.8 us: add_rows(): pl.pallas_call(functools.partial(add_kernel, part_count), grid=(tab_count...]
    all_to_all x1 -> x0, blocking collectives: 51.7 us -> none  [on_device(): lax.all_to_all(grad_slots, 'tab', split_axis=0, concat_axis=2, tiled=True)]
    psum x1 -> x0, blocking collectives: 42.1 us -> none  [on_device(): lax.psum((weight_stack, bias_stack, tower2_w_part, tower2_b_part, tower1_...]
  transfers between devices with their start and end apart: 5 -> 62, of which waited for: 3 -> 18; matrix products, arithmetic and copies ran while one was open for 8% -> 21% of each run, Pallas kernels for 9% -> 2%
where the time goes in v2:
time: 565 us
  Pallas kernels  178 us (32%)
  waiting for transfers between devices  126 us (22%)
  starting transfers between devices  122 us (22%)
  local copies, waits for them, and re-layouts  109 us (19%)
  other arithmetic  26.1 us (5%)
    ppermute x59, waiting for transfers between devices, swap(): lax.ppermute(value, axis, [(at, at ^ mask) for at in range(lax.axis_size(...  106 us
    pallas_call x5, Pallas kernels, add_rows(): pl.pallas_call(functools.partial(add_kernel, part_count), grid=(tab_count...  69.8 us
    ppermute x59, starting transfers between devices, swap(): lax.ppermute(value, axis, [(at, at ^ mask) for at in range(lax.axis_size(...  68 us
    pallas_call x1, Pallas kernels, lookup(): pl.pallas_call(lookup_kernel, grid_spec=pltpu.PrefetchScalarGridSpec(num_...  55.3 us
    all_to_all x1, starting transfers between devices, on_device(): lax.all_to_all(looked, 'tab', split_axis=0, concat_axis=0, tiled=True)  43.2 us
    unnamed x36, local copies, waits for them, and re-layouts  34.6 us
    pallas_call x1, Pallas kernels, dense_step(): pl.pallas_call(functools.partial(dense_kernel, dense_width), in_specs=[sm...  27.1 us
    all_to_all x1, waiting for transfers between devices, on_device(): lax.all_to_all(looked, 'tab', split_axis=0, concat_axis=0, tiled=True)  19.4 us
  transfers between devices with their start and end apart: 62, of which 18 were waited for; matrix products, arithmetic and copies ran while one was open for 21% of the time, Pallas kernels for 2%

profile of v2, /device:TPU:0, one launch (start us, length us, event | category | flops | bytes accessed | tf_op | source)
XLA Modules:
  0.0 564.5 jit_solution(2198619752490355305)
XLA Ops:
  5.2 7.3 %all-to-all-start = ((s32[8,5,512]{2,1,0:T(8,128)}), s32[8,5,512]{2,1,0:T(8,128)S(1)}, u32[]{:S(2)}, u32[]{:S(2)}) async-start(s32[8,5,512]{2,1,0:T(8,128)} %reshape.136), calls=%async_computation | async-start | bytes 262144 | tf_op jit(solution)/shard_map/all_to_all | solution.py:529
  16.9 5.9 %slice_bitcast_fusion = (bf16[1027,1027]{1,0:T(8,128)(2,1)}, bf16[1027,1027]{1,0:T(8,128)(2,1)S(1)}, bf16[1027,1027]{1,0:T(8,128)(2,1)}) fusion(bf16[3,1027,1027]{2,1,0:T(8,128)(2,1)} %param.20), kind=kLoop, calls=%fused_computation.13 | loop fusion | bytes 12656748 | tf_op jit(solution)/shard_map/squeeze | solution.py:537
  24.7 55.3 %lookup.1 = bf16[8,5,39,512]{3,2,1,0:T(8,128)(2,1)} custom-call(s32[5]{0:T(128)S(1)} %and_select_fusion.group_ref, s32[8,5,1,512]{3,2,1,0:T(1,128)S(1)} %copy.352.ids_ref.refs_0_, bf16[5,39,32768]{2,1,0:T(8,128)(2,1)} %table_ref.1), custom_call_target="tpu_custom_call" | custom-call | flops 64424509440 | bytes 14376960 | tf_op jit(solution)/shard_map/lookup/pallas_call | solution.py:81
  80.0 43.2 %all-to-all-start.1 = ((bf16[8,5,39,512]{3,2,1,0:T(8,128)(2,1)}), bf16[8,5,39,512]{3,2,1,0:T(8,128)(2,1)S(1)}, u32[]{:S(2)}, u32[]{:S(2)}) async-start(bf16[8,5,39,512]{3,2,1,0:T(8,128)(2,1)} %lookup.1), calls=%async_computation.1 | async-start | bytes 3276800 | tf_op jit(solution)/shard_map/all_to_all | solution.py:544
  125.8 4.2 copy.353
  141.7 19.4 %all-to-all-done.1 = bf16[8,5,39,512]{3,2,1,0:T(8,128)(2,1)S(1)} async-done(((bf16[8,5,39,512]{3,2,1,0:T(8,128)(2,1)}), bf16[8,5,39,512]{3,2,1,0:T(8,128)(2,1)S(1)}, u32[]{:S(2)}, u32[]{:S(2)}) %all-to-all-start.1) | async-done | bytes 1597472 | tf_op jit(solution)/shard_map/all_to_all | solution.py:544
  162.3 27.1 %dense.1 = (f32[1,512]{1,0:T(1,128)}, f32[16,512]{1,0:T(8,128)}, bf16[40,39,512]{2,1,0:T(8,128)(2,1)}, bf16[5,1152,512]{2,1,0:T(8,128)(2,1)}, bf16[5,1152,512]{2,1,0:T(8,128)(2,1)}, /*index=5*/f32[8,1152]{1,0:T(8,128)}) custom-call(s32[26]{0:T(128)} %place_ref.1, f32[1]{0:T(128)S(6)} %convert.84.bias_ref, bf16[40,39,512]{2,1,0:T(8,128)(2,1)} %bitcast.283, ...), custom_call_target="tpu_custom_call" | custom-call | flops 13589544960 | bytes 30965760 | tf_op jit(solution)/shard_map/dense/pallas_call | solution.py:311
  192.1 11.7 %weight_parts.1 = (f32[5,512,1024]{2,1,0:T(8,128)}, bf16[5,512,1024]{2,1,0:T(8,128)(2,1)S(1)}, f32[5,8,1152]{2,1,0:T(8,128)S(1)}) custom-call(s32[1]{0:T(128)} %bitcast.own_ref, bf16[5,1152,512]{2,1,0:T(8,128)(2,1)S(1)} %copy-done.3, bf16[5,1152,512]{2,1,0:T(8,128)(2,1)} %get-tuple-element.25.right_ref), custom_call_target="tpu_custom_call" | custom-call | flops 6794772480 | bytes 66355200 | tf_op jit(solution)/shard_map/weight_parts/pallas_call | solution.py:367
  209.9 9.5 %reshape.142 = bf16[5,2,2,2,2,2,16,2,512]{8,7,6,5,4,3,2,1,0:T(2,128)(2,1)} reshape(bf16[5,512,1024]{2,1,0:T(8,128)(2,1)} %copy-done) | data formatting | bytes 10485760 | tf_op jit(solution)/shard_map/reshape | solution.py:577
  221.0 13.5 %fusion.55 = (bf16[5,2,2,2,2,1,16,1,512]{8,7,6,5,4,3,2,1,0:T(2,128)(2,1)S(1)}, bf16[5,2,2,2,2,1,16,1,512]{8,7,6,5,4,3,2,1,0:T(2,128)(2,1)S(1)}, bf16[5,2,2,2,2,1...) fusion(bf16[5,2,2,2,2,2,16,2,512]{8,7,6,5,4,3,2,1,0:T(2,128)(2,1)} %reshape.142), kind=kLoop, calls=%fused_computation.145 | loop fusion | bytes 10485760 | tf_op jit(solution)/shard_map/slice | solution.py:582
  241.6 14.3 %reshape.141 = f32[5,2,2,2,2,2,16,2,512]{8,7,6,5,4,3,2,1,0:T(2,128)} reshape(f32[5,512,1024]{2,1,0:T(8,128)} %get-tuple-element.30) | data formatting | bytes 20971520 | tf_op jit(solution)/shard_map/reshape | solution.py:576
  259.0 15.2 %fusion.54 = (f32[5,2,2,2,2,1,16,1,512]{8,7,6,5,4,3,2,1,0:T(1,128)S(1)}, f32[5,2,2,2,2,1,16,1,512]{8,7,6,5,4,3,2,1,0:T(1,128)S(1)}, f32[5,2,2,2,2,1,16,1,512]{8,...) fusion(f32[5,2,2,2,2,2,16,2,512]{8,7,6,5,4,3,2,1,0:T(2,128)} %reshape.141), kind=kLoop, calls=%fused_computation.144 | loop fusion | bytes 20971520 | tf_op jit(solution)/shard_map/slice | solution.py:582
  287.1 8.4 %collective-permute-done.42 = bf16[5,2,2,2,16,512]{5,4,0,3,2,1:T(8,128)(2,1)S(1)} collective-permute-done((bf16[5,2,2,2,16,512]{5,4,0,3,2,1:T(8,128)(2,1)S(1)}, bf16[5,2,2,2,16,512]{5,4,0,3,2,1:T(8,128)(2,1)S(1)}, u32[]{:S(2)}, u32[]{:S(2)}) %collective-permute-start.42) | collective-permute-done | bytes 655392 | tf_op jit(solution)/shard_map/ppermute | solution.py:37
  296.4 11.6 %collective-permute-done.18 = bf16[5,2,2,2,16,512]{5,4,0,3,2,1:T(8,128)(2,1)S(1)} collective-permute-done((bf16[5,2,2,2,16,512]{5,4,0,3,2,1:T(8,128)(2,1)S(1)}, bf16[5,2,2,2,16,512]{5,4,0,3,2,1:T(8,128)(2,1)S(1)}, u32[]{:S(2)}, u32[]{:S(2)}) %collective-permute-start.18) | collective-permute-done | bytes 655392 | tf_op jit(solution)/shard_map/ppermute | solution.py:37
  309.7 6.2 %collective-permute-done.30 = bf16[5,2,2,2,16,512]{5,4,0,3,2,1:T(8,128)(2,1)S(1)} collective-permute-done((bf16[5,2,2,2,16,512]{5,4,0,3,2,1:T(8,128)(2,1)S(1)}, bf16[5,2,2,2,16,512]{5,4,0,3,2,1:T(8,128)(2,1)S(1)}, u32[]{:S(2)}, u32[]{:S(2)}) %collective-permute-start.30) | collective-permute-done | bytes 655392 | tf_op jit(solution)/shard_map/ppermute | solution.py:37
  316.8 6.1 %collective-permute-done.43 = bf16[5,2,2,16,512]{4,3,0,2,1:T(8,128)(2,1)S(1)} collective-permute-done((bf16[5,2,2,16,512]{4,3,0,2,1:T(8,128)(2,1)S(1)}, bf16[5,2,2,16,512]{4,3,0,2,1:T(8,128)(2,1)S(1)}, u32[]{:S(2)}, u32[]{:S(2)}) %collective-permute-start.43) | collective-permute-done | bytes 327712 | tf_op jit(solution)/shard_map/ppermute | solution.py:37
  323.7 4.1 collective-permute-done.19
  346.7 5.4 collective-permute-start.34
  363.1 4.1 collective-permute-start.24
  382.5 3.8 collective-permute-done.11
  393.9 29.5 %collective-permute-done.26 = bf16[5,2,2,16,512]{4,3,2,1,0:T(8,128)(2,1)S(1)} collective-permute-done((bf16[5,2,2,16,512]{4,3,2,1,0:T(8,128)(2,1)S(1)}, bf16[5,2,2,16,512]{4,3,2,1,0:T(8,128)(2,1)S(1)}, u32[]{:S(2)}, u32[]{:S(2)}) %collective-permute-start.26) | collective-permute-done | bytes 327712 | tf_op jit(solution)/shard_map/ppermute | solution.py:37
  425.6 8.4 %collective-permute-done.38 = bf16[5,2,2,16,512]{4,3,2,1,0:T(8,128)(2,1)S(1)} collective-permute-done((bf16[5,2,2,16,512]{4,3,2,1,0:T(8,128)(2,1)S(1)}, bf16[5,2,2,16,512]{4,3,2,1,0:T(8,128)(2,1)S(1)}, u32[]{:S(2)}, u32[]{:S(2)}) %collective-permute-start.38) | collective-permute-done | bytes 327712 | tf_op jit(solution)/shard_map/ppermute | solution.py:37
  438.4 4.7 collective-permute-done.27
  444.9 5.6 collective-permute-done.15
  451.6 7.2 %collective-permute-done.53 = s32[8,5,512]{2,1,0:T(8,128)S(1)} collective-permute-done((s32[8,5,512]{2,1,0:T(8,128)S(1)}, s32[8,5,512]{2,1,0:T(8,128)S(1)}, u32[]{:S(2)}, u32[]{:S(2)}) %collective-permute-start.53) | collective-permute-done | bytes 81952 | tf_op jit(solution)/shard_map/ppermute | solution.py:37
  471.7 13.6 %assemble.1 = (f32[3,1027,1027]{2,1,0:T(8,128)}, f32[1,1024,1027]{2,1,0:T(8,128)}, f32[1,1024,1024]{2,1,0:T(8,128)}) custom-call(s32[1]{0:T(128)} %bitcast.own_ref, bf16[5,16,16,512]{3,2,1,0:T(8,128)(2,1)} %bitcast.42.refs_0_, bf16[5,16,16,512]{3,2,1,0:T(8,128)(2,1)} %collective-permute-done.16.refs_1_, bf16[5,16,16,512]{3,2,1,0:T(8,128)(2,1)} %bitcast.66.refs_2_, ...), custom_call_target="tpu_custom_call" | custom-call | bytes 39813120 | tf_op jit(solution)/shard_map/assemble/pallas_call | solution.py:474
  485.4 5.9 %copy.419 = f32[1024,1027]{0,1:T(8,128)} copy(f32[1024,1027]{1,0:T(8,128)} %bitcast.282) | data formatting | bytes 8413184
  493.3 14.0 %add_rows.5.refs_8_ = f32[5,39,8192]{2,1,0:T(8,128)} custom-call(s32[1]{0:T(128)} %bitcast.122.base_ref, s32[8,5,1,512]{3,2,1,0:T(1,128)S(1)} %copy.352.ids_ref.refs_0_, s32[8,5,1,512]{3,2,1,0:T(1,128)S(1)} %copy.413.refs_1_, s32[8,5,1,512]{3,2,1,0:T(1,128)S(1)} %copy.414.refs_2_, s32[8,5,1,512]{3,2,1,0:T(1,128)S(1)} %copy-done.2, ...), custom_call_target="tpu_custom_call" | custom-call | flops 10468982784 | bytes 2555904 | tf_op jit(solution)/shard_map/add_rows/pallas_call | solution.py:148
  507.3 14.0 %add_rows.6.refs_8_ = f32[5,39,8192]{2,1,0:T(8,128)} custom-call(s32[1]{0:T(128)} %bitcast.122.base_ref, s32[8,5,1,512]{3,2,1,0:T(1,128)S(1)} %copy.352.ids_ref.refs_0_, s32[8,5,1,512]{3,2,1,0:T(1,128)S(1)} %copy.413.refs_1_, s32[8,5,1,512]{3,2,1,0:T(1,128)S(1)} %copy.414.refs_2_, s32[8,5,1,512]{3,2,1,0:T(1,128)S(1)} %copy-done.2, ...), custom_call_target="tpu_custom_call", output_to_operand_aliasing={{}: (9, {})} | custom-call | flops 10468982784 | bytes 2555904 | tf_op jit(solution)/shard_map/add_rows/pallas_call | solution.py:148
  521.3 14.0 %add_rows.7.refs_8_ = f32[5,39,8192]{2,1,0:T(8,128)} custom-call(s32[1]{0:T(128)} %bitcast.122.base_ref, s32[8,5,1,512]{3,2,1,0:T(1,128)S(1)} %copy.352.ids_ref.refs_0_, s32[8,5,1,512]{3,2,1,0:T(1,128)S(1)} %copy.413.refs_1_, s32[8,5,1,512]{3,2,1,0:T(1,128)S(1)} %copy.414.refs_2_, s32[8,5,1,512]{3,2,1,0:T(1,128)S(1)} %copy-done.2, ...), custom_call_target="tpu_custom_call", output_to_operand_aliasing={{}: (9, {})} | custom-call | flops 10468982784 | bytes 2555904 | tf_op jit(solution)/shard_map/add_rows/pallas_call | solution.py:148
  535.2 14.0 %add_rows.8.refs_8_ = f32[5,39,8192]{2,1,0:T(8,128)} custom-call(s32[1]{0:T(128)} %bitcast.122.base_ref, s32[8,5,1,512]{3,2,1,0:T(1,128)S(1)} %copy.352.ids_ref.refs_0_, s32[8,5,1,512]{3,2,1,0:T(1,128)S(1)} %copy.413.refs_1_, s32[8,5,1,512]{3,2,1,0:T(1,128)S(1)} %copy.414.refs_2_, s32[8,5,1,512]{3,2,1,0:T(1,128)S(1)} %copy-done.2, ...), custom_call_target="tpu_custom_call", output_to_operand_aliasing={{}: (9, {})} | custom-call | flops 10468982784 | bytes 2555904 | tf_op jit(solution)/shard_map/add_rows/pallas_call | solution.py:148
  549.2 14.0 %add_rows.9 = f32[5,39,8192]{2,1,0:T(8,128)} custom-call(s32[1]{0:T(128)} %bitcast.122.base_ref, s32[8,5,1,512]{3,2,1,0:T(1,128)S(1)} %copy.352.ids_ref.refs_0_, s32[8,5,1,512]{3,2,1,0:T(1,128)S(1)} %copy.413.refs_1_, s32[8,5,1,512]{3,2,1,0:T(1,128)S(1)} %copy.414.refs_2_, s32[8,5,1,512]{3,2,1,0:T(1,128)S(1)} %copy-done.2, ...), custom_call_target="tpu_custom_call", output_to_operand_aliasing={{}: (9, {})} | custom-call | flops 10468982784 | bytes 2555904 | tf_op jit(solution)/shard_map/add_rows/pallas_call | solution.py:148
  (236 shorter events, 139.6 us)
Async XLA Ops:
  5.2 19.4 %all-to-all-start = ((s32[8,5,512]{2,1,0:T(8,128)}), s32[8,5,512]{2,1,0:T(8,128)S(1)}, u32[]{:S(2)}, u32[]{:S(2)}) async-start(s32[8,5,512]{2,1,0:T(8,128)} %reshape.136), calls=%async_computation | async-start | bytes 262144 | tf_op jit(solution)/shard_map/all_to_all | solution.py:529
  80.0 81.1 %all-to-all-start.1 = ((bf16[8,5,39,512]{3,2,1,0:T(8,128)(2,1)}), bf16[8,5,39,512]{3,2,1,0:T(8,128)(2,1)S(1)}, u32[]{:S(2)}, u32[]{:S(2)}) async-start(bf16[8,5,39,512]{3,2,1,0:T(8,128)(2,1)} %lookup.1), calls=%async_computation.1 | async-start | bytes 3276800 | tf_op jit(solution)/shard_map/all_to_all | solution.py:544
  206.2 13.2 %collective-permute-start = (f32[48,1152]{1,0:T(8,128)S(1)}, f32[48,1152]{1,0:T(8,128)S(1)}, u32[]{:S(2)}, u32[]{:S(2)}) collective-permute-start(f32[48,1152]{1,0:T(8,128)S(1)} %pad_maximum_fusion.12), channel_id=1, source_target_pairs={{0,1},{1,0},{2,3},{3,2},{4,5},{5,4},{6,7},{7,6},{8,9},{9,8},{10,11... | collective-permute-start | bytes 663560 | tf_op jit(solution)/shard_map/ppermute | solution.py:37
  206.3 169.8 %all-to-all-start.2 = ((bf16[8,5,39,512]{3,2,1,0:T(8,128)(2,1)}), bf16[8,5,39,512]{3,2,1,0:T(8,128)(2,1)S(1)}, u32[]{:S(2)}, u32[]{:S(2)}) async-start(bf16[8,5,39,512]{3,2,1,0:T(8,128)(2,1)} %bitcast.126), calls=%async_computation.2 | async-start | bytes 3276800 | tf_op jit(solution)/shard_map/all_to_all | solution.py:549
  219.4 36.5 %collective-permute-start.1 = (f32[48,1152]{1,0:T(8,128)S(1)}, f32[48,1152]{1,0:T(8,128)}, u32[]{:S(2)}, u32[]{:S(2)}) collective-permute-start(f32[48,1152]{1,0:T(8,128)S(1)} %fusion.37), channel_id=1, source_target_pairs={{0,2},{1,3},{2,0},{3,1},{4,6},{5,7},{6,4},{7,5},{8,10},{9,11},{10,... | collective-permute-start | bytes 663560 | tf_op jit(solution)/shard_map/ppermute | solution.py:37
  240.6 44.1 %collective-permute-start.29 = (bf16[5,2,2,2,2,16,512]{6,5,0,4,3,2,1:T(8,128)(2,1)}, bf16[5,2,2,2,2,16,512]{6,5,0,4,3,2,1:T(8,128)(2,1)S(1)}, u32[]{:S(2)}, u32[]{:S(2)}) collective-permute-start(bf16[5,2,2,2,2,16,512]{6,5,0,4,3,2,1:T(8,128)(2,1)} %bitcast.276), channel_id=1, source_target_pairs={{0,1},{1,0},{2,3},{3,2},{4,5},{5,4},{6,7},{7,6},{8,9},{9,8},{10,11... | collective-permute-start | bytes 3932168 | tf_op jit(solution)/shard_map/ppermute | solution.py:37
  240.7 41.3 %collective-permute-start.5 = (bf16[5,2,2,2,2,16,512]{6,5,0,4,3,2,1:T(8,128)(2,1)}, bf16[5,2,2,2,2,16,512]{6,5,0,4,3,2,1:T(8,128)(2,1)}, u32[]{:S(2)}, u32[]{:S(2)}) collective-permute-start(bf16[5,2,2,2,2,16,512]{6,5,0,4,3,2,1:T(8,128)(2,1)} %bitcast.278), channel_id=1, source_target_pairs={{0,1},{1,0},{2,3},{3,2},{4,5},{5,4},{6,7},{7,6},{8,9},{9,8},{10,11... | collective-permute-start | bytes 3932168 | tf_op jit(solution)/shard_map/ppermute | solution.py:37
  241.1 37.3 %collective-permute-start.17 = (bf16[5,2,2,2,2,16,512]{6,5,0,4,3,1,2:T(8,128)(2,1)}, bf16[5,2,2,2,2,16,512]{6,5,0,4,3,1,2:T(8,128)(2,1)}, u32[]{:S(2)}, u32[]{:S(2)}) collective-permute-start(bf16[5,2,2,2,2,16,512]{6,5,0,4,3,1,2:T(8,128)(2,1)} %bitcast.277), channel_id=1, source_target_pairs={{0,1},{1,0},{2,3},{3,2},{4,5},{5,4},{6,7},{7,6},{8,9},{9,8},{10,11... | collective-permute-start | bytes 3932168 | tf_op jit(solution)/shard_map/ppermute | solution.py:37
  241.3 34.4 %collective-permute-start.41 = (bf16[5,2,2,2,2,16,512]{6,5,0,4,3,1,2:T(8,128)(2,1)}, bf16[5,2,2,2,2,16,512]{6,5,0,4,3,1,2:T(8,128)(2,1)}, u32[]{:S(2)}, u32[]{:S(2)}) collective-permute-start(bf16[5,2,2,2,2,16,512]{6,5,0,4,3,1,2:T(8,128)(2,1)} %bitcast.275), channel_id=1, source_target_pairs={{0,1},{1,0},{2,3},{3,2},{4,5},{5,4},{6,7},{7,6},{8,9},{9,8},{10,11... | collective-permute-start | bytes 3932168 | tf_op jit(solution)/shard_map/ppermute | solution.py:37
  256.9 17.2 %collective-permute-start.2 = (f32[48,1152]{1,0:T(8,128)S(1)}, f32[48,1152]{1,0:T(8,128)S(1)}, u32[]{:S(2)}, u32[]{:S(2)}) collective-permute-start(f32[48,1152]{1,0:T(8,128)S(1)} %add.148), channel_id=1, source_target_pairs={{0,4},{4,0},{8,12},{12,8},{16,20},{20,16},{24,28},{28,24},{1,5},{5... | collective-permute-start | bytes 663560 | tf_op jit(solution)/shard_map/ppermute | solution.py:37
  274.2 112.2 %collective-permute-start.3 = (f32[48,1152]{1,0:T(8,128)S(1)}, f32[48,1152]{1,0:T(8,128)}, u32[]{:S(2)}, u32[]{:S(2)}) collective-permute-start(f32[48,1152]{1,0:T(8,128)S(1)} %add.149), channel_id=1, source_target_pairs={{0,8},{4,12},{8,0},{12,4},{16,24},{20,28},{24,16},{28,20},{1,9},{5... | collective-permute-start | bytes 663560 | tf_op jit(solution)/shard_map/ppermute | solution.py:37
  277.8 17.7 %collective-permute-start.42 = (bf16[5,2,2,2,16,512]{5,4,0,3,2,1:T(8,128)(2,1)S(1)}, bf16[5,2,2,2,16,512]{5,4,0,3,2,1:T(8,128)(2,1)S(1)}, u32[]{:S(2)}, u32[]{:S(2)}) collective-permute-start(bf16[5,2,2,2,16,512]{5,4,0,3,2,1:T(8,128)(2,1)S(1)} %fusion.11), channel_id=1, source_target_pairs={{0,4},{4,0},{8,12},{12,8},{16,20},{20,16},{24,28},{28,24},{1,5},{5... | collective-permute-start | bytes 1966088 | tf_op jit(solution)/shard_map/ppermute | solution.py:37
  280.5 27.5 %collective-permute-start.18 = (bf16[5,2,2,2,16,512]{5,4,0,3,2,1:T(8,128)(2,1)S(1)}, bf16[5,2,2,2,16,512]{5,4,0,3,2,1:T(8,128)(2,1)S(1)}, u32[]{:S(2)}, u32[]{:S(2)}) collective-permute-start(bf16[5,2,2,2,16,512]{5,4,0,3,2,1:T(8,128)(2,1)S(1)} %fusion.9), channel_id=1, source_target_pairs={{0,4},{4,0},{8,12},{12,8},{16,20},{20,16},{24,28},{28,24},{1,5},{5... | collective-permute-start | bytes 1966088 | tf_op jit(solution)/shard_map/ppermute | solution.py:37
  284.1 24.7 %collective-permute-start.6 = (bf16[5,2,2,2,16,512]{5,4,0,3,2,1:T(8,128)(2,1)S(1)}, bf16[5,2,2,2,16,512]{5,4,0,3,2,1:T(8,128)(2,1)S(1)}, u32[]{:S(2)}, u32[]{:S(2)}) collective-permute-start(bf16[5,2,2,2,16,512]{5,4,0,3,2,1:T(8,128)(2,1)S(1)} %fusion.8), channel_id=1, source_target_pairs={{0,2},{1,3},{2,0},{3,1},{4,6},{5,7},{6,4},{7,5},{8,10},{9,11},{10,... | collective-permute-start | bytes 1966088 | tf_op jit(solution)/shard_map/ppermute | solution.py:37
  285.5 30.4 %collective-permute-start.30 = (bf16[5,2,2,2,16,512]{5,4,0,3,2,1:T(8,128)(2,1)S(1)}, bf16[5,2,2,2,16,512]{5,4,0,3,2,1:T(8,128)(2,1)S(1)}, u32[]{:S(2)}, u32[]{:S(2)}) collective-permute-start(bf16[5,2,2,2,16,512]{5,4,0,3,2,1:T(8,128)(2,1)S(1)} %fusion.10), channel_id=1, source_target_pairs={{0,2},{1,3},{2,0},{3,1},{4,6},{5,7},{6,4},{7,5},{8,10},{9,11},{10,... | collective-permute-start | bytes 1966088 | tf_op jit(solution)/shard_map/ppermute | solution.py:37
  295.8 27.2 %collective-permute-start.43 = (bf16[5,2,2,16,512]{4,3,0,2,1:T(8,128)(2,1)S(1)}, bf16[5,2,2,16,512]{4,3,0,2,1:T(8,128)(2,1)S(1)}, u32[]{:S(2)}, u32[]{:S(2)}) collective-permute-start(bf16[5,2,2,16,512]{4,3,0,2,1:T(8,128)(2,1)S(1)} %fusion.19), channel_id=1, source_target_pairs={{0,2},{1,3},{2,0},{3,1},{4,6},{5,7},{6,4},{7,5},{8,10},{9,11},{10,... | collective-permute-start | bytes 983048 | tf_op jit(solution)/shard_map/ppermute | solution.py:37
  308.2 19.6 %collective-permute-start.19 = (bf16[5,2,2,16,512]{4,3,0,2,1:T(8,128)(2,1)S(1)}, bf16[5,2,2,16,512]{4,3,0,2,1:T(8,128)(2,1)S(1)}, u32[]{:S(2)}, u32[]{:S(2)}) collective-permute-start(bf16[5,2,2,16,512]{4,3,0,2,1:T(8,128)(2,1)S(1)} %fusion.17), channel_id=1, source_target_pairs={{0,2},{1,3},{2,0},{3,1},{4,6},{5,7},{6,4},{7,5},{8,10},{9,11},{10,... | collective-permute-start | bytes 983048 | tf_op jit(solution)/shard_map/ppermute | solution.py:37
  309.1 21.2 %collective-permute-start.7 = (bf16[5,2,2,16,512]{4,3,0,2,1:T(8,128)(2,1)S(1)}, bf16[5,2,2,16,512]{4,3,0,2,1:T(8,128)(2,1)S(1)}, u32[]{:S(2)}, u32[]{:S(2)}) collective-permute-start(bf16[5,2,2,16,512]{4,3,0,2,1:T(8,128)(2,1)S(1)} %fusion.16), channel_id=1, source_target_pairs={{0,4},{4,0},{8,12},{12,8},{16,20},{20,16},{24,28},{28,24},{1,5},{5... | collective-permute-start | bytes 983048 | tf_op jit(solution)/shard_map/ppermute | solution.py:37
  316.2 14.4 %collective-permute-start.31 = (bf16[5,2,2,16,512]{4,3,0,2,1:T(8,128)(2,1)S(1)}, bf16[5,2,2,16,512]{4,3,0,2,1:T(8,128)(2,1)S(1)}, u32[]{:S(2)}, u32[]{:S(2)}) collective-permute-start(bf16[5,2,2,16,512]{4,3,0,2,1:T(8,128)(2,1)S(1)} %fusion.18), channel_id=1, source_target_pairs={{0,4},{4,0},{8,12},{12,8},{16,20},{20,16},{24,28},{28,24},{1,5},{5... | collective-permute-start | bytes 983048 | tf_op jit(solution)/shard_map/ppermute | solution.py:37
  343.6 12.8 %collective-permute-start.9 = (bf16[5,16,512]{2,1,0:T(8,128)(2,1)S(1)}, bf16[5,16,512]{2,1,0:T(8,128)(2,1)S(1)}, u32[]{:S(2)}, u32[]{:S(2)}) collective-permute-start(bf16[5,16,512]{2,1,0:T(8,128)(2,1)S(1)} %get-tuple-element.169), channel_id=1, source_target_pairs={{0,16},{4,20},{8,24},{12,28},{16,0},{20,4},{24,8},{28,12},{1,17},{... | collective-permute-start | bytes 245768 | tf_op jit(solution)/shard_map/ppermute | solution.py:37
  363.1 12.5 %collective-permute-start.24 = (bf16[5,16,512]{2,1,0:T(8,128)(2,1)S(1)}, bf16[5,16,512]{2,1,0:T(8,128)(2,1)S(1)}, u32[]{:S(2)}, u32[]{:S(2)}) collective-permute-start(bf16[5,16,512]{2,1,0:T(8,128)(2,1)S(1)} %fusion.31), channel_id=1, source_target_pairs={{0,16},{4,20},{8,24},{12,28},{16,0},{20,4},{24,8},{28,12},{1,17},{... | collective-permute-start | bytes 245768 | tf_op jit(solution)/shard_map/ppermute | solution.py:37
  375.6 13.5 %collective-permute-start.50 = (bf16[5,2,2,16,512]{4,3,2,1,0:T(8,128)(2,1)S(1)}, bf16[5,2,2,16,512]{4,3,2,1,0:T(8,128)(2,1)S(1)}, u32[]{:S(2)}, u32[]{:S(2)}) collective-permute-start(bf16[5,2,2,16,512]{4,3,2,1,0:T(8,128)(2,1)S(1)} %get-tuple-element.151), channel_id=1, source_target_pairs={{0,2},{1,3},{2,0},{3,1},{4,6},{5,7},{6,4},{7,5},{8,10},{9,11},{10,... | collective-permute-start | bytes 983048 | tf_op jit(solution)/shard_map/ppermute | solution.py:37
  376.7 73.8 %collective-permute-start.56 = (bf16[8,5,39,512]{3,0,2,1:T(8,128)(2,1)S(1)}, bf16[8,5,39,512]{3,0,2,1:T(8,128)(2,1)}, u32[]{:S(2)}, u32[]{:S(2)}) collective-permute-start(bf16[8,5,39,512]{3,0,2,1:T(8,128)(2,1)S(1)} %copy.382), channel_id=1, source_target_pairs={{0,2},{1,3},{2,0},{3,1},{4,6},{5,7},{6,4},{7,5},{8,10},{9,11},{10,... | collective-permute-start | bytes 4792328 | tf_op jit(solution)/shard_map/ppermute | solution.py:37
  388.5 34.9 %collective-permute-start.26 = (bf16[5,2,2,16,512]{4,3,2,1,0:T(8,128)(2,1)S(1)}, bf16[5,2,2,16,512]{4,3,2,1,0:T(8,128)(2,1)S(1)}, u32[]{:S(2)}, u32[]{:S(2)}) collective-permute-start(bf16[5,2,2,16,512]{4,3,2,1,0:T(8,128)(2,1)S(1)} %get-tuple-element.161), channel_id=1, source_target_pairs={{0,2},{1,3},{2,0},{3,1},{4,6},{5,7},{6,4},{7,5},{8,10},{9,11},{10,... | collective-permute-start | bytes 983048 | tf_op jit(solution)/shard_map/ppermute | solution.py:37
  389.0 72.2 %collective-permute-start.57 = (bf16[8,5,39,512]{3,0,2,1:T(8,128)(2,1)S(1)}, bf16[8,5,39,512]{3,0,2,1:T(8,128)(2,1)S(1)}, u32[]{:S(2)}, u32[]{:S(2)}) collective-permute-start(bf16[8,5,39,512]{3,0,2,1:T(8,128)(2,1)S(1)} %copy.382), channel_id=1, source_target_pairs={{0,1},{1,0},{2,3},{3,2},{4,5},{5,4},{6,7},{7,6},{8,9},{9,8},{10,11... | collective-permute-start | bytes 4792328 | tf_op jit(solution)/shard_map/ppermute | solution.py:37
  391.8 32.2 %collective-permute-start.14 = (bf16[5,2,2,16,512]{4,3,2,1,0:T(8,128)(2,1)S(1)}, bf16[5,2,2,16,512]{4,3,2,1,0:T(8,128)(2,1)S(1)}, u32[]{:S(2)}, u32[]{:S(2)}) collective-permute-start(bf16[5,2,2,16,512]{4,3,2,1,0:T(8,128)(2,1)S(1)} %get-tuple-element.166), channel_id=1, source_target_pairs={{0,4},{4,0},{8,12},{12,8},{16,20},{20,16},{24,28},{28,24},{1,5},{5... | collective-permute-start | bytes 983048 | tf_op jit(solution)/shard_map/ppermute | solution.py:37
  392.3 42.3 %collective-permute-start.51 = (bf16[5,2,2,2,16,512]{5,4,3,2,1,0:T(8,128)(2,1)S(1)}, bf16[5,2,2,2,16,512]{5,4,3,2,1,0:T(8,128)(2,1)S(1)}, u32[]{:S(2)}, u32[]{:S(2)}) collective-permute-start(bf16[5,2,2,2,16,512]{5,4,3,2,1,0:T(8,128)(2,1)S(1)} %get-tuple-element.143), channel_id=1, source_target_pairs={{0,4},{4,0},{8,12},{12,8},{16,20},{20,16},{24,28},{28,24},{1,5},{5... | collective-permute-start | bytes 1966088 | tf_op jit(solution)/shard_map/ppermute | solution.py:37
  424.0 19.1 %collective-permute-start.27 = (bf16[5,2,2,2,16,512]{5,4,3,2,1,0:T(8,128)(2,1)S(1)}, bf16[5,2,2,2,16,512]{5,4,3,2,1,0:T(8,128)(2,1)S(1)}, u32[]{:S(2)}, u32[]{:S(2)}) collective-permute-start(bf16[5,2,2,2,16,512]{5,4,3,2,1,0:T(8,128)(2,1)S(1)} %get-tuple-element.147), channel_id=1, source_target_pairs={{0,4},{4,0},{8,12},{12,8},{16,20},{20,16},{24,28},{28,24},{1,5},{5... | collective-permute-start | bytes 1966088 | tf_op jit(solution)/shard_map/ppermute | solution.py:37
  434.0 16.4 %collective-permute-start.15 = (bf16[5,2,2,2,16,512]{5,4,3,2,1,0:T(8,128)(2,1)S(1)}, bf16[5,2,2,2,16,512]{5,4,3,2,1,0:T(8,128)(2,1)S(1)}, u32[]{:S(2)}, u32[]{:S(2)}) collective-permute-start(bf16[5,2,2,2,16,512]{5,4,3,2,1,0:T(8,128)(2,1)S(1)} %get-tuple-element.149), channel_id=1, source_target_pairs={{0,2},{1,3},{2,0},{3,1},{4,6},{5,7},{6,4},{7,5},{8,10},{9,11},{10,... | collective-permute-start | bytes 1966088 | tf_op jit(solution)/shard_map/ppermute | solution.py:37
  434.6 24.2 %collective-permute-start.39 = (bf16[5,2,2,2,16,512]{5,4,3,2,1,0:T(8,128)(2,1)S(1)}, bf16[5,2,2,2,16,512]{5,4,3,2,1,0:T(8,128)(2,1)S(1)}, u32[]{:S(2)}, u32[]{:S(2)}) collective-permute-start(bf16[5,2,2,2,16,512]{5,4,3,2,1,0:T(8,128)(2,1)S(1)} %get-tuple-element.145), channel_id=1, source_target_pairs={{0,2},{1,3},{2,0},{3,1},{4,6},{5,7},{6,4},{7,5},{8,10},{9,11},{10,... | collective-permute-start | bytes 1966088 | tf_op jit(solution)/shard_map/ppermute | solution.py:37
  443.1 15.8 %collective-permute-start.53 = (s32[8,5,512]{2,1,0:T(8,128)S(1)}, s32[8,5,512]{2,1,0:T(8,128)S(1)}, u32[]{:S(2)}, u32[]{:S(2)}) collective-permute-start(s32[8,5,512]{2,1,0:T(8,128)S(1)} %all-to-all-done), channel_id=1, source_target_pairs={{0,2},{1,3},{2,0},{3,1},{4,6},{5,7},{6,4},{7,5},{8,10},{9,11},{10,... | collective-permute-start | bytes 245768 | tf_op jit(solution)/shard_map/ppermute | solution.py:37
  450.4 40.8 %collective-permute-start.58 = (bf16[8,5,39,512]{3,0,2,1:T(8,128)(2,1)}, bf16[8,5,39,512]{3,0,2,1:T(8,128)(2,1)}, u32[]{:S(2)}, u32[]{:S(2)}) collective-permute-start(bf16[8,5,39,512]{3,0,2,1:T(8,128)(2,1)} %collective-permute-done.56), channel_id=1, source_target_pairs={{0,1},{1,0},{2,3},{3,2},{4,5},{5,4},{6,7},{7,6},{8,9},{9,8},{10,11... | collective-permute-start | bytes 4792328 | tf_op jit(solution)/shard_map/ppermute | solution.py:37
  (43 other events, 369.8 us)

commit v3 on v2

v3 whole, which is shorter than its diff:
```python
import functools

import jax
import jax.numpy as jnp
from jax import lax
from jax.experimental import pallas as pl
from jax.experimental.pallas import tpu as pltpu
from jax.sharding import PartitionSpec as P

BF = jnp.bfloat16
F32 = jnp.float32
I32 = jnp.int32
LOOK_SLOTS = 3
LOOK_LANES = 40
LOOK_BLOCKS = 8
LOOK_ROWS = 32
ADD_LOW = 512
MAIN = 1024
CHUNK = 384
PIECE = 32
MIB = 1024 * 1024
NT = (((1,), (1,)), ((), ()))
TN = (((0,), (0,)), ((), ()))


def round_up(size, unit):
    return -(-size // unit) * unit


def params(mib):
    return pltpu.CompilerParams(vmem_limit_bytes=mib * MIB)


def cost(flops, size):
    return pl.CostEstimate(flops=flops, bytes_accessed=size, transcendentals=0)


def swap(value, axis, mask):
    return lax.ppermute(value, axis, [(at, at ^ mask) for at in range(lax.axis_size(axis))])


def masks_of(axis):
    size = lax.axis_size(axis)
    return [1 << bit for bit in range(size.bit_length() - 1)]


def lookup_kernel(first_slot, ids_ref, rows_ref, table_hbm, out_ref, raw, stack, major, picked, sems):
    tab_count, slot_count, pad_dim, count = out_ref.shape
    embed_dim = raw.shape[1]
    total = tab_count * count
    copies = [
        pltpu.make_async_copy(table_hbm.at[first_slot + at], raw.at[at], sems.at[at])
        for at in range(slot_count)
    ]
    for copy in copies:
        copy.start()
    lane = lax.broadcasted_iota(I32, (1, 128), 1)
    stack[...] = jnp.zeros_like(stack)
    most = jnp.maximum(rows_ref[first_slot], 1)
    for at in range(1, slot_count):
        most = jnp.maximum(most, rows_ref[first_slot + at])
    for copy in copies:
        copy.wait()
    unit = 128 * LOOK_BLOCKS

    @pl.loop(0, (most + unit - 1) // unit)
    def _(step):
        for block in range(LOOK_BLOCKS):
            first = pl.multiple_of((step * LOOK_BLOCKS + block) * 128, 128)
            for at in range(slot_count):
                stack[block, at * LOOK_LANES : at * LOOK_LANES + embed_dim, :] = raw[
                    at, :, pl.ds(first, 128)
                ].astype(F32)
            major[pl.ds(first, 128), :] = stack[block].T

    @pl.loop(0, total // LOOK_ROWS)
    def _(step):
        base = step * LOOK_ROWS
        starts = [(first_slot + at) * total + base for at in range(slot_count)]
        for row in range(LOOK_ROWS):
            value = None
            for at in reversed(range(slot_count)):
                one = major[pl.ds(ids_ref[starts[at] + row], 1), :]
                value = one if value is None else jnp.where(lane < (at + 1) * LOOK_LANES, one, value)
            picked[pl.ds(base + row, 1), :] = value

    @pl.loop(0, tab_count)
    def _(tab):
        for block in range(0, count, 128):
            turned = picked[pl.ds(pl.multiple_of(tab * count + block, 128), 128), :].T
            for at in range(slot_count):
                rows = turned[at * LOOK_LANES : at * LOOK_LANES + pad_dim]
                out_ref[tab, at, :, block : block + 128] = rows.astype(BF)


def lookup(tables, wanted, own_rows, tab_count, first_slot, slot_count):
    all_count, embed_dim, table_len = tables.shape
    count = wanted.shape[0] // (all_count * tab_count)
    smem = pl.BlockSpec(memory_space=pltpu.SMEM)
    return pl.pallas_call(
        functools.partial(lookup_kernel, first_slot),
        in_specs=[smem, smem, pl.BlockSpec(memory_space=pl.ANY)],
        out_specs=pl.BlockSpec(memory_space=pltpu.VMEM),
        out_shape=jax.ShapeDtypeStruct((tab_count, slot_count, round_up(embed_dim, 8), count), BF),
        scratch_shapes=[
            pltpu.VMEM((slot_count, embed_dim, table_len), BF),
            pltpu.VMEM((LOOK_BLOCKS, 128, 128), F32),
            pltpu.VMEM((table_len, 128), F32),
            pltpu.VMEM((tab_count * count, 128), F32),
            pltpu.SemaphoreType.DMA((slot_count,)),
        ],
        compiler_params=params(56),
        cost_estimate=cost(
            600 * tab_count * count * table_len * slot_count // 8,
            2 * slot_count * embed_dim * (table_len + tab_count * count),
        ),
        name="lookup",
    )(wanted, own_rows, tables)


def add_kernel(part_count, has_before, base_ref, *refs):
    ids_refs = refs[:part_count]
    grad_refs = refs[part_count : 2 * part_count]
    before_ref = refs[2 * part_count] if has_before else None
    out_ref, token_ref, total = refs[-3:]
    step = pl.program_id(0)
    embed_dim = out_ref.shape[1]
    cols = grad_refs[0].shape[3]
    high_count = total.shape[1] // embed_dim

    @pl.when(step == 0)
    def _():
        total[...] = jnp.zeros_like(total)
        token_ref[...] = jnp.zeros_like(token_ref)

    high_iota = lax.broadcasted_iota(I32, (high_count, cols), 0)
    low_iota = lax.broadcasted_iota(I32, (ADD_LOW, cols), 0)
    product = None
    for ids_ref, grad_ref in zip(ids_refs, grad_refs):
        local = ids_ref[0, 0] - base_ref[0]
        high = lax.shift_right_arithmetic(local, ADD_LOW.bit_length() - 1)
        low = local & (ADD_LOW - 1)
        high_hot = jnp.where(high_iota == high, 1.0, 0.0)
        low_hot = jnp.where(low_iota == low, 1.0, 0.0).astype(BF)
        grads = grad_ref[0, 0, :embed_dim].astype(F32)
        left = (grads[:, None, :] * high_hot[None, :, :]).astype(BF)
        left = left.reshape(embed_dim * high_count, cols)
        term = lax.dot_general(left, low_hot, NT, preferred_element_type=F32)
        product = term if product is None else product + term
    for lane in range(ADD_LOW // 128):
        total[lane] += product[:, lane * 128 : (lane + 1) * 128]

    @pl.when(step == pl.num_programs(0) - 1)
    def _():
        for at in range(high_count):
            for part in range(0, embed_dim, 8):
                size = min(8, embed_dim - part)
                for lane in range(ADD_LOW // 128):
                    first = at * ADD_LOW + lane * 128
                    value = total[lane, pl.ds(part * high_count + at, size, stride=high_count), :]
                    if before_ref is not None:
                        value = value + before_ref[0, part : part + size, first : first + 128]
                    out_ref[0, part : part + size, first : first + 128] = value


def add_rows(grads, wanted, base, share, embed_dim, slot, so_far, accumulate, after):
    tab_count, slot_count, pad_dim, count = grads[0].shape
    part_count = len(grads)
    anywhere = pl.BlockSpec(memory_space=pl.ANY)
    block = pl.BlockSpec((1, embed_dim, share), lambda t: (slot, 0, 0))
    whole = [] if so_far is None else [so_far]
    table_grad, token = pl.pallas_call(
        functools.partial(add_kernel, part_count, accumulate),
        grid=(tab_count,),
        in_specs=[pl.BlockSpec(memory_space=pltpu.SMEM)]
        + [pl.BlockSpec((1, 1, 1, count), lambda t: (t, slot, 0, 0))] * part_count
        + [pl.BlockSpec((1, 1, pad_dim, count), lambda t: (t, slot, 0, 0))] * part_count
        + [block if accumulate else anywhere] * len(whole)
        + [anywhere] * len(after),
        out_specs=[block, pl.BlockSpec((8, 128), lambda t: (0, 0))],
        scratch_shapes=[pltpu.VMEM((ADD_LOW // 128, embed_dim * (share // ADD_LOW), 128), F32)],
        out_shape=[
            jax.ShapeDtypeStruct((slot_count, embed_dim, share), F32),
            jax.ShapeDtypeStruct((8, 128), F32),
        ],
        input_output_aliases={1 + 2 * part_count: 0} if whole else {},
        compiler_params=params(40),
        cost_estimate=cost(
            2 * part_count * tab_count * count * share * embed_dim,
            2 * embed_dim * (2 * share + part_count * tab_count * count),
        ),
        name="add_rows",
    )(base, *[part[:, :, None, :] for part in wanted], *grads, *whole, *after)
    return table_grad, token[0, 0]


def row_sums(value):
    part = value[:, :128]
    for first in range(128, value.shape[1], 128):
        part = part + value[:, first : first + 128]
    return jnp.sum(part.T, axis=0, keepdims=True)


def dense_kernel(
    dense_width,
    width,
    starts,
    place_ref,
    bias_ref,
    *refs,
):
    group_count = len(starts)
    arrived_refs = refs[:group_count]
    dense_refs = refs[group_count:]
    dense_body(dense_width, width, starts, place_ref, bias_ref, arrived_refs, *dense_refs)


def dense_body(
    dense_width,
    width,
    starts,
    place_ref,
    bias_ref,
    arrived_refs,
    dense_ref,
    label_ref,
    weight_hbm,
    cols_ref,
    logits_ref,
    dense_grad_ref,
    slots_ref,
    left_ref,
    right_ref,
    sums_ref,
    weight,
    anchor,
    current,
    update,
    first_pre,
    second_pre,
    grad_anchor,
    grad_current,
    sems,
):
    layer_count = update.shape[0]
    tower1, tower2 = layer_count, layer_count + 1
    pad_dim = arrived_refs[0].shape[2]
    field_count = place_ref.shape[0]
    embed_dim = (width - dense_width) // field_count
    slot_count = sum(ref.shape[1] for ref in arrived_refs)
    size, cols = anchor.shape
    spans = [pl.ds(first, CHUNK) for first in range(0, size, CHUNK)]
    copies = [
        pltpu.make_async_copy(weight_hbm.at[at], weight.at[at], sems.at[at])
        for at in range(layer_count + 2)
    ]
    for copy in copies:
        copy.start()

    def column(at, span):
        return cols_ref[span, at : at + 1]

    def times(at, span, operand):
        return jnp.dot(weight[at, span, :], operand[...], preferred_element_type=F32)

    def transposed_times(at, span, operand):
        return lax.dot_general(weight[at, :, span], operand[...], TN, preferred_element_type=F32)

    anchor[0:16] = dense_ref[...]
    tail = width // 8 * 8
    anchor[tail:] = jnp.zeros((size - tail, cols), F32)
    for field in range(field_count):
        first = dense_width + field * embed_dim
        tab = place_ref[field] // slot_count
        slot = place_ref[field] - tab * slot_count
        value = arrived_refs[0][tab, jnp.minimum(slot, arrived_refs[0].shape[1] - 1)]
        for begin, ref in zip(starts[1:], arrived_refs[1:]):
            other = ref[tab, jnp.clip(slot - begin, 0, ref.shape[1] - 1)]
            value = jnp.where(slot >= begin, other, value)
        anchor[first : first + embed_dim] = value.astype(F32)[:embed_dim]
    for span in spans:
        left_ref[0, span] = anchor[span].astype(BF)
        left_ref[tower1, span] = anchor[span].astype(BF)
    for layer in range(layer_count):
        copies[layer].wait()
        for span in spans:
            value = transposed_times(layer, span, left_ref.at[layer]) + column(layer, span)
            update[layer, span] = value
            before = anchor if layer == 0 else current
            after = anchor[span] * value + before[span]
            current[span] = after
            if layer + 1 < layer_count:
                left_ref[layer + 1, span] = after.astype(BF)
    copies[tower1].wait()
    for span in spans:
        value = transposed_times(tower1, span, left_ref.at[0]) + column(tower1, span)
        first_pre[span] = value
        left_ref[tower2, span] = (value * jax.nn.sigmoid(value)).astype(BF)
    copies[tower2].wait()
    logits = jnp.full((1, cols), bias_ref[0], F32)
    for span in spans:
        value = transposed_times(tower2, span, left_ref.at[tower2]) + column(tower2, span)
        second_pre[span] = value
        act = value * jax.nn.sigmoid(value)
        terms = current[span] * column(layer_count + 2, span) + act * column(layer_count + 3, span)
        logits = logits + jnp.sum(terms, axis=0, keepdims=True)
    logits_ref[...] = logits
    target = label_ref[...]
    residue = jax.nn.sigmoid(logits) - target
    softplus = jnp.maximum(logits, 0.0) + jnp.log1p(jnp.exp(-jnp.abs(logits)))
    sums_ref[layer_count + 4 :, :] = jnp.zeros((sums_ref.shape[0] - layer_count - 4, size), F32)
    loss_row = jnp.sum(softplus - target * logits, axis=1, keepdims=True)
    bias_row = jnp.sum(residue, axis=1, keepdims=True)
    sums_ref[layer_count + 4 : layer_count + 5, 0:128] = jnp.broadcast_to(loss_row, (1, 128))
    sums_ref[layer_count + 4 : layer_count + 5, 128:256] = jnp.broadcast_to(bias_row, (1, 128))
    for span in spans:
        value = second_pre[span]
        sig = jax.nn.sigmoid(value)
        act = value * sig
        grad = residue * column(layer_count + 3, span) * (sig * (1.0 + value * (1.0 - sig)))
        low = grad.astype(BF)
        right_ref[tower2, span] = low
        sums_ref[tower2 : tower2 + 1, span] = row_sums(low.astype(F32))
        sums_ref[layer_count + 3 : layer_count + 4, span] = row_sums(residue * act)
        sums_ref[layer_count + 2 : layer_count + 3, span] = row_sums(residue * current[span])
        grad_current[span] = residue * column(layer_count + 2, span)
    for span in spans:
        value = first_pre[span]
        sig = jax.nn.sigmoid(value)
        grad = times(tower2, span, right_ref.at[tower2]) * (sig * (1.0 + value * (1.0 - sig)))
        low = grad.astype(BF)
        right_ref[tower1, span] = low
        sums_ref[tower1 : tower1 + 1, span] = row_sums(low.astype(F32))
    for span in spans:
        grad_anchor[span] = times(tower1, span, right_ref.at[tower1])
    for layer in reversed(range(layer_count)):
        for span in spans:
            grad = grad_current[span]
            low = (anchor[span] * grad).astype(BF)
            right_ref[layer, span] = low
            sums_ref[layer : layer + 1, span] = row_sums(low.astype(F32))
            grad_anchor[span] += grad * update[layer, span]
        for span in spans:
            grad_current[span] += times(layer, span, right_ref.at[layer])
    for span in spans:
        grad_anchor[span] += grad_current[span]
    dense_grad_ref[...] = grad_anchor[0:16]
    slots_ref[...] = jnp.zeros_like(slots_ref)
    for field in range(field_count):
        first = dense_width + field * embed_dim
        slots_ref[place_ref[field], :embed_dim] = grad_anchor[first : first + embed_dim].astype(BF)


def dense_step(arrived, starts, place, dense_in, labels, weights, cols, out_b, layer_count, width):
    tab_count, _, pad_dim, count = arrived[0].shape
    slot_count = tab_count * sum(part.shape[1] for part in arrived)
    dense_width = dense_in.shape[1]
    size = weights.shape[1]
    matrix_count = layer_count + 2
    dense_rows = jnp.pad(dense_in.T.astype(F32), ((0, 16 - dense_width), (0, 0)))
    vmem = pl.BlockSpec(memory_space=pltpu.VMEM)
    smem = pl.BlockSpec(memory_space=pltpu.SMEM)
    flat = pltpu.VMEM((size, count), F32)
    return pl.pallas_call(
        functools.partial(dense_kernel, dense_width, width, starts),
        in_specs=[smem, smem] + [vmem] * (len(arrived) + 2) + [ pl.BlockSpec(memory_space=pl.ANY), vmem],
        out_specs=[vmem] * 6,
        out_shape=[
            jax.ShapeDtypeStruct((1, count), F32),
            jax.ShapeDtypeStruct((16, count), F32),
            jax.ShapeDtypeStruct((slot_count, pad_dim, count), BF),
            jax.ShapeDtypeStruct((matrix_count, size, count), BF),
            jax.ShapeDtypeStruct((matrix_count, size, count), BF),
            jax.ShapeDtypeStruct((8, size), F32),
        ],
        scratch_shapes=[
            pltpu.VMEM(weights.shape, BF),
            flat,
            flat,
            pltpu.VMEM((layer_count, size, count), F32),
            flat,
            flat,
            flat,
            flat,
            pltpu.SemaphoreType.DMA((matrix_count,)),
        ],
        compiler_params=params(60),
        cost_estimate=cost(4 * matrix_count * size * size * count, 2 * weights.size + 30 * size * count),
        name="dense",
    )(
        place,
        out_b.astype(F32).reshape(1),
        *arrived,
        dense_rows,
        labels.astype(F32).reshape(1, count),
        weights,
        cols,
    )


def chunk_place(piece, swapped):
    if not swapped:
        return piece
    return (piece & 3) | ((piece & 4) << 1) | ((piece & 8) >> 1)


def weight_kernel(own_ref, left_ref, right_ref, *refs):
    keep_refs, send_refs = refs[:4], refs[4:8]
    strip_ref, moved = refs[8:]
    pieces = MAIN // PIECE
    rows = PIECE // 2
    half = MAIN // 2
    right = right_ref[0, :MAIN, :]
    for above in range(2):
        for at in range(pieces):
            first = pl.multiple_of((at ^ own_ref[0]) * PIECE + above * rows, rows)
            moved[(above * pieces + at) * rows : (above * pieces + at + 1) * rows] = left_ref[
                0, pl.ds(first, rows), :
            ]
    for above in range(2):
        product = lax.dot_general(
            moved[above * half : (above + 1) * half], right, NT, preferred_element_type=F32
        )
        for lane in range(2):
            part = product[:, lane * half : (lane + 1) * half]
            for at in range(pieces // 2):
                to = chunk_place(at, lane == 1)
                keep_refs[2 * above + lane][to, 0] = part[at * rows : (at + 1) * rows]
                other = (pieces // 2 + at) * rows
                send_refs[2 * above + lane][to, 0] = part[other : other + rows].astype(BF)
    below = lax.dot_general(left_ref[0, MAIN : MAIN + 16, :], right_ref[0], NT, preferred_element_type=F32)
    beside = lax.dot_general(right_ref[0, MAIN : MAIN + 16, :], left_ref[0], NT, preferred_element_type=F32)
    strip_ref[0, 0:3] = below[0:3]
    strip_ref[0, 3:6] = beside[0:3]
    strip_ref[0, 6:8] = jnp.zeros((2, strip_ref.shape[2]), F32)


def weight_parts(left, right, own):
    matrix_count, size, count = left.shape
    half = MAIN // 2
    pieces = MAIN // PIECE // 2
    chunk = pl.BlockSpec((pieces, 1, PIECE // 2, half), lambda m: (0, m, 0, 0))
    shape = (pieces, matrix_count, PIECE // 2, half)
    outs = pl.pallas_call(
        weight_kernel,
        grid=(matrix_count,),
        in_specs=[
            pl.BlockSpec(memory_space=pltpu.SMEM),
            pl.BlockSpec((1, size, count), lambda m: (m, 0, 0)),
            pl.BlockSpec((1, size, count), lambda m: (m, 0, 0)),
        ],
        out_specs=[chunk] * 8 + [pl.BlockSpec((1, 8, size), lambda m: (m, 0, 0))],
        out_shape=[jax.ShapeDtypeStruct(shape, F32)] * 4
        + [jax.ShapeDtypeStruct(shape, BF)] * 4
        + [jax.ShapeDtypeStruct((matrix_count, 8, size), F32)],
        scratch_shapes=[pltpu.VMEM((MAIN, count), BF)],
        compiler_params=params(40),
        cost_estimate=cost(2 * matrix_count * size * size * count, 10 * matrix_count * size * size),
        name="weight_parts",
    )(own, left, right)
    parts = (2, 2, 2, 2, matrix_count, PIECE // 2, half)
    return [v.reshape(parts) for v in outs[:4]], [v.reshape(parts) for v in outs[4:8]], outs[8]


def halving(swapped):
    order = [("rep", 2), ("tab", 1)]
    return order[::-1] if swapped else order


def sum_start(total, step, swapped):
    axis, mask = halving(swapped)[step]
    return total[0], swap(total[1].astype(BF), axis, mask)


def sum_end(kept, token):
    value = kept[0] + token
    for other in kept[1:]:
        value = value + other.astype(F32)
    return value


def far_start(total):
    sent = [
        swap(total[high, low].astype(BF), "tab", 4 * high + 2 * low)
        for high, low in ((0, 1), (1, 0), (1, 1))
    ]
    return (total[0, 0], *sent)


def far_end(kept, token):
    piece = sum_end(kept, token).astype(BF)
    for axis, known in (("rep", 2), ("tab", 3)):
        for mask in masks_of(axis)[known:]:
            piece = (piece.astype(F32) + swap(piece, axis, mask).astype(F32)).astype(BF)
    return piece


def spread_far(piece):
    return (piece, swap(piece, "tab", 2), swap(piece, "tab", 4), swap(piece, "tab", 6))


def spread_near(value, step, swapped):
    axis, mask = halving(swapped)[step]
    return value, swap(value, axis, mask)


def join(parts, token):
    one = (1.0 + token).astype(BF)
    return jnp.stack((parts[0] * one,) + tuple(parts[1:]))


def assemble_kernel(layer_count, chunk_count, own_ref, *refs):
    chunks = refs[: 2 * chunk_count]
    strip_ref, cross_ref, first_ref, second_ref = refs[2 * chunk_count :]
    matrix = pl.program_id(0)
    lanes_count = chunk_count // 2

    def fill(out_ref):
        for chunk in range(chunk_count):
            above, lane = divmod(chunk, lanes_count)
            for core in range(2):
                ref = chunks[2 * chunk + core]
                count, _, rows, lanes = ref.shape
                for at in range(count):
                    piece = (core * count + at) ^ own_ref[0]
                    first = pl.multiple_of(piece * PIECE + above * rows, rows)
                    out_ref[0, pl.ds(first, rows), lane * lanes : (lane + 1) * lanes] = ref[
                        chunk_place(at, lane == 1), 0
                    ].astype(F32)
        height, width = out_ref.shape[1:]
        if width > MAIN:
            extra = width - MAIN
            for first in range(0, MAIN, 128):
                turned = strip_ref[0, :, first : first + 128].T
                out_ref[0, first : first + 128, MAIN:] = turned[:, 3 : 3 + extra]
        if height > MAIN:
            out_ref[0, MAIN:, :] = strip_ref[0, 0 : height - MAIN, :width]

    @pl.when(matrix < layer_count)
    def _():
        fill(cross_ref)

    @pl.when(matrix == layer_count)
    def _():
        fill(first_ref)

    @pl.when(matrix == layer_count + 1)
    def _():
        fill(second_ref)


def assemble(chunks, strips, own, layer_count, width, hidden):
    matrix_count = layer_count + 2
    size = strips.shape[2]
    specs = []
    for chunk in chunks:
        specs.append(pl.BlockSpec((chunk.shape[0], 1) + chunk.shape[2:], lambda m: (0, m, 0, 0)))
    return pl.pallas_call(
        functools.partial(assemble_kernel, layer_count, len(chunks) // 2),
        grid=(matrix_count,),
        in_specs=[pl.BlockSpec(memory_space=pltpu.SMEM)]
        + specs
        + [pl.BlockSpec((1, 8, size), lambda m: (m, 0, 0))],
        out_specs=[
            pl.BlockSpec((1, width, width), lambda m: (jnp.minimum(m, layer_count - 1), 0, 0)),
            pl.BlockSpec((1, width, hidden), lambda m: (0, 0, 0)),
            pl.BlockSpec((1, hidden, hidden), lambda m: (0, 0, 0)),
        ],
        out_shape=[
            jax.ShapeDtypeStruct((layer_count, width, width), F32),
            jax.ShapeDtypeStruct((1, width, hidden), F32),
            jax.ShapeDtypeStruct((1, hidden, hidden), F32),
        ],
        compiler_params=params(56),
        cost_estimate=cost(0, 6 * matrix_count * size * size),
        name="assemble",
    )(own, *chunks, strips)


def on_device(
    ids,
    table_rows,
    table_place,
    dense_in,
    labels,
    tables,
    cross_w,
    cross_b,
    tower1_w,
    tower1_b,
    tower2_w,
    tower2_b,
    out_w,
    out_b,
):
    tab_count = lax.axis_size("tab")
    rep_count = lax.axis_size("rep")
    slot_count, embed_dim, table_len = tables.shape
    row_count, dense_width = dense_in.shape
    field_count = ids.shape[1]
    layer_count, width = cross_w.shape[:2]
    hidden = tower1_w.shape[0]
    size = round_up(width, 128)
    all_slots = slot_count * tab_count
    tab_at = lax.axis_index("tab")
    rep_at = lax.axis_index("rep")

    matches = table_place[:, None] == jnp.arange(all_slots, dtype=I32)[None, :]
    effective = ids % table_rows[None, :]
    by_slot = jnp.sum(jnp.where(matches[:, :, None], effective.T[:, None, :], 0), axis=0)
    slot_rows = jnp.sum(jnp.where(matches, table_rows[:, None], 0), axis=0)
    own_rows = lax.dynamic_slice_in_dim(slot_rows, tab_at * slot_count, slot_count)
    wanted = lax.all_to_all(
        by_slot.reshape(tab_count, slot_count, row_count), "tab", split_axis=0, concat_axis=0, tiled=True
    )
    listed = jnp.transpose(wanted, (1, 0, 2)).reshape(-1)

    starts = list(range(0, slot_count, LOOK_SLOTS))
    arrived = []
    for begin in starts:
        looked = lookup(
            tables, listed, own_rows, tab_count, begin, min(LOOK_SLOTS, slot_count - begin)
        )
        ready = 1.0 + looked[0, 0, embed_dim, 0]
        arrived.append(lax.all_to_all(looked, "tab", split_axis=0, concat_axis=0, tiled=True))

    def padded(weight):
        return jnp.pad(weight * ready, ((0, size - weight.shape[0]), (0, size - weight.shape[1])))

    weights = jnp.stack(
        [padded(cross_w[at]) for at in range(layer_count)] + [padded(tower1_w.T), padded(tower2_w)]
    )
    vectors = [cross_b[at] for at in range(layer_count)]
    vectors += [tower1_b, tower2_b, out_w[:width], out_w[width:], out_w[:0]]
    cols = jnp.stack([jnp.pad(v.astype(F32), (0, size - v.shape[0])) for v in vectors], axis=1)

    logits, dense_grad, slots, left, right, sums = dense_step(
        arrived, starts, table_place, dense_in, labels, weights, cols, out_b, layer_count, width
    )
    returned = lax.all_to_all(
        slots.reshape(tab_count, slot_count, slots.shape[1], row_count),
        "tab",
        split_axis=0,
        concat_axis=0,
        tiled=True,
    )

    share = table_len // rep_count
    base = (rep_at * share).astype(I32).reshape(1)

    def near_parts(own):
        return [own, swap(own, "rep", 1)]

    def far_parts(own):
        bases = [own]
        for mask in masks_of("rep")[1:]:
            bases = bases + [swap(part, "rep", mask) for part in bases]
        return [part for far in bases[1:] for part in near_parts(far)]

    bits = [rep_at & 1, (rep_at >> 1) & 1, tab_at & 1, (tab_at >> 2) & 1, (tab_at >> 1) & 1]
    own = sum(bit << (4 - at) for at, bit in enumerate(bits)).astype(I32).reshape(1)
    keep, send, strips = weight_parts(left, right, own)
    matrix_count = layer_count + 2
    near_ids = near_parts(wanted)
    far_ids = far_parts(wanted)
    near_grads = near_parts(returned)
    far_grads = None
    table_grad = None
    waves = [(0, 1), (2, 3)]
    token = jnp.zeros((), F32)
    state = [None] * 4
    for at in range(4):
        total = keep[at] + swap(send[at], "rep", 1).astype(F32)
        state[at] = sum_start(total, 0, at % 2 == 1)

    jobs = [(near_ids, True, slot) for slot in range(slot_count)]
    jobs += [(far_ids, False, slot) for slot in range(slot_count)]
    jobs = jobs[::-1]

    def add_next(after):
        nonlocal table_grad, token, far_grads
        if not jobs:
            return
        part_ids, near, slot = jobs.pop()
        if not near and far_grads is None:
            far_grads = far_parts(returned + token.astype(BF))
        table_grad, token = add_rows(
            near_grads if near else far_grads,
            part_ids,
            base,
            share,
            embed_dim,
            slot,
            table_grad,
            not near,
            after,
        )

    def start_far():
        nonlocal far_grads
        far_grads = far_parts(returned + token.astype(BF))

    def wave(chunks, act):
        for at in chunks:
            state[at] = act(at, state[at])

    def first_sum(at, kept):
        return sum_start(sum_end(kept, token), 1, at % 2 == 1)

    def second_sum(at, kept):
        return far_start(sum_end(kept, token))

    def last_sum(at, kept):
        return spread_far(far_end(kept, token))

    def far_join(at, parts):
        value = join(parts, token)
        return spread_near(value.reshape((2, 2) + value.shape[1:]), 1, at % 2 == 1)

    def second_join(at, parts):
        return spread_near(join(parts, token), 0, at % 2 == 1)

    def first_join(at, parts):
        value = join(parts, token)
        value = value.reshape((MAIN // PIECE // 2,) + value.shape[4:])
        return value, swap(value, "rep", 1)

    add_next([state[1][0]])
    wave(waves[0], first_sum)
    add_next([state[1][0]])
    wave(waves[1], first_sum)
    start_far()
    add_next([state[3][0]])
    wave(waves[0], second_sum)
    add_next([state[1][0]])
    wave(waves[1], second_sum)
    add_next([state[3][0]])
    wave(waves[0], last_sum)
    wave(waves[1], last_sum)
    add_next([state[3][0]])
    wave(waves[0], far_join)
    add_next([state[1][0]])
    wave(waves[1], far_join)
    add_next([state[3][0]])
    wave(waves[0], second_join)
    add_next([state[1][0]])
    wave(waves[1], second_join)
    while jobs:
        add_next([state[3][0]])
    wave(waves[0], first_join)
    wave(waves[1], first_join)
    chunks = [part for at in range(4) for part in state[at]]

    small = jnp.concatenate([strips.reshape(matrix_count * 8, size), sums], axis=0)
    for axis in ("rep", "tab"):
        for mask in masks_of(axis):
            small = small + swap(small, axis, mask)
    strips = small[:-8].reshape(matrix_count, 8, size)
    sums = small[-8:]
    cross_w_grad, tower1_w_grad, tower2_w_grad = assemble(
        chunks, strips, own, layer_count, width, hidden
    )
    scalars = sums[layer_count + 4]
    return (
        scalars[0] / (row_count * tab_count * rep_count),
        logits.reshape(row_count),
        dense_grad[:dense_width].T,
        cross_w_grad,
        sums[:layer_count, :width],
        tower1_w_grad[0].T,
        sums[layer_count, :hidden],
        tower2_w_grad[0],
        sums[layer_count + 1, :hidden],
        jnp.concatenate([sums[layer_count + 2, :width], sums[layer_count + 3, :hidden]]),
        scalars[128],
        table_grad,
    )


def solution(mesh):
    placed = (
        P(("tab", "rep"), None),
        P(),
        P(),
        P(("tab", "rep"), None),
        P(("tab", "rep")),
        P("tab", None, None),
        P(),
        P(),
        P(),
        P(),
        P(),
        P(),
        P(),
        P(),
    )
    return jax.shard_map(
        on_device,
        mesh=mesh,
        in_specs=placed,
        out_specs=(
            P(),
            P(("tab", "rep")),
            P(("tab", "rep"), None),
            P(),
            P(),
            P(),
            P(),
            P(),
            P(),
            P(),
            P(),
            P("tab", None, "rep"),
        ),
        check_vma=False,
    )
```

time: 565 us -> 467 us (0.83)
  local copies, waits for them, and re-layouts: 109 us -> 41.5 us
  waiting for transfers between devices: 126 us -> 87.4 us
  starting transfers between devices: 122 us -> 93.6 us
  other arithmetic: 26.1 us -> 45.8 us
  Pallas kernels: 178 us -> 185 us
    ppermute x59, waiting for transfers between devices: 106 us -> 71.7 us  [swap(): lax.ppermute(value, axis, [(at, at ^ mask) for at in range(lax.axis_size(...]
    all_to_all x1 -> x2, starting transfers between devices: 43.2 us -> 19.4 us  [on_device(): lax.all_to_all(looked, 'tab', split_axis=0, concat_axis=0, tiled=True)]
    reshape x2 -> x0, local copies, waits for them, and re-layouts: 23.8 us -> none  [the longest x1 14.3 us: on_device(): keep = keep.reshape(parts)]
    slice x2 -> x11, local copies, waits for them, and re-layouts: 28.6 us -> 6.32 us  [the longest x10 5.12 us: add_rows(): return (table_grad, token[0, 0])]
    unnamed x36 -> x63, local copies, waits for them, and re-layouts: 34.6 us -> 17.6 us
    add x8 -> x9, other arithmetic: 7.51 us -> 18.6 us  [the longest x4 11 us: on_device(): total = keep[at] + swap(send[at], 'rep', 1).astype(F32)]
    pallas_call x7 -> x13, Pallas kernels: 152 us -> 160 us  [the longest x10 95 us: add_rows(): pl.pallas_call(functools.partial(add_kernel, part_count, accumulate), gri...]
    ppermute x3 -> x0, local copies, waits for them, and re-layouts: 5.68 us -> none  [swap(): lax.ppermute(value, axis, [(at, at ^ mask) for at in range(lax.axis_size(...]
  transfers between devices with their start and end apart: 62 -> 63, of which waited for: 18 -> 14; matrix products, arithmetic and copies ran while one was open for 21% -> 15% of each run, Pallas kernels for 2% -> 28%
where the time goes in v3:
time: 467 us; the launch traced here: 463 us
  Pallas kernels  185 us (40%)
  starting transfers between devices  93.6 us (20%)
  waiting for transfers between devices  87.4 us (19%)
  other arithmetic  45.8 us (10%)
  local copies, waits for them, and re-layouts  41.5 us (9%)
  between operations  8.85 us (2%)
    pallas_call x10, Pallas kernels, add_rows(): pl.pallas_call(functools.partial(add_kernel, part_count, accumulate), gri...  95 us
    ppermute x59, waiting for transfers between devices, swap(): lax.ppermute(value, axis, [(at, at ^ mask) for at in range(lax.axis_size(...  71.7 us
    ppermute x59, starting transfers between devices, swap(): lax.ppermute(value, axis, [(at, at ^ mask) for at in range(lax.axis_size(...  63.4 us
    pallas_call x2, Pallas kernels, lookup(): pl.pallas_call(functools.partial(lookup_kernel, first_slot), in_specs=[sm...  36.8 us
    pallas_call x1, Pallas kernels, dense_step(): pl.pallas_call(functools.partial(dense_kernel, dense_width, width, starts...  27.8 us
    all_to_all x2, starting transfers between devices, on_device(): lax.all_to_all(looked, 'tab', split_axis=0, concat_axis=0, tiled=True)  19.4 us
    unnamed x63, local copies, waits for them, and re-layouts  17.6 us
    all_to_all x2, waiting for transfers between devices, on_device(): lax.all_to_all(looked, 'tab', split_axis=0, concat_axis=0, tiled=True)  15.8 us
  transfers between devices with their start and end apart: 63, of which 14 were waited for; matrix products, arithmetic and copies ran while one was open for 15% of the time, Pallas kernels for 28%

profile of v3, /device:TPU:0, one launch (start us, length us, event | category | flops | bytes accessed | tf_op | source)
XLA Modules:
  0.0 462.6 jit_solution(316409534266601248)
XLA Ops:
  5.2 7.3 %all-to-all-start = ((s32[8,5,512]{2,1,0:T(8,128)}), s32[8,5,512]{2,1,0:T(8,128)S(1)}, u32[]{:S(2)}, u32[]{:S(2)}) async-start(s32[8,5,512]{2,1,0:T(8,128)} %reshape.376), calls=%async_computation | async-start | bytes 262144 | tf_op jit(solution)/shard_map/all_to_all | solution.py:613
  22.7 13.4 %lookup.3 = bf16[8,2,40,512]{3,2,1,0:T(8,128)(2,1)} custom-call(s32[20480]{0:T(1024)} %bitcast.291, s32[5]{0:T(128)} %dynamic_slice.3.rows_ref, bf16[5,39,32768]{2,1,0:T(8,128)(2,1)} %table_hbm.3), custom_call_target="tpu_custom_call" | custom-call | flops 20132659200 | bytes 5750784 | tf_op jit(solution)/shard_map/lookup/pallas_call | solution.py:100
  37.4 11.8 %all-to-all-start.2 = ((bf16[8,2,40,512]{3,2,1,0:T(8,128)(2,1)}), bf16[8,2,40,512]{3,2,1,0:T(8,128)(2,1)S(1)}, u32[]{:S(2)}, u32[]{:S(2)}) async-start(bf16[8,2,40,512]{3,2,1,0:T(8,128)(2,1)} %lookup.3), calls=%async_computation.2 | async-start | bytes 1310720 | tf_op jit(solution)/shard_map/all_to_all | solution.py:625
  49.2 23.3 %lookup.2 = bf16[8,3,40,512]{3,2,1,0:T(8,128)(2,1)} custom-call(s32[20480]{0:T(1024)} %bitcast.292, s32[5]{0:T(128)} %dynamic_slice.3.rows_ref, bf16[5,39,32768]{2,1,0:T(8,128)(2,1)} %table_hbm.3), custom_call_target="tpu_custom_call" | custom-call | flops 30198988800 | bytes 8626176 | tf_op jit(solution)/shard_map/lookup/pallas_call | solution.py:100
  74.7 3.3 multiply_bitcast_fusion
  81.4 7.5 %all-to-all-start.1 = ((bf16[8,3,40,512]{3,2,1,0:T(8,128)(2,1)}), bf16[8,3,40,512]{3,2,1,0:T(8,128)(2,1)}, u32[]{:S(2)}, u32[]{:S(2)}) async-start(bf16[8,3,40,512]{3,2,1,0:T(8,128)(2,1)} %lookup.2), calls=%async_computation.1 | async-start | bytes 1966080 | tf_op jit(solution)/shard_map/all_to_all | solution.py:625
  96.6 15.8 %all-to-all-done.1.refs_0_ = bf16[8,3,40,512]{3,2,1,0:T(8,128)(2,1)} async-done(((bf16[8,3,40,512]{3,2,1,0:T(8,128)(2,1)}), bf16[8,3,40,512]{3,2,1,0:T(8,128)(2,1)}, u32[]{:S(2)}, u32[]{:S(2)}) %all-to-all-start.1) | async-done | bytes 983072 | tf_op jit(solution)/shard_map/all_to_all | solution.py:625
  112.3 27.8 %dense.1 = (f32[1,512]{1,0:T(1,128)}, f32[16,512]{1,0:T(8,128)}, bf16[40,40,512]{2,1,0:T(8,128)(2,1)}, bf16[5,1152,512]{2,1,0:T(8,128)(2,1)}, bf16[5,1152,512]{2,1,0:T(8,128)(2,1)}, /*index=5*/f32[8,1152]{1,0:T(8,128)}) custom-call(s32[26]{0:T(128)} %place_ref.1, f32[1]{0:T(128)S(6)} %convert.84.bias_ref, bf16[8,3,40,512]{3,2,1,0:T(8,128)(2,1)} %all-to-all-done.1.refs_0_, ...), custom_call_target="tpu_custom_call" | custom-call | flops 13589544960 | bytes 30965760 | tf_op jit(solution)/shard_map/dense/pallas_call | solution.py:364
  140.1 3.6 all-to-all-start.3
  143.8 12.6 %weight_parts.1 = (f32[16,5,16,512]{3,2,1,0:T(8,128)S(1)}, f32[16,5,16,512]{3,2,1,0:T(8,128)S(1)}, f32[16,5,16,512]{3,2,1,0:T(8,128)S(1)}, f32[16,5,16,512]{3,2,...) custom-call(s32[1]{0:T(128)} %bitcast.own_ref, ...), custom_call_target="tpu_custom_call" | custom-call | flops 6794772480 | bytes 66355200 | tf_op jit(solution)/shard_map/weight_parts/pallas_call | solution.py:444
  166.8 6.2 %collective-permute-done.1 = f32[48,1152]{1,0:T(8,128)S(1)} collective-permute-done((f32[48,1152]{1,0:T(8,128)S(1)}, f32[48,1152]{1,0:T(8,128)S(1)}, u32[]{:S(2)}, u32[]{:S(2)}) %collective-permute-start.1) | collective-permute-done | bytes 221216 | tf_op jit(solution)/shard_map/ppermute | solution.py:39
  177.2 3.5 collective-permute-done.19
  191.6 3.3 convert_add_fusion.2
  197.0 2.9 convert_add_fusion.1
  206.6 8.7 %add_rows.10 = (f32[5,39,8192]{2,1,0:T(8,128)}, f32[8,128]{1,0:T(8,128)S(1)}) custom-call(s32[1]{0:T(128)} %bitcast.22.base_ref, s32[8,5,1,512]{3,2,1,0:T(1,128)S(1)} %copy.187.refs_0_, s32[8,5,1,512]{3,2,1,0:T(1,128)S(1)} %copy.188.refs_1_, bf16[8,5,40,512]{3,2,1,0:T(8,128)(2,1)S(1)} %all-to-all-done.3.refs_2_, ...), custom_call_target="tpu_custom_call" | custom-call | flops 5234491392 | bytes 1916928 | tf_op jit(solution)/shard_map/add_rows/pallas_call | solution.py:172
  223.3 8.8 %add_rows.11 = (f32[5,39,8192]{2,1,0:T(8,128)}, f32[8,128]{1,0:T(8,128)S(1)}) custom-call(s32[1]{0:T(128)} %bitcast.22.base_ref, s32[8,5,1,512]{3,2,1,0:T(1,128)S(1)} %copy.187.refs_0_, s32[8,5,1,512]{3,2,1,0:T(1,128)S(1)} %copy.188.refs_1_, bf16[8,5,40,512]{3,2,1,0:T(8,128)(2,1)S(1)} %all-to-all-done.3.refs_2_, ...), custom_call_target="tpu_custom_call", output_to_operand_aliasing={{0}: (5, {})} | custom-call | flops 5234491392 | bytes 1916928 | tf_op jit(solution)/shard_map/add_rows/pallas_call | solution.py:172
  239.5 8.7 %add_rows.12 = (f32[5,39,8192]{2,1,0:T(8,128)}, f32[8,128]{1,0:T(8,128)S(1)}) custom-call(s32[1]{0:T(128)} %bitcast.22.base_ref, s32[8,5,1,512]{3,2,1,0:T(1,128)S(1)} %copy.187.refs_0_, s32[8,5,1,512]{3,2,1,0:T(1,128)S(1)} %copy.188.refs_1_, bf16[8,5,40,512]{3,2,1,0:T(8,128)(2,1)S(1)} %all-to-all-done.3.refs_2_, ...), custom_call_target="tpu_custom_call", output_to_operand_aliasing={{0}: (5, {})} | custom-call | flops 5234491392 | bytes 1916928 | tf_op jit(solution)/shard_map/add_rows/pallas_call | solution.py:172
  253.8 8.9 %add_rows.13 = (f32[5,39,8192]{2,1,0:T(8,128)}, f32[8,128]{1,0:T(8,128)S(1)}) custom-call(s32[1]{0:T(128)} %bitcast.22.base_ref, s32[8,5,1,512]{3,2,1,0:T(1,128)S(1)} %copy.187.refs_0_, s32[8,5,1,512]{3,2,1,0:T(1,128)S(1)} %copy.188.refs_1_, bf16[8,5,40,512]{3,2,1,0:T(8,128)(2,1)S(1)} %all-to-all-done.3.refs_2_, ...), custom_call_target="tpu_custom_call", output_to_operand_aliasing={{0}: (5, {})} | custom-call | flops 5234491392 | bytes 1916928 | tf_op jit(solution)/shard_map/add_rows/pallas_call | solution.py:172
  264.1 21.3 %collective-permute-done.21.refs_2_ = bf16[8,5,40,512]{3,2,1,0:T(8,128)(2,1)S(1)} collective-permute-done((bf16[8,5,40,512]{3,2,1,0:T(8,128)(2,1)S(1)}, bf16[8,5,40,512]{3,2,1,0:T(8,128)(2,1)S(1)}, u32[]{:S(2)}, u32[]{:S(2)}) %collective-permute-start.21) | collective-permute-done | bytes 1638432 | tf_op jit(solution)/shard_map/ppermute | solution.py:39
  286.0 3.4 collective-permute-start.25
  290.3 8.8 %add_rows.14 = (f32[5,39,8192]{2,1,0:T(8,128)}, f32[8,128]{1,0:T(8,128)S(1)}) custom-call(s32[1]{0:T(128)} %bitcast.22.base_ref, s32[8,5,1,512]{3,2,1,0:T(1,128)S(1)} %copy.187.refs_0_, s32[8,5,1,512]{3,2,1,0:T(1,128)S(1)} %copy.188.refs_1_, bf16[8,5,40,512]{3,2,1,0:T(8,128)(2,1)S(1)} %all-to-all-done.3.refs_2_, ...), custom_call_target="tpu_custom_call", output_to_operand_aliasing={{0}: (5, {})} | custom-call | flops 5234491392 | bytes 1916928 | tf_op jit(solution)/shard_map/add_rows/pallas_call | solution.py:172
  305.3 10.2 %add_rows.15 = (f32[5,39,8192]{2,1,0:T(8,128)}, f32[8,128]{1,0:T(8,128)S(1)}) custom-call(s32[1]{0:T(128)} %bitcast.22.base_ref, s32[8,5,1,512]{3,2,1,0:T(1,128)S(1)} %copy.199.refs_0_, s32[8,5,1,512]{3,2,1,0:T(1,128)S(1)} %copy.200.refs_1_, bf16[8,5,40,512]{3,2,1,0:T(8,128)(2,1)S(1)} %collective-permute-done.21.refs_2_, ...), custom_call_target="tpu_custom_call", output_to_operand_aliasing={{0}: (5, {})} | custom-call | flops 5234491392 | bytes 1916928 | tf_op jit(solution)/shard_map/add_rows/pallas_call | solution.py:172
  316.6 3.0 collective-permute-start.18
  323.4 3.5 collective-permute-start.32
  336.6 10.2 %add_rows.16 = (f32[5,39,8192]{2,1,0:T(8,128)}, f32[8,128]{1,0:T(8,128)S(1)}) custom-call(s32[1]{0:T(128)} %bitcast.22.base_ref, s32[8,5,1,512]{3,2,1,0:T(1,128)S(1)} %copy.199.refs_0_, s32[8,5,1,512]{3,2,1,0:T(1,128)S(1)} %copy.200.refs_1_, bf16[8,5,40,512]{3,2,1,0:T(8,128)(2,1)S(1)} %collective-permute-done.21.refs_2_, ...), custom_call_target="tpu_custom_call", output_to_operand_aliasing={{0}: (5, {})} | custom-call | flops 5234491392 | bytes 1916928 | tf_op jit(solution)/shard_map/add_rows/pallas_call | solution.py:172
  353.0 10.2 %add_rows.17 = (f32[5,39,8192]{2,1,0:T(8,128)}, f32[8,128]{1,0:T(8,128)S(1)}) custom-call(s32[1]{0:T(128)} %bitcast.22.base_ref, s32[8,5,1,512]{3,2,1,0:T(1,128)S(1)} %copy.199.refs_0_, s32[8,5,1,512]{3,2,1,0:T(1,128)S(1)} %copy.200.refs_1_, bf16[8,5,40,512]{3,2,1,0:T(8,128)(2,1)S(1)} %collective-permute-done.21.refs_2_, ...), custom_call_target="tpu_custom_call", output_to_operand_aliasing={{0}: (5, {})} | custom-call | flops 5234491392 | bytes 1916928 | tf_op jit(solution)/shard_map/add_rows/pallas_call | solution.py:172
  377.6 10.4 %add_rows.18 = (f32[5,39,8192]{2,1,0:T(8,128)}, f32[8,128]{1,0:T(8,128)S(1)}) custom-call(s32[1]{0:T(128)} %bitcast.22.base_ref, s32[8,5,1,512]{3,2,1,0:T(1,128)S(1)} %copy.199.refs_0_, s32[8,5,1,512]{3,2,1,0:T(1,128)S(1)} %copy.200.refs_1_, bf16[8,5,40,512]{3,2,1,0:T(8,128)(2,1)S(1)} %collective-permute-done.21.refs_2_, ...), custom_call_target="tpu_custom_call", output_to_operand_aliasing={{0}: (5, {})} | custom-call | flops 5234491392 | bytes 1916928 | tf_op jit(solution)/shard_map/add_rows/pallas_call | solution.py:172
  393.6 10.2 %add_rows.19 = (f32[5,39,8192]{2,1,0:T(8,128)}, f32[8,128]{1,0:T(8,128)S(1)}) custom-call(s32[1]{0:T(128)} %bitcast.22.base_ref, s32[8,5,1,512]{3,2,1,0:T(1,128)S(1)} %copy.199.refs_0_, s32[8,5,1,512]{3,2,1,0:T(1,128)S(1)} %copy.200.refs_1_, bf16[8,5,40,512]{3,2,1,0:T(8,128)(2,1)S(1)} %collective-permute-done.21.refs_2_, ...), custom_call_target="tpu_custom_call", output_to_operand_aliasing={{0}: (5, {})} | custom-call | flops 5234491392 | bytes 1916928 | tf_op jit(solution)/shard_map/add_rows/pallas_call | solution.py:172
  405.8 11.2 %collective-permute-done.54 = bf16[2,2,5,16,512]{4,3,2,1,0:T(8,128)(2,1)S(1)} collective-permute-done((bf16[2,2,5,16,512]{4,3,2,1,0:T(8,128)(2,1)S(1)}, bf16[2,2,5,16,512]{4,3,2,1,0:T(8,128)(2,1)S(1)}, u32[]{:S(2)}, u32[]{:S(2)}) %collective-permute-start.54) | collective-permute-done | bytes 327712 | tf_op jit(solution)/shard_map/ppermute | solution.py:39
  418.9 5.2 %collective-permute-done.57 = bf16[2,2,2,5,16,512]{5,4,3,2,1,0:T(8,128)(2,1)S(1)} collective-permute-done((bf16[2,2,2,5,16,512]{5,4,3,2,1,0:T(8,128)(2,1)S(1)}, bf16[2,2,2,5,16,512]{5,4,3,2,1,0:T(8,128)(2,1)S(1)}, u32[]{:S(2)}, u32[]{:S(2)}) %collective-permute-start.57) | collective-permute-done | bytes 655392 | tf_op jit(solution)/shard_map/ppermute | solution.py:39
  430.9 11.3 %collective-permute-done.4 = f32[48,1152]{1,0:T(8,128)S(1)} collective-permute-done((f32[48,1152]{1,0:T(8,128)S(1)}, f32[48,1152]{1,0:T(8,128)S(1)}, u32[]{:S(2)}, u32[]{:S(2)}) %collective-permute-start.4) | collective-permute-done | bytes 221216 | tf_op jit(solution)/shard_map/ppermute | solution.py:39
  447.9 13.3 %assemble.1 = (f32[3,1027,1027]{2,1,0:T(8,128)}, f32[1,1027,1024]{2,1,0:T(8,128)}, f32[1,1024,1024]{2,1,0:T(8,128)}) custom-call(s32[1]{0:T(128)} %bitcast.own_ref, bf16[16,5,16,512]{3,2,1,0:T(8,128)(2,1)} %bitcast.242, bf16[16,5,16,512]{3,2,1,0:T(8,128)(2,1)} %copy-done.25, bf16[16,5,16,512]{3,2,1,0:T(8,128)(2,1)} %bitcast.238, ...), custom_call_target="tpu_custom_call" | custom-call | bytes 39813120 | tf_op jit(solution)/shard_map/assemble/pallas_call | solution.py:558
  (286 shorter events, 144.1 us)
Async XLA Ops:
  37.4 44.1 %all-to-all-start.2 = ((bf16[8,2,40,512]{3,2,1,0:T(8,128)(2,1)}), bf16[8,2,40,512]{3,2,1,0:T(8,128)(2,1)S(1)}, u32[]{:S(2)}, u32[]{:S(2)}) async-start(bf16[8,2,40,512]{3,2,1,0:T(8,128)(2,1)} %lookup.3), calls=%async_computation.2 | async-start | bytes 1310720 | tf_op jit(solution)/shard_map/all_to_all | solution.py:625
  81.4 30.9 %all-to-all-start.1 = ((bf16[8,3,40,512]{3,2,1,0:T(8,128)(2,1)}), bf16[8,3,40,512]{3,2,1,0:T(8,128)(2,1)}, u32[]{:S(2)}, u32[]{:S(2)}) async-start(bf16[8,3,40,512]{3,2,1,0:T(8,128)(2,1)} %lookup.2), calls=%async_computation.1 | async-start | bytes 1966080 | tf_op jit(solution)/shard_map/all_to_all | solution.py:625
  140.1 54.8 %all-to-all-start.3 = ((bf16[8,5,40,512]{3,2,1,0:T(8,128)(2,1)}), bf16[8,5,40,512]{3,2,1,0:T(8,128)(2,1)S(1)}, u32[]{:S(2)}, u32[]{:S(2)}) async-start(bf16[8,5,40,512]{3,2,1,0:T(8,128)(2,1)} %bitcast.254), calls=%async_computation.3 | async-start | bytes 3276800 | tf_op jit(solution)/shard_map/all_to_all | solution.py:640
  162.0 24.4 %collective-permute-start.5 = (bf16[2,2,2,2,5,16,512]{6,5,4,3,2,1,0:T(8,128)(2,1)}, bf16[2,2,2,2,5,16,512]{6,5,4,3,2,1,0:T(8,128)(2,1)}, u32[]{:S(2)}, u32[]{:S(2)}) collective-permute-start(bf16[2,2,2,2,5,16,512]{6,5,4,3,2,1,0:T(8,128)(2,1)} %bitcast.21), channel_id=1, source_target_pairs={{0,1},{1,0},{2,3},{3,2},{4,5},{5,4},{6,7},{7,6},{8,9},{9,8},{10,11... | collective-permute-start | bytes 3932168 | tf_op jit(solution)/shard_map/ppermute | solution.py:39
  162.6 29.0 %collective-permute-start.8 = (bf16[2,2,2,2,5,16,512]{6,5,4,3,2,1,0:T(8,128)(2,1)}, bf16[2,2,2,2,5,16,512]{6,5,4,3,2,1,0:T(8,128)(2,1)}, u32[]{:S(2)}, u32[]{:S(2)}) collective-permute-start(bf16[2,2,2,2,5,16,512]{6,5,4,3,2,1,0:T(8,128)(2,1)} %bitcast.27), channel_id=1, source_target_pairs={{0,1},{1,0},{2,3},{3,2},{4,5},{5,4},{6,7},{7,6},{8,9},{9,8},{10,11... | collective-permute-start | bytes 3932168 | tf_op jit(solution)/shard_map/ppermute | solution.py:39
  183.4 17.6 %collective-permute-start.45 = (bf16[2,2,2,2,5,16,512]{6,5,4,3,2,1,0:T(8,128)(2,1)S(1)}, bf16[2,2,2,2,5,16,512]{6,5,4,3,2,1,0:T(8,128)(2,1)}, u32[]{:S(2)}, u32[]{:S(2)}) collective-permute-start(bf16[2,2,2,2,5,16,512]{6,5,4,3,2,1,0:T(8,128)(2,1)S(1)} %bitcast.235), channel_id=1, source_target_pairs={{0,1},{1,0},{2,3},{3,2},{4,5},{5,4},{6,7},{7,6},{8,9},{9,8},{10,11... | collective-permute-start | bytes 3932168 | tf_op jit(solution)/shard_map/ppermute | solution.py:39
  184.8 243.2 %collective-permute-start.3 = (f32[48,1152]{1,0:T(8,128)S(1)}, f32[48,1152]{1,0:T(8,128)}, u32[]{:S(2)}, u32[]{:S(2)}) collective-permute-start(f32[48,1152]{1,0:T(8,128)S(1)} %add.264), channel_id=1, source_target_pairs={{0,8},{4,12},{8,0},{12,4},{16,24},{20,28},{24,16},{28,20},{1,9},{5... | collective-permute-start | bytes 663560 | tf_op jit(solution)/shard_map/ppermute | solution.py:39
  190.1 25.7 %collective-permute-start.9 = (bf16[2,2,2,5,16,512]{5,4,3,2,1,0:T(8,128)(2,1)}, bf16[2,2,2,5,16,512]{5,4,3,2,1,0:T(8,128)(2,1)}, u32[]{:S(2)}, u32[]{:S(2)}) collective-permute-start(bf16[2,2,2,5,16,512]{5,4,3,2,1,0:T(8,128)(2,1)} %fusion.6), channel_id=1, source_target_pairs={{0,2},{1,3},{2,0},{3,1},{4,6},{5,7},{6,4},{7,5},{8,10},{9,11},{10,... | collective-permute-start | bytes 1966088 | tf_op jit(solution)/shard_map/ppermute | solution.py:39
  196.4 22.4 %collective-permute-start.10 = (bf16[2,2,2,5,16,512]{5,4,3,2,1,0:T(8,128)(2,1)S(1)}, bf16[2,2,2,5,16,512]{5,4,3,2,1,0:T(8,128)(2,1)S(1)}, u32[]{:S(2)}, u32[]{:S(2)}) collective-permute-start(bf16[2,2,2,5,16,512]{5,4,3,2,1,0:T(8,128)(2,1)S(1)} %fusion.7), channel_id=1, source_target_pairs={{0,4},{4,0},{8,12},{12,8},{16,20},{20,16},{24,28},{28,24},{1,5},{5... | collective-permute-start | bytes 1966088 | tf_op jit(solution)/shard_map/ppermute | solution.py:39
  201.0 32.2 %collective-permute-start.12 = (bf16[2,2,2,5,16,512]{5,4,3,2,1,0:T(8,128)(2,1)}, bf16[2,2,2,5,16,512]{5,4,3,2,1,0:T(8,128)(2,1)}, u32[]{:S(2)}, u32[]{:S(2)}) collective-permute-start(bf16[2,2,2,5,16,512]{5,4,3,2,1,0:T(8,128)(2,1)} %fusion.8), channel_id=1, source_target_pairs={{0,4},{4,0},{8,12},{12,8},{16,20},{20,16},{24,28},{28,24},{1,5},{5... | collective-permute-start | bytes 1966088 | tf_op jit(solution)/shard_map/ppermute | solution.py:39
  205.9 30.1 %collective-permute-start.46 = (bf16[2,2,2,5,16,512]{5,4,3,2,1,0:T(8,128)(2,1)}, bf16[2,2,2,5,16,512]{5,4,3,2,1,0:T(8,128)(2,1)}, u32[]{:S(2)}, u32[]{:S(2)}) collective-permute-start(bf16[2,2,2,5,16,512]{5,4,3,2,1,0:T(8,128)(2,1)} %fusion.9), channel_id=1, source_target_pairs={{0,2},{1,3},{2,0},{3,1},{4,6},{5,7},{6,4},{7,5},{8,10},{9,11},{10,... | collective-permute-start | bytes 1966088 | tf_op jit(solution)/shard_map/ppermute | solution.py:39
  220.4 28.4 %collective-permute-start.14 = (bf16[2,2,5,16,512]{4,3,2,1,0:T(8,128)(2,1)}, bf16[2,2,5,16,512]{4,3,2,1,0:T(8,128)(2,1)}, u32[]{:S(2)}, u32[]{:S(2)}) collective-permute-start(bf16[2,2,5,16,512]{4,3,2,1,0:T(8,128)(2,1)} %fusion.15), channel_id=1, source_target_pairs={{0,2},{1,3},{2,0},{3,1},{4,6},{5,7},{6,4},{7,5},{8,10},{9,11},{10,... | collective-permute-start | bytes 983048 | tf_op jit(solution)/shard_map/ppermute | solution.py:39
  221.8 30.3 %collective-permute-start.13 = (bf16[2,2,5,16,512]{4,3,2,1,0:T(8,128)(2,1)}, bf16[2,2,5,16,512]{4,3,2,1,0:T(8,128)(2,1)}, u32[]{:S(2)}, u32[]{:S(2)}) collective-permute-start(bf16[2,2,5,16,512]{4,3,2,1,0:T(8,128)(2,1)} %fusion.14), channel_id=1, source_target_pairs={{0,4},{4,0},{8,12},{12,8},{16,20},{20,16},{24,28},{28,24},{1,5},{5... | collective-permute-start | bytes 983048 | tf_op jit(solution)/shard_map/ppermute | solution.py:39
  238.2 25.1 %collective-permute-start.15 = (bf16[2,2,5,16,512]{4,3,2,1,0:T(8,128)(2,1)S(1)}, bf16[2,2,5,16,512]{4,3,2,1,0:T(8,128)(2,1)S(1)}, u32[]{:S(2)}, u32[]{:S(2)}) collective-permute-start(bf16[2,2,5,16,512]{4,3,2,1,0:T(8,128)(2,1)S(1)} %fusion.16), channel_id=1, source_target_pairs={{0,2},{1,3},{2,0},{3,1},{4,6},{5,7},{6,4},{7,5},{8,10},{9,11},{10,... | collective-permute-start | bytes 983048 | tf_op jit(solution)/shard_map/ppermute | solution.py:39
  238.9 50.5 %collective-permute-start.47 = (bf16[2,2,5,16,512]{4,3,2,1,0:T(8,128)(2,1)S(1)}, bf16[2,2,5,16,512]{4,3,2,1,0:T(8,128)(2,1)S(1)}, u32[]{:S(2)}, u32[]{:S(2)}) collective-permute-start(bf16[2,2,5,16,512]{4,3,2,1,0:T(8,128)(2,1)S(1)} %fusion.17), channel_id=1, source_target_pairs={{0,4},{4,0},{8,12},{12,8},{16,20},{20,16},{24,28},{28,24},{1,5},{5... | collective-permute-start | bytes 983048 | tf_op jit(solution)/shard_map/ppermute | solution.py:39
  248.8 36.6 %collective-permute-start.21 = (bf16[8,5,40,512]{3,2,1,0:T(8,128)(2,1)S(1)}, bf16[8,5,40,512]{3,2,1,0:T(8,128)(2,1)S(1)}, u32[]{:S(2)}, u32[]{:S(2)}) collective-permute-start(bf16[8,5,40,512]{3,2,1,0:T(8,128)(2,1)S(1)} %broadcast_add_fusion), channel_id=1, source_target_pairs={{0,2},{1,3},{2,0},{3,1},{4,6},{5,7},{6,4},{7,5},{8,10},{9,11},{10,... | collective-permute-start | bytes 4915208 | tf_op jit(solution)/shard_map/ppermute | solution.py:39
  285.4 19.3 %collective-permute-start.22 = (bf16[8,5,40,512]{3,2,1,0:T(8,128)(2,1)S(1)}, bf16[8,5,40,512]{3,2,1,0:T(8,128)(2,1)S(1)}, u32[]{:S(2)}, u32[]{:S(2)}) collective-permute-start(bf16[8,5,40,512]{3,2,1,0:T(8,128)(2,1)S(1)} %collective-permute-done.21.refs_2_), channel_id=1, source_target_pairs={{0,1},{1,0},{2,3},{3,2},{4,5},{5,4},{6,7},{7,6},{8,9},{9,8},{10,11... | collective-permute-start | bytes 4915208 | tf_op jit(solution)/shard_map/ppermute | solution.py:39
  299.6 22.2 %collective-permute-start.16 = (bf16[5,16,512]{2,1,0:T(8,128)(2,1)S(1)}, bf16[5,16,512]{2,1,0:T(8,128)(2,1)S(1)}, u32[]{:S(2)}, u32[]{:S(2)}) collective-permute-start(bf16[5,16,512]{2,1,0:T(8,128)(2,1)S(1)} %get-tuple-element.118), channel_id=1, source_target_pairs={{0,8},{4,12},{8,0},{12,4},{16,24},{20,28},{24,16},{28,20},{1,9},{5... | collective-permute-start | bytes 245768 | tf_op jit(solution)/shard_map/ppermute | solution.py:39
  301.6 18.0 %collective-permute-start.31 = (bf16[5,16,512]{2,1,0:T(8,128)(2,1)S(1)}, bf16[5,16,512]{2,1,0:T(8,128)(2,1)S(1)}, u32[]{:S(2)}, u32[]{:S(2)}) collective-permute-start(bf16[5,16,512]{2,1,0:T(8,128)(2,1)S(1)} %get-tuple-element.116), channel_id=1, source_target_pairs={{0,24},{4,28},{8,16},{12,20},{16,8},{20,12},{24,0},{28,4},{1,25},{... | collective-permute-start | bytes 245768 | tf_op jit(solution)/shard_map/ppermute | solution.py:39
  319.6 43.6 %collective-permute-start.48 = (bf16[5,16,512]{2,1,0:T(8,128)(2,1)S(1)}, bf16[5,16,512]{2,1,0:T(8,128)(2,1)S(1)}, u32[]{:S(2)}, u32[]{:S(2)}) collective-permute-start(bf16[5,16,512]{2,1,0:T(8,128)(2,1)S(1)} %get-tuple-element.110), channel_id=1, source_target_pairs={{0,8},{4,12},{8,0},{12,4},{16,24},{20,28},{24,16},{28,20},{1,9},{5... | collective-permute-start | bytes 245768 | tf_op jit(solution)/shard_map/ppermute | solution.py:39
  351.3 17.9 %collective-permute-start.27 = (bf16[5,16,512]{2,1,0:T(8,128)(2,1)S(1)}, bf16[5,16,512]{2,1,0:T(8,128)(2,1)S(1)}, u32[]{:S(2)}, u32[]{:S(2)}) collective-permute-start(bf16[5,16,512]{2,1,0:T(8,128)(2,1)S(1)} %get-tuple-element.100), channel_id=1, source_target_pairs={{0,16},{4,20},{8,24},{12,28},{16,0},{20,4},{24,8},{28,12},{1,17},{... | collective-permute-start | bytes 245768 | tf_op jit(solution)/shard_map/ppermute | solution.py:39
  369.2 20.0 %collective-permute-start.52 = (bf16[5,16,512]{2,1,0:T(8,128)(2,1)S(1)}, bf16[5,16,512]{2,1,0:T(8,128)(2,1)S(1)}, u32[]{:S(2)}, u32[]{:S(2)}) collective-permute-start(bf16[5,16,512]{2,1,0:T(8,128)(2,1)S(1)} %get-tuple-element.92), channel_id=1, source_target_pairs={{0,16},{4,20},{8,24},{12,28},{16,0},{20,4},{24,8},{28,12},{1,17},{... | collective-permute-start | bytes 245768 | tf_op jit(solution)/shard_map/ppermute | solution.py:39
  370.1 20.7 %collective-permute-start.51 = (bf16[5,16,512]{2,1,0:T(8,128)(2,1)S(1)}, bf16[5,16,512]{2,1,0:T(8,128)(2,1)S(1)}, u32[]{:S(2)}, u32[]{:S(2)}) collective-permute-start(bf16[5,16,512]{2,1,0:T(8,128)(2,1)S(1)} %get-tuple-element.92), channel_id=1, source_target_pairs={{0,8},{4,12},{8,0},{12,4},{16,24},{20,28},{24,16},{28,20},{1,9},{5... | collective-permute-start | bytes 245768 | tf_op jit(solution)/shard_map/ppermute | solution.py:39
  372.1 19.2 %collective-permute-start.53 = (bf16[5,16,512]{2,1,0:T(8,128)(2,1)S(1)}, bf16[5,16,512]{2,1,0:T(8,128)(2,1)S(1)}, u32[]{:S(2)}, u32[]{:S(2)}) collective-permute-start(bf16[5,16,512]{2,1,0:T(8,128)(2,1)S(1)} %get-tuple-element.92), channel_id=1, source_target_pairs={{0,24},{4,28},{8,16},{12,20},{16,8},{20,12},{24,0},{28,4},{1,25},{... | collective-permute-start | bytes 245768 | tf_op jit(solution)/shard_map/ppermute | solution.py:39
  390.7 28.0 %collective-permute-start.43 = (bf16[2,2,2,5,16,512]{5,4,3,2,1,0:T(8,128)(2,1)S(1)}, bf16[2,2,2,5,16,512]{5,4,3,2,1,0:T(8,128)(2,1)S(1)}, u32[]{:S(2)}, u32[]{:S(2)}) collective-permute-start(bf16[2,2,2,5,16,512]{5,4,3,2,1,0:T(8,128)(2,1)S(1)} %pad_maximum_fusion.4.refs_5_), channel_id=1, source_target_pairs={{0,4},{4,0},{8,12},{12,8},{16,20},{20,16},{24,28},{28,24},{1,5},{5... | collective-permute-start | bytes 1966088 | tf_op jit(solution)/shard_map/ppermute | solution.py:39
  391.3 25.7 %collective-permute-start.54 = (bf16[2,2,5,16,512]{4,3,2,1,0:T(8,128)(2,1)S(1)}, bf16[2,2,5,16,512]{4,3,2,1,0:T(8,128)(2,1)S(1)}, u32[]{:S(2)}, u32[]{:S(2)}) collective-permute-start(bf16[2,2,5,16,512]{4,3,2,1,0:T(8,128)(2,1)S(1)} %bitcast.270), channel_id=1, source_target_pairs={{0,4},{4,0},{8,12},{12,8},{16,20},{20,16},{24,28},{28,24},{1,5},{5... | collective-permute-start | bytes 983048 | tf_op jit(solution)/shard_map/ppermute | solution.py:39
  393.0 31.1 %collective-permute-start.57 = (bf16[2,2,2,5,16,512]{5,4,3,2,1,0:T(8,128)(2,1)S(1)}, bf16[2,2,2,5,16,512]{5,4,3,2,1,0:T(8,128)(2,1)S(1)}, u32[]{:S(2)}, u32[]{:S(2)}) collective-permute-start(bf16[2,2,2,5,16,512]{5,4,3,2,1,0:T(8,128)(2,1)S(1)} %pad_maximum_fusion.5.refs_5_), channel_id=1, source_target_pairs={{0,4},{4,0},{8,12},{12,8},{16,20},{20,16},{24,28},{28,24},{1,5},{5... | collective-permute-start | bytes 1966088 | tf_op jit(solution)/shard_map/ppermute | solution.py:39
  405.0 19.3 %collective-permute-start.41 = (bf16[2,2,2,5,16,512]{5,4,3,2,1,0:T(8,128)(2,1)S(1)}, bf16[2,2,2,5,16,512]{5,4,3,2,1,0:T(8,128)(2,1)S(1)}, u32[]{:S(2)}, u32[]{:S(2)}) collective-permute-start(bf16[2,2,2,5,16,512]{5,4,3,2,1,0:T(8,128)(2,1)S(1)} %pad_maximum_fusion.6), channel_id=1, source_target_pairs={{0,2},{1,3},{2,0},{3,1},{4,6},{5,7},{6,4},{7,5},{8,10},{9,11},{10,... | collective-permute-start | bytes 1966088 | tf_op jit(solution)/shard_map/ppermute | solution.py:39
  418.8 27.2 %collective-permute-start.44 = (bf16[16,5,16,512]{3,2,1,0:T(8,128)(2,1)S(1)}, bf16[16,5,16,512]{3,2,1,0:T(8,128)(2,1)S(1)}, u32[]{:S(2)}, u32[]{:S(2)}) collective-permute-start(bf16[16,5,16,512]{3,2,1,0:T(8,128)(2,1)S(1)} %bitcast.237), channel_id=1, source_target_pairs={{0,1},{1,0},{2,3},{3,2},{4,5},{5,4},{6,7},{7,6},{8,9},{9,8},{10,11... | collective-permute-start | bytes 3932168 | tf_op jit(solution)/shard_map/ppermute | solution.py:39
  424.2 21.8 %collective-permute-start.58 = (bf16[16,5,16,512]{3,2,1,0:T(8,128)(2,1)S(1)}, bf16[16,5,16,512]{3,2,1,0:T(8,128)(2,1)S(1)}, u32[]{:S(2)}, u32[]{:S(2)}) collective-permute-start(bf16[16,5,16,512]{3,2,1,0:T(8,128)(2,1)S(1)} %bitcast.239), channel_id=1, source_target_pairs={{0,1},{1,0},{2,3},{3,2},{4,5},{5,4},{6,7},{7,6},{8,9},{9,8},{10,11... | collective-permute-start | bytes 3932168 | tf_op jit(solution)/shard_map/ppermute | solution.py:39
  424.5 21.6 %collective-permute-start.42 = (bf16[16,5,16,512]{3,2,1,0:T(8,128)(2,1)S(1)}, bf16[16,5,16,512]{3,2,1,0:T(8,128)(2,1)S(1)}, u32[]{:S(2)}, u32[]{:S(2)}) collective-permute-start(bf16[16,5,16,512]{3,2,1,0:T(8,128)(2,1)S(1)} %bitcast.241), channel_id=1, source_target_pairs={{0,1},{1,0},{2,3},{3,2},{4,5},{5,4},{6,7},{7,6},{8,9},{9,8},{10,11... | collective-permute-start | bytes 3932168 | tf_op jit(solution)/shard_map/ppermute | solution.py:39
  427.9 19.3 %collective-permute-start.56 = (bf16[16,5,16,512]{3,2,1,0:T(8,128)(2,1)S(1)}, bf16[16,5,16,512]{3,2,1,0:T(8,128)(2,1)}, u32[]{:S(2)}, u32[]{:S(2)}) collective-permute-start(bf16[16,5,16,512]{3,2,1,0:T(8,128)(2,1)S(1)} %bitcast.243), channel_id=1, source_target_pairs={{0,1},{1,0},{2,3},{3,2},{4,5},{5,4},{6,7},{7,6},{8,9},{9,8},{10,11... | collective-permute-start | bytes 3932168 | tf_op jit(solution)/shard_map/ppermute | solution.py:39
  (60 other events, 538.2 us)

commit v4 on v3

--- a/solution.py
+++ b/solution.py
@@ -32,7 +32,7 @@
 
 
 def cost(flops, size):
-    return pl.CostEstimate(flops=flops, bytes_accessed=size, transcendentals=0)
+    return pl.CostEstimate(flops=flops // 1000, bytes_accessed=size // 1000, transcendentals=0)
 
 
 def swap(value, axis, mask):
@@ -404,30 +404,22 @@
     return (piece & 3) | ((piece & 4) << 1) | ((piece & 8) >> 1)
 
 
-def weight_kernel(own_ref, left_ref, right_ref, *refs):
-    keep_refs, send_refs = refs[:4], refs[4:8]
-    strip_ref, moved = refs[8:]
-    pieces = MAIN // PIECE
-    rows = PIECE // 2
+def weight_kernel(own_ref, left_ref, right_ref, keep_ref, send_ref, strip_ref, moved):
+    pieces = MAIN // PIECE // 2
     half = MAIN // 2
     right = right_ref[0, :MAIN, :]
-    for above in range(2):
-        for at in range(pieces):
-            first = pl.multiple_of((at ^ own_ref[0]) * PIECE + above * rows, rows)
-            moved[(above * pieces + at) * rows : (above * pieces + at + 1) * rows] = left_ref[
-                0, pl.ds(first, rows), :
-            ]
-    for above in range(2):
+    for at in range(2 * pieces):
+        first = pl.multiple_of((at ^ own_ref[0]) * PIECE, PIECE)
+        moved[at * PIECE : (at + 1) * PIECE] = left_ref[0, pl.ds(first, PIECE), :]
+    for core, out_ref in ((1, send_ref), (0, keep_ref)):
         product = lax.dot_general(
-            moved[above * half : (above + 1) * half], right, NT, preferred_element_type=F32
-        )
-        for lane in range(2):
-            part = product[:, lane * half : (lane + 1) * half]
-            for at in range(pieces // 2):
-                to = chunk_place(at, lane == 1)
-                keep_refs[2 * above + lane][to, 0] = part[at * rows : (at + 1) * rows]
-                other = (pieces // 2 + at) * rows
-                send_refs[2 * above + lane][to, 0] = part[other : other + rows].astype(BF)
+            moved[core * half : (core + 1) * half], right, NT, preferred_element_type=F32
+        ).astype(out_ref.dtype)
+        for chunk in range(2):
+            for at in range(pieces):
+                out_ref[chunk, chunk_place(at, chunk == 1), 0] = product[
+                    at * PIECE : (at + 1) * PIECE, chunk * half : (chunk + 1) * half
+                ]
     below = lax.dot_general(left_ref[0, MAIN : MAIN + 16, :], right_ref[0], NT, preferred_element_type=F32)
     beside = lax.dot_general(right_ref[0, MAIN : MAIN + 16, :], left_ref[0], NT, preferred_element_type=F32)
     strip_ref[0, 0:3] = below[0:3]
@@ -439,9 +431,9 @@
     matrix_count, size, count = left.shape
     half = MAIN // 2
     pieces = MAIN // PIECE // 2
-    chunk = pl.BlockSpec((pieces, 1, PIECE // 2, half), lambda m: (0, m, 0, 0))
-    shape = (pieces, matrix_count, PIECE // 2, half)
-    outs = pl.pallas_call(
+    chunk = pl.BlockSpec((2, pieces, 1, PIECE, half), lambda m: (0, 0, m, 0, 0))
+    shape = (2, pieces, matrix_count, PIECE, half)
+    keep, send, strips = pl.pallas_call(
         weight_kernel,
         grid=(matrix_count,),
         in_specs=[
@@ -449,84 +441,50 @@
             pl.BlockSpec((1, size, count), lambda m: (m, 0, 0)),
             pl.BlockSpec((1, size, count), lambda m: (m, 0, 0)),
         ],
-        out_specs=[chunk] * 8 + [pl.BlockSpec((1, 8, size), lambda m: (m, 0, 0))],
-        out_shape=[jax.ShapeDtypeStruct(shape, F32)] * 4
-        + [jax.ShapeDtypeStruct(shape, BF)] * 4
-        + [jax.ShapeDtypeStruct((matrix_count, 8, size), F32)],
+        out_specs=[chunk, chunk, pl.BlockSpec((1, 8, size), lambda m: (m, 0, 0))],
+        out_shape=[
+            jax.ShapeDtypeStruct(shape, F32),
+            jax.ShapeDtypeStruct(shape, BF),
+            jax.ShapeDtypeStruct((matrix_count, 8, size), F32),
+        ],
         scratch_shapes=[pltpu.VMEM((MAIN, count), BF)],
         compiler_params=params(40),
         cost_estimate=cost(2 * matrix_count * size * size * count, 10 * matrix_count * size * size),
         name="weight_parts",
     )(own, left, right)
-    parts = (2, 2, 2, 2, matrix_count, PIECE // 2, half)
-    return [v.reshape(parts) for v in outs[:4]], [v.reshape(parts) for v in outs[4:8]], outs[8]
-
-
-def halving(swapped):
-    order = [("rep", 2), ("tab", 1)]
-    return order[::-1] if swapped else order
-
-
-def sum_start(total, step, swapped):
-    axis, mask = halving(swapped)[step]
-    return total[0], swap(total[1].astype(BF), axis, mask)
-
-
-def sum_end(kept, token):
-    value = kept[0] + token
-    for other in kept[1:]:
-        value = value + other.astype(F32)
-    return value
-
-
-def far_start(total):
-    sent = [
-        swap(total[high, low].astype(BF), "tab", 4 * high + 2 * low)
-        for high, low in ((0, 1), (1, 0), (1, 1))
-    ]
-    return (total[0, 0], *sent)
-
-
-def far_end(kept, token):
-    piece = sum_end(kept, token).astype(BF)
-    for axis, known in (("rep", 2), ("tab", 3)):
-        for mask in masks_of(axis)[known:]:
-            piece = (piece.astype(F32) + swap(piece, axis, mask).astype(F32)).astype(BF)
-    return piece
-
-
-def spread_far(piece):
-    return (piece, swap(piece, "tab", 2), swap(piece, "tab", 4), swap(piece, "tab", 6))
-
-
-def spread_near(value, step, swapped):
-    axis, mask = halving(swapped)[step]
-    return value, swap(value, axis, mask)
-
-
-def join(parts, token):
+    parts = (2, 2, 2, 2, 2, matrix_count, PIECE, half)
+    return keep.reshape(parts), send.reshape(parts), strips
+
+
+HALVES = [[("rep", 2), ("tab", 1)], [("tab", 1), ("rep", 2)]]
+FAR = [(0, 1), (1, 0), (1, 1)]
+
+
+def added(parts, index, token=None):
+    value = parts[0][index].astype(F32)
+    for other in parts[1:]:
+        value = value + other[index].astype(F32)
+    return value if token is None else value + token
+
+
+def joined(parts, token):
     one = (1.0 + token).astype(BF)
-    return jnp.stack((parts[0] * one,) + tuple(parts[1:]))
-
-
-def assemble_kernel(layer_count, chunk_count, own_ref, *refs):
-    chunks = refs[: 2 * chunk_count]
-    strip_ref, cross_ref, first_ref, second_ref = refs[2 * chunk_count :]
+    return jnp.concatenate([parts[0] * one] + list(parts[1:]))
+
+
+def assemble_kernel(layer_count, own_ref, *refs):
+    blocks = refs[:8]
+    strip_ref, cross_ref, first_ref, second_ref = refs[8:]
     matrix = pl.program_id(0)
-    lanes_count = chunk_count // 2
 
     def fill(out_ref):
-        for chunk in range(chunk_count):
-            above, lane = divmod(chunk, lanes_count)
-            for core in range(2):
-                ref = chunks[2 * chunk + core]
-                count, _, rows, lanes = ref.shape
-                for at in range(count):
-                    piece = (core * count + at) ^ own_ref[0]
-                    first = pl.multiple_of(piece * PIECE + above * rows, rows)
-                    out_ref[0, pl.ds(first, rows), lane * lanes : (lane + 1) * lanes] = ref[
-                        chunk_place(at, lane == 1), 0
-                    ].astype(F32)
+        for block, ref in enumerate(blocks):
+            chunk, core, upper = block >> 2, (block >> 1) & 1, block & 1
+            count, _, rows, lanes = ref.shape
+            for at in range(count):
+                piece = 2 * count * core + chunk_place(count * upper + at, chunk == 1)
+                first = pl.multiple_of((piece ^ own_ref[0]) * rows, rows)
+                out_ref[0, pl.ds(first, rows), chunk * lanes : (chunk + 1) * lanes] = ref[at, 0].astype(F32)
         height, width = out_ref.shape[1:]
         if width > MAIN:
             extra = width - MAIN
@@ -549,17 +507,16 @@
         fill(second_ref)
 
 
-def assemble(chunks, strips, own, layer_count, width, hidden):
+def assemble(blocks, strips, own, layer_count, width, hidden):
     matrix_count = layer_count + 2
     size = strips.shape[2]
-    specs = []
-    for chunk in chunks:
-        specs.append(pl.BlockSpec((chunk.shape[0], 1) + chunk.shape[2:], lambda m: (0, m, 0, 0)))
+    shape = blocks[0].shape
+    block = pl.BlockSpec(shape[:1] + (1,) + shape[2:], lambda m: (0, m, 0, 0))
     return pl.pallas_call(
-        functools.partial(assemble_kernel, layer_count, len(chunks) // 2),
+        functools.partial(assemble_kernel, layer_count),
         grid=(matrix_count,),
         in_specs=[pl.BlockSpec(memory_space=pltpu.SMEM)]
-        + specs
+        + [block] * 8
         + [pl.BlockSpec((1, 8, size), lambda m: (m, 0, 0))],
         out_specs=[
             pl.BlockSpec((1, width, width), lambda m: (jnp.minimum(m, layer_count - 1), 0, 0)),
@@ -574,7 +531,7 @@
         compiler_params=params(56),
         cost_estimate=cost(0, 6 * matrix_count * size * size),
         name="assemble",
-    )(own, *chunks, strips)
+    )(own, *blocks, strips)
 
 
 def on_device(
@@ -621,8 +578,9 @@
         looked = lookup(
             tables, listed, own_rows, tab_count, begin, min(LOOK_SLOTS, slot_count - begin)
         )
-        ready = 1.0 + looked[0, 0, embed_dim, 0]
         arrived.append(lax.all_to_all(looked, "tab", split_axis=0, concat_axis=0, tiled=True))
+
+    ready = 1.0 + arrived[0][0, 0, embed_dim, 0]
 
     def padded(weight):
         return jnp.pad(weight * ready, ((0, size - weight.shape[0]), (0, size - weight.shape[1])))
@@ -632,7 +590,9 @@
     )
     vectors = [cross_b[at] for at in range(layer_count)]
     vectors += [tower1_b, tower2_b, out_w[:width], out_w[width:], out_w[:0]]
-    cols = jnp.stack([jnp.pad(v.astype(F32), (0, size - v.shape[0])) for v in vectors], axis=1)
+    cols = jnp.stack(
+        [jnp.pad((v * ready).astype(F32), (0, size - v.shape[0])) for v in vectors], axis=1
+    )
 
     logits, dense_grad, slots, left, right, sums = dense_step(
         arrived, starts, table_place, dense_in, labels, weights, cols, out_b, layer_count, width
@@ -651,114 +611,96 @@
     def near_parts(own):
         return [own, swap(own, "rep", 1)]
 
-    def far_parts(own):
+    def far_bases(own):
         bases = [own]
         for mask in masks_of("rep")[1:]:
             bases = bases + [swap(part, "rep", mask) for part in bases]
-        return [part for far in bases[1:] for part in near_parts(far)]
+        return bases[1:]
+
+    def far_parts(bases):
+        return [part for far in bases for part in near_parts(far)]
+
+    def gate(value, result):
+        return value * (1.0 + 0.0 * result.astype(F32)).astype(value.dtype)
 
     bits = [rep_at & 1, (rep_at >> 1) & 1, tab_at & 1, (tab_at >> 2) & 1, (tab_at >> 1) & 1]
     own = sum(bit << (4 - at) for at, bit in enumerate(bits)).astype(I32).reshape(1)
     keep, send, strips = weight_parts(left, right, own)
     matrix_count = layer_count + 2
     near_ids = near_parts(wanted)
-    far_ids = far_parts(wanted)
-    near_grads = near_parts(returned)
+    far_ids = far_parts(far_bases(wanted))
     far_grads = None
     table_grad = None
-    waves = [(0, 1), (2, 3)]
     token = jnp.zeros((), F32)
-    state = [None] * 4
-    for at in range(4):
-        total = keep[at] + swap(send[at], "rep", 1).astype(F32)
-        state[at] = sum_start(total, 0, at % 2 == 1)
-
     jobs = [(near_ids, True, slot) for slot in range(slot_count)]
     jobs += [(far_ids, False, slot) for slot in range(slot_count)]
     jobs = jobs[::-1]
 
-    def add_next(after):
-        nonlocal table_grad, token, far_grads
-        if not jobs:
-            return
-        part_ids, near, slot = jobs.pop()
-        if not near and far_grads is None:
-            far_grads = far_parts(returned + token.astype(BF))
-        table_grad, token = add_rows(
-            near_grads if near else far_grads,
-            part_ids,
-            base,
-            share,
-            embed_dim,
-            slot,
-            table_grad,
-            not near,
-            after,
-        )
-
-    def start_far():
-        nonlocal far_grads
-        far_grads = far_parts(returned + token.astype(BF))
-
-    def wave(chunks, act):
-        for at in chunks:
-            state[at] = act(at, state[at])
-
-    def first_sum(at, kept):
-        return sum_start(sum_end(kept, token), 1, at % 2 == 1)
-
-    def second_sum(at, kept):
-        return far_start(sum_end(kept, token))
-
-    def last_sum(at, kept):
-        return spread_far(far_end(kept, token))
-
-    def far_join(at, parts):
-        value = join(parts, token)
-        return spread_near(value.reshape((2, 2) + value.shape[1:]), 1, at % 2 == 1)
-
-    def second_join(at, parts):
-        return spread_near(join(parts, token), 0, at % 2 == 1)
-
-    def first_join(at, parts):
-        value = join(parts, token)
-        value = value.reshape((MAIN // PIECE // 2,) + value.shape[4:])
-        return value, swap(value, "rep", 1)
-
-    add_next([state[1][0]])
-    wave(waves[0], first_sum)
-    add_next([state[1][0]])
-    wave(waves[1], first_sum)
-    start_far()
-    add_next([state[3][0]])
-    wave(waves[0], second_sum)
-    add_next([state[1][0]])
-    wave(waves[1], second_sum)
-    add_next([state[3][0]])
-    wave(waves[0], last_sum)
-    wave(waves[1], last_sum)
-    add_next([state[3][0]])
-    wave(waves[0], far_join)
-    add_next([state[1][0]])
-    wave(waves[1], far_join)
-    add_next([state[3][0]])
-    wave(waves[0], second_join)
-    add_next([state[1][0]])
-    wave(waves[1], second_join)
-    while jobs:
-        add_next([state[3][0]])
-    wave(waves[0], first_join)
-    wave(waves[1], first_join)
-    chunks = [part for at in range(4) for part in state[at]]
+    def add_next(times, after):
+        nonlocal table_grad, token
+        for _ in range(min(times, len(jobs))):
+            part_ids, near, slot = jobs.pop()
+            table_grad, token = add_rows(
+                near_grads if near else far_grads,
+                part_ids,
+                base,
+                share,
+                embed_dim,
+                slot,
+                table_grad,
+                not near,
+                after,
+            )
 
     small = jnp.concatenate([strips.reshape(matrix_count * 8, size), sums], axis=0)
     for axis in ("rep", "tab"):
         for mask in masks_of(axis):
             small = small + swap(small, axis, mask)
+
+    got = swap(send, "rep", 1)
+    sent = [swap(added((keep, got), (at, 1)).astype(BF), *HALVES[at][0]) for at in range(2)]
+    kept = [added((keep, got), (at, 0)) for at in range(2)]
+    parts = [(kept[at], sent[at]) for at in range(2)]
+    sent = [swap(added(parts[at], 1).astype(BF), *HALVES[at][1]) for at in range(2)]
+    kept = [added(parts[at], 0) for at in range(2)]
+    returned = gate(returned, kept[0][0, 0, 0, 0, 0])
+    near_grads = near_parts(returned)
+    add_next(1, kept + [small])
+    parts = [(kept[at], sent[at]) for at in range(2)]
+    sent = [
+        swap(
+            jnp.stack([added(part, (high, low), token) for part in parts]).astype(BF),
+            "tab",
+            4 * high + 2 * low,
+        )
+        for high, low in FAR
+    ]
+    kept = jnp.stack([added(part, (0, 0), token) for part in parts])
+    bases = far_bases(gate(returned, kept[0, 0, 0, 0]))
+    add_next(slot_count - 2, [kept])
+    piece = added((kept, *sent), slice(None), token).astype(BF)
+    for axis, known in (("rep", 2), ("tab", 3)):
+        for mask in masks_of(axis)[known:]:
+            piece = (piece.astype(F32) + swap(piece, axis, mask).astype(F32)).astype(BF)
+    parts = [piece, swap(piece, "tab", 2), swap(piece, "tab", 4), swap(piece, "tab", 6)]
+    far_grads = far_parts([gate(part, piece[0, 0, 0, 0]) for part in bases])
+    add_next(2, [piece])
+    values = [joined([part[at : at + 1] for part in parts], token) for at in range(2)]
+    sent = [swap(values[at], *HALVES[at][1]) for at in range(2)]
+    add_next(1, values)
+    values = [joined((values[at], sent[at]), token) for at in range(2)]
+    sent = [swap(values[at], *HALVES[at][0]) for at in range(2)]
+    blocks = [[values[at], None, swap(values[at], "rep", 1), None] for at in range(2)]
+    add_next(slot_count, values)
+    for at in range(2):
+        blocks[at][1] = sent[at]
+        blocks[at][3] = swap(sent[at], "rep", 1)
+    blocks = blocks[0] + blocks[1]
+
     strips = small[:-8].reshape(matrix_count, 8, size)
     sums = small[-8:]
     cross_w_grad, tower1_w_grad, tower2_w_grad = assemble(
-        chunks, strips, own, layer_count, width, hidden
+        blocks, strips, own, layer_count, width, hidden
     )
     scalars = sums[layer_count + 4]
     return (

time: 467 us -> 428 us (0.916)
  starting transfers between devices: 93.6 us -> 55.9 us
  waiting for transfers between devices: 87.4 us -> 108 us
  other arithmetic: 45.8 us -> 33.6 us
  local copies, waits for them, and re-layouts: 41.5 us -> 30.8 us
    ppermute x59 -> x30, starting transfers between devices: 63.4 us -> 31.5 us  [swap(): lax.ppermute(value, axis, [(at, at ^ mask) for at in range(lax.axis_size(...]
    ppermute x59 -> x30, waiting for transfers between devices: 71.7 us -> 98.1 us  [swap(): lax.ppermute(value, axis, [(at, at ^ mask) for at in range(lax.axis_size(...]
    add x9 -> x2, other arithmetic: 18.6 us -> 2.89 us  [added(): return value if token is None else value + token]
    convert_element_type x1 -> x4, other arithmetic: 0.69 us -> 13.2 us  [the longest x1 8.44 us: on_device(): added((keep, got), (at, 1)).astype(BF)]
    all_to_all x2, waiting for transfers between devices: 15.8 us -> 3.68 us  [on_device(): lax.all_to_all(looked, 'tab', split_axis=0, concat_axis=0, tiled=True)]
    another operation x24 -> x10, other arithmetic: 10.1 us -> 0.17 us  [the longest x3 0.1 us: on_device(): jnp.stack([added(part, (high, low), token) for part in parts]).astype(BF)]
    all_to_all x2, starting transfers between devices: 19.4 us -> 10.7 us  [on_device(): lax.all_to_all(looked, 'tab', split_axis=0, concat_axis=0, tiled=True)]
    convert_element_type x12 -> x0, local copies, waits for them, and re-layouts: 6.27 us -> none  [the longest x8 6.2 us: sum_start(): return (total[0], swap(total[1].astype(BF), axis, mask))]
  transfers between devices with their start and end apart: 63 -> 34, of which waited for: 14 -> 17; matrix products, arithmetic and copies ran while one was open for 15% -> 12% of each run, Pallas kernels for 28% -> 24%
where the time goes in v4:
time: 428 us; the launch traced here: 423 us
  Pallas kernels  187 us (44%)
  waiting for transfers between devices  108 us (25%)
  starting transfers between devices  55.9 us (13%)
  other arithmetic  33.6 us (8%)
  local copies, waits for them, and re-layouts  30.8 us (7%)
  between operations  7.81 us (2%)
    ppermute x30, waiting for transfers between devices, swap(): lax.ppermute(value, axis, [(at, at ^ mask) for at in range(lax.axis_size(...  98.1 us
    pallas_call x10, Pallas kernels, add_rows(): pl.pallas_call(functools.partial(add_kernel, part_count, accumulate), gri...  94.9 us
    pallas_call x2, Pallas kernels, lookup(): pl.pallas_call(functools.partial(lookup_kernel, first_slot), in_specs=[sm...  38.5 us
    ppermute x30, starting transfers between devices, swap(): lax.ppermute(value, axis, [(at, at ^ mask) for at in range(lax.axis_size(...  31.5 us
    pallas_call x1, Pallas kernels, dense_step(): pl.pallas_call(functools.partial(dense_kernel, dense_width, width, starts...  27.5 us
    unnamed x51, local copies, waits for them, and re-layouts  16.3 us
    pallas_call x1, Pallas kernels, assemble(): pl.pallas_call(functools.partial(assemble_kernel, layer_count), grid=(mat...  13.3 us
    pallas_call x1, Pallas kernels, weight_parts(): pl.pallas_call(weight_kernel, grid=(matrix_count,), in_specs=[pl.BlockSpe...  12.7 us
  transfers between devices with their start and end apart: 34, of which 17 were waited for; matrix products, arithmetic and copies ran while one was open for 12% of the time, Pallas kernels for 24%

profile of v4, /device:TPU:0, one launch (start us, length us, event | category | flops | bytes accessed | tf_op | source)
XLA Modules:
  0.0 423.0 jit_solution(1935706270936393134)
XLA Ops:
  5.2 7.3 %all-to-all-start = ((s32[8,5,512]{2,1,0:T(8,128)}), s32[8,5,512]{2,1,0:T(8,128)}, u32[]{:S(2)}, u32[]{:S(2)}) async-start(s32[8,5,512]{2,1,0:T(8,128)} %reshape.387), calls=%async_computation | async-start | bytes 262144 | tf_op jit(solution)/shard_map/all_to_all | solution.py:570
  13.8 6.1 %all-to-all-done = s32[8,5,512]{2,1,0:T(8,128)} async-done(((s32[8,5,512]{2,1,0:T(8,128)}), s32[8,5,512]{2,1,0:T(8,128)}, u32[]{:S(2)}, u32[]{:S(2)}) %all-to-all-start) | async-done | bytes 81952 | tf_op jit(solution)/shard_map/all_to_all | solution.py:570
  21.5 20.7 %lookup.2 = bf16[8,3,40,512]{3,2,1,0:T(8,128)(2,1)} custom-call(s32[20480]{0:T(1024)} %bitcast.121, s32[5]{0:T(128)} %dynamic_slice.3.rows_ref, bf16[5,39,32768]{2,1,0:T(8,128)(2,1)} %table_hbm.3), custom_call_target="tpu_custom_call" | custom-call | flops 30198988 | bytes 8626 | tf_op jit(solution)/shard_map/lookup/pallas_call | solution.py:100
  42.2 6.2 %all-to-all-start.1 = ((bf16[8,3,40,512]{3,2,1,0:T(8,128)(2,1)}), bf16[8,3,40,512]{3,2,1,0:T(8,128)(2,1)S(1)}, u32[]{:S(2)}, u32[]{:S(2)}) async-start(bf16[8,3,40,512]{3,2,1,0:T(8,128)(2,1)} %lookup.2), calls=%async_computation.1 | async-start | bytes 1966080 | tf_op jit(solution)/shard_map/all_to_all | solution.py:581
  50.3 17.9 %lookup.3 = bf16[8,2,40,512]{3,2,1,0:T(8,128)(2,1)} custom-call(s32[20480]{0:T(1024)} %bitcast.122, s32[5]{0:T(128)} %dynamic_slice.3.rows_ref, bf16[5,39,32768]{2,1,0:T(8,128)(2,1)} %table_hbm.3), custom_call_target="tpu_custom_call" | custom-call | flops 20132660 | bytes 5750 | tf_op jit(solution)/shard_map/lookup/pallas_call | solution.py:100
  68.1 3.7 all-to-all-done.1.refs_0_
  71.8 4.5 %all-to-all-start.2 = ((bf16[8,2,40,512]{3,2,1,0:T(8,128)(2,1)}), bf16[8,2,40,512]{3,2,1,0:T(8,128)(2,1)S(1)}, u32[]{:S(2)}, u32[]{:S(2)}) async-start(bf16[8,2,40,512]{3,2,1,0:T(8,128)(2,1)} %lookup.3), calls=%async_computation.2 | async-start | bytes 1310720 | tf_op jit(solution)/shard_map/all_to_all | solution.py:581
  79.5 3.5 multiply_bitcast_fusion
  95.4 27.5 %dense.1 = (f32[1,512]{1,0:T(1,128)}, f32[16,512]{1,0:T(8,128)}, bf16[40,40,512]{2,1,0:T(8,128)(2,1)}, bf16[5,1152,512]{2,1,0:T(8,128)(2,1)}, bf16[5,1152,512]{2,1,0:T(8,128)(2,1)}, /*index=5*/f32[8,1152]{1,0:T(8,128)}) custom-call(s32[26]{0:T(128)} %place_ref.1, f32[1]{0:T(128)S(6)} %convert.58.bias_ref, bf16[8,3,40,512]{3,2,1,0:T(8,128)(2,1)} %copy-done.7, ...), custom_call_target="tpu_custom_call" | custom-call | flops 13589544 | bytes 30965 | tf_op jit(solution)/shard_map/dense/pallas_call | solution.py:364
  125.6 12.7 %weight_parts.1 = (f32[2,16,5,32,512]{4,3,2,1,0:T(8,128)}, bf16[2,16,5,32,512]{4,3,2,1,0:T(8,128)(2,1)}, f32[5,8,1152]{2,1,0:T(8,128)S(1)}) custom-call(s32[1]{0:T(128)} %bitcast.own_ref, bf16[5,1152,512]{2,1,0:T(8,128)(2,1)S(1)} %copy-done.4, bf16[5,1152,512]{2,1,0:T(8,128)(2,1)} %get-tuple-element.39.right_ref), custom_call_target="tpu_custom_call" | custom-call | flops 6794772 | bytes 66355 | tf_op jit(solution)/shard_map/weight_parts/pallas_call | solution.py:436
  138.3 6.4 %all-to-all-start.3 = ((bf16[8,5,40,512]{3,2,1,0:T(8,128)(2,1)}), bf16[8,5,40,512]{3,2,1,0:T(8,128)(2,1)S(1)}, u32[]{:S(2)}, u32[]{:S(2)}) async-start(bf16[8,5,40,512]{3,2,1,0:T(8,128)(2,1)} %bitcast.30), calls=%async_computation.3 | async-start | bytes 3276800 | tf_op jit(solution)/shard_map/all_to_all | solution.py:600
  147.3 8.4 %fusion.2 = (bf16[2,2,2,5,32,512]{5,4,3,2,1,0:T(8,128)(2,1)S(1)}, bf16[2,2,2,5,32,512]{5,4,3,2,1,0:T(8,128)(2,1)}, f32[1,1,2,2,2,5,32,512]{7,6,5,4,3,2,1,0:T(8,128)}, f32[1,1,2,2,2,5,32,512]{7,6,5,4,3,2,1,0:T(8,128)S(1)}) fusion(f32[2,2,2,2,2,5,32,512]{7,6,5,4,3,2,1,0:T(8,128)} %bitcast.120, bf16[2,2,2,2,2,5,32,512]{7,6,5,4,3,2,1,0:T(8,128)(2,1)} %collective-permute-done.5), kind=kLoop, calls=%fused_computation.16 | loop fusion | flops 6553600 | bytes 23592960 | tf_op jit(solution)/shard_map/convert_element_type | solution.py:661
  160.0 26.6 %collective-permute-done.6 = bf16[2,2,2,5,32,512]{5,4,3,2,1,0:T(8,128)(2,1)S(1)} collective-permute-done((bf16[2,2,2,5,32,512]{5,4,3,2,1,0:T(8,128)(2,1)S(1)}, bf16[2,2,2,5,32,512]{5,4,3,2,1,0:T(8,128)(2,1)S(1)}, u32[]{:S(2)}, u32[]{:S(2)}) %collective-permute-start.6) | collective-permute-done | bytes 1310752 | tf_op jit(solution)/shard_map/ppermute | solution.py:39
  194.1 6.3 %collective-permute-done.1 = f32[48,1152]{1,0:T(8,128)S(1)} collective-permute-done((f32[48,1152]{1,0:T(8,128)S(1)}, f32[48,1152]{1,0:T(8,128)S(1)}, u32[]{:S(2)}, u32[]{:S(2)}) %collective-permute-start.1) | collective-permute-done | bytes 221216 | tf_op jit(solution)/shard_map/ppermute | solution.py:39
  202.5 5.3 %collective-permute-done.2 = f32[48,1152]{1,0:T(8,128)S(1)} collective-permute-done((f32[48,1152]{1,0:T(8,128)S(1)}, f32[48,1152]{1,0:T(8,128)S(1)}, u32[]{:S(2)}, u32[]{:S(2)}) %collective-permute-start.2) | collective-permute-done | bytes 221216 | tf_op jit(solution)/shard_map/ppermute | solution.py:39
  211.1 3.3 collective-permute-done.3
  219.5 6.3 %collective-permute-done.4 = f32[48,1152]{1,0:T(8,128)} collective-permute-done((f32[48,1152]{1,0:T(8,128)S(1)}, f32[48,1152]{1,0:T(8,128)}, u32[]{:S(2)}, u32[]{:S(2)}) %collective-permute-start.4) | collective-permute-done | bytes 221216 | tf_op jit(solution)/shard_map/ppermute | solution.py:39
  231.0 8.7 %add_rows.10 = (f32[5,39,8192]{2,1,0:T(8,128)}, f32[8,128]{1,0:T(8,128)S(1)}) custom-call(s32[1]{0:T(128)} %bitcast.27.base_ref, s32[8,5,1,512]{3,2,1,0:T(1,128)S(1)} %copy.187.refs_0_, s32[8,5,1,512]{3,2,1,0:T(1,128)S(1)} %copy.188.refs_1_, bf16[8,5,40,512]{3,2,1,0:T(8,128)(2,1)S(1)} %broadcast_multiply_fusion.3.refs_2_, ...), custom_call_target="tpu_custom_call" | custom-call | flops 5234491 | bytes 1916 | tf_op jit(solution)/shard_map/add_rows/pallas_call | solution.py:172
  246.6 3.4 collective-permute-start.13
  251.2 8.8 %add_rows.11 = (f32[5,39,8192]{2,1,0:T(8,128)}, f32[8,128]{1,0:T(8,128)}) custom-call(s32[1]{0:T(128)} %bitcast.27.base_ref, s32[8,5,1,512]{3,2,1,0:T(1,128)S(1)} %copy.187.refs_0_, s32[8,5,1,512]{3,2,1,0:T(1,128)S(1)} %copy.188.refs_1_, bf16[8,5,40,512]{3,2,1,0:T(8,128)(2,1)S(1)} %broadcast_multiply_fusion.3.refs_2_, ...), custom_call_target="tpu_custom_call", output_to_operand_aliasing={{0}: (5, {})} | custom-call | flops 5234491 | bytes 1916 | tf_op jit(solution)/shard_map/add_rows/pallas_call | solution.py:172
  260.0 8.8 %add_rows.12 = (f32[5,39,8192]{2,1,0:T(8,128)}, f32[8,128]{1,0:T(8,128)}) custom-call(s32[1]{0:T(128)} %bitcast.27.base_ref, s32[8,5,1,512]{3,2,1,0:T(1,128)S(1)} %copy.187.refs_0_, s32[8,5,1,512]{3,2,1,0:T(1,128)S(1)} %copy.188.refs_1_, bf16[8,5,40,512]{3,2,1,0:T(8,128)(2,1)S(1)} %broadcast_multiply_fusion.3.refs_2_, ...), custom_call_target="tpu_custom_call", output_to_operand_aliasing={{0}: (5, {})} | custom-call | flops 5234491 | bytes 1916 | tf_op jit(solution)/shard_map/add_rows/pallas_call | solution.py:172
  268.8 8.7 %add_rows.13 = (f32[5,39,8192]{2,1,0:T(8,128)}, f32[8,128]{1,0:T(8,128)S(1)}) custom-call(s32[1]{0:T(128)} %bitcast.27.base_ref, s32[8,5,1,512]{3,2,1,0:T(1,128)S(1)} %copy.187.refs_0_, s32[8,5,1,512]{3,2,1,0:T(1,128)S(1)} %copy.188.refs_1_, bf16[8,5,40,512]{3,2,1,0:T(8,128)(2,1)S(1)} %broadcast_multiply_fusion.3.refs_2_, ...), custom_call_target="tpu_custom_call", output_to_operand_aliasing={{0}: (5, {})} | custom-call | flops 5234491 | bytes 1916 | tf_op jit(solution)/shard_map/add_rows/pallas_call | solution.py:172
  285.6 4.0 collective-permute-done.15
  291.2 9.0 %add_rows.14 = (f32[5,39,8192]{2,1,0:T(8,128)}, f32[8,128]{1,0:T(8,128)}) custom-call(s32[1]{0:T(128)} %bitcast.27.base_ref, s32[8,5,1,512]{3,2,1,0:T(1,128)S(1)} %copy.187.refs_0_, s32[8,5,1,512]{3,2,1,0:T(1,128)S(1)} %copy.188.refs_1_, bf16[8,5,40,512]{3,2,1,0:T(8,128)(2,1)S(1)} %broadcast_multiply_fusion.3.refs_2_, ...), custom_call_target="tpu_custom_call", output_to_operand_aliasing={{0}: (5, {})} | custom-call | flops 5234491 | bytes 1916 | tf_op jit(solution)/shard_map/add_rows/pallas_call | solution.py:172
  300.1 11.2 %collective-permute-done.20 = bf16[2,5,32,512]{3,2,1,0:T(8,128)(2,1)S(1)} collective-permute-done((bf16[2,5,32,512]{3,2,1,0:T(8,128)(2,1)S(1)}, bf16[2,5,32,512]{3,2,1,0:T(8,128)(2,1)S(1)}, u32[]{:S(2)}, u32[]{:S(2)}) %collective-permute-start.20) | collective-permute-done | bytes 327712 | tf_op jit(solution)/shard_map/ppermute | solution.py:39
  311.4 10.2 %add_rows.15 = (f32[5,39,8192]{2,1,0:T(8,128)}, f32[8,128]{1,0:T(8,128)S(1)}) custom-call(s32[1]{0:T(128)} %bitcast.27.base_ref, s32[8,5,1,512]{3,2,1,0:T(1,128)S(1)} %copy.199.refs_0_, s32[8,5,1,512]{3,2,1,0:T(1,128)S(1)} %copy.200.refs_1_, bf16[8,5,40,512]{3,2,1,0:T(8,128)(2,1)S(1)} %broadcast_multiply_fusion.1.refs_2_, ...), custom_call_target="tpu_custom_call", output_to_operand_aliasing={{0}: (5, {})} | custom-call | flops 5234491 | bytes 1916 | tf_op jit(solution)/shard_map/add_rows/pallas_call | solution.py:172
  326.2 10.2 %add_rows.16 = (f32[5,39,8192]{2,1,0:T(8,128)}, f32[8,128]{1,0:T(8,128)S(1)}) custom-call(s32[1]{0:T(128)} %bitcast.27.base_ref, s32[8,5,1,512]{3,2,1,0:T(1,128)S(1)} %copy.199.refs_0_, s32[8,5,1,512]{3,2,1,0:T(1,128)S(1)} %copy.200.refs_1_, bf16[8,5,40,512]{3,2,1,0:T(8,128)(2,1)S(1)} %broadcast_multiply_fusion.1.refs_2_, ...), custom_call_target="tpu_custom_call", output_to_operand_aliasing={{0}: (5, {})} | custom-call | flops 5234491 | bytes 1916 | tf_op jit(solution)/shard_map/add_rows/pallas_call | solution.py:172
  343.2 25.7 %collective-permute-done.27.refs_5_ = bf16[8,5,32,512]{3,2,1,0:T(8,128)(2,1)S(1)} collective-permute-done((bf16[8,5,32,512]{3,2,1,0:T(8,128)(2,1)S(1)}, bf16[8,5,32,512]{3,2,1,0:T(8,128)(2,1)S(1)}, u32[]{:S(2)}, u32[]{:S(2)}) %collective-permute-start.27) | collective-permute-done | bytes 1310752 | tf_op jit(solution)/shard_map/ppermute | solution.py:39
  374.7 10.2 %add_rows.17 = (f32[5,39,8192]{2,1,0:T(8,128)}, f32[8,128]{1,0:T(8,128)}) custom-call(s32[1]{0:T(128)} %bitcast.27.base_ref, s32[8,5,1,512]{3,2,1,0:T(1,128)S(1)} %copy.199.refs_0_, s32[8,5,1,512]{3,2,1,0:T(1,128)S(1)} %copy.200.refs_1_, bf16[8,5,40,512]{3,2,1,0:T(8,128)(2,1)S(1)} %broadcast_multiply_fusion.1.refs_2_, ...), custom_call_target="tpu_custom_call", output_to_operand_aliasing={{0}: (5, {})} | custom-call | flops 5234491 | bytes 1916 | tf_op jit(solution)/shard_map/add_rows/pallas_call | solution.py:172
  384.9 10.2 %add_rows.18 = (f32[5,39,8192]{2,1,0:T(8,128)}, f32[8,128]{1,0:T(8,128)}) custom-call(s32[1]{0:T(128)} %bitcast.27.base_ref, s32[8,5,1,512]{3,2,1,0:T(1,128)S(1)} %copy.199.refs_0_, s32[8,5,1,512]{3,2,1,0:T(1,128)S(1)} %copy.200.refs_1_, bf16[8,5,40,512]{3,2,1,0:T(8,128)(2,1)S(1)} %broadcast_multiply_fusion.1.refs_2_, ...), custom_call_target="tpu_custom_call", output_to_operand_aliasing={{0}: (5, {})} | custom-call | flops 5234491 | bytes 1916 | tf_op jit(solution)/shard_map/add_rows/pallas_call | solution.py:172
  395.1 10.2 %add_rows.19 = (f32[5,39,8192]{2,1,0:T(8,128)}, f32[8,128]{1,0:T(8,128)}) custom-call(s32[1]{0:T(128)} %bitcast.27.base_ref, s32[8,5,1,512]{3,2,1,0:T(1,128)S(1)} %copy.199.refs_0_, s32[8,5,1,512]{3,2,1,0:T(1,128)S(1)} %copy.200.refs_1_, bf16[8,5,40,512]{3,2,1,0:T(8,128)(2,1)S(1)} %broadcast_multiply_fusion.1.refs_2_, ...), custom_call_target="tpu_custom_call", output_to_operand_aliasing={{0}: (5, {})} | custom-call | flops 5234491 | bytes 1916 | tf_op jit(solution)/shard_map/add_rows/pallas_call | solution.py:172
  408.4 13.3 %assemble.1 = (f32[3,1027,1027]{2,1,0:T(8,128)}, f32[1,1027,1024]{2,1,0:T(8,128)}, f32[1,1024,1024]{2,1,0:T(8,128)}) custom-call(s32[1]{0:T(128)} %bitcast.own_ref, bf16[8,5,32,512]{3,2,1,0:T(8,128)(2,1)} %copy-done.1, bf16[8,5,32,512]{3,2,1,0:T(8,128)(2,1)} %copy-done.10, bf16[8,5,32,512]{3,2,1,0:T(8,128)(2,1)} %copy-done.12, ...), custom_call_target="tpu_custom_call" | custom-call | bytes 39813 | tf_op jit(solution)/shard_map/assemble/pallas_call | solution.py:515
  (185 shorter events, 90.0 us)
Async XLA Ops:
  5.2 14.7 %all-to-all-start = ((s32[8,5,512]{2,1,0:T(8,128)}), s32[8,5,512]{2,1,0:T(8,128)}, u32[]{:S(2)}, u32[]{:S(2)}) async-start(s32[8,5,512]{2,1,0:T(8,128)} %reshape.387), calls=%async_computation | async-start | bytes 262144 | tf_op jit(solution)/shard_map/all_to_all | solution.py:570
  42.2 29.6 %all-to-all-start.1 = ((bf16[8,3,40,512]{3,2,1,0:T(8,128)(2,1)}), bf16[8,3,40,512]{3,2,1,0:T(8,128)(2,1)S(1)}, u32[]{:S(2)}, u32[]{:S(2)}) async-start(bf16[8,3,40,512]{3,2,1,0:T(8,128)(2,1)} %lookup.2), calls=%async_computation.1 | async-start | bytes 1966080 | tf_op jit(solution)/shard_map/all_to_all | solution.py:581
  71.8 22.7 %all-to-all-start.2 = ((bf16[8,2,40,512]{3,2,1,0:T(8,128)(2,1)}), bf16[8,2,40,512]{3,2,1,0:T(8,128)(2,1)S(1)}, u32[]{:S(2)}, u32[]{:S(2)}) async-start(bf16[8,2,40,512]{3,2,1,0:T(8,128)(2,1)} %lookup.3), calls=%async_computation.2 | async-start | bytes 1310720 | tf_op jit(solution)/shard_map/all_to_all | solution.py:581
  138.3 9.0 %collective-permute-start.5 = (bf16[2,2,2,2,2,5,32,512]{7,6,5,4,3,2,1,0:T(8,128)(2,1)}, bf16[2,2,2,2,2,5,32,512]{7,6,5,4,3,2,1,0:T(8,128)(2,1)}, u32[]{:S(2)}, u32[]{:S(2)}) collective-permute-start(bf16[2,2,2,2,2,5,32,512]{7,6,5,4,3,2,1,0:T(8,128)(2,1)} %bitcast.21), channel_id=1, source_target_pairs={{0,1},{1,0},{2,3},{3,2},{4,5},{5,4},{6,7},{7,6},{8,9},{9,8},{10,11... | collective-permute-start | bytes 15728648 | tf_op jit(solution)/shard_map/ppermute | solution.py:39
  138.3 51.9 %all-to-all-start.3 = ((bf16[8,5,40,512]{3,2,1,0:T(8,128)(2,1)}), bf16[8,5,40,512]{3,2,1,0:T(8,128)(2,1)S(1)}, u32[]{:S(2)}, u32[]{:S(2)}) async-start(bf16[8,5,40,512]{3,2,1,0:T(8,128)(2,1)} %bitcast.30), calls=%async_computation.3 | async-start | bytes 3276800 | tf_op jit(solution)/shard_map/all_to_all | solution.py:600
  155.7 30.9 %collective-permute-start.6 = (bf16[2,2,2,5,32,512]{5,4,3,2,1,0:T(8,128)(2,1)S(1)}, bf16[2,2,2,5,32,512]{5,4,3,2,1,0:T(8,128)(2,1)S(1)}, u32[]{:S(2)}, u32[]{:S(2)}) collective-permute-start(bf16[2,2,2,5,32,512]{5,4,3,2,1,0:T(8,128)(2,1)S(1)} %get-tuple-element.67), channel_id=1, source_target_pairs={{0,2},{1,3},{2,0},{3,1},{4,6},{5,7},{6,4},{7,5},{8,10},{9,11},{10,... | collective-permute-start | bytes 3932168 | tf_op jit(solution)/shard_map/ppermute | solution.py:39
  158.0 33.6 %collective-permute-start = (f32[48,1152]{1,0:T(8,128)}, f32[48,1152]{1,0:T(8,128)}, u32[]{:S(2)}, u32[]{:S(2)}) collective-permute-start(f32[48,1152]{1,0:T(8,128)} %pad_maximum_fusion.8), channel_id=1, source_target_pairs={{0,1},{1,0},{2,3},{3,2},{4,5},{5,4},{6,7},{7,6},{8,9},{9,8},{10,11... | collective-permute-start | bytes 663560 | tf_op jit(solution)/shard_map/ppermute | solution.py:39
  158.0 68.8 %collective-permute-start.10 = (bf16[2,2,2,5,32,512]{5,4,3,2,1,0:T(8,128)(2,1)}, bf16[2,2,2,5,32,512]{5,4,3,2,1,0:T(8,128)(2,1)}, u32[]{:S(2)}, u32[]{:S(2)}) collective-permute-start(bf16[2,2,2,5,32,512]{5,4,3,2,1,0:T(8,128)(2,1)} %get-tuple-element.68), channel_id=1, source_target_pairs={{0,4},{4,0},{8,12},{12,8},{16,20},{20,16},{24,28},{28,24},{1,5},{5... | collective-permute-start | bytes 3932168 | tf_op jit(solution)/shard_map/ppermute | solution.py:39
  191.5 39.5 %collective-permute-start.9 = (bf16[8,5,40,512]{3,2,1,0:T(8,128)(2,1)S(1)}, bf16[8,5,40,512]{3,2,1,0:T(8,128)(2,1)S(1)}, u32[]{:S(2)}, u32[]{:S(2)}) collective-permute-start(bf16[8,5,40,512]{3,2,1,0:T(8,128)(2,1)S(1)} %broadcast_multiply_fusion.3.refs_2_), channel_id=1, source_target_pairs={{0,1},{1,0},{2,3},{3,2},{4,5},{5,4},{6,7},{7,6},{8,9},{9,8},{10,11... | collective-permute-start | bytes 4915208 | tf_op jit(solution)/shard_map/ppermute | solution.py:39
  192.5 7.9 %collective-permute-start.1 = (f32[48,1152]{1,0:T(8,128)S(1)}, f32[48,1152]{1,0:T(8,128)S(1)}, u32[]{:S(2)}, u32[]{:S(2)}) collective-permute-start(f32[48,1152]{1,0:T(8,128)S(1)} %fusion.37), channel_id=1, source_target_pairs={{0,2},{1,3},{2,0},{3,1},{4,6},{5,7},{6,4},{7,5},{8,10},{9,11},{10,... | collective-permute-start | bytes 663560 | tf_op jit(solution)/shard_map/ppermute | solution.py:39
  200.4 7.4 %collective-permute-start.2 = (f32[48,1152]{1,0:T(8,128)S(1)}, f32[48,1152]{1,0:T(8,128)S(1)}, u32[]{:S(2)}, u32[]{:S(2)}) collective-permute-start(f32[48,1152]{1,0:T(8,128)S(1)} %add.346), channel_id=1, source_target_pairs={{0,4},{4,0},{8,12},{12,8},{16,20},{20,16},{24,28},{28,24},{1,5},{5... | collective-permute-start | bytes 663560 | tf_op jit(solution)/shard_map/ppermute | solution.py:39
  207.9 6.5 %collective-permute-start.3 = (f32[48,1152]{1,0:T(8,128)S(1)}, f32[48,1152]{1,0:T(8,128)S(1)}, u32[]{:S(2)}, u32[]{:S(2)}) collective-permute-start(f32[48,1152]{1,0:T(8,128)S(1)} %add.347), channel_id=1, source_target_pairs={{0,8},{4,12},{8,0},{12,4},{16,24},{20,28},{24,16},{28,20},{1,9},{5... | collective-permute-start | bytes 663560 | tf_op jit(solution)/shard_map/ppermute | solution.py:39
  209.7 30.6 %collective-permute-start.7 = (bf16[2,2,5,32,512]{4,3,2,1,0:T(8,128)(2,1)}, bf16[2,2,5,32,512]{4,3,2,1,0:T(8,128)(2,1)}, u32[]{:S(2)}, u32[]{:S(2)}) collective-permute-start(bf16[2,2,5,32,512]{4,3,2,1,0:T(8,128)(2,1)} %get-tuple-element.74), channel_id=1, source_target_pairs={{0,4},{4,0},{8,12},{12,8},{16,20},{20,16},{24,28},{28,24},{1,5},{5... | collective-permute-start | bytes 1966088 | tf_op jit(solution)/shard_map/ppermute | solution.py:39
  214.4 11.4 %collective-permute-start.4 = (f32[48,1152]{1,0:T(8,128)S(1)}, f32[48,1152]{1,0:T(8,128)}, u32[]{:S(2)}, u32[]{:S(2)}) collective-permute-start(f32[48,1152]{1,0:T(8,128)S(1)} %add.348), channel_id=1, source_target_pairs={{0,16},{4,20},{8,24},{12,28},{16,0},{20,4},{24,8},{28,12},{1,17},{... | collective-permute-start | bytes 663560 | tf_op jit(solution)/shard_map/ppermute | solution.py:39
  229.4 16.2 %collective-permute-start.11 = (bf16[2,2,5,32,512]{4,3,2,1,0:T(8,128)(2,1)S(1)}, bf16[2,2,5,32,512]{4,3,2,1,0:T(8,128)(2,1)S(1)}, u32[]{:S(2)}, u32[]{:S(2)}) collective-permute-start(bf16[2,2,5,32,512]{4,3,2,1,0:T(8,128)(2,1)S(1)} %get-tuple-element.76), channel_id=1, source_target_pairs={{0,2},{1,3},{2,0},{3,1},{4,6},{5,7},{6,4},{7,5},{8,10},{9,11},{10,... | collective-permute-start | bytes 1966088 | tf_op jit(solution)/shard_map/ppermute | solution.py:39
  243.6 37.0 %collective-permute-start.17 = (bf16[8,5,40,512]{3,2,1,0:T(8,128)(2,1)S(1)}, bf16[8,5,40,512]{3,2,1,0:T(8,128)(2,1)S(1)}, u32[]{:S(2)}, u32[]{:S(2)}) collective-permute-start(bf16[8,5,40,512]{3,2,1,0:T(8,128)(2,1)S(1)} %broadcast_multiply_fusion.2), channel_id=1, source_target_pairs={{0,2},{1,3},{2,0},{3,1},{4,6},{5,7},{6,4},{7,5},{8,10},{9,11},{10,... | collective-permute-start | bytes 4915208 | tf_op jit(solution)/shard_map/ppermute | solution.py:39
  246.5 31.5 %collective-permute-start.12 = (bf16[2,5,32,512]{3,2,1,0:T(8,128)(2,1)S(1)}, bf16[2,5,32,512]{3,2,1,0:T(8,128)(2,1)S(1)}, u32[]{:S(2)}, u32[]{:S(2)}) collective-permute-start(bf16[2,5,32,512]{3,2,1,0:T(8,128)(2,1)S(1)} %pad_maximum_fusion.5), channel_id=1, source_target_pairs={{0,8},{4,12},{8,0},{12,4},{16,24},{20,28},{24,16},{28,20},{1,9},{5... | collective-permute-start | bytes 983048 | tf_op jit(solution)/shard_map/ppermute | solution.py:39
  246.6 31.4 %collective-permute-start.13 = (bf16[2,5,32,512]{3,2,1,0:T(8,128)(2,1)S(1)}, bf16[2,5,32,512]{3,2,1,0:T(8,128)(2,1)S(1)}, u32[]{:S(2)}, u32[]{:S(2)}) collective-permute-start(bf16[2,5,32,512]{3,2,1,0:T(8,128)(2,1)S(1)} %pad_maximum_fusion.6), channel_id=1, source_target_pairs={{0,16},{4,20},{8,24},{12,28},{16,0},{20,4},{24,8},{28,12},{1,17},{... | collective-permute-start | bytes 983048 | tf_op jit(solution)/shard_map/ppermute | solution.py:39
  250.1 27.9 %collective-permute-start.14 = (bf16[2,5,32,512]{3,2,1,0:T(8,128)(2,1)S(1)}, bf16[2,5,32,512]{3,2,1,0:T(8,128)(2,1)S(1)}, u32[]{:S(2)}, u32[]{:S(2)}) collective-permute-start(bf16[2,5,32,512]{3,2,1,0:T(8,128)(2,1)S(1)} %pad_maximum_fusion.7), channel_id=1, source_target_pairs={{0,24},{4,28},{8,16},{12,20},{16,8},{20,12},{24,0},{28,4},{1,25},{... | collective-permute-start | bytes 983048 | tf_op jit(solution)/shard_map/ppermute | solution.py:39
  280.7 30.7 %collective-permute-start.18 = (bf16[8,5,40,512]{3,2,1,0:T(8,128)(2,1)S(1)}, bf16[8,5,40,512]{3,2,1,0:T(8,128)(2,1)S(1)}, u32[]{:S(2)}, u32[]{:S(2)}) collective-permute-start(bf16[8,5,40,512]{3,2,1,0:T(8,128)(2,1)S(1)} %broadcast_multiply_fusion.1.refs_2_), channel_id=1, source_target_pairs={{0,1},{1,0},{2,3},{3,2},{4,5},{5,4},{6,7},{7,6},{8,9},{9,8},{10,11... | collective-permute-start | bytes 4915208 | tf_op jit(solution)/shard_map/ppermute | solution.py:39
  280.8 19.3 %collective-permute-start.21 = (bf16[2,5,32,512]{3,2,1,0:T(8,128)(2,1)S(1)}, bf16[2,5,32,512]{3,2,1,0:T(8,128)(2,1)S(1)}, u32[]{:S(2)}, u32[]{:S(2)}) collective-permute-start(bf16[2,5,32,512]{3,2,1,0:T(8,128)(2,1)S(1)} %add_convert_fusion.refs_5_), channel_id=1, source_target_pairs={{0,24},{4,28},{8,16},{12,20},{16,8},{20,12},{24,0},{28,4},{1,25},{... | collective-permute-start | bytes 983048 | tf_op jit(solution)/shard_map/ppermute | solution.py:39
  283.7 5.9 %collective-permute-start.15 = (s32[8,5,512]{2,1,0:T(8,128)}, s32[8,5,512]{2,1,0:T(8,128)S(1)}, u32[]{:S(2)}, u32[]{:S(2)}) collective-permute-start(s32[8,5,512]{2,1,0:T(8,128)} %all-to-all-done), channel_id=1, source_target_pairs={{0,2},{1,3},{2,0},{3,1},{4,6},{5,7},{6,4},{7,5},{8,10},{9,11},{10,... | collective-permute-start | bytes 245768 | tf_op jit(solution)/shard_map/ppermute | solution.py:39
  285.6 25.8 %collective-permute-start.20 = (bf16[2,5,32,512]{3,2,1,0:T(8,128)(2,1)S(1)}, bf16[2,5,32,512]{3,2,1,0:T(8,128)(2,1)S(1)}, u32[]{:S(2)}, u32[]{:S(2)}) collective-permute-start(bf16[2,5,32,512]{3,2,1,0:T(8,128)(2,1)S(1)} %add_convert_fusion.refs_5_), channel_id=1, source_target_pairs={{0,16},{4,20},{8,24},{12,28},{16,0},{20,4},{24,8},{28,12},{1,17},{... | collective-permute-start | bytes 983048 | tf_op jit(solution)/shard_map/ppermute | solution.py:39
  291.1 20.3 %collective-permute-start.19 = (bf16[2,5,32,512]{3,2,1,0:T(8,128)(2,1)S(1)}, bf16[2,5,32,512]{3,2,1,0:T(8,128)(2,1)S(1)}, u32[]{:S(2)}, u32[]{:S(2)}) collective-permute-start(bf16[2,5,32,512]{3,2,1,0:T(8,128)(2,1)S(1)} %add_convert_fusion.refs_5_), channel_id=1, source_target_pairs={{0,8},{4,12},{8,0},{12,4},{16,24},{20,28},{24,16},{28,20},{1,9},{5... | collective-permute-start | bytes 983048 | tf_op jit(solution)/shard_map/ppermute | solution.py:39
  322.9 16.4 %collective-permute-start.26 = (bf16[4,5,32,512]{3,2,1,0:T(8,128)(2,1)S(1)}, bf16[4,5,32,512]{3,2,1,0:T(8,128)(2,1)S(1)}, u32[]{:S(2)}, u32[]{:S(2)}) collective-permute-start(bf16[4,5,32,512]{3,2,1,0:T(8,128)(2,1)S(1)} %pad_maximum_fusion.4.refs_6_), channel_id=1, source_target_pairs={{0,2},{1,3},{2,0},{3,1},{4,6},{5,7},{6,4},{7,5},{8,10},{9,11},{10,... | collective-permute-start | bytes 1966088 | tf_op jit(solution)/shard_map/ppermute | solution.py:39
  324.6 16.3 %collective-permute-start.22 = (bf16[4,5,32,512]{3,2,1,0:T(8,128)(2,1)S(1)}, bf16[4,5,32,512]{3,2,1,0:T(8,128)(2,1)S(1)}, u32[]{:S(2)}, u32[]{:S(2)}) collective-permute-start(bf16[4,5,32,512]{3,2,1,0:T(8,128)(2,1)S(1)} %pad_maximum_fusion.3.refs_5_), channel_id=1, source_target_pairs={{0,4},{4,0},{8,12},{12,8},{16,20},{20,16},{24,28},{28,24},{1,5},{5... | collective-permute-start | bytes 1966088 | tf_op jit(solution)/shard_map/ppermute | solution.py:39
  339.4 29.5 %collective-permute-start.27 = (bf16[8,5,32,512]{3,2,1,0:T(8,128)(2,1)S(1)}, bf16[8,5,32,512]{3,2,1,0:T(8,128)(2,1)S(1)}, u32[]{:S(2)}, u32[]{:S(2)}) collective-permute-start(bf16[8,5,32,512]{3,2,1,0:T(8,128)(2,1)S(1)} %pad_maximum_fusion.1.refs_4_.refs_6_), channel_id=1, source_target_pairs={{0,4},{4,0},{8,12},{12,8},{16,20},{20,16},{24,28},{28,24},{1,5},{5... | collective-permute-start | bytes 3932168 | tf_op jit(solution)/shard_map/ppermute | solution.py:39
  341.1 29.2 %collective-permute-start.23 = (bf16[8,5,32,512]{3,2,1,0:T(8,128)(2,1)S(1)}, bf16[8,5,32,512]{3,2,1,0:T(8,128)(2,1)S(1)}, u32[]{:S(2)}, u32[]{:S(2)}) collective-permute-start(bf16[8,5,32,512]{3,2,1,0:T(8,128)(2,1)S(1)} %pad_maximum_fusion.refs_0_.refs_5_), channel_id=1, source_target_pairs={{0,2},{1,3},{2,0},{3,1},{4,6},{5,7},{6,4},{7,5},{8,10},{9,11},{10,... | collective-permute-start | bytes 3932168 | tf_op jit(solution)/shard_map/ppermute | solution.py:39
  342.7 62.6 %collective-permute-start.28 = (bf16[8,5,32,512]{3,2,1,0:T(8,128)(2,1)S(1)}, bf16[8,5,32,512]{3,2,1,0:T(8,128)(2,1)S(1)}, u32[]{:S(2)}, u32[]{:S(2)}) collective-permute-start(bf16[8,5,32,512]{3,2,1,0:T(8,128)(2,1)S(1)} %pad_maximum_fusion.1.refs_4_.refs_6_), channel_id=1, source_target_pairs={{0,1},{1,0},{2,3},{3,2},{4,5},{5,4},{6,7},{7,6},{8,9},{9,8},{10,11... | collective-permute-start | bytes 3932168 | tf_op jit(solution)/shard_map/ppermute | solution.py:39
  342.7 62.6 %collective-permute-start.24 = (bf16[8,5,32,512]{3,2,1,0:T(8,128)(2,1)S(1)}, bf16[8,5,32,512]{3,2,1,0:T(8,128)(2,1)S(1)}, u32[]{:S(2)}, u32[]{:S(2)}) collective-permute-start(bf16[8,5,32,512]{3,2,1,0:T(8,128)(2,1)S(1)} %pad_maximum_fusion.refs_0_.refs_5_), channel_id=1, source_target_pairs={{0,1},{1,0},{2,3},{3,2},{4,5},{5,4},{6,7},{7,6},{8,9},{9,8},{10,11... | collective-permute-start | bytes 3932168 | tf_op jit(solution)/shard_map/ppermute | solution.py:39
  368.9 36.4 %collective-permute-start.29 = (bf16[8,5,32,512]{3,2,1,0:T(8,128)(2,1)S(1)}, bf16[8,5,32,512]{3,2,1,0:T(8,128)(2,1)S(1)}, u32[]{:S(2)}, u32[]{:S(2)}) collective-permute-start(bf16[8,5,32,512]{3,2,1,0:T(8,128)(2,1)S(1)} %collective-permute-done.27.refs_5_), channel_id=1, source_target_pairs={{0,1},{1,0},{2,3},{3,2},{4,5},{5,4},{6,7},{7,6},{8,9},{9,8},{10,11... | collective-permute-start | bytes 3932168 | tf_op jit(solution)/shard_map/ppermute | solution.py:39
  370.3 35.0 %collective-permute-start.25 = (bf16[8,5,32,512]{3,2,1,0:T(8,128)(2,1)S(1)}, bf16[8,5,32,512]{3,2,1,0:T(8,128)(2,1)S(1)}, u32[]{:S(2)}, u32[]{:S(2)}) collective-permute-start(bf16[8,5,32,512]{3,2,1,0:T(8,128)(2,1)S(1)} %collective-permute-done.23.refs_1_), channel_id=1, source_target_pairs={{0,1},{1,0},{2,3},{3,2},{4,5},{5,4},{6,7},{7,6},{8,9},{9,8},{10,11... | collective-permute-start | bytes 3932168 | tf_op jit(solution)/shard_map/ppermute | solution.py:39
  (25 other events, 377.8 us)

commit v5 on v4

--- a/solution.py
+++ b/solution.py
@@ -15,6 +15,7 @@
 LOOK_BLOCKS = 8
 LOOK_ROWS = 32
 ADD_LOW = 512
+ADD_TABS = 4
 MAIN = 1024
 CHUNK = 384
 PIECE = 32
@@ -137,16 +138,17 @@
     low_iota = lax.broadcasted_iota(I32, (ADD_LOW, cols), 0)
     product = None
     for ids_ref, grad_ref in zip(ids_refs, grad_refs):
-        local = ids_ref[0, 0] - base_ref[0]
-        high = lax.shift_right_arithmetic(local, ADD_LOW.bit_length() - 1)
-        low = local & (ADD_LOW - 1)
-        high_hot = jnp.where(high_iota == high, 1.0, 0.0)
-        low_hot = jnp.where(low_iota == low, 1.0, 0.0).astype(BF)
-        grads = grad_ref[0, 0, :embed_dim].astype(F32)
-        left = (grads[:, None, :] * high_hot[None, :, :]).astype(BF)
-        left = left.reshape(embed_dim * high_count, cols)
-        term = lax.dot_general(left, low_hot, NT, preferred_element_type=F32)
-        product = term if product is None else product + term
+        for tab in range(ids_ref.shape[0]):
+            local = ids_ref[tab, 0] - base_ref[0]
+            high = lax.shift_right_arithmetic(local, ADD_LOW.bit_length() - 1)
+            low = local & (ADD_LOW - 1)
+            high_hot = jnp.where(high_iota == high, 1.0, 0.0)
+            low_hot = jnp.where(low_iota == low, 1.0, 0.0).astype(BF)
+            grads = grad_ref[tab, 0, :embed_dim].astype(F32)
+            left = (grads[:, None, :] * high_hot[None, :, :]).astype(BF)
+            left = left.reshape(embed_dim * high_count, cols)
+            term = lax.dot_general(left, low_hot, NT, preferred_element_type=F32)
+            product = term if product is None else product + term
     for lane in range(ADD_LOW // 128):
         total[lane] += product[:, lane * 128 : (lane + 1) * 128]
 
@@ -171,10 +173,10 @@
     whole = [] if so_far is None else [so_far]
     table_grad, token = pl.pallas_call(
         functools.partial(add_kernel, part_count, accumulate),
-        grid=(tab_count,),
+        grid=(tab_count // ADD_TABS,),
         in_specs=[pl.BlockSpec(memory_space=pltpu.SMEM)]
-        + [pl.BlockSpec((1, 1, 1, count), lambda t: (t, slot, 0, 0))] * part_count
-        + [pl.BlockSpec((1, 1, pad_dim, count), lambda t: (t, slot, 0, 0))] * part_count
+        + [pl.BlockSpec((ADD_TABS, 1, 1, count), lambda t: (t, slot, 0, 0))] * part_count
+        + [pl.BlockSpec((ADD_TABS, 1, pad_dim, count), lambda t: (t, slot, 0, 0))] * part_count
         + [block if accumulate else anywhere] * len(whole)
         + [anywhere] * len(after),
         out_specs=[block, pl.BlockSpec((8, 128), lambda t: (0, 0))],
@@ -460,11 +462,13 @@
 FAR = [(0, 1), (1, 0), (1, 1)]
 
 
-def added(parts, index, token=None):
-    value = parts[0][index].astype(F32)
+def added(parts, *gates):
+    value = parts[0].astype(F32)
     for other in parts[1:]:
-        value = value + other[index].astype(F32)
-    return value if token is None else value + token
+        value = value + other.astype(F32)
+    for gate in gates:
+        value = value + gate
+    return value
 
 
 def joined(parts, token):
@@ -572,11 +576,12 @@
     )
     listed = jnp.transpose(wanted, (1, 0, 2)).reshape(-1)
 
-    starts = list(range(0, slot_count, LOOK_SLOTS))
+    first_size = slot_count % LOOK_SLOTS
+    starts = ([0] if first_size else []) + list(range(first_size, slot_count, LOOK_SLOTS))
     arrived = []
     for begin in starts:
         looked = lookup(
-            tables, listed, own_rows, tab_count, begin, min(LOOK_SLOTS, slot_count - begin)
+            tables, listed, own_rows, tab_count, begin, LOOK_SLOTS if begin or not first_size else first_size
         )
         arrived.append(lax.all_to_all(looked, "tab", split_axis=0, concat_axis=0, tiled=True))
 
@@ -653,39 +658,56 @@
             )
 
     small = jnp.concatenate([strips.reshape(matrix_count * 8, size), sums], axis=0)
-    for axis in ("rep", "tab"):
-        for mask in masks_of(axis):
-            small = small + swap(small, axis, mask)
+    small_jobs = [(axis, mask) for axis in ("rep", "tab") for mask in masks_of(axis)]
+    early = [job for job in small_jobs if job[1] < 4 and job != ("tab", 2)]
+    late = [job for job in small_jobs if job not in early]
+
+    def zero_of(value):
+        return 0.0 * value.astype(F32)
 
     got = swap(send, "rep", 1)
-    sent = [swap(added((keep, got), (at, 1)).astype(BF), *HALVES[at][0]) for at in range(2)]
-    kept = [added((keep, got), (at, 0)) for at in range(2)]
-    parts = [(kept[at], sent[at]) for at in range(2)]
-    sent = [swap(added(parts[at], 1).astype(BF), *HALVES[at][1]) for at in range(2)]
-    kept = [added(parts[at], 0) for at in range(2)]
-    returned = gate(returned, kept[0][0, 0, 0, 0, 0])
+    sources = [[keep[at], got[at]] for at in range(2)]
+
+    def take(at, *index):
+        whole = keep.ndim - 1
+        return [part[index[whole - part.ndim :]] for part in sources[at]]
+
+    sent = [swap(added(take(at, 1)).astype(BF), *HALVES[at][0]) for at in range(2)]
+    for axis, mask in early:
+        small = small + swap(small, axis, mask)
+    ready = zero_of(small[0, 0])
+    for at in range(2):
+        sources[at].append(sent[at])
+        ready = ready + zero_of(sent[at][0, 0, 0, 0, 0, 0])
+    sent = [swap(added(take(at, 0, 1), ready).astype(BF), *HALVES[at][1]) for at in range(2)]
+    returned = gate(returned, ready)
     near_grads = near_parts(returned)
-    add_next(1, kept + [small])
-    parts = [(kept[at], sent[at]) for at in range(2)]
-    sent = [
-        swap(
-            jnp.stack([added(part, (high, low), token) for part in parts]).astype(BF),
-            "tab",
-            4 * high + 2 * low,
-        )
-        for high, low in FAR
-    ]
-    kept = jnp.stack([added(part, (0, 0), token) for part in parts])
-    bases = far_bases(gate(returned, kept[0, 0, 0, 0]))
-    add_next(slot_count - 2, [kept])
-    piece = added((kept, *sent), slice(None), token).astype(BF)
+    add_next(1, [sources[0][2]])
+    for at in range(2):
+        sources[at].append(sent[at])
+
+    def take_far(high, low):
+        both = [added(take(at, 0, 0, high, low), token) for at in range(2)]
+        return jnp.stack(both)
+
+    kept = take_far(0, 0)
+    sends = [take_far(high, low).astype(BF) for high, low in FAR]
+    far = [swap(value, "tab", 4 * high + 2 * low) for value, (high, low) in zip(sends, FAR)]
+    bases = far_bases(gate(returned, sends[0][0, 0, 0, 0]))
+    add_next(slot_count - 2, [kept] + sends)
+    for axis, mask in late[:1]:
+        small = small + swap(small, axis, mask)
+    piece = added([kept, *far], token, zero_of(small[0, 0])).astype(BF)
     for axis, known in (("rep", 2), ("tab", 3)):
         for mask in masks_of(axis)[known:]:
             piece = (piece.astype(F32) + swap(piece, axis, mask).astype(F32)).astype(BF)
     parts = [piece, swap(piece, "tab", 2), swap(piece, "tab", 4), swap(piece, "tab", 6)]
     far_grads = far_parts([gate(part, piece[0, 0, 0, 0]) for part in bases])
     add_next(2, [piece])
-    values = [joined([part[at : at + 1] for part in parts], token) for at in range(2)]
+    for axis, mask in late[1:]:
+        small = small + swap(small, axis, mask)
+    done = token + zero_of(small[0, 0])
+    values = [joined([part[at : at + 1] for part in parts], done) for at in range(2)]
     sent = [swap(values[at], *HALVES[at][1]) for at in range(2)]
     add_next(1, values)
     values = [joined((values[at], sent[at]), token) for at in range(2)]
@@ -693,8 +715,8 @@
     blocks = [[values[at], None, swap(values[at], "rep", 1), None] for at in range(2)]
     add_next(slot_count, values)
     for at in range(2):
-        blocks[at][1] = sent[at]
-        blocks[at][3] = swap(sent[at], "rep", 1)
+        blocks[at][1] = gate(sent[at], token)
+        blocks[at][3] = swap(blocks[at][1], "rep", 1)
     blocks = blocks[0] + blocks[1]
 
     strips = small[:-8].reshape(matrix_count, 8, size)

time: 428 us -> 414 us (0.967)
  local copies, waits for them, and re-layouts: 30.8 us -> 49.6 us
  starting transfers between devices: 55.9 us -> 44.9 us
  Pallas kernels: 187 us -> 177 us
  waiting for transfers between devices: 108 us -> 98.4 us
  other arithmetic: 33.6 us -> 27.5 us
    pallas_call x10, Pallas kernels: 94.9 us -> 81.5 us  [add_rows(): pl.pallas_call(functools.partial(add_kernel, part_count, accumulate), gri...]
    slice x2 -> x7, local copies, waits for them, and re-layouts: 1.02 us -> 14 us  [the longest x1 8.26 us: on_device(): sources = [[keep[at], got[at]] for at in range(2)]]
    ppermute x30, waiting for transfers between devices: 98.1 us -> 87.8 us  [swap(): lax.ppermute(value, axis, [(at, at ^ mask) for at in range(lax.axis_size(...]
    ppermute x30, starting transfers between devices: 31.5 us -> 23.6 us  [swap(): lax.ppermute(value, axis, [(at, at ^ mask) for at in range(lax.axis_size(...]
    squeeze x0 -> x1, local copies, waits for them, and re-layouts: none -> 6.6 us  [on_device(): sources = [[keep[at], got[at]] for at in range(2)]]
    convert_element_type x4, other arithmetic: 13.2 us -> 7.1 us  [the longest x2 3.45 us: on_device(): added(take(at, 0, 1), ready).astype(BF)]
    unnamed x51 -> x65, local copies, waits for them, and re-layouts: 16.3 us -> 17.7 us
  transfers between devices with their start and end apart: 34 -> 34, of which waited for: 17 -> 15; matrix products, arithmetic and copies ran while one was open for 12% -> 15% of each run, Pallas kernels for 24% -> 24%
where the time goes in v5:
time: 414 us; the launch traced here: 409 us
  Pallas kernels  177 us (43%)
  waiting for transfers between devices  98.4 us (24%)
  local copies, waits for them, and re-layouts  49.6 us (12%)
  starting transfers between devices  44.9 us (11%)
  other arithmetic  27.5 us (7%)
  between operations  11.5 us (3%)
    ppermute x30, waiting for transfers between devices, swap(): lax.ppermute(value, axis, [(at, at ^ mask) for at in range(lax.axis_size(...  87.8 us
    pallas_call x10, Pallas kernels, add_rows(): pl.pallas_call(functools.partial(add_kernel, part_count, accumulate), gri...  81.5 us
    pallas_call x2, Pallas kernels, lookup(): pl.pallas_call(functools.partial(lookup_kernel, first_slot), in_specs=[sm...  41.7 us
    pallas_call x1, Pallas kernels, dense_step(): pl.pallas_call(functools.partial(dense_kernel, dense_width, width, starts...  27.6 us
    ppermute x30, starting transfers between devices, swap(): lax.ppermute(value, axis, [(at, at ^ mask) for at in range(lax.axis_size(...  23.6 us
    unnamed x65, local copies, waits for them, and re-layouts  17.7 us
    pallas_call x1, Pallas kernels, assemble(): pl.pallas_call(functools.partial(assemble_kernel, layer_count), grid=(mat...  13.3 us
    pallas_call x1, Pallas kernels, weight_parts(): pl.pallas_call(weight_kernel, grid=(matrix_count,), in_specs=[pl.BlockSpe...  12.7 us
  transfers between devices with their start and end apart: 34, of which 15 were waited for; matrix products, arithmetic and copies ran while one was open for 15% of the time, Pallas kernels for 24%

profile of v5, /device:TPU:0, one launch (start us, length us, event | category | flops | bytes accessed | tf_op | source)
XLA Modules:
  0.0 408.6 jit_solution(4093527572389685947)
XLA Ops:
  5.2 7.3 %all-to-all-start = ((s32[8,5,512]{2,1,0:T(8,128)}), s32[8,5,512]{2,1,0:T(8,128)S(1)}, u32[]{:S(2)}, u32[]{:S(2)}) async-start(s32[8,5,512]{2,1,0:T(8,128)} %reshape.617), calls=%async_computation | async-start | bytes 262144 | tf_op jit(solution)/shard_map/all_to_all | solution.py:574
  13.8 6.0 %all-to-all-done = s32[8,5,512]{2,1,0:T(8,128)S(1)} async-done(((s32[8,5,512]{2,1,0:T(8,128)}), s32[8,5,512]{2,1,0:T(8,128)S(1)}, u32[]{:S(2)}, u32[]{:S(2)}) %all-to-all-start) | async-done | bytes 81952 | tf_op jit(solution)/shard_map/all_to_all | solution.py:574
  20.5 17.9 %lookup.2 = bf16[8,2,40,512]{3,2,1,0:T(8,128)(2,1)} custom-call(s32[20480]{0:T(1024)} %bitcast.276, s32[5]{0:T(128)} %dynamic_slice.3.rows_ref, bf16[5,39,32768]{2,1,0:T(8,128)(2,1)} %table_hbm.3), custom_call_target="tpu_custom_call" | custom-call | flops 20132660 | bytes 5750 | tf_op jit(solution)/shard_map/lookup/pallas_call | solution.py:101
  38.4 4.4 %all-to-all-start.1 = ((bf16[8,2,40,512]{3,2,1,0:T(8,128)(2,1)}), bf16[8,2,40,512]{3,2,1,0:T(8,128)(2,1)S(1)}, u32[]{:S(2)}, u32[]{:S(2)}) async-start(bf16[8,2,40,512]{3,2,1,0:T(8,128)(2,1)} %lookup.2), calls=%async_computation.1 | async-start | bytes 1310720 | tf_op jit(solution)/shard_map/all_to_all | solution.py:586
  44.7 23.8 %lookup.3 = bf16[8,3,40,512]{3,2,1,0:T(8,128)(2,1)} custom-call(s32[20480]{0:T(1024)} %bitcast.277, s32[5]{0:T(128)} %dynamic_slice.3.rows_ref, bf16[5,39,32768]{2,1,0:T(8,128)(2,1)} %table_hbm.3), custom_call_target="tpu_custom_call" | custom-call | flops 30198988 | bytes 8626 | tf_op jit(solution)/shard_map/lookup/pallas_call | solution.py:101
  68.5 5.6 %all-to-all-start.2 = ((bf16[8,3,40,512]{3,2,1,0:T(8,128)(2,1)}), bf16[8,3,40,512]{3,2,1,0:T(8,128)(2,1)S(1)}, u32[]{:S(2)}, u32[]{:S(2)}) async-start(bf16[8,3,40,512]{3,2,1,0:T(8,128)(2,1)} %lookup.3), calls=%async_computation.2 | async-start | bytes 1966080 | tf_op jit(solution)/shard_map/all_to_all | solution.py:586
  77.3 3.6 multiply_bitcast_fusion
  92.4 4.6 %all-to-all-done.2.refs_1_ = bf16[8,3,40,512]{3,2,1,0:T(8,128)(2,1)S(1)} async-done(((bf16[8,3,40,512]{3,2,1,0:T(8,128)(2,1)}), bf16[8,3,40,512]{3,2,1,0:T(8,128)(2,1)S(1)}, u32[]{:S(2)}, u32[]{:S(2)}) %all-to-all-start.2) | async-done | bytes 983072 | tf_op jit(solution)/shard_map/all_to_all | solution.py:586
  97.9 27.6 %dense.1 = (f32[1,512]{1,0:T(1,128)}, f32[16,512]{1,0:T(8,128)}, bf16[40,40,512]{2,1,0:T(8,128)(2,1)}, bf16[5,1152,512]{2,1,0:T(8,128)(2,1)}, bf16[5,1152,512]{2,1,0:T(8,128)(2,1)}, /*index=5*/f32[8,1152]{1,0:T(8,128)}) custom-call(s32[26]{0:T(128)} %place_ref.1, f32[1]{0:T(128)S(6)} %convert.72.bias_ref, bf16[8,2,40,512]{3,2,1,0:T(8,128)(2,1)} %copy-done.13, ...), custom_call_target="tpu_custom_call" | custom-call | flops 13589544 | bytes 30965 | tf_op jit(solution)/shard_map/dense/pallas_call | solution.py:366
  128.1 12.7 %weight_parts.1 = (f32[2,16,5,32,512]{4,3,2,1,0:T(8,128)}, bf16[2,16,5,32,512]{4,3,2,1,0:T(8,128)(2,1)}, f32[5,8,1152]{2,1,0:T(8,128)S(1)}) custom-call(s32[1]{0:T(128)} %bitcast.own_ref, bf16[5,1152,512]{2,1,0:T(8,128)(2,1)S(1)} %copy-done.2, bf16[5,1152,512]{2,1,0:T(8,128)(2,1)} %get-tuple-element.40.right_ref), custom_call_target="tpu_custom_call" | custom-call | flops 6794772 | bytes 66355 | tf_op jit(solution)/shard_map/weight_parts/pallas_call | solution.py:438
  140.8 4.0 all-to-all-start.3
  157.6 30.7 %collective-permute-done.1 = f32[48,1152]{1,0:T(8,128)S(1)} collective-permute-done((f32[48,1152]{1,0:T(8,128)S(1)}, f32[48,1152]{1,0:T(8,128)S(1)}, u32[]{:S(2)}, u32[]{:S(2)}) %collective-permute-start.1) | collective-permute-done | bytes 221216 | tf_op jit(solution)/shard_map/ppermute | solution.py:40
  189.6 9.8 %collective-permute-done.2 = f32[48,1152]{1,0:T(8,128)S(1)} collective-permute-done((f32[48,1152]{1,0:T(8,128)S(1)}, f32[48,1152]{1,0:T(8,128)S(1)}, u32[]{:S(2)}, u32[]{:S(2)}) %collective-permute-start.2) | collective-permute-done | bytes 221216 | tf_op jit(solution)/shard_map/ppermute | solution.py:40
  206.6 8.3 %fusion.50 = (f32[1,16,5,32,512]{4,3,2,1,0:T(8,128)S(1)}, f32[1,16,5,32,512]{4,3,2,1,0:T(8,128)}) fusion(f32[2,16,5,32,512]{4,3,2,1,0:T(8,128)} %get-tuple-element.45), kind=kLoop, calls=%fused_computation.139 | loop fusion | bytes 20971520 | tf_op jit(solution)/shard_map/slice | solution.py:669
  214.9 6.6 %slice_bitcast_fusion.1 = (bf16[2,2,2,2,5,32,512]{6,5,4,3,2,1,0:T(8,128)(2,1)S(1)}, bf16[2,2,2,2,5,32,512]{6,5,4,3,2,1,0:T(8,128)(2,1)}) fusion(bf16[2,2,2,2,2,5,32,512]{7,6,5,4,3,2,1,0:T(8,128)(2,1)} %collective-permute-done.5), kind=kLoop, calls=%fused_computation.6 | loop fusion | bytes 10485760 | tf_op jit(solution)/shard_map/squeeze | solution.py:669
  228.4 7.4 %add_rows.10 = (f32[5,39,8192]{2,1,0:T(8,128)}, f32[8,128]{1,0:T(8,128)S(1)}) custom-call(s32[1]{0:T(128)} %bitcast.35.base_ref, s32[8,5,1,512]{3,2,1,0:T(1,128)S(1)} %copy.187.refs_0_, s32[8,5,1,512]{3,2,1,0:T(1,128)S(1)} %copy.188.refs_1_, bf16[8,5,40,512]{3,2,1,0:T(8,128)(2,1)S(1)} %broadcast_multiply_fusion.3.refs_2_, ...), custom_call_target="tpu_custom_call" | custom-call | flops 5234491 | bytes 1916 | tf_op jit(solution)/shard_map/add_rows/pallas_call | solution.py:174
  236.3 4.4 %collective-permute-done.8 = bf16[2,2,5,32,512]{4,3,2,1,0:T(8,128)(2,1)} collective-permute-done((bf16[2,2,5,32,512]{4,3,2,1,0:T(8,128)(2,1)}, bf16[2,2,5,32,512]{4,3,2,1,0:T(8,128)(2,1)}, u32[]{:S(2)}, u32[]{:S(2)}) %collective-permute-start.8) | collective-permute-done | bytes 655392 | tf_op jit(solution)/shard_map/ppermute | solution.py:40
  255.2 5.5 %collective-permute-done.3 = f32[48,1152]{1,0:T(8,128)S(1)} collective-permute-done((f32[48,1152]{1,0:T(8,128)S(1)}, f32[48,1152]{1,0:T(8,128)S(1)}, u32[]{:S(2)}, u32[]{:S(2)}) %collective-permute-start.3) | collective-permute-done | bytes 221216 | tf_op jit(solution)/shard_map/ppermute | solution.py:40
  262.0 7.6 %add_rows.11 = (f32[5,39,8192]{2,1,0:T(8,128)}, f32[8,128]{1,0:T(8,128)}) custom-call(s32[1]{0:T(128)} %bitcast.35.base_ref, s32[8,5,1,512]{3,2,1,0:T(1,128)S(1)} %copy.187.refs_0_, s32[8,5,1,512]{3,2,1,0:T(1,128)S(1)} %copy.188.refs_1_, bf16[8,5,40,512]{3,2,1,0:T(8,128)(2,1)S(1)} %broadcast_multiply_fusion.3.refs_2_, ...), custom_call_target="tpu_custom_call", output_to_operand_aliasing={{0}: (5, {})} | custom-call | flops 5234491 | bytes 1916 | tf_op jit(solution)/shard_map/add_rows/pallas_call | solution.py:174
  269.6 7.4 %add_rows.12 = (f32[5,39,8192]{2,1,0:T(8,128)}, f32[8,128]{1,0:T(8,128)}) custom-call(s32[1]{0:T(128)} %bitcast.35.base_ref, s32[8,5,1,512]{3,2,1,0:T(1,128)S(1)} %copy.187.refs_0_, s32[8,5,1,512]{3,2,1,0:T(1,128)S(1)} %copy.188.refs_1_, bf16[8,5,40,512]{3,2,1,0:T(8,128)(2,1)S(1)} %broadcast_multiply_fusion.3.refs_2_, ...), custom_call_target="tpu_custom_call", output_to_operand_aliasing={{0}: (5, {})} | custom-call | flops 5234491 | bytes 1916 | tf_op jit(solution)/shard_map/add_rows/pallas_call | solution.py:174
  277.0 7.4 %add_rows.13 = (f32[5,39,8192]{2,1,0:T(8,128)}, f32[8,128]{1,0:T(8,128)S(1)}) custom-call(s32[1]{0:T(128)} %bitcast.35.base_ref, s32[8,5,1,512]{3,2,1,0:T(1,128)S(1)} %copy.187.refs_0_, s32[8,5,1,512]{3,2,1,0:T(1,128)S(1)} %copy.188.refs_1_, bf16[8,5,40,512]{3,2,1,0:T(8,128)(2,1)S(1)} %broadcast_multiply_fusion.3.refs_2_, ...), custom_call_target="tpu_custom_call", output_to_operand_aliasing={{0}: (5, {})} | custom-call | flops 5234491 | bytes 1916 | tf_op jit(solution)/shard_map/add_rows/pallas_call | solution.py:174
  290.8 4.9 %collective-permute-done.15 = s32[8,5,512]{2,1,0:T(8,128)S(1)} collective-permute-done((s32[8,5,512]{2,1,0:T(8,128)S(1)}, s32[8,5,512]{2,1,0:T(8,128)S(1)}, u32[]{:S(2)}, u32[]{:S(2)}) %collective-permute-start.15) | collective-permute-done | bytes 81952 | tf_op jit(solution)/shard_map/ppermute | solution.py:40
  297.1 10.8 %collective-permute-done.4 = f32[48,1152]{1,0:T(8,128)S(1)} collective-permute-done((f32[48,1152]{1,0:T(8,128)S(1)}, f32[48,1152]{1,0:T(8,128)S(1)}, u32[]{:S(2)}, u32[]{:S(2)}) %collective-permute-start.4) | collective-permute-done | bytes 221216 | tf_op jit(solution)/shard_map/ppermute | solution.py:40
  311.1 7.6 %add_rows.14 = (f32[5,39,8192]{2,1,0:T(8,128)}, f32[8,128]{1,0:T(8,128)}) custom-call(s32[1]{0:T(128)} %bitcast.35.base_ref, s32[8,5,1,512]{3,2,1,0:T(1,128)S(1)} %copy.187.refs_0_, s32[8,5,1,512]{3,2,1,0:T(1,128)S(1)} %copy.188.refs_1_, bf16[8,5,40,512]{3,2,1,0:T(8,128)(2,1)S(1)} %broadcast_multiply_fusion.3.refs_2_, ...), custom_call_target="tpu_custom_call", output_to_operand_aliasing={{0}: (5, {})} | custom-call | flops 5234491 | bytes 1916 | tf_op jit(solution)/shard_map/add_rows/pallas_call | solution.py:174
  318.8 9.9 %collective-permute-done.20 = bf16[2,5,32,512]{3,2,1,0:T(8,128)(2,1)S(1)} collective-permute-done((bf16[2,5,32,512]{3,2,1,0:T(8,128)(2,1)S(1)}, bf16[2,5,32,512]{3,2,1,0:T(8,128)(2,1)S(1)}, u32[]{:S(2)}, u32[]{:S(2)}) %collective-permute-start.20) | collective-permute-done | bytes 327712 | tf_op jit(solution)/shard_map/ppermute | solution.py:40
  328.8 8.8 %add_rows.15 = (f32[5,39,8192]{2,1,0:T(8,128)}, f32[8,128]{1,0:T(8,128)S(1)}) custom-call(s32[1]{0:T(128)} %bitcast.35.base_ref, s32[8,5,1,512]{3,2,1,0:T(1,128)S(1)} %copy.199.refs_0_, s32[8,5,1,512]{3,2,1,0:T(1,128)S(1)} %copy.200.refs_1_, bf16[8,5,40,512]{3,2,1,0:T(8,128)(2,1)S(1)} %broadcast_multiply_fusion.1.refs_2_, ...), custom_call_target="tpu_custom_call", output_to_operand_aliasing={{0}: (5, {})} | custom-call | flops 5234491 | bytes 1916 | tf_op jit(solution)/shard_map/add_rows/pallas_call | solution.py:174
  339.4 8.8 %add_rows.16 = (f32[5,39,8192]{2,1,0:T(8,128)}, f32[8,128]{1,0:T(8,128)S(1)}) custom-call(s32[1]{0:T(128)} %bitcast.35.base_ref, s32[8,5,1,512]{3,2,1,0:T(1,128)S(1)} %copy.199.refs_0_, s32[8,5,1,512]{3,2,1,0:T(1,128)S(1)} %copy.200.refs_1_, bf16[8,5,40,512]{3,2,1,0:T(8,128)(2,1)S(1)} %broadcast_multiply_fusion.1.refs_2_, ...), custom_call_target="tpu_custom_call", output_to_operand_aliasing={{0}: (5, {})} | custom-call | flops 5234491 | bytes 1916 | tf_op jit(solution)/shard_map/add_rows/pallas_call | solution.py:174
  349.4 6.0 %collective-permute-done.24 = bf16[4,5,32,512]{3,2,1,0:T(8,128)(2,1)S(1)} collective-permute-done((bf16[4,5,32,512]{3,2,1,0:T(8,128)(2,1)S(1)}, bf16[4,5,32,512]{3,2,1,0:T(8,128)(2,1)S(1)}, u32[]{:S(2)}, u32[]{:S(2)}) %collective-permute-start.24) | collective-permute-done | bytes 655392 | tf_op jit(solution)/shard_map/ppermute | solution.py:40
  358.0 9.0 %add_rows.17 = (f32[5,39,8192]{2,1,0:T(8,128)}, f32[8,128]{1,0:T(8,128)}) custom-call(s32[1]{0:T(128)} %bitcast.35.base_ref, s32[8,5,1,512]{3,2,1,0:T(1,128)S(1)} %copy.199.refs_0_, s32[8,5,1,512]{3,2,1,0:T(1,128)S(1)} %copy.200.refs_1_, bf16[8,5,40,512]{3,2,1,0:T(8,128)(2,1)S(1)} %broadcast_multiply_fusion.1.refs_2_, ...), custom_call_target="tpu_custom_call", output_to_operand_aliasing={{0}: (5, {})} | custom-call | flops 5234491 | bytes 1916 | tf_op jit(solution)/shard_map/add_rows/pallas_call | solution.py:174
  367.0 8.8 %add_rows.18 = (f32[5,39,8192]{2,1,0:T(8,128)}, f32[8,128]{1,0:T(8,128)}) custom-call(s32[1]{0:T(128)} %bitcast.35.base_ref, s32[8,5,1,512]{3,2,1,0:T(1,128)S(1)} %copy.199.refs_0_, s32[8,5,1,512]{3,2,1,0:T(1,128)S(1)} %copy.200.refs_1_, bf16[8,5,40,512]{3,2,1,0:T(8,128)(2,1)S(1)} %broadcast_multiply_fusion.1.refs_2_, ...), custom_call_target="tpu_custom_call", output_to_operand_aliasing={{0}: (5, {})} | custom-call | flops 5234491 | bytes 1916 | tf_op jit(solution)/shard_map/add_rows/pallas_call | solution.py:174
  375.8 8.8 %add_rows.19 = (f32[5,39,8192]{2,1,0:T(8,128)}, f32[8,128]{1,0:T(8,128)S(1)}) custom-call(s32[1]{0:T(128)} %bitcast.35.base_ref, s32[8,5,1,512]{3,2,1,0:T(1,128)S(1)} %copy.199.refs_0_, s32[8,5,1,512]{3,2,1,0:T(1,128)S(1)} %copy.200.refs_1_, bf16[8,5,40,512]{3,2,1,0:T(8,128)(2,1)S(1)} %broadcast_multiply_fusion.1.refs_2_, ...), custom_call_target="tpu_custom_call", output_to_operand_aliasing={{0}: (5, {})} | custom-call | flops 5234491 | bytes 1916 | tf_op jit(solution)/shard_map/add_rows/pallas_call | solution.py:174
  393.7 13.3 %assemble.1 = (f32[3,1027,1027]{2,1,0:T(8,128)}, f32[1,1027,1024]{2,1,0:T(8,128)}, f32[1,1024,1024]{2,1,0:T(8,128)}) custom-call(s32[1]{0:T(128)} %bitcast.own_ref, bf16[8,5,32,512]{3,2,1,0:T(8,128)(2,1)} %copy-done.1, bf16[8,5,32,512]{3,2,1,0:T(8,128)(2,1)} %copy-done.11, bf16[8,5,32,512]{3,2,1,0:T(8,128)(2,1)} %copy-done.15, ...), custom_call_target="tpu_custom_call" | custom-call | bytes 39813 | tf_op jit(solution)/shard_map/assemble/pallas_call | solution.py:519
  (208 shorter events, 88.0 us)
Async XLA Ops:
  5.2 14.6 %all-to-all-start = ((s32[8,5,512]{2,1,0:T(8,128)}), s32[8,5,512]{2,1,0:T(8,128)S(1)}, u32[]{:S(2)}, u32[]{:S(2)}) async-start(s32[8,5,512]{2,1,0:T(8,128)} %reshape.617), calls=%async_computation | async-start | bytes 262144 | tf_op jit(solution)/shard_map/all_to_all | solution.py:574
  38.4 30.1 %all-to-all-start.1 = ((bf16[8,2,40,512]{3,2,1,0:T(8,128)(2,1)}), bf16[8,2,40,512]{3,2,1,0:T(8,128)(2,1)S(1)}, u32[]{:S(2)}, u32[]{:S(2)}) async-start(bf16[8,2,40,512]{3,2,1,0:T(8,128)(2,1)} %lookup.2), calls=%async_computation.1 | async-start | bytes 1310720 | tf_op jit(solution)/shard_map/all_to_all | solution.py:586
  68.5 28.4 %all-to-all-start.2 = ((bf16[8,3,40,512]{3,2,1,0:T(8,128)(2,1)}), bf16[8,3,40,512]{3,2,1,0:T(8,128)(2,1)S(1)}, u32[]{:S(2)}, u32[]{:S(2)}) async-start(bf16[8,3,40,512]{3,2,1,0:T(8,128)(2,1)} %lookup.3), calls=%async_computation.2 | async-start | bytes 1966080 | tf_op jit(solution)/shard_map/all_to_all | solution.py:586
  140.8 9.0 %collective-permute-start.5 = (bf16[2,2,2,2,2,5,32,512]{7,6,5,4,3,2,1,0:T(8,128)(2,1)}, bf16[2,2,2,2,2,5,32,512]{7,6,5,4,3,2,1,0:T(8,128)(2,1)}, u32[]{:S(2)}, u32[]{:S(2)}) collective-permute-start(bf16[2,2,2,2,2,5,32,512]{7,6,5,4,3,2,1,0:T(8,128)(2,1)} %bitcast.21), channel_id=1, source_target_pairs={{0,1},{1,0},{2,3},{3,2},{4,5},{5,4},{6,7},{7,6},{8,9},{9,8},{10,11... | collective-permute-start | bytes 15728648 | tf_op jit(solution)/shard_map/ppermute | solution.py:40
  140.8 64.3 %all-to-all-start.3 = ((bf16[8,5,40,512]{3,2,1,0:T(8,128)(2,1)}), bf16[8,5,40,512]{3,2,1,0:T(8,128)(2,1)S(1)}, u32[]{:S(2)}, u32[]{:S(2)}) async-start(bf16[8,5,40,512]{3,2,1,0:T(8,128)(2,1)} %bitcast.273), calls=%async_computation.3 | async-start | bytes 3276800 | tf_op jit(solution)/shard_map/all_to_all | solution.py:605
  152.6 48.0 %collective-permute-start.6 = (bf16[2,2,2,5,32,512]{5,4,3,2,1,0:T(8,128)(2,1)S(1)}, bf16[2,2,2,5,32,512]{5,4,3,2,1,0:T(8,128)(2,1)S(1)}, u32[]{:S(2)}, u32[]{:S(2)}) collective-permute-start(bf16[2,2,2,5,32,512]{5,4,3,2,1,0:T(8,128)(2,1)S(1)} %get-tuple-element.86), channel_id=1, source_target_pairs={{0,2},{1,3},{2,0},{3,1},{4,6},{5,7},{6,4},{7,5},{8,10},{9,11},{10,... | collective-permute-start | bytes 3932168 | tf_op jit(solution)/shard_map/ppermute | solution.py:40
  154.2 48.7 %collective-permute-start.7 = (bf16[2,2,2,5,32,512]{5,4,3,2,1,0:T(8,128)(2,1)S(1)}, bf16[2,2,2,5,32,512]{5,4,3,2,1,0:T(8,128)(2,1)S(1)}, u32[]{:S(2)}, u32[]{:S(2)}) collective-permute-start(bf16[2,2,2,5,32,512]{5,4,3,2,1,0:T(8,128)(2,1)S(1)} %get-tuple-element.87), channel_id=1, source_target_pairs={{0,4},{4,0},{8,12},{12,8},{16,20},{20,16},{24,28},{28,24},{1,5},{5... | collective-permute-start | bytes 3932168 | tf_op jit(solution)/shard_map/ppermute | solution.py:40
  155.4 1.5 collective-permute-start
  157.0 31.3 %collective-permute-start.1 = (f32[48,1152]{1,0:T(8,128)S(1)}, f32[48,1152]{1,0:T(8,128)S(1)}, u32[]{:S(2)}, u32[]{:S(2)}) collective-permute-start(f32[48,1152]{1,0:T(8,128)S(1)} %fusion.49), channel_id=1, source_target_pairs={{0,2},{1,3},{2,0},{3,1},{4,6},{5,7},{6,4},{7,5},{8,10},{9,11},{10,... | collective-permute-start | bytes 663560 | tf_op jit(solution)/shard_map/ppermute | solution.py:40
  188.3 11.1 %collective-permute-start.2 = (f32[48,1152]{1,0:T(8,128)S(1)}, f32[48,1152]{1,0:T(8,128)S(1)}, u32[]{:S(2)}, u32[]{:S(2)}) collective-permute-start(f32[48,1152]{1,0:T(8,128)S(1)} %add.518), channel_id=1, source_target_pairs={{0,4},{4,0},{8,12},{12,8},{16,20},{20,16},{24,28},{28,24},{1,5},{5... | collective-permute-start | bytes 663560 | tf_op jit(solution)/shard_map/ppermute | solution.py:40
  206.5 21.8 %collective-permute-start.10 = (bf16[8,5,40,512]{3,2,1,0:T(8,128)(2,1)S(1)}, bf16[8,5,40,512]{3,2,1,0:T(8,128)(2,1)S(1)}, u32[]{:S(2)}, u32[]{:S(2)}) collective-permute-start(bf16[8,5,40,512]{3,2,1,0:T(8,128)(2,1)S(1)} %broadcast_multiply_fusion.3.refs_2_), channel_id=1, source_target_pairs={{0,1},{1,0},{2,3},{3,2},{4,5},{5,4},{6,7},{7,6},{8,9},{9,8},{10,11... | collective-permute-start | bytes 4915208 | tf_op jit(solution)/shard_map/ppermute | solution.py:40
  223.2 17.4 %collective-permute-start.8 = (bf16[2,2,5,32,512]{4,3,2,1,0:T(8,128)(2,1)}, bf16[2,2,5,32,512]{4,3,2,1,0:T(8,128)(2,1)}, u32[]{:S(2)}, u32[]{:S(2)}) collective-permute-start(bf16[2,2,5,32,512]{4,3,2,1,0:T(8,128)(2,1)} %fusion.9), channel_id=1, source_target_pairs={{0,4},{4,0},{8,12},{12,8},{16,20},{20,16},{24,28},{28,24},{1,5},{5... | collective-permute-start | bytes 1966088 | tf_op jit(solution)/shard_map/ppermute | solution.py:40
  226.8 20.1 %collective-permute-start.11 = (bf16[2,2,5,32,512]{4,3,2,1,0:T(8,128)(2,1)S(1)}, bf16[2,2,5,32,512]{4,3,2,1,0:T(8,128)(2,1)S(1)}, u32[]{:S(2)}, u32[]{:S(2)}) collective-permute-start(bf16[2,2,5,32,512]{4,3,2,1,0:T(8,128)(2,1)S(1)} %fusion.5), channel_id=1, source_target_pairs={{0,2},{1,3},{2,0},{3,1},{4,6},{5,7},{6,4},{7,5},{8,10},{9,11},{10,... | collective-permute-start | bytes 1966088 | tf_op jit(solution)/shard_map/ppermute | solution.py:40
  244.7 42.2 %collective-permute-start.17 = (bf16[8,5,40,512]{3,2,1,0:T(8,128)(2,1)S(1)}, bf16[8,5,40,512]{3,2,1,0:T(8,128)(2,1)S(1)}, u32[]{:S(2)}, u32[]{:S(2)}) collective-permute-start(bf16[8,5,40,512]{3,2,1,0:T(8,128)(2,1)S(1)} %broadcast_multiply_fusion.2), channel_id=1, source_target_pairs={{0,2},{1,3},{2,0},{3,1},{4,6},{5,7},{6,4},{7,5},{8,10},{9,11},{10,... | collective-permute-start | bytes 4915208 | tf_op jit(solution)/shard_map/ppermute | solution.py:40
  246.3 14.5 %collective-permute-start.3 = (f32[48,1152]{1,0:T(8,128)S(1)}, f32[48,1152]{1,0:T(8,128)S(1)}, u32[]{:S(2)}, u32[]{:S(2)}) collective-permute-start(f32[48,1152]{1,0:T(8,128)S(1)} %copy-done.21), channel_id=1, source_target_pairs={{0,8},{4,12},{8,0},{12,4},{16,24},{20,28},{24,16},{28,20},{1,9},{5... | collective-permute-start | bytes 663560 | tf_op jit(solution)/shard_map/ppermute | solution.py:40
  249.4 35.5 %collective-permute-start.12 = (bf16[2,5,32,512]{3,2,1,0:T(8,128)(2,1)S(1)}, bf16[2,5,32,512]{3,2,1,0:T(8,128)(2,1)S(1)}, u32[]{:S(2)}, u32[]{:S(2)}) collective-permute-start(bf16[2,5,32,512]{3,2,1,0:T(8,128)(2,1)S(1)} %pad_maximum_fusion.5.refs_6_), channel_id=1, source_target_pairs={{0,8},{4,12},{8,0},{12,4},{16,24},{20,28},{24,16},{28,20},{1,9},{5... | collective-permute-start | bytes 983048 | tf_op jit(solution)/shard_map/ppermute | solution.py:40
  251.0 33.9 %collective-permute-start.13 = (bf16[2,5,32,512]{3,2,1,0:T(8,128)(2,1)S(1)}, bf16[2,5,32,512]{3,2,1,0:T(8,128)(2,1)S(1)}, u32[]{:S(2)}, u32[]{:S(2)}) collective-permute-start(bf16[2,5,32,512]{3,2,1,0:T(8,128)(2,1)S(1)} %pad_maximum_fusion.6.refs_7_), channel_id=1, source_target_pairs={{0,16},{4,20},{8,24},{12,28},{16,0},{20,4},{24,8},{28,12},{1,17},{... | collective-permute-start | bytes 983048 | tf_op jit(solution)/shard_map/ppermute | solution.py:40
  253.7 31.2 %collective-permute-start.14 = (bf16[2,5,32,512]{3,2,1,0:T(8,128)(2,1)S(1)}, bf16[2,5,32,512]{3,2,1,0:T(8,128)(2,1)S(1)}, u32[]{:S(2)}, u32[]{:S(2)}) collective-permute-start(bf16[2,5,32,512]{3,2,1,0:T(8,128)(2,1)S(1)} %pad_maximum_fusion.7.refs_8_), channel_id=1, source_target_pairs={{0,24},{4,28},{8,16},{12,20},{16,8},{20,12},{24,0},{28,4},{1,25},{... | collective-permute-start | bytes 983048 | tf_op jit(solution)/shard_map/ppermute | solution.py:40
  287.1 41.7 %collective-permute-start.18 = (bf16[8,5,40,512]{3,2,1,0:T(8,128)(2,1)S(1)}, bf16[8,5,40,512]{3,2,1,0:T(8,128)(2,1)S(1)}, u32[]{:S(2)}, u32[]{:S(2)}) collective-permute-start(bf16[8,5,40,512]{3,2,1,0:T(8,128)(2,1)S(1)} %broadcast_multiply_fusion.1.refs_2_), channel_id=1, source_target_pairs={{0,1},{1,0},{2,3},{3,2},{4,5},{5,4},{6,7},{7,6},{8,9},{9,8},{10,11... | collective-permute-start | bytes 4915208 | tf_op jit(solution)/shard_map/ppermute | solution.py:40
  287.1 20.8 %collective-permute-start.4 = (f32[48,1152]{1,0:T(8,128)S(1)}, f32[48,1152]{1,0:T(8,128)S(1)}, u32[]{:S(2)}, u32[]{:S(2)}) collective-permute-start(f32[48,1152]{1,0:T(8,128)S(1)} %add.520), channel_id=1, source_target_pairs={{0,16},{4,20},{8,24},{12,28},{16,0},{20,4},{24,8},{28,12},{1,17},{... | collective-permute-start | bytes 663560 | tf_op jit(solution)/shard_map/ppermute | solution.py:40
  287.9 30.9 %collective-permute-start.21 = (bf16[2,5,32,512]{3,2,1,0:T(8,128)(2,1)S(1)}, bf16[2,5,32,512]{3,2,1,0:T(8,128)(2,1)S(1)}, u32[]{:S(2)}, u32[]{:S(2)}) collective-permute-start(bf16[2,5,32,512]{3,2,1,0:T(8,128)(2,1)S(1)} %add_convert_fusion.refs_5_), channel_id=1, source_target_pairs={{0,24},{4,28},{8,16},{12,20},{16,8},{20,12},{24,0},{28,4},{1,25},{... | collective-permute-start | bytes 983048 | tf_op jit(solution)/shard_map/ppermute | solution.py:40
  290.2 5.5 %collective-permute-start.15 = (s32[8,5,512]{2,1,0:T(8,128)S(1)}, s32[8,5,512]{2,1,0:T(8,128)S(1)}, u32[]{:S(2)}, u32[]{:S(2)}) collective-permute-start(s32[8,5,512]{2,1,0:T(8,128)S(1)} %all-to-all-done), channel_id=1, source_target_pairs={{0,2},{1,3},{2,0},{3,1},{4,6},{5,7},{6,4},{7,5},{8,10},{9,11},{10,... | collective-permute-start | bytes 245768 | tf_op jit(solution)/shard_map/ppermute | solution.py:40
  308.0 20.7 %collective-permute-start.20 = (bf16[2,5,32,512]{3,2,1,0:T(8,128)(2,1)S(1)}, bf16[2,5,32,512]{3,2,1,0:T(8,128)(2,1)S(1)}, u32[]{:S(2)}, u32[]{:S(2)}) collective-permute-start(bf16[2,5,32,512]{3,2,1,0:T(8,128)(2,1)S(1)} %add_convert_fusion.refs_5_), channel_id=1, source_target_pairs={{0,16},{4,20},{8,24},{12,28},{16,0},{20,4},{24,8},{28,12},{1,17},{... | collective-permute-start | bytes 983048 | tf_op jit(solution)/shard_map/ppermute | solution.py:40
  309.2 19.5 %collective-permute-start.19 = (bf16[2,5,32,512]{3,2,1,0:T(8,128)(2,1)S(1)}, bf16[2,5,32,512]{3,2,1,0:T(8,128)(2,1)S(1)}, u32[]{:S(2)}, u32[]{:S(2)}) collective-permute-start(bf16[2,5,32,512]{3,2,1,0:T(8,128)(2,1)S(1)} %add_convert_fusion.refs_5_), channel_id=1, source_target_pairs={{0,8},{4,12},{8,0},{12,4},{16,24},{20,28},{24,16},{28,20},{1,9},{5... | collective-permute-start | bytes 983048 | tf_op jit(solution)/shard_map/ppermute | solution.py:40
  338.9 16.5 %collective-permute-start.24 = (bf16[4,5,32,512]{3,2,1,0:T(8,128)(2,1)S(1)}, bf16[4,5,32,512]{3,2,1,0:T(8,128)(2,1)S(1)}, u32[]{:S(2)}, u32[]{:S(2)}) collective-permute-start(bf16[4,5,32,512]{3,2,1,0:T(8,128)(2,1)S(1)} %pad_maximum_fusion.4.refs_6_), channel_id=1, source_target_pairs={{0,2},{1,3},{2,0},{3,1},{4,6},{5,7},{6,4},{7,5},{8,10},{9,11},{10,... | collective-permute-start | bytes 1966088 | tf_op jit(solution)/shard_map/ppermute | solution.py:40
  339.0 16.8 %collective-permute-start.22 = (bf16[4,5,32,512]{3,2,1,0:T(8,128)(2,1)S(1)}, bf16[4,5,32,512]{3,2,1,0:T(8,128)(2,1)S(1)}, u32[]{:S(2)}, u32[]{:S(2)}) collective-permute-start(bf16[4,5,32,512]{3,2,1,0:T(8,128)(2,1)S(1)} %pad_maximum_fusion.3.refs_5_), channel_id=1, source_target_pairs={{0,4},{4,0},{8,12},{12,8},{16,20},{20,16},{24,28},{28,24},{1,5},{5... | collective-permute-start | bytes 1966088 | tf_op jit(solution)/shard_map/ppermute | solution.py:40
  355.5 30.2 %collective-permute-start.27 = (bf16[8,5,32,512]{3,2,1,0:T(8,128)(2,1)S(1)}, bf16[8,5,32,512]{3,2,1,0:T(8,128)(2,1)S(1)}, u32[]{:S(2)}, u32[]{:S(2)}) collective-permute-start(bf16[8,5,32,512]{3,2,1,0:T(8,128)(2,1)S(1)} %pad_maximum_fusion.1.refs_6_.refs_4_), channel_id=1, source_target_pairs={{0,4},{4,0},{8,12},{12,8},{16,20},{20,16},{24,28},{28,24},{1,5},{5... | collective-permute-start | bytes 3932168 | tf_op jit(solution)/shard_map/ppermute | solution.py:40
  356.0 30.0 %collective-permute-start.23 = (bf16[8,5,32,512]{3,2,1,0:T(8,128)(2,1)S(1)}, bf16[8,5,32,512]{3,2,1,0:T(8,128)(2,1)S(1)}, u32[]{:S(2)}, u32[]{:S(2)}) collective-permute-start(bf16[8,5,32,512]{3,2,1,0:T(8,128)(2,1)S(1)} %pad_maximum_fusion.refs_5_.refs_0_), channel_id=1, source_target_pairs={{0,2},{1,3},{2,0},{3,1},{4,6},{5,7},{6,4},{7,5},{8,10},{9,11},{10,... | collective-permute-start | bytes 3932168 | tf_op jit(solution)/shard_map/ppermute | solution.py:40
  357.5 33.1 %collective-permute-start.28 = (bf16[8,5,32,512]{3,2,1,0:T(8,128)(2,1)S(1)}, bf16[8,5,32,512]{3,2,1,0:T(8,128)(2,1)S(1)}, u32[]{:S(2)}, u32[]{:S(2)}) collective-permute-start(bf16[8,5,32,512]{3,2,1,0:T(8,128)(2,1)S(1)} %pad_maximum_fusion.1.refs_6_.refs_4_), channel_id=1, source_target_pairs={{0,1},{1,0},{2,3},{3,2},{4,5},{5,4},{6,7},{7,6},{8,9},{9,8},{10,11... | collective-permute-start | bytes 3932168 | tf_op jit(solution)/shard_map/ppermute | solution.py:40
  357.5 33.1 %collective-permute-start.25 = (bf16[8,5,32,512]{3,2,1,0:T(8,128)(2,1)S(1)}, bf16[8,5,32,512]{3,2,1,0:T(8,128)(2,1)S(1)}, u32[]{:S(2)}, u32[]{:S(2)}) collective-permute-start(bf16[8,5,32,512]{3,2,1,0:T(8,128)(2,1)S(1)} %pad_maximum_fusion.refs_5_.refs_0_), channel_id=1, source_target_pairs={{0,1},{1,0},{2,3},{3,2},{4,5},{5,4},{6,7},{7,6},{8,9},{9,8},{10,11... | collective-permute-start | bytes 3932168 | tf_op jit(solution)/shard_map/ppermute | solution.py:40
  385.9 4.7 %collective-permute-start.29 = (bf16[8,5,32,512]{3,2,1,0:T(8,128)(2,1)S(1)}, bf16[8,5,32,512]{3,2,1,0:T(8,128)(2,1)S(1)}, u32[]{:S(2)}, u32[]{:S(2)}) collective-permute-start(bf16[8,5,32,512]{3,2,1,0:T(8,128)(2,1)S(1)} %broadcast_multiply_fusion.4.refs_5_), channel_id=1, source_target_pairs={{0,1},{1,0},{2,3},{3,2},{4,5},{5,4},{6,7},{7,6},{8,9},{9,8},{10,11... | collective-permute-start | bytes 3932168 | tf_op jit(solution)/shard_map/ppermute | solution.py:40
  386.1 4.8 %collective-permute-start.26 = (bf16[8,5,32,512]{3,2,1,0:T(8,128)(2,1)S(1)}, bf16[8,5,32,512]{3,2,1,0:T(8,128)(2,1)S(1)}, u32[]{:S(2)}, u32[]{:S(2)}) collective-permute-start(bf16[8,5,32,512]{3,2,1,0:T(8,128)(2,1)S(1)} %broadcast_multiply_fusion.5.refs_1_), channel_id=1, source_target_pairs={{0,1},{1,0},{2,3},{3,2},{4,5},{5,4},{6,7},{7,6},{8,9},{9,8},{10,11... | collective-permute-start | bytes 3932168 | tf_op jit(solution)/shard_map/ppermute | solution.py:40
  (32 other events, 287.7 us)

commit v6 on v5

--- a/solution.py
+++ b/solution.py
@@ -38,6 +38,15 @@
 
 def swap(value, axis, mask):
     return lax.ppermute(value, axis, [(at, at ^ mask) for at in range(lax.axis_size(axis))])
+
+
+def swap_both(value, rep_mask, tab_mask):
+    rep_count = lax.axis_size("rep")
+    perm = []
+    for tab in range(lax.axis_size("tab")):
+        for at in range(rep_count):
+            perm.append((tab * rep_count + at, (tab ^ tab_mask) * rep_count + (at ^ rep_mask)))
+    return lax.ppermute(value, ("tab", "rep"), perm)
 
 
 def masks_of(axis):
@@ -192,7 +201,7 @@
             2 * embed_dim * (2 * share + part_count * tab_count * count),
         ),
         name="add_rows",
-    )(base, *[part[:, :, None, :] for part in wanted], *grads, *whole, *after)
+    )(base, *wanted, *grads, *whole, *after)
     return table_grad, token[0, 0]
 
 
@@ -207,13 +216,15 @@
     dense_width,
     width,
     starts,
+    after_count,
     place_ref,
     bias_ref,
     *refs,
 ):
     group_count = len(starts)
     arrived_refs = refs[:group_count]
-    dense_refs = refs[group_count:]
+    first = group_count + 4
+    dense_refs = refs[group_count:first] + refs[first + after_count :]
     dense_body(dense_width, width, starts, place_ref, bias_ref, arrived_refs, *dense_refs)
 
 
@@ -353,7 +364,7 @@
         slots_ref[place_ref[field], :embed_dim] = grad_anchor[first : first + embed_dim].astype(BF)
 
 
-def dense_step(arrived, starts, place, dense_in, labels, weights, cols, out_b, layer_count, width):
+def dense_step(arrived, starts, place, dense_in, labels, weights, cols, out_b, layer_count, width, after):
     tab_count, _, pad_dim, count = arrived[0].shape
     slot_count = tab_count * sum(part.shape[1] for part in arrived)
     dense_width = dense_in.shape[1]
@@ -364,8 +375,9 @@
     smem = pl.BlockSpec(memory_space=pltpu.SMEM)
     flat = pltpu.VMEM((size, count), F32)
     return pl.pallas_call(
-        functools.partial(dense_kernel, dense_width, width, starts),
-        in_specs=[smem, smem] + [vmem] * (len(arrived) + 2) + [ pl.BlockSpec(memory_space=pl.ANY), vmem],
+        functools.partial(dense_kernel, dense_width, width, starts, len(after)),
+        in_specs=[smem, smem] + [vmem] * (len(arrived) + 2) + [ pl.BlockSpec(memory_space=pl.ANY), vmem]
+        + [pl.BlockSpec(memory_space=pl.ANY)] * len(after),
         out_specs=[vmem] * 6,
         out_shape=[
             jax.ShapeDtypeStruct((1, count), F32),
@@ -397,6 +409,7 @@
         labels.astype(F32).reshape(1, count),
         weights,
         cols,
+        *after,
     )
 
 
@@ -599,8 +612,24 @@
         [jnp.pad((v * ready).astype(F32), (0, size - v.shape[0])) for v in vectors], axis=1
     )
 
+
+    def near_parts(own):
+        return [own, swap(own, "rep", 1)]
+
+    def far_bases(own):
+        bases = [own]
+        for mask in masks_of("rep")[1:]:
+            bases = bases + [swap(part, "rep", mask) for part in bases]
+        return bases[1:]
+
+    def far_parts(bases):
+        return [part for far in bases for part in near_parts(far)]
+
+    near_ids = [part[:, :, None, :] for part in near_parts(wanted)]
+    far_ids = [part[:, :, None, :] for part in far_parts(far_bases(wanted))]
     logits, dense_grad, slots, left, right, sums = dense_step(
-        arrived, starts, table_place, dense_in, labels, weights, cols, out_b, layer_count, width
+        arrived, starts, table_place, dense_in, labels, weights, cols, out_b, layer_count, width,
+        near_ids + far_ids,
     )
     returned = lax.all_to_all(
         slots.reshape(tab_count, slot_count, slots.shape[1], row_count),
@@ -613,18 +642,6 @@
     share = table_len // rep_count
     base = (rep_at * share).astype(I32).reshape(1)
 
-    def near_parts(own):
-        return [own, swap(own, "rep", 1)]
-
-    def far_bases(own):
-        bases = [own]
-        for mask in masks_of("rep")[1:]:
-            bases = bases + [swap(part, "rep", mask) for part in bases]
-        return bases[1:]
-
-    def far_parts(bases):
-        return [part for far in bases for part in near_parts(far)]
-
     def gate(value, result):
         return value * (1.0 + 0.0 * result.astype(F32)).astype(value.dtype)
 
@@ -632,8 +649,6 @@
     own = sum(bit << (4 - at) for at, bit in enumerate(bits)).astype(I32).reshape(1)
     keep, send, strips = weight_parts(left, right, own)
     matrix_count = layer_count + 2
-    near_ids = near_parts(wanted)
-    far_ids = far_parts(far_bases(wanted))
     far_grads = None
     table_grad = None
     token = jnp.zeros((), F32)
@@ -658,36 +673,36 @@
             )
 
     small = jnp.concatenate([strips.reshape(matrix_count * 8, size), sums], axis=0)
-    small_jobs = [(axis, mask) for axis in ("rep", "tab") for mask in masks_of(axis)]
-    early = [job for job in small_jobs if job[1] < 4 and job != ("tab", 2)]
-    late = [job for job in small_jobs if job not in early]
-
     def zero_of(value):
         return 0.0 * value.astype(F32)
 
     got = swap(send, "rep", 1)
-    sources = [[keep[at], got[at]] for at in range(2)]
+    small = small + swap(small, "rep", 1)
+    sends = [added((keep[at, 1], got[at, 1])).astype(BF) for at in range(2)]
+    sent = [swap(sends[at], *HALVES[at][0]) for at in range(2)]
+    keep, got, sends = lax.optimization_barrier((keep, got, sends))
+    kept = [added((keep[at, 0], got[at, 0])) for at in range(2)]
+    for part in kept:
+        small = small + zero_of(part[0, 0, 0, 0, 0, 0])
+    small = added([small, swap(small, "rep", 2), swap(small, "tab", 1), swap_both(small, 2, 1)])
+    sources = [[kept[at], sent[at]] for at in range(2)]
+    ready = zero_of(small[0, 0])
+    for part in kept + sent:
+        ready = ready + zero_of(part[0, 0, 0, 0, 0, 0])
 
     def take(at, *index):
-        whole = keep.ndim - 1
+        whole = keep.ndim - 2
         return [part[index[whole - part.ndim :]] for part in sources[at]]
 
-    sent = [swap(added(take(at, 1)).astype(BF), *HALVES[at][0]) for at in range(2)]
-    for axis, mask in early:
-        small = small + swap(small, axis, mask)
-    ready = zero_of(small[0, 0])
+    sent = [swap(added(take(at, 1), ready).astype(BF), *HALVES[at][1]) for at in range(2)]
+    returned = gate(returned, ready)
+    near_grads = near_parts(returned)
+    add_next(1, [sources[0][1]])
     for at in range(2):
         sources[at].append(sent[at])
-        ready = ready + zero_of(sent[at][0, 0, 0, 0, 0, 0])
-    sent = [swap(added(take(at, 0, 1), ready).astype(BF), *HALVES[at][1]) for at in range(2)]
-    returned = gate(returned, ready)
-    near_grads = near_parts(returned)
-    add_next(1, [sources[0][2]])
-    for at in range(2):
-        sources[at].append(sent[at])
 
     def take_far(high, low):
-        both = [added(take(at, 0, 0, high, low), token) for at in range(2)]
+        both = [added(take(at, 0, high, low), token) for at in range(2)]
         return jnp.stack(both)
 
     kept = take_far(0, 0)
@@ -695,8 +710,10 @@
     far = [swap(value, "tab", 4 * high + 2 * low) for value, (high, low) in zip(sends, FAR)]
     bases = far_bases(gate(returned, sends[0][0, 0, 0, 0]))
     add_next(slot_count - 2, [kept] + sends)
-    for axis, mask in late[:1]:
-        small = small + swap(small, axis, mask)
+    small = added([small] + [swap(small, "tab", mask) for mask in (2, 4, 6)])
+    for axis, known in (("rep", 2), ("tab", 3)):
+        for mask in masks_of(axis)[known:]:
+            small = small + swap(small, axis, mask)
     piece = added([kept, *far], token, zero_of(small[0, 0])).astype(BF)
     for axis, known in (("rep", 2), ("tab", 3)):
         for mask in masks_of(axis)[known:]:
@@ -704,10 +721,7 @@
     parts = [piece, swap(piece, "tab", 2), swap(piece, "tab", 4), swap(piece, "tab", 6)]
     far_grads = far_parts([gate(part, piece[0, 0, 0, 0]) for part in bases])
     add_next(2, [piece])
-    for axis, mask in late[1:]:
-        small = small + swap(small, axis, mask)
-    done = token + zero_of(small[0, 0])
-    values = [joined([part[at : at + 1] for part in parts], done) for at in range(2)]
+    values = [joined([part[at : at + 1] for part in parts], token) for at in range(2)]
     sent = [swap(values[at], *HALVES[at][1]) for at in range(2)]
     add_next(1, values)
     values = [joined((values[at], sent[at]), token) for at in range(2)]

time: 414 us -> 411 us (level)
  local copies, waits for them, and re-layouts: 49.6 us -> 35.8 us
  starting transfers between devices: 44.9 us -> 56.7 us
  other arithmetic: 27.5 us -> 34 us
  waiting for transfers between devices: 98.4 us -> 93.4 us
    ppermute x30 -> x31, waiting for transfers between devices: 87.8 us -> 55 us  [swap(): lax.ppermute(value, axis, [(at, at ^ mask) for at in range(lax.axis_size(...]
    ppermute x0 -> x1, waiting for transfers between devices: none -> 25.7 us  [swap_both(): return lax.ppermute(value, ('tab', 'rep'), perm)]
    slice x5 -> x4, local copies, waits for them, and re-layouts: 12.9 us -> 3.15 us  [the longest x2 1.7 us: on_device(): ready = ready + zero_of(part[0, 0, 0, 0, 0, 0])]
    ppermute x30 -> x31, starting transfers between devices: 23.6 us -> 32.5 us  [swap(): lax.ppermute(value, axis, [(at, at ^ mask) for at in range(lax.axis_size(...]
    squeeze x1 -> x0, local copies, waits for them, and re-layouts: 6.6 us -> none  [on_device(): sources = [[keep[at], got[at]] for at in range(2)]]
    convert_element_type x3, other arithmetic: 6.24 us -> 10.6 us  [the longest x1 6.01 us: on_device(): sends = [added((keep[at, 1], got[at, 1])).astype(BF) for at in range(2)]]
    unnamed x65 -> x77, local copies, waits for them, and re-layouts: 17.7 us -> 17.7 us
  transfers between devices with their start and end apart: 34 -> 36, of which waited for: 15 -> 15; matrix products, arithmetic and copies ran while one was open for 15% -> 13% of each run, Pallas kernels for 24% -> 23%
where the time goes in v6:
time: 411 us; the launch traced here: 407 us
  Pallas kernels  175 us (43%)
  waiting for transfers between devices  93.4 us (23%)
  starting transfers between devices  56.7 us (14%)
  local copies, waits for them, and re-layouts  35.8 us (9%)
  other arithmetic  34 us (8%)
  between operations  12.4 us (3%)
    pallas_call x10, Pallas kernels, add_rows(): pl.pallas_call(functools.partial(add_kernel, part_count, accumulate), gri...  81.5 us
    ppermute x31, waiting for transfers between devices, swap(): lax.ppermute(value, axis, [(at, at ^ mask) for at in range(lax.axis_size(...  55 us
    pallas_call x2, Pallas kernels, lookup(): pl.pallas_call(functools.partial(lookup_kernel, first_slot), in_specs=[sm...  39.9 us
    ppermute x31, starting transfers between devices, swap(): lax.ppermute(value, axis, [(at, at ^ mask) for at in range(lax.axis_size(...  32.5 us
    pallas_call x1, Pallas kernels, dense_step(): pl.pallas_call(functools.partial(dense_kernel, dense_width, width, starts...  27.6 us
    ppermute x1, waiting for transfers between devices, swap_both(): return lax.ppermute(value, ('tab', 'rep'), perm)  25.7 us
    unnamed x77, local copies, waits for them, and re-layouts  17.7 us
    pallas_call x1, Pallas kernels, assemble(): pl.pallas_call(functools.partial(assemble_kernel, layer_count), grid=(mat...  13.3 us
  transfers between devices with their start and end apart: 36, of which 15 were waited for; matrix products, arithmetic and copies ran while one was open for 13% of the time, Pallas kernels for 23%

profile of v6, /device:TPU:0, one launch (start us, length us, event | category | flops | bytes accessed | tf_op | source)
XLA Modules:
  0.0 407.3 jit_solution(2164867298831199015)
XLA Ops:
  5.2 7.3 %all-to-all-start = ((s32[8,5,512]{2,1,0:T(8,128)}), s32[8,5,512]{2,1,0:T(8,128)S(1)}, u32[]{:S(2)}, u32[]{:S(2)}) async-start(s32[8,5,512]{2,1,0:T(8,128)} %reshape.498), calls=%async_computation | async-start | bytes 262144 | tf_op jit(solution)/shard_map/all_to_all | solution.py:587
  13.8 6.0 %all-to-all-done = s32[8,5,512]{2,1,0:T(8,128)S(1)} async-done(((s32[8,5,512]{2,1,0:T(8,128)}), s32[8,5,512]{2,1,0:T(8,128)S(1)}, u32[]{:S(2)}, u32[]{:S(2)}) %all-to-all-start) | async-done | bytes 81952 | tf_op jit(solution)/shard_map/all_to_all | solution.py:587
  20.5 20.3 %lookup.2 = bf16[8,2,40,512]{3,2,1,0:T(8,128)(2,1)} custom-call(s32[20480]{0:T(1024)} %bitcast.209, s32[5]{0:T(128)} %dynamic_slice.3.rows_ref, bf16[5,39,32768]{2,1,0:T(8,128)(2,1)} %table_hbm.3), custom_call_target="tpu_custom_call" | custom-call | flops 20132660 | bytes 5750 | tf_op jit(solution)/shard_map/lookup/pallas_call | solution.py:110
  40.8 3.6 all-to-all-start.1
  50.7 19.6 %lookup.3 = bf16[8,3,40,512]{3,2,1,0:T(8,128)(2,1)} custom-call(s32[20480]{0:T(1024)} %bitcast.210, s32[5]{0:T(128)} %dynamic_slice.3.rows_ref, bf16[5,39,32768]{2,1,0:T(8,128)(2,1)} %table_hbm.3), custom_call_target="tpu_custom_call" | custom-call | flops 30198988 | bytes 8626 | tf_op jit(solution)/shard_map/lookup/pallas_call | solution.py:110
  72.6 8.5 %all-to-all-start.2 = ((bf16[8,3,40,512]{3,2,1,0:T(8,128)(2,1)}), bf16[8,3,40,512]{3,2,1,0:T(8,128)(2,1)S(1)}, u32[]{:S(2)}, u32[]{:S(2)}) async-start(bf16[8,3,40,512]{3,2,1,0:T(8,128)(2,1)} %lookup.3), calls=%async_computation.2 | async-start | bytes 1966080 | tf_op jit(solution)/shard_map/all_to_all | solution.py:599
  99.3 6.8 %all-to-all-done.2.refs_1_ = bf16[8,3,40,512]{3,2,1,0:T(8,128)(2,1)S(1)} async-done(((bf16[8,3,40,512]{3,2,1,0:T(8,128)(2,1)}), bf16[8,3,40,512]{3,2,1,0:T(8,128)(2,1)S(1)}, u32[]{:S(2)}, u32[]{:S(2)}) %all-to-all-start.2) | async-done | bytes 983072 | tf_op jit(solution)/shard_map/all_to_all | solution.py:599
  107.0 27.6 %dense.1 = (f32[1,512]{1,0:T(1,128)}, f32[16,512]{1,0:T(8,128)}, bf16[40,40,512]{2,1,0:T(8,128)(2,1)}, bf16[5,1152,512]{2,1,0:T(8,128)(2,1)}, bf16[5,1152,512]{2,1,0:T(8,128)(2,1)}, /*index=5*/f32[8,1152]{1,0:T(8,128)}) custom-call(s32[26]{0:T(128)} %place_ref.1, f32[1]{0:T(128)S(6)} %convert.60.bias_ref, bf16[8,2,40,512]{3,2,1,0:T(8,128)(2,1)} %copy-done.21, ...), custom_call_target="tpu_custom_call" | custom-call | flops 13589544 | bytes 30965 | tf_op jit(solution)/shard_map/dense/pallas_call | solution.py:377
  137.3 12.7 %weight_parts.1 = (f32[2,16,5,32,512]{4,3,2,1,0:T(8,128)}, bf16[2,16,5,32,512]{4,3,2,1,0:T(8,128)(2,1)}, f32[5,8,1152]{2,1,0:T(8,128)S(1)}) custom-call(s32[1]{0:T(128)} %bitcast.own_ref, bf16[5,1152,512]{2,1,0:T(8,128)(2,1)S(1)} %copy-done.2, bf16[5,1152,512]{2,1,0:T(8,128)(2,1)} %get-tuple-element.42.right_ref), custom_call_target="tpu_custom_call" | custom-call | flops 6794772 | bytes 66355 | tf_op jit(solution)/shard_map/weight_parts/pallas_call | solution.py:451
  150.1 4.1 %all-to-all-start.3 = ((bf16[8,5,40,512]{3,2,1,0:T(8,128)(2,1)}), bf16[8,5,40,512]{3,2,1,0:T(8,128)(2,1)S(1)}, u32[]{:S(2)}, u32[]{:S(2)}) async-start(bf16[8,5,40,512]{3,2,1,0:T(8,128)(2,1)} %bitcast.206), calls=%async_computation.3 | async-start | bytes 3276800 | tf_op jit(solution)/shard_map/all_to_all | solution.py:634
  154.7 4.4 %collective-permute-done.4 = bf16[2,2,2,2,2,5,32,512]{7,6,5,4,3,2,1,0:T(8,128)(2,1)} collective-permute-done((bf16[2,2,2,2,2,5,32,512]{7,6,5,4,3,2,1,0:T(8,128)(2,1)}, bf16[2,2,2,2,2,5,32,512]{7,6,5,4,3,2,1,0:T(8,128)(2,1)}, u32[]{:S(2)}, u32[]{:S(2)}) %collective-permute-start.4) | collective-permute-done | bytes 5242912 | tf_op jit(solution)/shard_map/ppermute | solution.py:40
  159.1 6.0 %fusion.3 = (bf16[2,2,2,5,32,512]{5,4,3,2,1,0:T(8,128)(2,1)}, bf16[2,2,2,5,32,512]{5,4,3,2,1,0:T(8,128)(2,1)}) fusion(f32[2,2,2,2,2,5,32,512]{7,6,5,4,3,2,1,0:T(8,128)} %bitcast.200, bf16[2,2,2,2,2,5,32,512]{7,6,5,4,3,2,1,0:T(8,128)(2,1)} %collective-permute-done.4), kind=kLoop, calls=%fused_computation.17 | loop fusion | flops 3932160 | bytes 10485760 | tf_op jit(solution)/shard_map/convert_element_type | solution.py:681
  177.5 25.7 %collective-permute-done.7 = f32[48,1152]{1,0:T(8,128)S(1)} collective-permute-done((f32[48,1152]{1,0:T(8,128)S(1)}, f32[48,1152]{1,0:T(8,128)S(1)}, u32[]{:S(2)}, u32[]{:S(2)}) %collective-permute-start.7) | collective-permute-done | bytes 221216 | tf_op jit(solution)/shard_map/ppermute | solution.py:49
  203.2 10.1 %collective-permute-done.6 = f32[48,1152]{1,0:T(8,128)S(1)} collective-permute-done((f32[48,1152]{1,0:T(8,128)S(1)}, f32[48,1152]{1,0:T(8,128)S(1)}, u32[]{:S(2)}, u32[]{:S(2)}) %collective-permute-start.6) | collective-permute-done | bytes 221216 | tf_op jit(solution)/shard_map/ppermute | solution.py:40
  227.5 7.4 %add_rows.10 = (f32[5,39,8192]{2,1,0:T(8,128)}, f32[8,128]{1,0:T(8,128)S(1)}) custom-call(s32[1]{0:T(128)} %bitcast.39.base_ref, s32[8,5,1,512]{3,2,1,0:T(1,128)S(1)} %copy-done.8, s32[8,5,1,512]{3,2,1,0:T(1,128)S(1)} %copy-done.9, bf16[8,5,40,512]{3,2,1,0:T(8,128)(2,1)S(1)} %broadcast_multiply_fusion.3.refs_2_, ...), custom_call_target="tpu_custom_call" | custom-call | flops 5234491 | bytes 1916 | tf_op jit(solution)/shard_map/add_rows/pallas_call | solution.py:183
  235.4 3.9 collective-permute-done.13
  244.6 6.8 %collective-permute-start.10 = (f32[48,1152]{1,0:T(8,128)S(1)}, f32[48,1152]{1,0:T(8,128)S(1)}, u32[]{:S(2)}, u32[]{:S(2)}) collective-permute-start(f32[48,1152]{1,0:T(8,128)S(1)} %copy-done.27), channel_id=1, source_target_pairs={{0,24},{4,28},{8,16},{12,20},{16,8},{20,12},{24,0},{28,4},{1,25},{... | collective-permute-start | bytes 663560 | tf_op jit(solution)/shard_map/ppermute | solution.py:40
  259.0 6.6 %collective-permute-done.9 = f32[48,1152]{1,0:T(8,128)S(1)} collective-permute-done((f32[48,1152]{1,0:T(8,128)S(1)}, f32[48,1152]{1,0:T(8,128)S(1)}, u32[]{:S(2)}, u32[]{:S(2)}) %collective-permute-start.9) | collective-permute-done | bytes 221216 | tf_op jit(solution)/shard_map/ppermute | solution.py:40
  265.6 3.7 collective-permute-start.18
  272.7 7.4 %add_rows.11 = (f32[5,39,8192]{2,1,0:T(8,128)}, f32[8,128]{1,0:T(8,128)}) custom-call(s32[1]{0:T(128)} %bitcast.39.base_ref, s32[8,5,1,512]{3,2,1,0:T(1,128)S(1)} %copy-done.8, s32[8,5,1,512]{3,2,1,0:T(1,128)S(1)} %copy-done.9, bf16[8,5,40,512]{3,2,1,0:T(8,128)(2,1)S(1)} %broadcast_multiply_fusion.3.refs_2_, ...), custom_call_target="tpu_custom_call", output_to_operand_aliasing={{0}: (5, {})} | custom-call | flops 5234491 | bytes 1916 | tf_op jit(solution)/shard_map/add_rows/pallas_call | solution.py:183
  280.2 7.6 %add_rows.12 = (f32[5,39,8192]{2,1,0:T(8,128)}, f32[8,128]{1,0:T(8,128)}) custom-call(s32[1]{0:T(128)} %bitcast.39.base_ref, s32[8,5,1,512]{3,2,1,0:T(1,128)S(1)} %copy-done.8, s32[8,5,1,512]{3,2,1,0:T(1,128)S(1)} %copy-done.9, bf16[8,5,40,512]{3,2,1,0:T(8,128)(2,1)S(1)} %broadcast_multiply_fusion.3.refs_2_, ...), custom_call_target="tpu_custom_call", output_to_operand_aliasing={{0}: (5, {})} | custom-call | flops 5234491 | bytes 1916 | tf_op jit(solution)/shard_map/add_rows/pallas_call | solution.py:183
  287.7 7.4 %add_rows.13 = (f32[5,39,8192]{2,1,0:T(8,128)}, f32[8,128]{1,0:T(8,128)S(1)}) custom-call(s32[1]{0:T(128)} %bitcast.39.base_ref, s32[8,5,1,512]{3,2,1,0:T(1,128)S(1)} %copy-done.8, s32[8,5,1,512]{3,2,1,0:T(1,128)S(1)} %copy-done.9, bf16[8,5,40,512]{3,2,1,0:T(8,128)(2,1)S(1)} %broadcast_multiply_fusion.3.refs_2_, ...), custom_call_target="tpu_custom_call", output_to_operand_aliasing={{0}: (5, {})} | custom-call | flops 5234491 | bytes 1916 | tf_op jit(solution)/shard_map/add_rows/pallas_call | solution.py:183
  298.5 3.9 collective-permute-start.21
  302.4 7.4 %add_rows.14 = (f32[5,39,8192]{2,1,0:T(8,128)}, f32[8,128]{1,0:T(8,128)}) custom-call(s32[1]{0:T(128)} %bitcast.39.base_ref, s32[8,5,1,512]{3,2,1,0:T(1,128)S(1)} %copy-done.8, s32[8,5,1,512]{3,2,1,0:T(1,128)S(1)} %copy-done.9, bf16[8,5,40,512]{3,2,1,0:T(8,128)(2,1)S(1)} %broadcast_multiply_fusion.3.refs_2_, ...), custom_call_target="tpu_custom_call", output_to_operand_aliasing={{0}: (5, {})} | custom-call | flops 5234491 | bytes 1916 | tf_op jit(solution)/shard_map/add_rows/pallas_call | solution.py:183
  310.4 17.1 %collective-permute-done.22 = bf16[2,5,32,512]{3,2,1,0:T(8,128)(2,1)S(1)} collective-permute-done((bf16[2,5,32,512]{3,2,1,0:T(8,128)(2,1)S(1)}, bf16[2,5,32,512]{3,2,1,0:T(8,128)(2,1)S(1)}, u32[]{:S(2)}, u32[]{:S(2)}) %collective-permute-start.22) | collective-permute-done | bytes 327712 | tf_op jit(solution)/shard_map/ppermute | solution.py:40
  327.7 9.0 %add_rows.15 = (f32[5,39,8192]{2,1,0:T(8,128)}, f32[8,128]{1,0:T(8,128)S(1)}) custom-call(s32[1]{0:T(128)} %bitcast.39.base_ref, s32[8,5,1,512]{3,2,1,0:T(1,128)S(1)} %copy-done.6, s32[8,5,1,512]{3,2,1,0:T(1,128)S(1)} %copy-done.7, bf16[8,5,40,512]{3,2,1,0:T(8,128)(2,1)S(1)} %broadcast_multiply_fusion.1.refs_2_, ...), custom_call_target="tpu_custom_call", output_to_operand_aliasing={{0}: (5, {})} | custom-call | flops 5234491 | bytes 1916 | tf_op jit(solution)/shard_map/add_rows/pallas_call | solution.py:183
  338.7 8.8 %add_rows.16 = (f32[5,39,8192]{2,1,0:T(8,128)}, f32[8,128]{1,0:T(8,128)S(1)}) custom-call(s32[1]{0:T(128)} %bitcast.39.base_ref, s32[8,5,1,512]{3,2,1,0:T(1,128)S(1)} %copy-done.6, s32[8,5,1,512]{3,2,1,0:T(1,128)S(1)} %copy-done.7, bf16[8,5,40,512]{3,2,1,0:T(8,128)(2,1)S(1)} %broadcast_multiply_fusion.1.refs_2_, ...), custom_call_target="tpu_custom_call", output_to_operand_aliasing={{0}: (5, {})} | custom-call | flops 5234491 | bytes 1916 | tf_op jit(solution)/shard_map/add_rows/pallas_call | solution.py:183
  348.8 5.6 %collective-permute-done.26 = bf16[4,5,32,512]{3,2,1,0:T(8,128)(2,1)S(1)} collective-permute-done((bf16[4,5,32,512]{3,2,1,0:T(8,128)(2,1)S(1)}, bf16[4,5,32,512]{3,2,1,0:T(8,128)(2,1)S(1)}, u32[]{:S(2)}, u32[]{:S(2)}) %collective-permute-start.26) | collective-permute-done | bytes 655392 | tf_op jit(solution)/shard_map/ppermute | solution.py:40
  356.9 8.8 %add_rows.17 = (f32[5,39,8192]{2,1,0:T(8,128)}, f32[8,128]{1,0:T(8,128)}) custom-call(s32[1]{0:T(128)} %bitcast.39.base_ref, s32[8,5,1,512]{3,2,1,0:T(1,128)S(1)} %copy-done.6, s32[8,5,1,512]{3,2,1,0:T(1,128)S(1)} %copy-done.7, bf16[8,5,40,512]{3,2,1,0:T(8,128)(2,1)S(1)} %broadcast_multiply_fusion.1.refs_2_, ...), custom_call_target="tpu_custom_call", output_to_operand_aliasing={{0}: (5, {})} | custom-call | flops 5234491 | bytes 1916 | tf_op jit(solution)/shard_map/add_rows/pallas_call | solution.py:183
  365.7 9.0 %add_rows.18 = (f32[5,39,8192]{2,1,0:T(8,128)}, f32[8,128]{1,0:T(8,128)}) custom-call(s32[1]{0:T(128)} %bitcast.39.base_ref, s32[8,5,1,512]{3,2,1,0:T(1,128)S(1)} %copy-done.6, s32[8,5,1,512]{3,2,1,0:T(1,128)S(1)} %copy-done.7, bf16[8,5,40,512]{3,2,1,0:T(8,128)(2,1)S(1)} %broadcast_multiply_fusion.1.refs_2_, ...), custom_call_target="tpu_custom_call", output_to_operand_aliasing={{0}: (5, {})} | custom-call | flops 5234491 | bytes 1916 | tf_op jit(solution)/shard_map/add_rows/pallas_call | solution.py:183
  374.7 8.8 %add_rows.19 = (f32[5,39,8192]{2,1,0:T(8,128)}, f32[8,128]{1,0:T(8,128)S(1)}) custom-call(s32[1]{0:T(128)} %bitcast.39.base_ref, s32[8,5,1,512]{3,2,1,0:T(1,128)S(1)} %copy-done.6, s32[8,5,1,512]{3,2,1,0:T(1,128)S(1)} %copy-done.7, bf16[8,5,40,512]{3,2,1,0:T(8,128)(2,1)S(1)} %broadcast_multiply_fusion.1.refs_2_, ...), custom_call_target="tpu_custom_call", output_to_operand_aliasing={{0}: (5, {})} | custom-call | flops 5234491 | bytes 1916 | tf_op jit(solution)/shard_map/add_rows/pallas_call | solution.py:183
  392.6 13.3 %assemble.1 = (f32[3,1027,1027]{2,1,0:T(8,128)}, f32[1,1027,1024]{2,1,0:T(8,128)}, f32[1,1024,1024]{2,1,0:T(8,128)}) custom-call(s32[1]{0:T(128)} %bitcast.own_ref, bf16[8,5,32,512]{3,2,1,0:T(8,128)(2,1)} %copy-done.1, bf16[8,5,32,512]{3,2,1,0:T(8,128)(2,1)} %copy-done.19, bf16[8,5,32,512]{3,2,1,0:T(8,128)(2,1)} %copy-done.23, ...), custom_call_target="tpu_custom_call" | custom-call | bytes 39813 | tf_op jit(solution)/shard_map/assemble/pallas_call | solution.py:532
  (221 shorter events, 90.0 us)
Async XLA Ops:
  5.2 14.6 %all-to-all-start = ((s32[8,5,512]{2,1,0:T(8,128)}), s32[8,5,512]{2,1,0:T(8,128)S(1)}, u32[]{:S(2)}, u32[]{:S(2)}) async-start(s32[8,5,512]{2,1,0:T(8,128)} %reshape.498), calls=%async_computation | async-start | bytes 262144 | tf_op jit(solution)/shard_map/all_to_all | solution.py:587
  40.8 31.8 %all-to-all-start.1 = ((bf16[8,2,40,512]{3,2,1,0:T(8,128)(2,1)}), bf16[8,2,40,512]{3,2,1,0:T(8,128)(2,1)S(1)}, u32[]{:S(2)}, u32[]{:S(2)}) async-start(bf16[8,2,40,512]{3,2,1,0:T(8,128)(2,1)} %lookup.2), calls=%async_computation.1 | async-start | bytes 1310720 | tf_op jit(solution)/shard_map/all_to_all | solution.py:599
  47.2 24.0 %collective-permute-start = (s32[8,5,512]{2,1,0:T(8,128)S(1)}, s32[8,5,512]{2,1,0:T(8,128)S(1)}, u32[]{:S(2)}, u32[]{:S(2)}) collective-permute-start(s32[8,5,512]{2,1,0:T(8,128)S(1)} %all-to-all-done), channel_id=1, source_target_pairs={{0,1},{1,0},{2,3},{3,2},{4,5},{5,4},{6,7},{7,6},{8,9},{9,8},{10,11... | collective-permute-start | bytes 245768 | tf_op jit(solution)/shard_map/ppermute | solution.py:40
  49.4 22.5 %collective-permute-start.2 = (s32[8,5,512]{2,1,0:T(8,128)S(1)}, s32[8,5,512]{2,1,0:T(8,128)S(1)}, u32[]{:S(2)}, u32[]{:S(2)}) collective-permute-start(s32[8,5,512]{2,1,0:T(8,128)S(1)} %collective-permute-done.1), channel_id=1, source_target_pairs={{0,1},{1,0},{2,3},{3,2},{4,5},{5,4},{6,7},{7,6},{8,9},{9,8},{10,11... | collective-permute-start | bytes 245768 | tf_op jit(solution)/shard_map/ppermute | solution.py:40
  72.6 33.5 %all-to-all-start.2 = ((bf16[8,3,40,512]{3,2,1,0:T(8,128)(2,1)}), bf16[8,3,40,512]{3,2,1,0:T(8,128)(2,1)S(1)}, u32[]{:S(2)}, u32[]{:S(2)}) async-start(bf16[8,3,40,512]{3,2,1,0:T(8,128)(2,1)} %lookup.3), calls=%async_computation.2 | async-start | bytes 1966080 | tf_op jit(solution)/shard_map/all_to_all | solution.py:599
  150.0 9.0 %collective-permute-start.4 = (bf16[2,2,2,2,2,5,32,512]{7,6,5,4,3,2,1,0:T(8,128)(2,1)}, bf16[2,2,2,2,2,5,32,512]{7,6,5,4,3,2,1,0:T(8,128)(2,1)}, u32[]{:S(2)}, u32[]{:S(2)}) collective-permute-start(bf16[2,2,2,2,2,5,32,512]{7,6,5,4,3,2,1,0:T(8,128)(2,1)} %bitcast.22), channel_id=1, source_target_pairs={{0,1},{1,0},{2,3},{3,2},{4,5},{5,4},{6,7},{7,6},{8,9},{9,8},{10,11... | collective-permute-start | bytes 15728648 | tf_op jit(solution)/shard_map/ppermute | solution.py:40
  150.1 67.6 %all-to-all-start.3 = ((bf16[8,5,40,512]{3,2,1,0:T(8,128)(2,1)}), bf16[8,5,40,512]{3,2,1,0:T(8,128)(2,1)S(1)}, u32[]{:S(2)}, u32[]{:S(2)}) async-start(bf16[8,5,40,512]{3,2,1,0:T(8,128)(2,1)} %bitcast.206), calls=%async_computation.3 | async-start | bytes 3276800 | tf_op jit(solution)/shard_map/all_to_all | solution.py:634
  154.2 19.6 %collective-permute-start.3 = (f32[48,1152]{1,0:T(8,128)S(1)}, f32[48,1152]{1,0:T(8,128)S(1)}, u32[]{:S(2)}, u32[]{:S(2)}) collective-permute-start(f32[48,1152]{1,0:T(8,128)S(1)} %pad_maximum_fusion.8), channel_id=1, source_target_pairs={{0,1},{1,0},{2,3},{3,2},{4,5},{5,4},{6,7},{7,6},{8,9},{9,8},{10,11... | collective-permute-start | bytes 663560 | tf_op jit(solution)/shard_map/ppermute | solution.py:40
  165.1 49.5 %collective-permute-start.12 = (bf16[2,2,2,5,32,512]{5,4,3,2,1,0:T(8,128)(2,1)}, bf16[2,2,2,5,32,512]{5,4,3,2,1,0:T(8,128)(2,1)}, u32[]{:S(2)}, u32[]{:S(2)}) collective-permute-start(bf16[2,2,2,5,32,512]{5,4,3,2,1,0:T(8,128)(2,1)} %get-tuple-element.75), channel_id=1, source_target_pairs={{0,4},{4,0},{8,12},{12,8},{16,20},{20,16},{24,28},{28,24},{1,5},{5... | collective-permute-start | bytes 3932168 | tf_op jit(solution)/shard_map/ppermute | solution.py:40
  166.5 49.9 %collective-permute-start.11 = (bf16[2,2,2,5,32,512]{5,4,3,2,1,0:T(8,128)(2,1)}, bf16[2,2,2,5,32,512]{5,4,3,2,1,0:T(8,128)(2,1)S(1)}, u32[]{:S(2)}, u32[]{:S(2)}) collective-permute-start(bf16[2,2,2,5,32,512]{5,4,3,2,1,0:T(8,128)(2,1)} %get-tuple-element.76), channel_id=1, source_target_pairs={{0,2},{1,3},{2,0},{3,1},{4,6},{5,7},{6,4},{7,5},{8,10},{9,11},{10,... | collective-permute-start | bytes 3932168 | tf_op jit(solution)/shard_map/ppermute | solution.py:40
  173.9 29.3 %collective-permute-start.7 = (f32[48,1152]{1,0:T(8,128)S(1)}, f32[48,1152]{1,0:T(8,128)S(1)}, u32[]{:S(2)}, u32[]{:S(2)}) collective-permute-start(f32[48,1152]{1,0:T(8,128)S(1)} %add_add_fusion.2), channel_id=1, source_target_pairs={{0,6},{1,7},{2,4},{3,5},{4,2},{5,3},{6,0},{7,1},{8,14},{9,15},{10,... | collective-permute-start | bytes 663560 | tf_op jit(solution)/shard_map/ppermute | solution.py:49
  174.6 38.6 %collective-permute-start.6 = (f32[48,1152]{1,0:T(8,128)S(1)}, f32[48,1152]{1,0:T(8,128)S(1)}, u32[]{:S(2)}, u32[]{:S(2)}) collective-permute-start(f32[48,1152]{1,0:T(8,128)S(1)} %add_add_fusion.2), channel_id=1, source_target_pairs={{0,4},{4,0},{8,12},{12,8},{16,20},{20,16},{24,28},{28,24},{1,5},{5... | collective-permute-start | bytes 663560 | tf_op jit(solution)/shard_map/ppermute | solution.py:40
  176.0 37.3 %collective-permute-start.5 = (f32[48,1152]{1,0:T(8,128)S(1)}, f32[48,1152]{1,0:T(8,128)S(1)}, u32[]{:S(2)}, u32[]{:S(2)}) collective-permute-start(f32[48,1152]{1,0:T(8,128)S(1)} %add_add_fusion.2), channel_id=1, source_target_pairs={{0,2},{1,3},{2,0},{3,1},{4,6},{5,7},{6,4},{7,5},{8,10},{9,11},{10,... | collective-permute-start | bytes 663560 | tf_op jit(solution)/shard_map/ppermute | solution.py:40
  222.5 16.8 %collective-permute-start.13 = (bf16[2,2,5,32,512]{4,3,2,1,0:T(8,128)(2,1)}, bf16[2,2,5,32,512]{4,3,2,1,0:T(8,128)(2,1)}, u32[]{:S(2)}, u32[]{:S(2)}) collective-permute-start(bf16[2,2,5,32,512]{4,3,2,1,0:T(8,128)(2,1)} %fusion.10), channel_id=1, source_target_pairs={{0,4},{4,0},{8,12},{12,8},{16,20},{20,16},{24,28},{28,24},{1,5},{5... | collective-permute-start | bytes 1966088 | tf_op jit(solution)/shard_map/ppermute | solution.py:40
  224.7 27.3 %collective-permute-start.15 = (bf16[2,2,5,32,512]{4,3,2,1,0:T(8,128)(2,1)}, bf16[2,2,5,32,512]{4,3,2,1,0:T(8,128)(2,1)}, u32[]{:S(2)}, u32[]{:S(2)}) collective-permute-start(bf16[2,2,5,32,512]{4,3,2,1,0:T(8,128)(2,1)} %fusion.11), channel_id=1, source_target_pairs={{0,2},{1,3},{2,0},{3,1},{4,6},{5,7},{6,4},{7,5},{8,10},{9,11},{10,... | collective-permute-start | bytes 1966088 | tf_op jit(solution)/shard_map/ppermute | solution.py:40
  243.1 54.6 %collective-permute-start.19 = (bf16[8,5,40,512]{3,2,1,0:T(8,128)(2,1)S(1)}, bf16[8,5,40,512]{3,2,1,0:T(8,128)(2,1)S(1)}, u32[]{:S(2)}, u32[]{:S(2)}) collective-permute-start(bf16[8,5,40,512]{3,2,1,0:T(8,128)(2,1)S(1)} %broadcast_multiply_fusion.2), channel_id=1, source_target_pairs={{0,2},{1,3},{2,0},{3,1},{4,6},{5,7},{6,4},{7,5},{8,10},{9,11},{10,... | collective-permute-start | bytes 4915208 | tf_op jit(solution)/shard_map/ppermute | solution.py:40
  244.6 13.2 %collective-permute-start.10 = (f32[48,1152]{1,0:T(8,128)S(1)}, f32[48,1152]{1,0:T(8,128)S(1)}, u32[]{:S(2)}, u32[]{:S(2)}) collective-permute-start(f32[48,1152]{1,0:T(8,128)S(1)} %copy-done.27), channel_id=1, source_target_pairs={{0,24},{4,28},{8,16},{12,20},{16,8},{20,12},{24,0},{28,4},{1,25},{... | collective-permute-start | bytes 663560 | tf_op jit(solution)/shard_map/ppermute | solution.py:40
  251.4 14.2 %collective-permute-start.9 = (f32[48,1152]{1,0:T(8,128)S(1)}, f32[48,1152]{1,0:T(8,128)S(1)}, u32[]{:S(2)}, u32[]{:S(2)}) collective-permute-start(f32[48,1152]{1,0:T(8,128)S(1)} %copy-done.27), channel_id=1, source_target_pairs={{0,16},{4,20},{8,24},{12,28},{16,0},{20,4},{24,8},{28,12},{1,17},{... | collective-permute-start | bytes 663560 | tf_op jit(solution)/shard_map/ppermute | solution.py:40
  251.4 20.0 %collective-permute-start.8 = (f32[48,1152]{1,0:T(8,128)S(1)}, f32[48,1152]{1,0:T(8,128)S(1)}, u32[]{:S(2)}, u32[]{:S(2)}) collective-permute-start(f32[48,1152]{1,0:T(8,128)S(1)} %copy-done.27), channel_id=1, source_target_pairs={{0,8},{4,12},{8,0},{12,4},{16,24},{20,28},{24,16},{28,20},{1,9},{5... | collective-permute-start | bytes 663560 | tf_op jit(solution)/shard_map/ppermute | solution.py:40
  254.4 41.3 %collective-permute-start.16 = (bf16[2,5,32,512]{3,2,1,0:T(8,128)(2,1)S(1)}, bf16[2,5,32,512]{3,2,1,0:T(8,128)(2,1)S(1)}, u32[]{:S(2)}, u32[]{:S(2)}) collective-permute-start(bf16[2,5,32,512]{3,2,1,0:T(8,128)(2,1)S(1)} %pad_maximum_fusion.5.refs_6_), channel_id=1, source_target_pairs={{0,8},{4,12},{8,0},{12,4},{16,24},{20,28},{24,16},{28,20},{1,9},{5... | collective-permute-start | bytes 983048 | tf_op jit(solution)/shard_map/ppermute | solution.py:40
  257.8 37.8 %collective-permute-start.17 = (bf16[2,5,32,512]{3,2,1,0:T(8,128)(2,1)S(1)}, bf16[2,5,32,512]{3,2,1,0:T(8,128)(2,1)S(1)}, u32[]{:S(2)}, u32[]{:S(2)}) collective-permute-start(bf16[2,5,32,512]{3,2,1,0:T(8,128)(2,1)S(1)} %pad_maximum_fusion.6.refs_7_), channel_id=1, source_target_pairs={{0,16},{4,20},{8,24},{12,28},{16,0},{20,4},{24,8},{28,12},{1,17},{... | collective-permute-start | bytes 983048 | tf_op jit(solution)/shard_map/ppermute | solution.py:40
  265.6 30.1 %collective-permute-start.18 = (bf16[2,5,32,512]{3,2,1,0:T(8,128)(2,1)S(1)}, bf16[2,5,32,512]{3,2,1,0:T(8,128)(2,1)S(1)}, u32[]{:S(2)}, u32[]{:S(2)}) collective-permute-start(bf16[2,5,32,512]{3,2,1,0:T(8,128)(2,1)S(1)} %pad_maximum_fusion.7.refs_8_), channel_id=1, source_target_pairs={{0,24},{4,28},{8,16},{12,20},{16,8},{20,12},{24,0},{28,4},{1,25},{... | collective-permute-start | bytes 983048 | tf_op jit(solution)/shard_map/ppermute | solution.py:40
  297.8 29.8 %collective-permute-start.20 = (bf16[8,5,40,512]{3,2,1,0:T(8,128)(2,1)S(1)}, bf16[8,5,40,512]{3,2,1,0:T(8,128)(2,1)S(1)}, u32[]{:S(2)}, u32[]{:S(2)}) collective-permute-start(bf16[8,5,40,512]{3,2,1,0:T(8,128)(2,1)S(1)} %broadcast_multiply_fusion.1.refs_2_), channel_id=1, source_target_pairs={{0,1},{1,0},{2,3},{3,2},{4,5},{5,4},{6,7},{7,6},{8,9},{9,8},{10,11... | collective-permute-start | bytes 4915208 | tf_op jit(solution)/shard_map/ppermute | solution.py:40
  297.9 12.5 %collective-permute-start.23 = (bf16[2,5,32,512]{3,2,1,0:T(8,128)(2,1)S(1)}, bf16[2,5,32,512]{3,2,1,0:T(8,128)(2,1)S(1)}, u32[]{:S(2)}, u32[]{:S(2)}) collective-permute-start(bf16[2,5,32,512]{3,2,1,0:T(8,128)(2,1)S(1)} %add_convert_fusion.refs_5_), channel_id=1, source_target_pairs={{0,24},{4,28},{8,16},{12,20},{16,8},{20,12},{24,0},{28,4},{1,25},{... | collective-permute-start | bytes 983048 | tf_op jit(solution)/shard_map/ppermute | solution.py:40
  298.0 29.6 %collective-permute-start.22 = (bf16[2,5,32,512]{3,2,1,0:T(8,128)(2,1)S(1)}, bf16[2,5,32,512]{3,2,1,0:T(8,128)(2,1)S(1)}, u32[]{:S(2)}, u32[]{:S(2)}) collective-permute-start(bf16[2,5,32,512]{3,2,1,0:T(8,128)(2,1)S(1)} %add_convert_fusion.refs_5_), channel_id=1, source_target_pairs={{0,16},{4,20},{8,24},{12,28},{16,0},{20,4},{24,8},{28,12},{1,17},{... | collective-permute-start | bytes 983048 | tf_op jit(solution)/shard_map/ppermute | solution.py:40
  298.5 29.1 %collective-permute-start.21 = (bf16[2,5,32,512]{3,2,1,0:T(8,128)(2,1)S(1)}, bf16[2,5,32,512]{3,2,1,0:T(8,128)(2,1)S(1)}, u32[]{:S(2)}, u32[]{:S(2)}) collective-permute-start(bf16[2,5,32,512]{3,2,1,0:T(8,128)(2,1)S(1)} %add_convert_fusion.refs_5_), channel_id=1, source_target_pairs={{0,8},{4,12},{8,0},{12,4},{16,24},{20,28},{24,16},{28,20},{1,9},{5... | collective-permute-start | bytes 983048 | tf_op jit(solution)/shard_map/ppermute | solution.py:40
  338.0 16.4 %collective-permute-start.26 = (bf16[4,5,32,512]{3,2,1,0:T(8,128)(2,1)S(1)}, bf16[4,5,32,512]{3,2,1,0:T(8,128)(2,1)S(1)}, u32[]{:S(2)}, u32[]{:S(2)}) collective-permute-start(bf16[4,5,32,512]{3,2,1,0:T(8,128)(2,1)S(1)} %pad_maximum_fusion.4.refs_6_), channel_id=1, source_target_pairs={{0,2},{1,3},{2,0},{3,1},{4,6},{5,7},{6,4},{7,5},{8,10},{9,11},{10,... | collective-permute-start | bytes 1966088 | tf_op jit(solution)/shard_map/ppermute | solution.py:40
  338.6 16.1 %collective-permute-start.24 = (bf16[4,5,32,512]{3,2,1,0:T(8,128)(2,1)S(1)}, bf16[4,5,32,512]{3,2,1,0:T(8,128)(2,1)S(1)}, u32[]{:S(2)}, u32[]{:S(2)}) collective-permute-start(bf16[4,5,32,512]{3,2,1,0:T(8,128)(2,1)S(1)} %pad_maximum_fusion.3.refs_5_), channel_id=1, source_target_pairs={{0,4},{4,0},{8,12},{12,8},{16,20},{20,16},{24,28},{28,24},{1,5},{5... | collective-permute-start | bytes 1966088 | tf_op jit(solution)/shard_map/ppermute | solution.py:40
  354.5 30.2 %collective-permute-start.29 = (bf16[8,5,32,512]{3,2,1,0:T(8,128)(2,1)S(1)}, bf16[8,5,32,512]{3,2,1,0:T(8,128)(2,1)S(1)}, u32[]{:S(2)}, u32[]{:S(2)}) collective-permute-start(bf16[8,5,32,512]{3,2,1,0:T(8,128)(2,1)S(1)} %pad_maximum_fusion.1.refs_6_.refs_4_), channel_id=1, source_target_pairs={{0,4},{4,0},{8,12},{12,8},{16,20},{20,16},{24,28},{28,24},{1,5},{5... | collective-permute-start | bytes 3932168 | tf_op jit(solution)/shard_map/ppermute | solution.py:40
  354.8 30.0 %collective-permute-start.25 = (bf16[8,5,32,512]{3,2,1,0:T(8,128)(2,1)S(1)}, bf16[8,5,32,512]{3,2,1,0:T(8,128)(2,1)S(1)}, u32[]{:S(2)}, u32[]{:S(2)}) collective-permute-start(bf16[8,5,32,512]{3,2,1,0:T(8,128)(2,1)S(1)} %pad_maximum_fusion.refs_5_.refs_0_), channel_id=1, source_target_pairs={{0,2},{1,3},{2,0},{3,1},{4,6},{5,7},{6,4},{7,5},{8,10},{9,11},{10,... | collective-permute-start | bytes 3932168 | tf_op jit(solution)/shard_map/ppermute | solution.py:40
  356.4 33.1 %collective-permute-start.30 = (bf16[8,5,32,512]{3,2,1,0:T(8,128)(2,1)S(1)}, bf16[8,5,32,512]{3,2,1,0:T(8,128)(2,1)S(1)}, u32[]{:S(2)}, u32[]{:S(2)}) collective-permute-start(bf16[8,5,32,512]{3,2,1,0:T(8,128)(2,1)S(1)} %pad_maximum_fusion.1.refs_6_.refs_4_), channel_id=1, source_target_pairs={{0,1},{1,0},{2,3},{3,2},{4,5},{5,4},{6,7},{7,6},{8,9},{9,8},{10,11... | collective-permute-start | bytes 3932168 | tf_op jit(solution)/shard_map/ppermute | solution.py:40
  356.4 33.1 %collective-permute-start.27 = (bf16[8,5,32,512]{3,2,1,0:T(8,128)(2,1)S(1)}, bf16[8,5,32,512]{3,2,1,0:T(8,128)(2,1)S(1)}, u32[]{:S(2)}, u32[]{:S(2)}) collective-permute-start(bf16[8,5,32,512]{3,2,1,0:T(8,128)(2,1)S(1)} %pad_maximum_fusion.refs_5_.refs_0_), channel_id=1, source_target_pairs={{0,1},{1,0},{2,3},{3,2},{4,5},{5,4},{6,7},{7,6},{8,9},{9,8},{10,11... | collective-permute-start | bytes 3932168 | tf_op jit(solution)/shard_map/ppermute | solution.py:40
  (40 other events, 325.6 us)

commit v7 on v6

--- a/solution.py
+++ b/solution.py
@@ -16,6 +16,7 @@
 LOOK_ROWS = 32
 ADD_LOW = 512
 ADD_TABS = 4
+NEAR_FIRST = 3
 MAIN = 1024
 CHUNK = 384
 PIECE = 32
@@ -419,56 +420,59 @@
     return (piece & 3) | ((piece & 4) << 1) | ((piece & 8) >> 1)
 
 
-def weight_kernel(own_ref, left_ref, right_ref, keep_ref, send_ref, strip_ref, moved):
+def weight_kernel(core, own_ref, left_ref, right_ref, out_ref, *refs):
     pieces = MAIN // PIECE // 2
     half = MAIN // 2
-    right = right_ref[0, :MAIN, :]
-    for at in range(2 * pieces):
-        first = pl.multiple_of((at ^ own_ref[0]) * PIECE, PIECE)
+    moved = refs[-1]
+    for at in range(pieces):
+        first = pl.multiple_of(((core * pieces + at) ^ own_ref[0]) * PIECE, PIECE)
         moved[at * PIECE : (at + 1) * PIECE] = left_ref[0, pl.ds(first, PIECE), :]
-    for core, out_ref in ((1, send_ref), (0, keep_ref)):
-        product = lax.dot_general(
-            moved[core * half : (core + 1) * half], right, NT, preferred_element_type=F32
-        ).astype(out_ref.dtype)
-        for chunk in range(2):
-            for at in range(pieces):
-                out_ref[chunk, chunk_place(at, chunk == 1), 0] = product[
-                    at * PIECE : (at + 1) * PIECE, chunk * half : (chunk + 1) * half
-                ]
-    below = lax.dot_general(left_ref[0, MAIN : MAIN + 16, :], right_ref[0], NT, preferred_element_type=F32)
-    beside = lax.dot_general(right_ref[0, MAIN : MAIN + 16, :], left_ref[0], NT, preferred_element_type=F32)
-    strip_ref[0, 0:3] = below[0:3]
-    strip_ref[0, 3:6] = beside[0:3]
-    strip_ref[0, 6:8] = jnp.zeros((2, strip_ref.shape[2]), F32)
-
-
-def weight_parts(left, right, own):
+    product = lax.dot_general(
+        moved[...], right_ref[0, :MAIN, :], NT, preferred_element_type=F32
+    ).astype(out_ref.dtype)
+    for chunk in range(2):
+        for at in range(pieces):
+            out_ref[chunk, chunk_place(at, chunk == 1), 0] = product[
+                at * PIECE : (at + 1) * PIECE, chunk * half : (chunk + 1) * half
+            ]
+    if core == 0:
+        strip_ref = refs[0]
+        below = lax.dot_general(
+            left_ref[0, MAIN : MAIN + 16, :], right_ref[0], NT, preferred_element_type=F32
+        )
+        beside = lax.dot_general(
+            right_ref[0, MAIN : MAIN + 16, :], left_ref[0], NT, preferred_element_type=F32
+        )
+        strip_ref[0, 0:3] = below[0:3]
+        strip_ref[0, 3:6] = beside[0:3]
+        strip_ref[0, 6:8] = jnp.zeros((2, strip_ref.shape[2]), F32)
+
+
+def weight_parts(left, right, own, core):
     matrix_count, size, count = left.shape
     half = MAIN // 2
     pieces = MAIN // PIECE // 2
-    chunk = pl.BlockSpec((2, pieces, 1, PIECE, half), lambda m: (0, 0, m, 0, 0))
-    shape = (2, pieces, matrix_count, PIECE, half)
-    keep, send, strips = pl.pallas_call(
-        weight_kernel,
+    out_specs = [pl.BlockSpec((2, pieces, 1, PIECE, half), lambda m: (0, 0, m, 0, 0))]
+    shapes = [jax.ShapeDtypeStruct((2, pieces, matrix_count, PIECE, half), BF if core else F32)]
+    if core == 0:
+        out_specs.append(pl.BlockSpec((1, 8, size), lambda m: (m, 0, 0)))
+        shapes.append(jax.ShapeDtypeStruct((matrix_count, 8, size), F32))
+    outs = pl.pallas_call(
+        functools.partial(weight_kernel, core),
         grid=(matrix_count,),
         in_specs=[
             pl.BlockSpec(memory_space=pltpu.SMEM),
             pl.BlockSpec((1, size, count), lambda m: (m, 0, 0)),
             pl.BlockSpec((1, size, count), lambda m: (m, 0, 0)),
         ],
-        out_specs=[chunk, chunk, pl.BlockSpec((1, 8, size), lambda m: (m, 0, 0))],
-        out_shape=[
-            jax.ShapeDtypeStruct(shape, F32),
-            jax.ShapeDtypeStruct(shape, BF),
-            jax.ShapeDtypeStruct((matrix_count, 8, size), F32),
-        ],
-        scratch_shapes=[pltpu.VMEM((MAIN, count), BF)],
+        out_specs=out_specs,
+        out_shape=shapes,
+        scratch_shapes=[pltpu.VMEM((half, count), BF)],
         compiler_params=params(40),
-        cost_estimate=cost(2 * matrix_count * size * size * count, 10 * matrix_count * size * size),
+        cost_estimate=cost(matrix_count * size * size * count, 5 * matrix_count * size * size),
         name="weight_parts",
     )(own, left, right)
-    parts = (2, 2, 2, 2, 2, matrix_count, PIECE, half)
-    return keep.reshape(parts), send.reshape(parts), strips
+    return [outs[0].reshape((2, 2, 2, 2, 2, matrix_count, PIECE, half))] + list(outs[1:])
 
 
 HALVES = [[("rep", 2), ("tab", 1)], [("tab", 1), ("rep", 2)]]
@@ -625,6 +629,7 @@
     def far_parts(bases):
         return [part for far in bases for part in near_parts(far)]
 
+    wanted = wanted + (ready - 1.0).astype(I32)
     near_ids = [part[:, :, None, :] for part in near_parts(wanted)]
     far_ids = [part[:, :, None, :] for part in far_parts(far_bases(wanted))]
     logits, dense_grad, slots, left, right, sums = dense_step(
@@ -647,87 +652,86 @@
 
     bits = [rep_at & 1, (rep_at >> 1) & 1, tab_at & 1, (tab_at >> 2) & 1, (tab_at >> 1) & 1]
     own = sum(bit << (4 - at) for at, bit in enumerate(bits)).astype(I32).reshape(1)
-    keep, send, strips = weight_parts(left, right, own)
+    (send,) = weight_parts(left, right, own, 1)
+    keep, strips = weight_parts(left, right, own, 0)
     matrix_count = layer_count + 2
     far_grads = None
     table_grad = None
     token = jnp.zeros((), F32)
-    jobs = [(near_ids, True, slot) for slot in range(slot_count)]
-    jobs += [(far_ids, False, slot) for slot in range(slot_count)]
-    jobs = jobs[::-1]
-
-    def add_next(times, after):
+    near_jobs = list(range(slot_count))[::-1]
+    far_jobs = list(range(slot_count))[::-1]
+
+    def add_next(near, times, after):
         nonlocal table_grad, token
+        jobs = near_jobs if near else far_jobs
         for _ in range(min(times, len(jobs))):
-            part_ids, near, slot = jobs.pop()
             table_grad, token = add_rows(
                 near_grads if near else far_grads,
-                part_ids,
+                near_ids if near else far_ids,
                 base,
                 share,
                 embed_dim,
-                slot,
+                jobs.pop(),
                 table_grad,
                 not near,
                 after,
             )
 
-    small = jnp.concatenate([strips.reshape(matrix_count * 8, size), sums], axis=0)
     def zero_of(value):
         return 0.0 * value.astype(F32)
 
+    small = jnp.concatenate([strips.reshape(matrix_count * 8, size), sums], axis=0)
     got = swap(send, "rep", 1)
     small = small + swap(small, "rep", 1)
-    sends = [added((keep[at, 1], got[at, 1])).astype(BF) for at in range(2)]
-    sent = [swap(sends[at], *HALVES[at][0]) for at in range(2)]
-    keep, got, sends = lax.optimization_barrier((keep, got, sends))
+    ahead = [added((keep[at, 1, 1], got[at, 1, 1])).astype(BF) for at in range(2)]
+    first = [swap(ahead[at], *HALVES[at][0]) for at in range(2)]
+    keep, got, _ = lax.optimization_barrier((keep, got, ahead))
+    behind = [added((keep[at, 1, 0], got[at, 1, 0])).astype(BF) for at in range(2)]
+    later = [swap(behind[at], *HALVES[at][0]) for at in range(2)]
+    keep, got, _ = lax.optimization_barrier((keep, got, behind))
     kept = [added((keep[at, 0], got[at, 0])) for at in range(2)]
-    for part in kept:
-        small = small + zero_of(part[0, 0, 0, 0, 0, 0])
-    small = added([small, swap(small, "rep", 2), swap(small, "tab", 1), swap_both(small, 2, 1)])
-    sources = [[kept[at], sent[at]] for at in range(2)]
-    ready = zero_of(small[0, 0])
-    for part in kept + sent:
-        ready = ready + zero_of(part[0, 0, 0, 0, 0, 0])
-
-    def take(at, *index):
-        whole = keep.ndim - 2
-        return [part[index[whole - part.ndim :]] for part in sources[at]]
-
-    sent = [swap(added(take(at, 1), ready).astype(BF), *HALVES[at][1]) for at in range(2)]
-    returned = gate(returned, ready)
+    sends = [added((kept[at][1], first[at])).astype(BF) for at in range(2)]
+    sent = [swap(sends[at], *HALVES[at][1]) for at in range(2)]
+    small = small + zero_of(sends[0][0, 0, 0, 0, 0])
+    small = added([small] + [swap(small, "tab", mask) for mask in (2, 4, 6)])
+    returned = gate(returned, sends[0][0, 0, 0, 0, 0] + sends[1][0, 0, 0, 0, 0])
     near_grads = near_parts(returned)
-    add_next(1, [sources[0][1]])
-    for at in range(2):
-        sources[at].append(sent[at])
+    add_next(True, 1, behind + sends)
+    bases = far_bases(gate(returned, token))
+    add_next(True, NEAR_FIRST - 1, sends)
+    sources = [[kept[at][0], later[at], sent[at]] for at in range(2)]
+
+    token = token + zero_of(small[0, 0])
 
     def take_far(high, low):
-        both = [added(take(at, 0, high, low), token) for at in range(2)]
+        both = [added([part[high, low] for part in sources[at]], token) for at in range(2)]
         return jnp.stack(both)
 
     kept = take_far(0, 0)
     sends = [take_far(high, low).astype(BF) for high, low in FAR]
     far = [swap(value, "tab", 4 * high + 2 * low) for value, (high, low) in zip(sends, FAR)]
-    bases = far_bases(gate(returned, sends[0][0, 0, 0, 0]))
-    add_next(slot_count - 2, [kept] + sends)
-    small = added([small] + [swap(small, "tab", mask) for mask in (2, 4, 6)])
-    for axis, known in (("rep", 2), ("tab", 3)):
-        for mask in masks_of(axis)[known:]:
-            small = small + swap(small, axis, mask)
-    piece = added([kept, *far], token, zero_of(small[0, 0])).astype(BF)
+    add_next(True, slot_count - NEAR_FIRST - 1, [kept] + sends)
+    piece = added([kept, *far], token).astype(BF)
     for axis, known in (("rep", 2), ("tab", 3)):
         for mask in masks_of(axis)[known:]:
             piece = (piece.astype(F32) + swap(piece, axis, mask).astype(F32)).astype(BF)
     parts = [piece, swap(piece, "tab", 2), swap(piece, "tab", 4), swap(piece, "tab", 6)]
+    add_next(True, slot_count, [piece])
     far_grads = far_parts([gate(part, piece[0, 0, 0, 0]) for part in bases])
-    add_next(2, [piece])
+    add_next(False, 1, [piece])
     values = [joined([part[at : at + 1] for part in parts], token) for at in range(2)]
     sent = [swap(values[at], *HALVES[at][1]) for at in range(2)]
-    add_next(1, values)
+    small = small + zero_of(values[1][0, 0, 0, 0])
+    small = added([small, swap(small, "rep", 2), swap(small, "tab", 1), swap_both(small, 2, 1)])
+    for axis, known in (("rep", 2), ("tab", 3)):
+        for mask in masks_of(axis)[known:]:
+            small = small + swap(small, axis, mask)
+    add_next(False, 1, values)
+    token = token + zero_of(small[0, 0])
     values = [joined((values[at], sent[at]), token) for at in range(2)]
     sent = [swap(values[at], *HALVES[at][0]) for at in range(2)]
     blocks = [[values[at], None, swap(values[at], "rep", 1), None] for at in range(2)]
-    add_next(slot_count, values)
+    add_next(False, slot_count, values)
     for at in range(2):
         blocks[at][1] = gate(sent[at], token)
         blocks[at][3] = swap(blocks[at][1], "rep", 1)

time: 411 us -> 393 us (0.956)
  the two profiles are of different devices: /device:TPU:0 before, /device:TPU:9 now
where the time goes in v7:
time: 393 us; the launch traced here: 387 us
  Pallas kernels  182 us (46%)
  waiting for transfers between devices  76 us (19%)
  starting transfers between devices  50.2 us (13%)
  local copies, waits for them, and re-layouts  40.4 us (10%)
  other arithmetic  25 us (6%)
  between operations  13.5 us (3%)
    pallas_call x10, Pallas kernels, add_rows(): pl.pallas_call(functools.partial(add_kernel, part_count, accumulate), gri...  81.5 us
    ppermute x33, waiting for transfers between devices, swap(): lax.ppermute(value, axis, [(at, at ^ mask) for at in range(lax.axis_size(...  72.9 us
    pallas_call x2, Pallas kernels, lookup(): pl.pallas_call(functools.partial(lookup_kernel, first_slot), in_specs=[sm...  43.5 us
    ppermute x33, starting transfers between devices, swap(): lax.ppermute(value, axis, [(at, at ^ mask) for at in range(lax.axis_size(...  28.3 us
    pallas_call x1, Pallas kernels, dense_step(): pl.pallas_call(functools.partial(dense_kernel, dense_width, width, starts...  27.6 us
    unnamed x81, local copies, waits for them, and re-layouts  22.2 us
    pallas_call x2, Pallas kernels, weight_parts(): pl.pallas_call(functools.partial(weight_kernel, core), grid=(matrix_count...  15.7 us
    pallas_call x1, Pallas kernels, assemble(): pl.pallas_call(functools.partial(assemble_kernel, layer_count), grid=(mat...  13.3 us
  transfers between devices with their start and end apart: 38, of which 13 were waited for; matrix products, arithmetic and copies ran while one was open for 11% of the time, Pallas kernels for 27%

profile of v7, /device:TPU:9, one launch (start us, length us, event | category | flops | bytes accessed | tf_op | source)
XLA Modules:
  0.0 386.7 jit_solution(8944224279887188179)
XLA Ops:
  5.2 5.7 %all-to-all-start = ((s32[8,5,512]{2,1,0:T(8,128)}), s32[8,5,512]{2,1,0:T(8,128)S(1)}, u32[]{:S(2)}, u32[]{:S(2)}) async-start(s32[8,5,512]{2,1,0:T(8,128)} %reshape.528), calls=%async_computation | async-start | bytes 262144 | tf_op jit(solution)/shard_map/all_to_all | solution.py:591
  12.2 3.0 all-to-all-done
  16.0 19.0 %lookup.2 = bf16[8,2,40,512]{3,2,1,0:T(8,128)(2,1)} custom-call(s32[20480]{0:T(1024)} %bitcast.114, s32[5]{0:T(128)} %dynamic_slice.3.rows_ref, bf16[5,39,32768]{2,1,0:T(8,128)(2,1)} %table_hbm.3), custom_call_target="tpu_custom_call" | custom-call | flops 20132660 | bytes 5750 | tf_op jit(solution)/shard_map/lookup/pallas_call | solution.py:111
  35.0 5.1 %all-to-all-start.1 = ((bf16[8,2,40,512]{3,2,1,0:T(8,128)(2,1)}), bf16[8,2,40,512]{3,2,1,0:T(8,128)(2,1)S(1)}, u32[]{:S(2)}, u32[]{:S(2)}) async-start(bf16[8,2,40,512]{3,2,1,0:T(8,128)(2,1)} %lookup.2), calls=%async_computation.1 | async-start | bytes 1310720 | tf_op jit(solution)/shard_map/all_to_all | solution.py:603
  42.0 24.5 %lookup.3 = bf16[8,3,40,512]{3,2,1,0:T(8,128)(2,1)} custom-call(s32[20480]{0:T(1024)} %bitcast.115, s32[5]{0:T(128)} %dynamic_slice.3.rows_ref, bf16[5,39,32768]{2,1,0:T(8,128)(2,1)} %table_hbm.3), custom_call_target="tpu_custom_call" | custom-call | flops 30198988 | bytes 8626 | tf_op jit(solution)/shard_map/lookup/pallas_call | solution.py:111
  66.6 3.5 all-to-all-start.2
  78.7 3.5 multiply_bitcast_fusion
  96.2 27.6 %dense.1 = (f32[1,512]{1,0:T(1,128)}, f32[16,512]{1,0:T(8,128)}, bf16[40,40,512]{2,1,0:T(8,128)(2,1)}, bf16[5,1152,512]{2,1,0:T(8,128)(2,1)}, bf16[5,1152,512]{2,1,0:T(8,128)(2,1)}, /*index=5*/f32[8,1152]{1,0:T(8,128)}) custom-call(s32[26]{0:T(128)} %place_ref.1, f32[1]{0:T(128)S(6)} %convert.63.bias_ref, bf16[8,2,40,512]{3,2,1,0:T(8,128)(2,1)} %copy-done.24, ...), custom_call_target="tpu_custom_call" | custom-call | flops 13589544 | bytes 30965 | tf_op jit(solution)/shard_map/dense/pallas_call | solution.py:378
  126.5 7.9 %weight_parts.3 = bf16[2,16,5,32,512]{4,3,2,1,0:T(8,128)(2,1)} custom-call(s32[1]{0:T(128)} %bitcast.own_ref, bf16[5,1152,512]{2,1,0:T(8,128)(2,1)S(1)} %copy-done.2, bf16[5,1152,512]{2,1,0:T(8,128)(2,1)} %get-tuple-element.44.right_ref), custom_call_target="tpu_custom_call" | custom-call | flops 3397386 | bytes 33177 | tf_op jit(solution)/shard_map/weight_parts/pallas_call | solution.py:460
  134.5 5.9 %all-to-all-start.3 = ((bf16[8,5,40,512]{3,2,1,0:T(8,128)(2,1)}), bf16[8,5,40,512]{3,2,1,0:T(8,128)(2,1)S(1)}, u32[]{:S(2)}, u32[]{:S(2)}) async-start(bf16[8,5,40,512]{3,2,1,0:T(8,128)(2,1)} %bitcast.32), calls=%async_computation.3 | async-start | bytes 3276800 | tf_op jit(solution)/shard_map/all_to_all | solution.py:639
  145.7 7.8 %weight_parts.2 = (f32[2,16,5,32,512]{4,3,2,1,0:T(8,128)}, f32[5,8,1152]{2,1,0:T(8,128)S(1)}) custom-call(s32[1]{0:T(128)} %bitcast.own_ref, bf16[5,1152,512]{2,1,0:T(8,128)(2,1)S(1)} %copy-done.3, bf16[5,1152,512]{2,1,0:T(8,128)(2,1)S(1)} %copy-done.4), custom_call_target="tpu_custom_call" | custom-call | flops 3397386 | bytes 33177 | tf_op jit(solution)/shard_map/weight_parts/pallas_call | solution.py:460
  157.8 3.7 fusion.7
  161.5 3.0 convert_add_fusion
  164.5 16.3 %collective-permute-done.11 = bf16[2,2,5,32,512]{4,3,2,1,0:T(8,128)(2,1)S(1)} collective-permute-done((bf16[2,2,5,32,512]{4,3,2,1,0:T(8,128)(2,1)S(1)}, bf16[2,2,5,32,512]{4,3,2,1,0:T(8,128)(2,1)S(1)}, u32[]{:S(2)}, u32[]{:S(2)}) %collective-permute-start.11) | collective-permute-done | bytes 655392 | tf_op jit(solution)/shard_map/ppermute | solution.py:41
  194.1 7.4 %add_rows.10 = (f32[5,39,8192]{2,1,0:T(8,128)}, f32[8,128]{1,0:T(8,128)S(1)}) custom-call(s32[1]{0:T(128)} %bitcast.31.base_ref, s32[8,5,1,512]{3,2,1,0:T(1,128)S(1)} %copy-done.11, s32[8,5,1,512]{3,2,1,0:T(1,128)S(1)} %copy-done.12, bf16[8,5,40,512]{3,2,1,0:T(8,128)(2,1)S(1)} %broadcast_multiply_fusion.3.refs_2_, ...), custom_call_target="tpu_custom_call" | custom-call | flops 5234491 | bytes 1916 | tf_op jit(solution)/shard_map/add_rows/pallas_call | solution.py:184
  202.8 3.5 collective-permute-done.8
  206.5 3.7 collective-permute-done.7
  212.4 7.4 %add_rows.11 = (f32[5,39,8192]{2,1,0:T(8,128)}, f32[8,128]{1,0:T(8,128)}) custom-call(s32[1]{0:T(128)} %bitcast.31.base_ref, s32[8,5,1,512]{3,2,1,0:T(1,128)S(1)} %copy-done.11, s32[8,5,1,512]{3,2,1,0:T(1,128)S(1)} %copy-done.12, bf16[8,5,40,512]{3,2,1,0:T(8,128)(2,1)S(1)} %broadcast_multiply_fusion.3.refs_2_, ...), custom_call_target="tpu_custom_call", output_to_operand_aliasing={{0}: (5, {})} | custom-call | flops 5234491 | bytes 1916 | tf_op jit(solution)/shard_map/add_rows/pallas_call | solution.py:184
  219.8 7.6 %add_rows.12 = (f32[5,39,8192]{2,1,0:T(8,128)}, f32[8,128]{1,0:T(8,128)S(1)}) custom-call(s32[1]{0:T(128)} %bitcast.31.base_ref, s32[8,5,1,512]{3,2,1,0:T(1,128)S(1)} %copy-done.11, s32[8,5,1,512]{3,2,1,0:T(1,128)S(1)} %copy-done.12, bf16[8,5,40,512]{3,2,1,0:T(8,128)(2,1)S(1)} %broadcast_multiply_fusion.3.refs_2_, ...), custom_call_target="tpu_custom_call", output_to_operand_aliasing={{0}: (5, {})} | custom-call | flops 5234491 | bytes 1916 | tf_op jit(solution)/shard_map/add_rows/pallas_call | solution.py:184
  232.9 7.4 %add_rows.13 = (f32[5,39,8192]{2,1,0:T(8,128)}, f32[8,128]{1,0:T(8,128)S(1)}) custom-call(s32[1]{0:T(128)} %bitcast.31.base_ref, s32[8,5,1,512]{3,2,1,0:T(1,128)S(1)} %copy-done.11, s32[8,5,1,512]{3,2,1,0:T(1,128)S(1)} %copy-done.12, bf16[8,5,40,512]{3,2,1,0:T(8,128)(2,1)S(1)} %broadcast_multiply_fusion.3.refs_2_, ...), custom_call_target="tpu_custom_call", output_to_operand_aliasing={{0}: (5, {})} | custom-call | flops 5234491 | bytes 1916 | tf_op jit(solution)/shard_map/add_rows/pallas_call | solution.py:184
  243.5 3.0 collective-permute-done.16
  246.5 14.2 %collective-permute-done.17 = bf16[2,5,32,512]{3,2,1,0:T(8,128)(2,1)S(1)} collective-permute-done((bf16[2,5,32,512]{3,2,1,0:T(8,128)(2,1)S(1)}, bf16[2,5,32,512]{3,2,1,0:T(8,128)(2,1)S(1)}, u32[]{:S(2)}, u32[]{:S(2)}) %collective-permute-start.17) | collective-permute-done | bytes 327712 | tf_op jit(solution)/shard_map/ppermute | solution.py:41
  267.4 7.4 %add_rows.14 = (f32[5,39,8192]{2,1,0:T(8,128)}, f32[8,128]{1,0:T(8,128)}) custom-call(s32[1]{0:T(128)} %bitcast.31.base_ref, s32[8,5,1,512]{3,2,1,0:T(1,128)S(1)} %copy-done.11, s32[8,5,1,512]{3,2,1,0:T(1,128)S(1)} %copy-done.12, bf16[8,5,40,512]{3,2,1,0:T(8,128)(2,1)S(1)} %broadcast_multiply_fusion.3.refs_2_, ...), custom_call_target="tpu_custom_call", output_to_operand_aliasing={{0}: (5, {})} | custom-call | flops 5234491 | bytes 1916 | tf_op jit(solution)/shard_map/add_rows/pallas_call | solution.py:184
  274.8 4.2 %collective-permute-done.24 = bf16[2,5,32,512]{3,2,1,0:T(8,128)(2,1)S(1)} collective-permute-done((bf16[2,5,32,512]{3,2,1,0:T(8,128)(2,1)S(1)}, bf16[2,5,32,512]{3,2,1,0:T(8,128)(2,1)S(1)}, u32[]{:S(2)}, u32[]{:S(2)}) %collective-permute-start.24) | collective-permute-done | bytes 327712 | tf_op jit(solution)/shard_map/ppermute | solution.py:41
  282.0 13.0 %collective-permute-done.25 = bf16[2,5,32,512]{3,2,1,0:T(8,128)(2,1)S(1)} collective-permute-done((bf16[2,5,32,512]{3,2,1,0:T(8,128)(2,1)S(1)}, bf16[2,5,32,512]{3,2,1,0:T(8,128)(2,1)S(1)}, u32[]{:S(2)}, u32[]{:S(2)}) %collective-permute-start.25) | collective-permute-done | bytes 327712 | tf_op jit(solution)/shard_map/ppermute | solution.py:41
  295.1 9.0 %add_rows.15 = (f32[5,39,8192]{2,1,0:T(8,128)}, f32[8,128]{1,0:T(8,128)S(1)}) custom-call(s32[1]{0:T(128)} %bitcast.31.base_ref, s32[8,5,1,512]{3,2,1,0:T(1,128)S(1)} %copy-done.9, s32[8,5,1,512]{3,2,1,0:T(1,128)S(1)} %copy-done.10, bf16[8,5,40,512]{3,2,1,0:T(8,128)(2,1)S(1)} %broadcast_multiply_fusion.1.refs_2_, ...), custom_call_target="tpu_custom_call", output_to_operand_aliasing={{0}: (5, {})} | custom-call | flops 5234491 | bytes 1916 | tf_op jit(solution)/shard_map/add_rows/pallas_call | solution.py:184
  311.6 8.8 %add_rows.16 = (f32[5,39,8192]{2,1,0:T(8,128)}, f32[8,128]{1,0:T(8,128)S(1)}) custom-call(s32[1]{0:T(128)} %bitcast.31.base_ref, s32[8,5,1,512]{3,2,1,0:T(1,128)S(1)} %copy-done.9, s32[8,5,1,512]{3,2,1,0:T(1,128)S(1)} %copy-done.10, bf16[8,5,40,512]{3,2,1,0:T(8,128)(2,1)S(1)} %broadcast_multiply_fusion.1.refs_2_, ...), custom_call_target="tpu_custom_call", output_to_operand_aliasing={{0}: (5, {})} | custom-call | flops 5234491 | bytes 1916 | tf_op jit(solution)/shard_map/add_rows/pallas_call | solution.py:184
  322.9 8.8 %collective-permute-done.26 = bf16[4,5,32,512]{3,2,1,0:T(8,128)(2,1)S(1)} collective-permute-done((bf16[4,5,32,512]{3,2,1,0:T(8,128)(2,1)S(1)}, bf16[4,5,32,512]{3,2,1,0:T(8,128)(2,1)S(1)}, u32[]{:S(2)}, u32[]{:S(2)}) %collective-permute-start.26) | collective-permute-done | bytes 655392 | tf_op jit(solution)/shard_map/ppermute | solution.py:41
  336.3 8.8 %add_rows.17 = (f32[5,39,8192]{2,1,0:T(8,128)}, f32[8,128]{1,0:T(8,128)}) custom-call(s32[1]{0:T(128)} %bitcast.31.base_ref, s32[8,5,1,512]{3,2,1,0:T(1,128)S(1)} %copy-done.9, s32[8,5,1,512]{3,2,1,0:T(1,128)S(1)} %copy-done.10, bf16[8,5,40,512]{3,2,1,0:T(8,128)(2,1)S(1)} %broadcast_multiply_fusion.1.refs_2_, ...), custom_call_target="tpu_custom_call", output_to_operand_aliasing={{0}: (5, {})} | custom-call | flops 5234491 | bytes 1916 | tf_op jit(solution)/shard_map/add_rows/pallas_call | solution.py:184
  345.1 9.0 %add_rows.18 = (f32[5,39,8192]{2,1,0:T(8,128)}, f32[8,128]{1,0:T(8,128)}) custom-call(s32[1]{0:T(128)} %bitcast.31.base_ref, s32[8,5,1,512]{3,2,1,0:T(1,128)S(1)} %copy-done.9, s32[8,5,1,512]{3,2,1,0:T(1,128)S(1)} %copy-done.10, bf16[8,5,40,512]{3,2,1,0:T(8,128)(2,1)S(1)} %broadcast_multiply_fusion.1.refs_2_, ...), custom_call_target="tpu_custom_call", output_to_operand_aliasing={{0}: (5, {})} | custom-call | flops 5234491 | bytes 1916 | tf_op jit(solution)/shard_map/add_rows/pallas_call | solution.py:184
  354.1 8.8 %add_rows.19 = (f32[5,39,8192]{2,1,0:T(8,128)}, f32[8,128]{1,0:T(8,128)S(1)}) custom-call(s32[1]{0:T(128)} %bitcast.31.base_ref, s32[8,5,1,512]{3,2,1,0:T(1,128)S(1)} %copy-done.9, s32[8,5,1,512]{3,2,1,0:T(1,128)S(1)} %copy-done.10, bf16[8,5,40,512]{3,2,1,0:T(8,128)(2,1)S(1)} %broadcast_multiply_fusion.1.refs_2_, ...), custom_call_target="tpu_custom_call", output_to_operand_aliasing={{0}: (5, {})} | custom-call | flops 5234491 | bytes 1916 | tf_op jit(solution)/shard_map/add_rows/pallas_call | solution.py:184
  372.0 13.3 %assemble.1 = (f32[3,1027,1027]{2,1,0:T(8,128)}, f32[1,1027,1024]{2,1,0:T(8,128)}, f32[1,1024,1024]{2,1,0:T(8,128)}) custom-call(s32[1]{0:T(128)} %bitcast.own_ref, bf16[8,5,32,512]{3,2,1,0:T(8,128)(2,1)} %copy-done, bf16[8,5,32,512]{3,2,1,0:T(8,128)(2,1)} %copy-done.21, bf16[8,5,32,512]{3,2,1,0:T(8,128)(2,1)} %copy-done.26, ...), custom_call_target="tpu_custom_call" | custom-call | bytes 39813 | tf_op jit(solution)/shard_map/assemble/pallas_call | solution.py:536
  (235 shorter events, 91.3 us)
Async XLA Ops:
  35.0 31.6 %all-to-all-start.1 = ((bf16[8,2,40,512]{3,2,1,0:T(8,128)(2,1)}), bf16[8,2,40,512]{3,2,1,0:T(8,128)(2,1)S(1)}, u32[]{:S(2)}, u32[]{:S(2)}) async-start(bf16[8,2,40,512]{3,2,1,0:T(8,128)(2,1)} %lookup.2), calls=%async_computation.1 | async-start | bytes 1310720 | tf_op jit(solution)/shard_map/all_to_all | solution.py:603
  66.6 28.6 %all-to-all-start.2 = ((bf16[8,3,40,512]{3,2,1,0:T(8,128)(2,1)}), bf16[8,3,40,512]{3,2,1,0:T(8,128)(2,1)S(1)}, u32[]{:S(2)}, u32[]{:S(2)}) async-start(bf16[8,3,40,512]{3,2,1,0:T(8,128)(2,1)} %lookup.3), calls=%async_computation.2 | async-start | bytes 1966080 | tf_op jit(solution)/shard_map/all_to_all | solution.py:603
  71.3 21.8 %collective-permute-start = (s32[8,5,512]{2,1,0:T(8,128)S(1)}, s32[8,5,512]{2,1,0:T(8,128)S(1)}, u32[]{:S(2)}, u32[]{:S(2)}) collective-permute-start(s32[8,5,512]{2,1,0:T(8,128)S(1)} %broadcast_add_fusion.1), channel_id=1, source_target_pairs={{0,1},{1,0},{2,3},{3,2},{4,5},{5,4},{6,7},{7,6},{8,9},{9,8},{10,11... | collective-permute-start | bytes 245768 | tf_op jit(solution)/shard_map/ppermute | solution.py:41
  74.2 16.6 %collective-permute-start.1 = (s32[8,5,512]{2,1,0:T(8,128)S(1)}, s32[8,5,512]{2,1,0:T(8,128)S(1)}, u32[]{:S(2)}, u32[]{:S(2)}) collective-permute-start(s32[8,5,512]{2,1,0:T(8,128)S(1)} %broadcast_add_fusion.1), channel_id=1, source_target_pairs={{0,2},{1,3},{2,0},{3,1},{4,6},{5,7},{6,4},{7,5},{8,10},{9,11},{10,... | collective-permute-start | bytes 245768 | tf_op jit(solution)/shard_map/ppermute | solution.py:41
  134.3 19.2 %collective-permute-start.4 = (bf16[2,2,2,2,2,5,32,512]{7,6,5,4,3,2,1,0:T(8,128)(2,1)}, bf16[2,2,2,2,2,5,32,512]{7,6,5,4,3,2,1,0:T(8,128)(2,1)}, u32[]{:S(2)}, u32[]{:S(2)}) collective-permute-start(bf16[2,2,2,2,2,5,32,512]{7,6,5,4,3,2,1,0:T(8,128)(2,1)} %bitcast.23), channel_id=1, source_target_pairs={{0,1},{1,0},{2,3},{3,2},{4,5},{5,4},{6,7},{7,6},{8,9},{9,8},{10,11... | collective-permute-start | bytes 15728648 | tf_op jit(solution)/shard_map/ppermute | solution.py:41
  134.5 50.4 %all-to-all-start.3 = ((bf16[8,5,40,512]{3,2,1,0:T(8,128)(2,1)}), bf16[8,5,40,512]{3,2,1,0:T(8,128)(2,1)S(1)}, u32[]{:S(2)}, u32[]{:S(2)}) async-start(bf16[8,5,40,512]{3,2,1,0:T(8,128)(2,1)} %bitcast.32), calls=%async_computation.3 | async-start | bytes 3276800 | tf_op jit(solution)/shard_map/all_to_all | solution.py:639
  156.3 24.6 %collective-permute-start.11 = (bf16[2,2,5,32,512]{4,3,2,1,0:T(8,128)(2,1)S(1)}, bf16[2,2,5,32,512]{4,3,2,1,0:T(8,128)(2,1)S(1)}, u32[]{:S(2)}, u32[]{:S(2)}) collective-permute-start(bf16[2,2,5,32,512]{4,3,2,1,0:T(8,128)(2,1)S(1)} %get-tuple-element.81), channel_id=1, source_target_pairs={{0,4},{4,0},{8,12},{12,8},{16,20},{20,16},{24,28},{28,24},{1,5},{5... | collective-permute-start | bytes 1966088 | tf_op jit(solution)/shard_map/ppermute | solution.py:41
  157.5 24.2 %collective-permute-start.5 = (bf16[2,2,5,32,512]{4,3,2,1,0:T(8,128)(2,1)S(1)}, bf16[2,2,5,32,512]{4,3,2,1,0:T(8,128)(2,1)S(1)}, u32[]{:S(2)}, u32[]{:S(2)}) collective-permute-start(bf16[2,2,5,32,512]{4,3,2,1,0:T(8,128)(2,1)S(1)} %get-tuple-element.82), channel_id=1, source_target_pairs={{0,2},{1,3},{2,0},{3,1},{4,6},{5,7},{6,4},{7,5},{8,10},{9,11},{10,... | collective-permute-start | bytes 1966088 | tf_op jit(solution)/shard_map/ppermute | solution.py:41
  187.7 40.8 %collective-permute-start.13 = (bf16[2,2,5,32,512]{4,3,2,1,0:T(8,128)(2,1)}, bf16[2,2,5,32,512]{4,3,2,1,0:T(8,128)(2,1)S(1)}, u32[]{:S(2)}, u32[]{:S(2)}) collective-permute-start(bf16[2,2,5,32,512]{4,3,2,1,0:T(8,128)(2,1)} %get-tuple-element.79.refs_5_), channel_id=1, source_target_pairs={{0,4},{4,0},{8,12},{12,8},{16,20},{20,16},{24,28},{28,24},{1,5},{5... | collective-permute-start | bytes 1966088 | tf_op jit(solution)/shard_map/ppermute | solution.py:41
  191.1 15.2 %collective-permute-start.8 = (f32[48,1152]{1,0:T(8,128)S(1)}, f32[48,1152]{1,0:T(8,128)S(1)}, u32[]{:S(2)}, u32[]{:S(2)}) collective-permute-start(f32[48,1152]{1,0:T(8,128)S(1)} %add_add_fusion.2), channel_id=1, source_target_pairs={{0,24},{4,28},{8,16},{12,20},{16,8},{20,12},{24,0},{28,4},{1,25},{... | collective-permute-start | bytes 663560 | tf_op jit(solution)/shard_map/ppermute | solution.py:41
  191.2 19.1 %collective-permute-start.7 = (f32[48,1152]{1,0:T(8,128)S(1)}, f32[48,1152]{1,0:T(8,128)S(1)}, u32[]{:S(2)}, u32[]{:S(2)}) collective-permute-start(f32[48,1152]{1,0:T(8,128)S(1)} %add_add_fusion.2), channel_id=1, source_target_pairs={{0,16},{4,20},{8,24},{12,28},{16,0},{20,4},{24,8},{28,12},{1,17},{... | collective-permute-start | bytes 663560 | tf_op jit(solution)/shard_map/ppermute | solution.py:41
  191.3 19.7 %collective-permute-start.6 = (f32[48,1152]{1,0:T(8,128)S(1)}, f32[48,1152]{1,0:T(8,128)S(1)}, u32[]{:S(2)}, u32[]{:S(2)}) collective-permute-start(f32[48,1152]{1,0:T(8,128)S(1)} %add_add_fusion.2), channel_id=1, source_target_pairs={{0,8},{4,12},{8,0},{12,4},{16,24},{20,28},{24,16},{28,20},{1,9},{5... | collective-permute-start | bytes 663560 | tf_op jit(solution)/shard_map/ppermute | solution.py:41
  193.8 34.7 %collective-permute-start.14 = (bf16[2,2,5,32,512]{4,3,2,1,0:T(8,128)(2,1)S(1)}, bf16[2,2,5,32,512]{4,3,2,1,0:T(8,128)(2,1)S(1)}, u32[]{:S(2)}, u32[]{:S(2)}) collective-permute-start(bf16[2,2,5,32,512]{4,3,2,1,0:T(8,128)(2,1)S(1)} %copy-done.8), channel_id=1, source_target_pairs={{0,2},{1,3},{2,0},{3,1},{4,6},{5,7},{6,4},{7,5},{8,10},{9,11},{10,... | collective-permute-start | bytes 1966088 | tf_op jit(solution)/shard_map/ppermute | solution.py:41
  206.3 22.5 %collective-permute-start.9 = (bf16[2,2,5,32,512]{4,3,2,1,0:T(8,128)(2,1)S(1)}, bf16[2,2,5,32,512]{4,3,2,1,0:T(8,128)(2,1)S(1)}, u32[]{:S(2)}, u32[]{:S(2)}) collective-permute-start(bf16[2,2,5,32,512]{4,3,2,1,0:T(8,128)(2,1)S(1)} %copy-done.13), channel_id=1, source_target_pairs={{0,2},{1,3},{2,0},{3,1},{4,6},{5,7},{6,4},{7,5},{8,10},{9,11},{10,... | collective-permute-start | bytes 1966088 | tf_op jit(solution)/shard_map/ppermute | solution.py:41
  210.3 18.6 %collective-permute-start.10 = (bf16[2,2,5,32,512]{4,3,2,1,0:T(8,128)(2,1)S(1)}, bf16[2,2,5,32,512]{4,3,2,1,0:T(8,128)(2,1)S(1)}, u32[]{:S(2)}, u32[]{:S(2)}) collective-permute-start(bf16[2,2,5,32,512]{4,3,2,1,0:T(8,128)(2,1)S(1)} %copy-done.6), channel_id=1, source_target_pairs={{0,4},{4,0},{8,12},{12,8},{16,20},{20,16},{24,28},{28,24},{1,5},{5... | collective-permute-start | bytes 1966088 | tf_op jit(solution)/shard_map/ppermute | solution.py:41
  210.9 51.7 %collective-permute-start.18 = (bf16[8,5,40,512]{3,2,1,0:T(8,128)(2,1)S(1)}, bf16[8,5,40,512]{3,2,1,0:T(8,128)(2,1)S(1)}, u32[]{:S(2)}, u32[]{:S(2)}) collective-permute-start(bf16[8,5,40,512]{3,2,1,0:T(8,128)(2,1)S(1)} %broadcast_multiply_fusion.2), channel_id=1, source_target_pairs={{0,2},{1,3},{2,0},{3,1},{4,6},{5,7},{6,4},{7,5},{8,10},{9,11},{10,... | collective-permute-start | bytes 4915208 | tf_op jit(solution)/shard_map/ppermute | solution.py:41
  229.2 14.3 %collective-permute-start.15 = (bf16[2,5,32,512]{3,2,1,0:T(8,128)(2,1)S(1)}, bf16[2,5,32,512]{3,2,1,0:T(8,128)(2,1)S(1)}, u32[]{:S(2)}, u32[]{:S(2)}) collective-permute-start(bf16[2,5,32,512]{3,2,1,0:T(8,128)(2,1)S(1)} %pad_maximum_fusion.5.refs_6_), channel_id=1, source_target_pairs={{0,8},{4,12},{8,0},{12,4},{16,24},{20,28},{24,16},{28,20},{1,9},{5... | collective-permute-start | bytes 983048 | tf_op jit(solution)/shard_map/ppermute | solution.py:41
  231.3 15.2 %collective-permute-start.16 = (bf16[2,5,32,512]{3,2,1,0:T(8,128)(2,1)S(1)}, bf16[2,5,32,512]{3,2,1,0:T(8,128)(2,1)S(1)}, u32[]{:S(2)}, u32[]{:S(2)}) collective-permute-start(bf16[2,5,32,512]{3,2,1,0:T(8,128)(2,1)S(1)} %pad_maximum_fusion.6.refs_7_), channel_id=1, source_target_pairs={{0,16},{4,20},{8,24},{12,28},{16,0},{20,4},{24,8},{28,12},{1,17},{... | collective-permute-start | bytes 983048 | tf_op jit(solution)/shard_map/ppermute | solution.py:41
  232.5 28.1 %collective-permute-start.17 = (bf16[2,5,32,512]{3,2,1,0:T(8,128)(2,1)S(1)}, bf16[2,5,32,512]{3,2,1,0:T(8,128)(2,1)S(1)}, u32[]{:S(2)}, u32[]{:S(2)}) collective-permute-start(bf16[2,5,32,512]{3,2,1,0:T(8,128)(2,1)S(1)} %pad_maximum_fusion.7.refs_8_), channel_id=1, source_target_pairs={{0,24},{4,28},{8,16},{12,20},{16,8},{20,12},{24,0},{28,4},{1,25},{... | collective-permute-start | bytes 983048 | tf_op jit(solution)/shard_map/ppermute | solution.py:41
  262.8 32.3 %collective-permute-start.19 = (bf16[8,5,40,512]{3,2,1,0:T(8,128)(2,1)S(1)}, bf16[8,5,40,512]{3,2,1,0:T(8,128)(2,1)S(1)}, u32[]{:S(2)}, u32[]{:S(2)}) collective-permute-start(bf16[8,5,40,512]{3,2,1,0:T(8,128)(2,1)S(1)} %broadcast_multiply_fusion.1.refs_2_), channel_id=1, source_target_pairs={{0,1},{1,0},{2,3},{3,2},{4,5},{5,4},{6,7},{7,6},{8,9},{9,8},{10,11... | collective-permute-start | bytes 4915208 | tf_op jit(solution)/shard_map/ppermute | solution.py:41
  264.7 14.3 %collective-permute-start.24 = (bf16[2,5,32,512]{3,2,1,0:T(8,128)(2,1)S(1)}, bf16[2,5,32,512]{3,2,1,0:T(8,128)(2,1)S(1)}, u32[]{:S(2)}, u32[]{:S(2)}) collective-permute-start(bf16[2,5,32,512]{3,2,1,0:T(8,128)(2,1)S(1)} %add_convert_fusion.2.refs_5_), channel_id=1, source_target_pairs={{0,16},{4,20},{8,24},{12,28},{16,0},{20,4},{24,8},{28,12},{1,17},{... | collective-permute-start | bytes 983048 | tf_op jit(solution)/shard_map/ppermute | solution.py:41
  264.7 17.3 %collective-permute-start.23 = (bf16[2,5,32,512]{3,2,1,0:T(8,128)(2,1)S(1)}, bf16[2,5,32,512]{3,2,1,0:T(8,128)(2,1)S(1)}, u32[]{:S(2)}, u32[]{:S(2)}) collective-permute-start(bf16[2,5,32,512]{3,2,1,0:T(8,128)(2,1)S(1)} %add_convert_fusion.2.refs_5_), channel_id=1, source_target_pairs={{0,8},{4,12},{8,0},{12,4},{16,24},{20,28},{24,16},{28,20},{1,9},{5... | collective-permute-start | bytes 983048 | tf_op jit(solution)/shard_map/ppermute | solution.py:41
  267.1 27.9 %collective-permute-start.25 = (bf16[2,5,32,512]{3,2,1,0:T(8,128)(2,1)S(1)}, bf16[2,5,32,512]{3,2,1,0:T(8,128)(2,1)S(1)}, u32[]{:S(2)}, u32[]{:S(2)}) collective-permute-start(bf16[2,5,32,512]{3,2,1,0:T(8,128)(2,1)S(1)} %add_convert_fusion.2.refs_5_), channel_id=1, source_target_pairs={{0,24},{4,28},{8,16},{12,20},{16,8},{20,12},{24,0},{28,4},{1,25},{... | collective-permute-start | bytes 983048 | tf_op jit(solution)/shard_map/ppermute | solution.py:41
  306.5 14.4 %collective-permute-start.21 = (f32[48,1152]{1,0:T(8,128)S(1)}, f32[48,1152]{1,0:T(8,128)S(1)}, u32[]{:S(2)}, u32[]{:S(2)}) collective-permute-start(f32[48,1152]{1,0:T(8,128)S(1)} %broadcast_add_fusion), channel_id=1, source_target_pairs={{0,4},{4,0},{8,12},{12,8},{16,20},{20,16},{24,28},{28,24},{1,5},{5... | collective-permute-start | bytes 663560 | tf_op jit(solution)/shard_map/ppermute | solution.py:41
  307.4 13.5 %collective-permute-start.22 = (f32[48,1152]{1,0:T(8,128)S(1)}, f32[48,1152]{1,0:T(8,128)S(1)}, u32[]{:S(2)}, u32[]{:S(2)}) collective-permute-start(f32[48,1152]{1,0:T(8,128)S(1)} %broadcast_add_fusion), channel_id=1, source_target_pairs={{0,6},{1,7},{2,4},{3,5},{4,2},{5,3},{6,0},{7,1},{8,14},{9,15},{10,... | collective-permute-start | bytes 663560 | tf_op jit(solution)/shard_map/ppermute | solution.py:50
  309.0 11.9 %collective-permute-start.20 = (f32[48,1152]{1,0:T(8,128)S(1)}, f32[48,1152]{1,0:T(8,128)S(1)}, u32[]{:S(2)}, u32[]{:S(2)}) collective-permute-start(f32[48,1152]{1,0:T(8,128)S(1)} %broadcast_add_fusion), channel_id=1, source_target_pairs={{0,2},{1,3},{2,0},{3,1},{4,6},{5,7},{6,4},{7,5},{8,10},{9,11},{10,... | collective-permute-start | bytes 663560 | tf_op jit(solution)/shard_map/ppermute | solution.py:41
  309.3 23.9 %collective-permute-start.28 = (bf16[4,5,32,512]{3,2,1,0:T(8,128)(2,1)S(1)}, bf16[4,5,32,512]{3,2,1,0:T(8,128)(2,1)S(1)}, u32[]{:S(2)}, u32[]{:S(2)}) collective-permute-start(bf16[4,5,32,512]{3,2,1,0:T(8,128)(2,1)S(1)} %pad_maximum_fusion.4.refs_6_), channel_id=1, source_target_pairs={{0,2},{1,3},{2,0},{3,1},{4,6},{5,7},{6,4},{7,5},{8,10},{9,11},{10,... | collective-permute-start | bytes 1966088 | tf_op jit(solution)/shard_map/ppermute | solution.py:41
  310.7 21.0 %collective-permute-start.26 = (bf16[4,5,32,512]{3,2,1,0:T(8,128)(2,1)S(1)}, bf16[4,5,32,512]{3,2,1,0:T(8,128)(2,1)S(1)}, u32[]{:S(2)}, u32[]{:S(2)}) collective-permute-start(bf16[4,5,32,512]{3,2,1,0:T(8,128)(2,1)S(1)} %pad_maximum_fusion.3.refs_5_), channel_id=1, source_target_pairs={{0,4},{4,0},{8,12},{12,8},{16,20},{20,16},{24,28},{28,24},{1,5},{5... | collective-permute-start | bytes 1966088 | tf_op jit(solution)/shard_map/ppermute | solution.py:41
  331.8 32.3 %collective-permute-start.27 = (bf16[8,5,32,512]{3,2,1,0:T(8,128)(2,1)S(1)}, bf16[8,5,32,512]{3,2,1,0:T(8,128)(2,1)S(1)}, u32[]{:S(2)}, u32[]{:S(2)}) collective-permute-start(bf16[8,5,32,512]{3,2,1,0:T(8,128)(2,1)S(1)} %pad_maximum_fusion.refs_5_.refs_0_), channel_id=1, source_target_pairs={{0,2},{1,3},{2,0},{3,1},{4,6},{5,7},{6,4},{7,5},{8,10},{9,11},{10,... | collective-permute-start | bytes 3932168 | tf_op jit(solution)/shard_map/ppermute | solution.py:41
  333.3 31.4 %collective-permute-start.31 = (bf16[8,5,32,512]{3,2,1,0:T(8,128)(2,1)S(1)}, bf16[8,5,32,512]{3,2,1,0:T(8,128)(2,1)S(1)}, u32[]{:S(2)}, u32[]{:S(2)}) collective-permute-start(bf16[8,5,32,512]{3,2,1,0:T(8,128)(2,1)S(1)} %pad_maximum_fusion.1.refs_6_.refs_4_), channel_id=1, source_target_pairs={{0,4},{4,0},{8,12},{12,8},{16,20},{20,16},{24,28},{28,24},{1,5},{5... | collective-permute-start | bytes 3932168 | tf_op jit(solution)/shard_map/ppermute | solution.py:41
  334.2 34.8 %collective-permute-start.29 = (bf16[8,5,32,512]{3,2,1,0:T(8,128)(2,1)S(1)}, bf16[8,5,32,512]{3,2,1,0:T(8,128)(2,1)S(1)}, u32[]{:S(2)}, u32[]{:S(2)}) collective-permute-start(bf16[8,5,32,512]{3,2,1,0:T(8,128)(2,1)S(1)} %pad_maximum_fusion.refs_5_.refs_0_), channel_id=1, source_target_pairs={{0,1},{1,0},{2,3},{3,2},{4,5},{5,4},{6,7},{7,6},{8,9},{9,8},{10,11... | collective-permute-start | bytes 3932168 | tf_op jit(solution)/shard_map/ppermute | solution.py:41
  336.3 32.7 %collective-permute-start.32 = (bf16[8,5,32,512]{3,2,1,0:T(8,128)(2,1)S(1)}, bf16[8,5,32,512]{3,2,1,0:T(8,128)(2,1)S(1)}, u32[]{:S(2)}, u32[]{:S(2)}) collective-permute-start(bf16[8,5,32,512]{3,2,1,0:T(8,128)(2,1)S(1)} %pad_maximum_fusion.1.refs_6_.refs_4_), channel_id=1, source_target_pairs={{0,1},{1,0},{2,3},{3,2},{4,5},{5,4},{6,7},{7,6},{8,9},{9,8},{10,11... | collective-permute-start | bytes 3932168 | tf_op jit(solution)/shard_map/ppermute | solution.py:41
  (44 other events, 350.7 us)

commit v8 on v7

--- a/solution.py
+++ b/solution.py
@@ -16,7 +16,8 @@
 LOOK_ROWS = 32
 ADD_LOW = 512
 ADD_TABS = 4
-NEAR_FIRST = 3
+NEAR_FIRST = 2
+FAR_FIRST = 2
 MAIN = 1024
 CHUNK = 384
 PIECE = 32
@@ -468,7 +469,7 @@
         out_specs=out_specs,
         out_shape=shapes,
         scratch_shapes=[pltpu.VMEM((half, count), BF)],
-        compiler_params=params(40),
+        compiler_params=params(60),
         cost_estimate=cost(matrix_count * size * size * count, 5 * matrix_count * size * size),
         name="weight_parts",
     )(own, left, right)
@@ -490,20 +491,20 @@
 
 def joined(parts, token):
     one = (1.0 + token).astype(BF)
-    return jnp.concatenate([parts[0] * one] + list(parts[1:]))
+    return jnp.concatenate([part * one for part in parts])
 
 
 def assemble_kernel(layer_count, own_ref, *refs):
-    blocks = refs[:8]
-    strip_ref, cross_ref, first_ref, second_ref = refs[8:]
+    blocks = refs[:16]
+    strip_ref, cross_ref, first_ref, second_ref = refs[16:]
     matrix = pl.program_id(0)
 
     def fill(out_ref):
         for block, ref in enumerate(blocks):
-            chunk, core, upper = block >> 2, (block >> 1) & 1, block & 1
+            chunk, core, upper = block >> 3, (block >> 2) & 1, block & 3
             count, _, rows, lanes = ref.shape
             for at in range(count):
-                piece = 2 * count * core + chunk_place(count * upper + at, chunk == 1)
+                piece = 4 * count * core + chunk_place(count * upper + at, chunk == 1)
                 first = pl.multiple_of((piece ^ own_ref[0]) * rows, rows)
                 out_ref[0, pl.ds(first, rows), chunk * lanes : (chunk + 1) * lanes] = ref[at, 0].astype(F32)
         height, width = out_ref.shape[1:]
@@ -537,7 +538,7 @@
         functools.partial(assemble_kernel, layer_count),
         grid=(matrix_count,),
         in_specs=[pl.BlockSpec(memory_space=pltpu.SMEM)]
-        + [block] * 8
+        + [block] * 16
         + [pl.BlockSpec((1, 8, size), lambda m: (m, 0, 0))],
         out_specs=[
             pl.BlockSpec((1, width, width), lambda m: (jnp.minimum(m, layer_count - 1), 0, 0)),
@@ -710,32 +711,33 @@
     kept = take_far(0, 0)
     sends = [take_far(high, low).astype(BF) for high, low in FAR]
     far = [swap(value, "tab", 4 * high + 2 * low) for value, (high, low) in zip(sends, FAR)]
-    add_next(True, slot_count - NEAR_FIRST - 1, [kept] + sends)
+    add_next(True, slot_count, [kept] + sends)
     piece = added([kept, *far], token).astype(BF)
     for axis, known in (("rep", 2), ("tab", 3)):
         for mask in masks_of(axis)[known:]:
             piece = (piece.astype(F32) + swap(piece, axis, mask).astype(F32)).astype(BF)
     parts = [piece, swap(piece, "tab", 2), swap(piece, "tab", 4), swap(piece, "tab", 6)]
-    add_next(True, slot_count, [piece])
     far_grads = far_parts([gate(part, piece[0, 0, 0, 0]) for part in bases])
-    add_next(False, 1, [piece])
+    add_next(False, FAR_FIRST, [piece])
     values = [joined([part[at : at + 1] for part in parts], token) for at in range(2)]
-    sent = [swap(values[at], *HALVES[at][1]) for at in range(2)]
-    small = small + zero_of(values[1][0, 0, 0, 0])
+    near = [swap(values[at], *HALVES[at][1]) for at in range(2)]
+    across = [swap(values[at], *HALVES[at][0]) for at in range(2)]
+    add_next(False, 1, values)
+    both = [swap(near[at], *HALVES[at][0]) for at in range(2)]
+    add_next(False, 1, near)
+    small = small + zero_of(token)
     small = added([small, swap(small, "rep", 2), swap(small, "tab", 1), swap_both(small, 2, 1)])
     for axis, known in (("rep", 2), ("tab", 3)):
         for mask in masks_of(axis)[known:]:
             small = small + swap(small, axis, mask)
-    add_next(False, 1, values)
-    token = token + zero_of(small[0, 0])
-    values = [joined((values[at], sent[at]), token) for at in range(2)]
-    sent = [swap(values[at], *HALVES[at][0]) for at in range(2)]
-    blocks = [[values[at], None, swap(values[at], "rep", 1), None] for at in range(2)]
-    add_next(False, slot_count, values)
+    other = []
     for at in range(2):
-        blocks[at][1] = gate(sent[at], token)
-        blocks[at][3] = swap(blocks[at][1], "rep", 1)
-    blocks = blocks[0] + blocks[1]
+        other.append([swap(part, "rep", 1) for part in (values[at], near[at], across[at])])
+    add_next(False, slot_count, other[0] + other[1])
+    blocks = []
+    for at in range(2):
+        last = gate(both[at], token)
+        blocks += [values[at], near[at], across[at], last] + other[at] + [swap(last, "rep", 1)]
 
     strips = small[:-8].reshape(matrix_count, 8, size)
     sums = small[-8:]

time: 393 us -> 379 us (0.964)
  the two profiles are of different devices: /device:TPU:9 before, /device:TPU:0 now
where the time goes in v8:
time: 379 us; the launch traced here: 374 us
  Pallas kernels  186 us (49%)
  waiting for transfers between devices  62.5 us (16%)
  starting transfers between devices  60.2 us (16%)
  local copies, waits for them, and re-layouts  29.3 us (8%)
  other arithmetic  24.4 us (6%)
  between operations  12.1 us (3%)
    pallas_call x10, Pallas kernels, add_rows(): pl.pallas_call(functools.partial(add_kernel, part_count, accumulate), gri...  82.1 us
    ppermute x39, waiting for transfers between devices, swap(): lax.ppermute(value, axis, [(at, at ^ mask) for at in range(lax.axis_size(...  55.7 us
    pallas_call x2, Pallas kernels, lookup(): pl.pallas_call(functools.partial(lookup_kernel, first_slot), in_specs=[sm...  40.3 us
    ppermute x39, starting transfers between devices, swap(): lax.ppermute(value, axis, [(at, at ^ mask) for at in range(lax.axis_size(...  33.7 us
    pallas_call x1, Pallas kernels, dense_step(): pl.pallas_call(functools.partial(dense_kernel, dense_width, width, starts...  27.5 us
    pallas_call x2, Pallas kernels, weight_parts(): pl.pallas_call(functools.partial(weight_kernel, core), grid=(matrix_count...  22.2 us
    pallas_call x1, Pallas kernels, assemble(): pl.pallas_call(functools.partial(assemble_kernel, layer_count), grid=(mat...  13.4 us
    all_to_all x2, starting transfers between devices, on_device(): lax.all_to_all(looked, 'tab', split_axis=0, concat_axis=0, tiled=True)  12.6 us
  transfers between devices with their start and end apart: 44, of which 18 were waited for; matrix products, arithmetic and copies ran while one was open for 12% of the time, Pallas kernels for 31%

profile of v8, /device:TPU:0, one launch (start us, length us, event | category | flops | bytes accessed | tf_op | source)
XLA Modules:
  0.0 374.1 jit_solution(14396871091583900962)
XLA Ops:
  5.2 7.3 %all-to-all-start = ((s32[8,5,512]{2,1,0:T(8,128)}), s32[8,5,512]{2,1,0:T(8,128)S(1)}, u32[]{:S(2)}, u32[]{:S(2)}) async-start(s32[8,5,512]{2,1,0:T(8,128)} %reshape.521), calls=%async_computation | async-start | bytes 262144 | tf_op jit(solution)/shard_map/all_to_all | solution.py:592
  13.8 6.0 %all-to-all-done = s32[8,5,512]{2,1,0:T(8,128)S(1)} async-done(((s32[8,5,512]{2,1,0:T(8,128)}), s32[8,5,512]{2,1,0:T(8,128)S(1)}, u32[]{:S(2)}, u32[]{:S(2)}) %all-to-all-start) | async-done | bytes 81952 | tf_op jit(solution)/shard_map/all_to_all | solution.py:592
  20.5 19.6 %lookup.2 = bf16[8,2,40,512]{3,2,1,0:T(8,128)(2,1)} custom-call(s32[20480]{0:T(1024)} %bitcast.112, s32[5]{0:T(128)} %dynamic_slice.3.rows_ref, bf16[5,39,32768]{2,1,0:T(8,128)(2,1)} %table_hbm.3), custom_call_target="tpu_custom_call" | custom-call | flops 20132660 | bytes 5750 | tf_op jit(solution)/shard_map/lookup/pallas_call | solution.py:112
  40.1 3.6 all-to-all-start.1
  45.6 20.7 %lookup.3 = bf16[8,3,40,512]{3,2,1,0:T(8,128)(2,1)} custom-call(s32[20480]{0:T(1024)} %bitcast.113, s32[5]{0:T(128)} %dynamic_slice.3.rows_ref, bf16[5,39,32768]{2,1,0:T(8,128)(2,1)} %table_hbm.3), custom_call_target="tpu_custom_call" | custom-call | flops 30198988 | bytes 8626 | tf_op jit(solution)/shard_map/lookup/pallas_call | solution.py:112
  66.3 9.0 %all-to-all-start.2 = ((bf16[8,3,40,512]{3,2,1,0:T(8,128)(2,1)}), bf16[8,3,40,512]{3,2,1,0:T(8,128)(2,1)S(1)}, u32[]{:S(2)}, u32[]{:S(2)}) async-start(bf16[8,3,40,512]{3,2,1,0:T(8,128)(2,1)} %lookup.3), calls=%async_computation.2 | async-start | bytes 1966080 | tf_op jit(solution)/shard_map/all_to_all | solution.py:604
  81.0 3.5 multiply_bitcast_fusion
  99.2 27.5 %dense.1 = (f32[1,512]{1,0:T(1,128)}, f32[16,512]{1,0:T(8,128)}, bf16[40,40,512]{2,1,0:T(8,128)(2,1)}, bf16[5,1152,512]{2,1,0:T(8,128)(2,1)}, bf16[5,1152,512]{2,1,0:T(8,128)(2,1)}, /*index=5*/f32[8,1152]{1,0:T(8,128)}) custom-call(s32[26]{0:T(128)} %place_ref.1, f32[1]{0:T(128)S(6)} %convert.63.bias_ref, bf16[8,2,40,512]{3,2,1,0:T(8,128)(2,1)} %copy-done.27, ...), custom_call_target="tpu_custom_call" | custom-call | flops 13589544 | bytes 30965 | tf_op jit(solution)/shard_map/dense/pallas_call | solution.py:379
  126.7 9.7 %weight_parts.3 = bf16[2,16,5,32,512]{4,3,2,1,0:T(8,128)(2,1)} custom-call(s32[1]{0:T(128)} %bitcast.own_ref, bf16[5,1152,512]{2,1,0:T(8,128)(2,1)} %get-tuple-element.43.left_ref, bf16[5,1152,512]{2,1,0:T(8,128)(2,1)} %get-tuple-element.44.right_ref), custom_call_target="tpu_custom_call" | custom-call | flops 3397386 | bytes 33177 | tf_op jit(solution)/shard_map/weight_parts/pallas_call | solution.py:461
  136.4 5.9 %all-to-all-start.3 = ((bf16[8,5,40,512]{3,2,1,0:T(8,128)(2,1)}), bf16[8,5,40,512]{3,2,1,0:T(8,128)(2,1)S(1)}, u32[]{:S(2)}, u32[]{:S(2)}) async-start(bf16[8,5,40,512]{3,2,1,0:T(8,128)(2,1)} %bitcast.31), calls=%async_computation.3 | async-start | bytes 3276800 | tf_op jit(solution)/shard_map/all_to_all | solution.py:640
  142.4 12.5 %weight_parts.2 = (f32[2,16,5,32,512]{4,3,2,1,0:T(8,128)}, f32[5,8,1152]{2,1,0:T(8,128)}) custom-call(s32[1]{0:T(128)} %bitcast.own_ref, bf16[5,1152,512]{2,1,0:T(8,128)(2,1)} %get-tuple-element.43.left_ref, bf16[5,1152,512]{2,1,0:T(8,128)(2,1)} %get-tuple-element.44.right_ref), custom_call_target="tpu_custom_call" | custom-call | flops 3397386 | bytes 33177 | tf_op jit(solution)/shard_map/weight_parts/pallas_call | solution.py:461
  160.2 3.6 fusion.7
  163.8 3.0 convert_add_fusion
  166.9 14.1 %collective-permute-done.9 = bf16[2,2,5,32,512]{4,3,2,1,0:T(8,128)(2,1)S(1)} collective-permute-done((bf16[2,2,5,32,512]{4,3,2,1,0:T(8,128)(2,1)S(1)}, bf16[2,2,5,32,512]{4,3,2,1,0:T(8,128)(2,1)S(1)}, u32[]{:S(2)}, u32[]{:S(2)}) %collective-permute-start.9) | collective-permute-done | bytes 655392 | tf_op jit(solution)/shard_map/ppermute | solution.py:42
  190.2 3.0 collective-permute-start.8
  196.1 7.4 %add_rows.10 = (f32[5,39,8192]{2,1,0:T(8,128)}, f32[8,128]{1,0:T(8,128)S(1)}) custom-call(s32[1]{0:T(128)} %bitcast.30.base_ref, s32[8,5,1,512]{3,2,1,0:T(1,128)S(1)} %copy-done.6, s32[8,5,1,512]{3,2,1,0:T(1,128)S(1)} %copy-done.7, bf16[8,5,40,512]{3,2,1,0:T(8,128)(2,1)S(1)} %broadcast_multiply_fusion.3.refs_2_, ...), custom_call_target="tpu_custom_call" | custom-call | flops 5234491 | bytes 1916 | tf_op jit(solution)/shard_map/add_rows/pallas_call | solution.py:185
  206.4 7.4 %collective-permute-done.7 = f32[48,1152]{1,0:T(8,128)S(1)} collective-permute-done((f32[48,1152]{1,0:T(8,128)S(1)}, f32[48,1152]{1,0:T(8,128)S(1)}, u32[]{:S(2)}, u32[]{:S(2)}) %collective-permute-start.7) | collective-permute-done | bytes 221216 | tf_op jit(solution)/shard_map/ppermute | solution.py:42
  216.3 7.6 %add_rows.11 = (f32[5,39,8192]{2,1,0:T(8,128)}, f32[8,128]{1,0:T(8,128)S(1)}) custom-call(s32[1]{0:T(128)} %bitcast.30.base_ref, s32[8,5,1,512]{3,2,1,0:T(1,128)S(1)} %copy-done.6, s32[8,5,1,512]{3,2,1,0:T(1,128)S(1)} %copy-done.7, bf16[8,5,40,512]{3,2,1,0:T(8,128)(2,1)S(1)} %broadcast_multiply_fusion.3.refs_2_, ...), custom_call_target="tpu_custom_call", output_to_operand_aliasing={{0}: (5, {})} | custom-call | flops 5234491 | bytes 1916 | tf_op jit(solution)/shard_map/add_rows/pallas_call | solution.py:185
  227.2 3.2 collective-permute-done.13
  235.4 7.4 %add_rows.12 = (f32[5,39,8192]{2,1,0:T(8,128)}, f32[8,128]{1,0:T(8,128)}) custom-call(s32[1]{0:T(128)} %bitcast.30.base_ref, s32[8,5,1,512]{3,2,1,0:T(1,128)S(1)} %copy-done.6, s32[8,5,1,512]{3,2,1,0:T(1,128)S(1)} %copy-done.7, bf16[8,5,40,512]{3,2,1,0:T(8,128)(2,1)S(1)} %broadcast_multiply_fusion.3.refs_2_, ...), custom_call_target="tpu_custom_call", output_to_operand_aliasing={{0}: (5, {})} | custom-call | flops 5234491 | bytes 1916 | tf_op jit(solution)/shard_map/add_rows/pallas_call | solution.py:185
  242.8 7.4 %add_rows.13 = (f32[5,39,8192]{2,1,0:T(8,128)}, f32[8,128]{1,0:T(8,128)}) custom-call(s32[1]{0:T(128)} %bitcast.30.base_ref, s32[8,5,1,512]{3,2,1,0:T(1,128)S(1)} %copy-done.6, s32[8,5,1,512]{3,2,1,0:T(1,128)S(1)} %copy-done.7, bf16[8,5,40,512]{3,2,1,0:T(8,128)(2,1)S(1)} %broadcast_multiply_fusion.3.refs_2_, ...), custom_call_target="tpu_custom_call", output_to_operand_aliasing={{0}: (5, {})} | custom-call | flops 5234491 | bytes 1916 | tf_op jit(solution)/shard_map/add_rows/pallas_call | solution.py:185
  250.2 7.4 %add_rows.14 = (f32[5,39,8192]{2,1,0:T(8,128)}, f32[8,128]{1,0:T(8,128)S(1)}) custom-call(s32[1]{0:T(128)} %bitcast.30.base_ref, s32[8,5,1,512]{3,2,1,0:T(1,128)S(1)} %copy-done.6, s32[8,5,1,512]{3,2,1,0:T(1,128)S(1)} %copy-done.7, bf16[8,5,40,512]{3,2,1,0:T(8,128)(2,1)S(1)} %broadcast_multiply_fusion.3.refs_2_, ...), custom_call_target="tpu_custom_call", output_to_operand_aliasing={{0}: (5, {})} | custom-call | flops 5234491 | bytes 1916 | tf_op jit(solution)/shard_map/add_rows/pallas_call | solution.py:185
  261.0 3.6 collective-permute-start.20
  266.4 9.0 %add_rows.15 = (f32[5,39,8192]{2,1,0:T(8,128)}, f32[8,128]{1,0:T(8,128)}) custom-call(s32[1]{0:T(128)} %bitcast.30.base_ref, s32[8,5,1,512]{3,2,1,0:T(1,128)S(1)} %copy-done.8, s32[8,5,1,512]{3,2,1,0:T(1,128)S(1)} %copy-done.9, bf16[8,5,40,512]{3,2,1,0:T(8,128)(2,1)S(1)} %broadcast_multiply_fusion.1.refs_2_, ...), custom_call_target="tpu_custom_call", output_to_operand_aliasing={{0}: (5, {})} | custom-call | flops 5234491 | bytes 1916 | tf_op jit(solution)/shard_map/add_rows/pallas_call | solution.py:185
  275.4 8.8 %add_rows.16 = (f32[5,39,8192]{2,1,0:T(8,128)}, f32[8,128]{1,0:T(8,128)S(1)}) custom-call(s32[1]{0:T(128)} %bitcast.30.base_ref, s32[8,5,1,512]{3,2,1,0:T(1,128)S(1)} %copy-done.8, s32[8,5,1,512]{3,2,1,0:T(1,128)S(1)} %copy-done.9, bf16[8,5,40,512]{3,2,1,0:T(8,128)(2,1)S(1)} %broadcast_multiply_fusion.1.refs_2_, ...), custom_call_target="tpu_custom_call", output_to_operand_aliasing={{0}: (5, {})} | custom-call | flops 5234491 | bytes 1916 | tf_op jit(solution)/shard_map/add_rows/pallas_call | solution.py:185
  285.4 9.7 %collective-permute-done.21 = bf16[2,5,32,512]{3,2,1,0:T(8,128)(2,1)S(1)} collective-permute-done((bf16[2,5,32,512]{3,2,1,0:T(8,128)(2,1)S(1)}, bf16[2,5,32,512]{3,2,1,0:T(8,128)(2,1)S(1)}, u32[]{:S(2)}, u32[]{:S(2)}) %collective-permute-start.21) | collective-permute-done | bytes 327712 | tf_op jit(solution)/shard_map/ppermute | solution.py:42
  299.6 8.8 %add_rows.17 = (f32[5,39,8192]{2,1,0:T(8,128)}, f32[8,128]{1,0:T(8,128)}) custom-call(s32[1]{0:T(128)} %bitcast.30.base_ref, s32[8,5,1,512]{3,2,1,0:T(1,128)S(1)} %copy-done.8, s32[8,5,1,512]{3,2,1,0:T(1,128)S(1)} %copy-done.9, bf16[8,5,40,512]{3,2,1,0:T(8,128)(2,1)S(1)} %broadcast_multiply_fusion.1.refs_2_, ...), custom_call_target="tpu_custom_call", output_to_operand_aliasing={{0}: (5, {})} | custom-call | flops 5234491 | bytes 1916 | tf_op jit(solution)/shard_map/add_rows/pallas_call | solution.py:185
  308.4 4.7 %collective-permute-done.23.refs_5_.refs_1_ = bf16[4,5,32,512]{3,2,1,0:T(8,128)(2,1)S(1)} collective-permute-done((bf16[4,5,32,512]{3,2,1,0:T(8,128)(2,1)S(1)}, bf16[4,5,32,512]{3,2,1,0:T(8,128)(2,1)S(1)}, u32[]{:S(2)}, u32[]{:S(2)}) %collective-permute-start.23) | collective-permute-done | bytes 655392 | tf_op jit(solution)/shard_map/ppermute | solution.py:42
  314.0 9.0 %add_rows.18 = (f32[5,39,8192]{2,1,0:T(8,128)}, f32[8,128]{1,0:T(8,128)S(1)}) custom-call(s32[1]{0:T(128)} %bitcast.30.base_ref, s32[8,5,1,512]{3,2,1,0:T(1,128)S(1)} %copy-done.8, s32[8,5,1,512]{3,2,1,0:T(1,128)S(1)} %copy-done.9, bf16[8,5,40,512]{3,2,1,0:T(8,128)(2,1)S(1)} %broadcast_multiply_fusion.1.refs_2_, ...), custom_call_target="tpu_custom_call", output_to_operand_aliasing={{0}: (5, {})} | custom-call | flops 5234491 | bytes 1916 | tf_op jit(solution)/shard_map/add_rows/pallas_call | solution.py:185
  330.5 8.4 %collective-permute-done.26 = f32[48,1152]{1,0:T(8,128)S(1)} collective-permute-done((f32[48,1152]{1,0:T(8,128)S(1)}, f32[48,1152]{1,0:T(8,128)S(1)}, u32[]{:S(2)}, u32[]{:S(2)}) %collective-permute-start.26) | collective-permute-done | bytes 221216 | tf_op jit(solution)/shard_map/ppermute | solution.py:42
  343.8 9.4 %add_rows.19 = (f32[5,39,8192]{2,1,0:T(8,128)}, f32[8,128]{1,0:T(8,128)S(1)}) custom-call(s32[1]{0:T(128)} %bitcast.30.base_ref, s32[8,5,1,512]{3,2,1,0:T(1,128)S(1)} %copy-done.8, s32[8,5,1,512]{3,2,1,0:T(1,128)S(1)} %copy-done.9, bf16[8,5,40,512]{3,2,1,0:T(8,128)(2,1)S(1)} %broadcast_multiply_fusion.1.refs_2_, ...), custom_call_target="tpu_custom_call", output_to_operand_aliasing={{0}: (5, {})} | custom-call | flops 5234491 | bytes 1916 | tf_op jit(solution)/shard_map/add_rows/pallas_call | solution.py:185
  359.3 13.4 %assemble.1 = (f32[3,1027,1027]{2,1,0:T(8,128)}, f32[1,1027,1024]{2,1,0:T(8,128)}, f32[1,1024,1024]{2,1,0:T(8,128)}) custom-call(s32[1]{0:T(128)} %bitcast.own_ref, bf16[4,5,32,512]{3,2,1,0:T(8,128)(2,1)} %copy-done, bf16[4,5,32,512]{3,2,1,0:T(8,128)(2,1)} %copy-done.10, bf16[4,5,32,512]{3,2,1,0:T(8,128)(2,1)} %copy-done.32, ...), custom_call_target="tpu_custom_call" | custom-call | bytes 39813 | tf_op jit(solution)/shard_map/assemble/pallas_call | solution.py:537
  (254 shorter events, 80.5 us)
Async XLA Ops:
  5.2 14.6 %all-to-all-start = ((s32[8,5,512]{2,1,0:T(8,128)}), s32[8,5,512]{2,1,0:T(8,128)S(1)}, u32[]{:S(2)}, u32[]{:S(2)}) async-start(s32[8,5,512]{2,1,0:T(8,128)} %reshape.521), calls=%async_computation | async-start | bytes 262144 | tf_op jit(solution)/shard_map/all_to_all | solution.py:592
  40.1 26.1 %all-to-all-start.1 = ((bf16[8,2,40,512]{3,2,1,0:T(8,128)(2,1)}), bf16[8,2,40,512]{3,2,1,0:T(8,128)(2,1)S(1)}, u32[]{:S(2)}, u32[]{:S(2)}) async-start(bf16[8,2,40,512]{3,2,1,0:T(8,128)(2,1)} %lookup.2), calls=%async_computation.1 | async-start | bytes 1310720 | tf_op jit(solution)/shard_map/all_to_all | solution.py:604
  66.3 31.9 %all-to-all-start.2 = ((bf16[8,3,40,512]{3,2,1,0:T(8,128)(2,1)}), bf16[8,3,40,512]{3,2,1,0:T(8,128)(2,1)S(1)}, u32[]{:S(2)}, u32[]{:S(2)}) async-start(bf16[8,3,40,512]{3,2,1,0:T(8,128)(2,1)} %lookup.3), calls=%async_computation.2 | async-start | bytes 1966080 | tf_op jit(solution)/shard_map/all_to_all | solution.py:604
  76.5 18.7 %collective-permute-start = (s32[8,5,512]{2,1,0:T(8,128)S(1)}, s32[8,5,512]{2,1,0:T(8,128)S(1)}, u32[]{:S(2)}, u32[]{:S(2)}) collective-permute-start(s32[8,5,512]{2,1,0:T(8,128)S(1)} %broadcast_add_fusion.1), channel_id=1, source_target_pairs={{0,1},{1,0},{2,3},{3,2},{4,5},{5,4},{6,7},{7,6},{8,9},{9,8},{10,11... | collective-permute-start | bytes 245768 | tf_op jit(solution)/shard_map/ppermute | solution.py:42
  76.6 16.5 %collective-permute-start.1 = (s32[8,5,512]{2,1,0:T(8,128)S(1)}, s32[8,5,512]{2,1,0:T(8,128)S(1)}, u32[]{:S(2)}, u32[]{:S(2)}) collective-permute-start(s32[8,5,512]{2,1,0:T(8,128)S(1)} %broadcast_add_fusion.1), channel_id=1, source_target_pairs={{0,2},{1,3},{2,0},{3,1},{4,6},{5,7},{6,4},{7,5},{8,10},{9,11},{10,... | collective-permute-start | bytes 245768 | tf_op jit(solution)/shard_map/ppermute | solution.py:42
  136.4 18.4 %collective-permute-start.4 = (bf16[2,2,2,2,2,5,32,512]{7,6,5,4,3,2,1,0:T(8,128)(2,1)}, bf16[2,2,2,2,2,5,32,512]{7,6,5,4,3,2,1,0:T(8,128)(2,1)}, u32[]{:S(2)}, u32[]{:S(2)}) collective-permute-start(bf16[2,2,2,2,2,5,32,512]{7,6,5,4,3,2,1,0:T(8,128)(2,1)} %bitcast.110), channel_id=1, source_target_pairs={{0,1},{1,0},{2,3},{3,2},{4,5},{5,4},{6,7},{7,6},{8,9},{9,8},{10,11... | collective-permute-start | bytes 15728648 | tf_op jit(solution)/shard_map/ppermute | solution.py:42
  136.4 48.5 %all-to-all-start.3 = ((bf16[8,5,40,512]{3,2,1,0:T(8,128)(2,1)}), bf16[8,5,40,512]{3,2,1,0:T(8,128)(2,1)S(1)}, u32[]{:S(2)}, u32[]{:S(2)}) async-start(bf16[8,5,40,512]{3,2,1,0:T(8,128)(2,1)} %bitcast.31), calls=%async_computation.3 | async-start | bytes 3276800 | tf_op jit(solution)/shard_map/all_to_all | solution.py:640
  157.6 23.4 %collective-permute-start.9 = (bf16[2,2,5,32,512]{4,3,2,1,0:T(8,128)(2,1)S(1)}, bf16[2,2,5,32,512]{4,3,2,1,0:T(8,128)(2,1)S(1)}, u32[]{:S(2)}, u32[]{:S(2)}) collective-permute-start(bf16[2,2,5,32,512]{4,3,2,1,0:T(8,128)(2,1)S(1)} %get-tuple-element.81), channel_id=1, source_target_pairs={{0,4},{4,0},{8,12},{12,8},{16,20},{20,16},{24,28},{28,24},{1,5},{5... | collective-permute-start | bytes 1966088 | tf_op jit(solution)/shard_map/ppermute | solution.py:42
  159.7 22.1 %collective-permute-start.5 = (bf16[2,2,5,32,512]{4,3,2,1,0:T(8,128)(2,1)S(1)}, bf16[2,2,5,32,512]{4,3,2,1,0:T(8,128)(2,1)S(1)}, u32[]{:S(2)}, u32[]{:S(2)}) collective-permute-start(bf16[2,2,5,32,512]{4,3,2,1,0:T(8,128)(2,1)S(1)} %get-tuple-element.82), channel_id=1, source_target_pairs={{0,2},{1,3},{2,0},{3,1},{4,6},{5,7},{6,4},{7,5},{8,10},{9,11},{10,... | collective-permute-start | bytes 1966088 | tf_op jit(solution)/shard_map/ppermute | solution.py:42
  187.0 38.1 %collective-permute-start.14 = (bf16[2,2,5,32,512]{4,3,2,1,0:T(8,128)(2,1)}, bf16[2,2,5,32,512]{4,3,2,1,0:T(8,128)(2,1)S(1)}, u32[]{:S(2)}, u32[]{:S(2)}) collective-permute-start(bf16[2,2,5,32,512]{4,3,2,1,0:T(8,128)(2,1)} %get-tuple-element.79.refs_5_), channel_id=1, source_target_pairs={{0,4},{4,0},{8,12},{12,8},{16,20},{20,16},{24,28},{28,24},{1,5},{5... | collective-permute-start | bytes 1966088 | tf_op jit(solution)/shard_map/ppermute | solution.py:42
  190.2 14.6 %collective-permute-start.8 = (f32[48,1152]{1,0:T(8,128)S(1)}, f32[48,1152]{1,0:T(8,128)S(1)}, u32[]{:S(2)}, u32[]{:S(2)}) collective-permute-start(f32[48,1152]{1,0:T(8,128)S(1)} %add_add_fusion.2), channel_id=1, source_target_pairs={{0,24},{4,28},{8,16},{12,20},{16,8},{20,12},{24,0},{28,4},{1,25},{... | collective-permute-start | bytes 663560 | tf_op jit(solution)/shard_map/ppermute | solution.py:42
  193.1 20.6 %collective-permute-start.7 = (f32[48,1152]{1,0:T(8,128)S(1)}, f32[48,1152]{1,0:T(8,128)S(1)}, u32[]{:S(2)}, u32[]{:S(2)}) collective-permute-start(f32[48,1152]{1,0:T(8,128)S(1)} %add_add_fusion.2), channel_id=1, source_target_pairs={{0,16},{4,20},{8,24},{12,28},{16,0},{20,4},{24,8},{28,12},{1,17},{... | collective-permute-start | bytes 663560 | tf_op jit(solution)/shard_map/ppermute | solution.py:42
  195.4 19.1 %collective-permute-start.6 = (f32[48,1152]{1,0:T(8,128)S(1)}, f32[48,1152]{1,0:T(8,128)S(1)}, u32[]{:S(2)}, u32[]{:S(2)}) collective-permute-start(f32[48,1152]{1,0:T(8,128)S(1)} %add_add_fusion.2), channel_id=1, source_target_pairs={{0,8},{4,12},{8,0},{12,4},{16,24},{20,28},{24,16},{28,20},{1,9},{5... | collective-permute-start | bytes 663560 | tf_op jit(solution)/shard_map/ppermute | solution.py:42
  195.4 29.6 %collective-permute-start.15 = (bf16[2,2,5,32,512]{4,3,2,1,0:T(8,128)(2,1)S(1)}, bf16[2,2,5,32,512]{4,3,2,1,0:T(8,128)(2,1)S(1)}, u32[]{:S(2)}, u32[]{:S(2)}) collective-permute-start(bf16[2,2,5,32,512]{4,3,2,1,0:T(8,128)(2,1)S(1)} %copy-done.5), channel_id=1, source_target_pairs={{0,2},{1,3},{2,0},{3,1},{4,6},{5,7},{6,4},{7,5},{8,10},{9,11},{10,... | collective-permute-start | bytes 1966088 | tf_op jit(solution)/shard_map/ppermute | solution.py:42
  204.8 22.4 %collective-permute-start.12 = (bf16[2,2,5,32,512]{4,3,2,1,0:T(8,128)(2,1)S(1)}, bf16[2,2,5,32,512]{4,3,2,1,0:T(8,128)(2,1)S(1)}, u32[]{:S(2)}, u32[]{:S(2)}) collective-permute-start(bf16[2,2,5,32,512]{4,3,2,1,0:T(8,128)(2,1)S(1)} %copy-done.14), channel_id=1, source_target_pairs={{0,2},{1,3},{2,0},{3,1},{4,6},{5,7},{6,4},{7,5},{8,10},{9,11},{10,... | collective-permute-start | bytes 1966088 | tf_op jit(solution)/shard_map/ppermute | solution.py:42
  213.7 16.7 %collective-permute-start.13 = (bf16[2,2,5,32,512]{4,3,2,1,0:T(8,128)(2,1)S(1)}, bf16[2,2,5,32,512]{4,3,2,1,0:T(8,128)(2,1)S(1)}, u32[]{:S(2)}, u32[]{:S(2)}) collective-permute-start(bf16[2,2,5,32,512]{4,3,2,1,0:T(8,128)(2,1)S(1)} %copy-done.3), channel_id=1, source_target_pairs={{0,4},{4,0},{8,12},{12,8},{16,20},{20,16},{24,28},{28,24},{1,5},{5... | collective-permute-start | bytes 1966088 | tf_op jit(solution)/shard_map/ppermute | solution.py:42
  214.5 46.3 %collective-permute-start.11 = (bf16[8,5,40,512]{3,2,1,0:T(8,128)(2,1)S(1)}, bf16[8,5,40,512]{3,2,1,0:T(8,128)(2,1)S(1)}, u32[]{:S(2)}, u32[]{:S(2)}) collective-permute-start(bf16[8,5,40,512]{3,2,1,0:T(8,128)(2,1)S(1)} %broadcast_multiply_fusion.2), channel_id=1, source_target_pairs={{0,2},{1,3},{2,0},{3,1},{4,6},{5,7},{6,4},{7,5},{8,10},{9,11},{10,... | collective-permute-start | bytes 4915208 | tf_op jit(solution)/shard_map/ppermute | solution.py:42
  230.7 27.4 %collective-permute-start.16 = (bf16[2,5,32,512]{3,2,1,0:T(8,128)(2,1)S(1)}, bf16[2,5,32,512]{3,2,1,0:T(8,128)(2,1)S(1)}, u32[]{:S(2)}, u32[]{:S(2)}) collective-permute-start(bf16[2,5,32,512]{3,2,1,0:T(8,128)(2,1)S(1)} %pad_maximum_fusion.3.refs_6_), channel_id=1, source_target_pairs={{0,8},{4,12},{8,0},{12,4},{16,24},{20,28},{24,16},{28,20},{1,9},{5... | collective-permute-start | bytes 983048 | tf_op jit(solution)/shard_map/ppermute | solution.py:42
  230.8 27.3 %collective-permute-start.17 = (bf16[2,5,32,512]{3,2,1,0:T(8,128)(2,1)S(1)}, bf16[2,5,32,512]{3,2,1,0:T(8,128)(2,1)S(1)}, u32[]{:S(2)}, u32[]{:S(2)}) collective-permute-start(bf16[2,5,32,512]{3,2,1,0:T(8,128)(2,1)S(1)} %pad_maximum_fusion.4.refs_7_), channel_id=1, source_target_pairs={{0,16},{4,20},{8,24},{12,28},{16,0},{20,4},{24,8},{28,12},{1,17},{... | collective-permute-start | bytes 983048 | tf_op jit(solution)/shard_map/ppermute | solution.py:42
  233.7 24.5 %collective-permute-start.18 = (bf16[2,5,32,512]{3,2,1,0:T(8,128)(2,1)S(1)}, bf16[2,5,32,512]{3,2,1,0:T(8,128)(2,1)S(1)}, u32[]{:S(2)}, u32[]{:S(2)}) collective-permute-start(bf16[2,5,32,512]{3,2,1,0:T(8,128)(2,1)S(1)} %pad_maximum_fusion.5.refs_8_), channel_id=1, source_target_pairs={{0,24},{4,28},{8,16},{12,20},{16,8},{20,12},{24,0},{28,4},{1,25},{... | collective-permute-start | bytes 983048 | tf_op jit(solution)/shard_map/ppermute | solution.py:42
  261.0 24.4 %collective-permute-start.20 = (bf16[2,5,32,512]{3,2,1,0:T(8,128)(2,1)S(1)}, bf16[2,5,32,512]{3,2,1,0:T(8,128)(2,1)S(1)}, u32[]{:S(2)}, u32[]{:S(2)}) collective-permute-start(bf16[2,5,32,512]{3,2,1,0:T(8,128)(2,1)S(1)} %add_convert_fusion.2.refs_5_), channel_id=1, source_target_pairs={{0,8},{4,12},{8,0},{12,4},{16,24},{20,28},{24,16},{28,20},{1,9},{5... | collective-permute-start | bytes 983048 | tf_op jit(solution)/shard_map/ppermute | solution.py:42
  264.6 30.6 %collective-permute-start.22 = (bf16[2,5,32,512]{3,2,1,0:T(8,128)(2,1)S(1)}, bf16[2,5,32,512]{3,2,1,0:T(8,128)(2,1)S(1)}, u32[]{:S(2)}, u32[]{:S(2)}) collective-permute-start(bf16[2,5,32,512]{3,2,1,0:T(8,128)(2,1)S(1)} %add_convert_fusion.2.refs_5_), channel_id=1, source_target_pairs={{0,24},{4,28},{8,16},{12,20},{16,8},{20,12},{24,0},{28,4},{1,25},{... | collective-permute-start | bytes 983048 | tf_op jit(solution)/shard_map/ppermute | solution.py:42
  266.4 28.8 %collective-permute-start.21 = (bf16[2,5,32,512]{3,2,1,0:T(8,128)(2,1)S(1)}, bf16[2,5,32,512]{3,2,1,0:T(8,128)(2,1)S(1)}, u32[]{:S(2)}, u32[]{:S(2)}) collective-permute-start(bf16[2,5,32,512]{3,2,1,0:T(8,128)(2,1)S(1)} %add_convert_fusion.2.refs_5_), channel_id=1, source_target_pairs={{0,16},{4,20},{8,24},{12,28},{16,0},{20,4},{24,8},{28,12},{1,17},{... | collective-permute-start | bytes 983048 | tf_op jit(solution)/shard_map/ppermute | solution.py:42
  295.3 17.7 %collective-permute-start.23 = (bf16[4,5,32,512]{3,2,1,0:T(8,128)(2,1)S(1)}, bf16[4,5,32,512]{3,2,1,0:T(8,128)(2,1)S(1)}, u32[]{:S(2)}, u32[]{:S(2)}) collective-permute-start(bf16[4,5,32,512]{3,2,1,0:T(8,128)(2,1)S(1)} %pad_maximum_fusion.1.refs_5_.refs_0_), channel_id=1, source_target_pairs={{0,4},{4,0},{8,12},{12,8},{16,20},{20,16},{24,28},{28,24},{1,5},{5... | collective-permute-start | bytes 1966088 | tf_op jit(solution)/shard_map/ppermute | solution.py:42
  296.3 17.7 %collective-permute-start.24 = (bf16[4,5,32,512]{3,2,1,0:T(8,128)(2,1)S(1)}, bf16[4,5,32,512]{3,2,1,0:T(8,128)(2,1)S(1)}, u32[]{:S(2)}, u32[]{:S(2)}) collective-permute-start(bf16[4,5,32,512]{3,2,1,0:T(8,128)(2,1)S(1)} %pad_maximum_fusion.2.refs_6_.refs_8_), channel_id=1, source_target_pairs={{0,2},{1,3},{2,0},{3,1},{4,6},{5,7},{6,4},{7,5},{8,10},{9,11},{10,... | collective-permute-start | bytes 1966088 | tf_op jit(solution)/shard_map/ppermute | solution.py:42
  296.9 29.4 %collective-permute-start.28 = (bf16[4,5,32,512]{3,2,1,0:T(8,128)(2,1)S(1)}, bf16[4,5,32,512]{3,2,1,0:T(8,128)(2,1)S(1)}, u32[]{:S(2)}, u32[]{:S(2)}) collective-permute-start(bf16[4,5,32,512]{3,2,1,0:T(8,128)(2,1)S(1)} %pad_maximum_fusion.1.refs_5_.refs_0_), channel_id=1, source_target_pairs={{0,2},{1,3},{2,0},{3,1},{4,6},{5,7},{6,4},{7,5},{8,10},{9,11},{10,... | collective-permute-start | bytes 1966088 | tf_op jit(solution)/shard_map/ppermute | solution.py:42
  298.4 29.3 %collective-permute-start.30 = (bf16[4,5,32,512]{3,2,1,0:T(8,128)(2,1)S(1)}, bf16[4,5,32,512]{3,2,1,0:T(8,128)(2,1)S(1)}, u32[]{:S(2)}, u32[]{:S(2)}) collective-permute-start(bf16[4,5,32,512]{3,2,1,0:T(8,128)(2,1)S(1)} %pad_maximum_fusion.1.refs_5_.refs_0_), channel_id=1, source_target_pairs={{0,1},{1,0},{2,3},{3,2},{4,5},{5,4},{6,7},{7,6},{8,9},{9,8},{10,11... | collective-permute-start | bytes 1966088 | tf_op jit(solution)/shard_map/ppermute | solution.py:42
  298.4 30.0 %collective-permute-start.35 = (bf16[4,5,32,512]{3,2,1,0:T(8,128)(2,1)S(1)}, bf16[4,5,32,512]{3,2,1,0:T(8,128)(2,1)S(1)}, u32[]{:S(2)}, u32[]{:S(2)}) collective-permute-start(bf16[4,5,32,512]{3,2,1,0:T(8,128)(2,1)S(1)} %pad_maximum_fusion.2.refs_6_.refs_8_), channel_id=1, source_target_pairs={{0,4},{4,0},{8,12},{12,8},{16,20},{20,16},{24,28},{28,24},{1,5},{5... | collective-permute-start | bytes 1966088 | tf_op jit(solution)/shard_map/ppermute | solution.py:42
  313.1 17.4 %collective-permute-start.33 = (bf16[4,5,32,512]{3,2,1,0:T(8,128)(2,1)S(1)}, bf16[4,5,32,512]{3,2,1,0:T(8,128)(2,1)S(1)}, u32[]{:S(2)}, u32[]{:S(2)}) collective-permute-start(bf16[4,5,32,512]{3,2,1,0:T(8,128)(2,1)S(1)} %pad_maximum_fusion.2.refs_6_.refs_8_), channel_id=1, source_target_pairs={{0,1},{1,0},{2,3},{3,2},{4,5},{5,4},{6,7},{7,6},{8,9},{9,8},{10,11... | collective-permute-start | bytes 1966088 | tf_op jit(solution)/shard_map/ppermute | solution.py:42
  326.3 14.5 %collective-permute-start.32 = (bf16[4,5,32,512]{3,2,1,0:T(8,128)(2,1)S(1)}, bf16[4,5,32,512]{3,2,1,0:T(8,128)(2,1)S(1)}, u32[]{:S(2)}, u32[]{:S(2)}) collective-permute-start(bf16[4,5,32,512]{3,2,1,0:T(8,128)(2,1)S(1)} %collective-permute-done.28.refs_2_), channel_id=1, source_target_pairs={{0,1},{1,0},{2,3},{3,2},{4,5},{5,4},{6,7},{7,6},{8,9},{9,8},{10,11... | collective-permute-start | bytes 1966088 | tf_op jit(solution)/shard_map/ppermute | solution.py:42
  339.0 16.4 %collective-permute-start.29 = (bf16[4,5,32,512]{3,2,1,0:T(8,128)(2,1)S(1)}, bf16[4,5,32,512]{3,2,1,0:T(8,128)(2,1)S(1)}, u32[]{:S(2)}, u32[]{:S(2)}) collective-permute-start(bf16[4,5,32,512]{3,2,1,0:T(8,128)(2,1)S(1)} %collective-permute-done.23.refs_5_.refs_1_), channel_id=1, source_target_pairs={{0,2},{1,3},{2,0},{3,1},{4,6},{5,7},{6,4},{7,5},{8,10},{9,11},{10,... | collective-permute-start | bytes 1966088 | tf_op jit(solution)/shard_map/ppermute | solution.py:42
  339.5 16.1 %collective-permute-start.38 = (bf16[4,5,32,512]{3,2,1,0:T(8,128)(2,1)S(1)}, bf16[4,5,32,512]{3,2,1,0:T(8,128)(2,1)S(1)}, u32[]{:S(2)}, u32[]{:S(2)}) collective-permute-start(bf16[4,5,32,512]{3,2,1,0:T(8,128)(2,1)S(1)} %collective-permute-done.24.refs_6_.refs_9_), channel_id=1, source_target_pairs={{0,4},{4,0},{8,12},{12,8},{16,20},{20,16},{24,28},{28,24},{1,5},{5... | collective-permute-start | bytes 1966088 | tf_op jit(solution)/shard_map/ppermute | solution.py:42
  (56 other events, 669.8 us)

commit v9 on v8

--- a/solution.py
+++ b/solution.py
@@ -491,22 +491,51 @@
 
 def joined(parts, token):
     one = (1.0 + token).astype(BF)
-    return jnp.concatenate([part * one for part in parts])
+    return jnp.stack([part * one for part in parts], axis=1)
+
+
+def pack(small, total_rows):
+    rounded = lax.reduce_precision(small, 8, 7)
+    rest = small[-total_rows:] - rounded[-total_rows:]
+    return jnp.concatenate([rounded.astype(BF), rest.astype(BF)], axis=0)
+
+
+def small_sum(small, total_rows, sends):
+    packed = pack(small, total_rows)
+    rounded = lax.reduce_precision(small, 8, 7)
+    rest = lax.reduce_precision(small[-total_rows:] - rounded[-total_rows:], 8, 7)
+    terms = [(rounded, rest)]
+    for send in sends:
+        got = send(packed).astype(F32)
+        terms.append((got[:-total_rows], got[-total_rows:]))
+    while len(terms) > 1:
+        terms = [
+            (left[0] + right[0], left[1] + right[1]) for left, right in zip(terms[::2], terms[1::2])
+        ]
+    total, rest = terms[0]
+    return jnp.concatenate([total[:-total_rows], total[-total_rows:] + rest], axis=0)
 
 
 def assemble_kernel(layer_count, own_ref, *refs):
-    blocks = refs[:16]
-    strip_ref, cross_ref, first_ref, second_ref = refs[16:]
+    blocks = refs[:10]
+    strip_ref, cross_ref, first_ref, second_ref = refs[10:]
     matrix = pl.program_id(0)
 
     def fill(out_ref):
-        for block, ref in enumerate(blocks):
-            chunk, core, upper = block >> 3, (block >> 2) & 1, block & 3
-            count, _, rows, lanes = ref.shape
-            for at in range(count):
-                piece = 4 * count * core + chunk_place(count * upper + at, chunk == 1)
-                first = pl.multiple_of((piece ^ own_ref[0]) * rows, rows)
-                out_ref[0, pl.ds(first, rows), chunk * lanes : (chunk + 1) * lanes] = ref[at, 0].astype(F32)
+        def put(core, chunk, upper, at, value):
+            rows, lanes = value.shape
+            piece = 16 * core + chunk_place(4 * upper + at, chunk == 1)
+            first = pl.multiple_of((piece ^ own_ref[0]) * rows, rows)
+            out_ref[0, pl.ds(first, rows), chunk * lanes : (chunk + 1) * lanes] = value.astype(F32)
+
+        for core in range(2):
+            refs_here = blocks[5 * core : 5 * core + 5]
+            for at in range(4):
+                for ref, uppers in zip(refs_here[:3], ((0, 0), (1, 2), (2, 1))):
+                    for chunk in range(2):
+                        put(core, chunk, uppers[chunk], at, ref[chunk, at, 0])
+                for chunk in range(2):
+                    put(core, chunk, 3, at, refs_here[3 + chunk][at, 0])
         height, width = out_ref.shape[1:]
         if width > MAIN:
             extra = width - MAIN
@@ -532,13 +561,13 @@
 def assemble(blocks, strips, own, layer_count, width, hidden):
     matrix_count = layer_count + 2
     size = strips.shape[2]
-    shape = blocks[0].shape
-    block = pl.BlockSpec(shape[:1] + (1,) + shape[2:], lambda m: (0, m, 0, 0))
+    both = pl.BlockSpec(blocks[0].shape[:2] + (1,) + blocks[0].shape[3:], lambda m: (0, 0, m, 0, 0))
+    single = pl.BlockSpec(blocks[3].shape[:1] + (1,) + blocks[3].shape[2:], lambda m: (0, m, 0, 0))
     return pl.pallas_call(
         functools.partial(assemble_kernel, layer_count),
         grid=(matrix_count,),
         in_specs=[pl.BlockSpec(memory_space=pltpu.SMEM)]
-        + [block] * 16
+        + ([both] * 3 + [single] * 2) * 2
         + [pl.BlockSpec((1, 8, size), lambda m: (m, 0, 0))],
         out_specs=[
             pl.BlockSpec((1, width, width), lambda m: (jnp.minimum(m, layer_count - 1), 0, 0)),
@@ -682,27 +711,32 @@
         return 0.0 * value.astype(F32)
 
     small = jnp.concatenate([strips.reshape(matrix_count * 8, size), sums], axis=0)
+    total_rows = sums.shape[0]
+
+    def small_step(value, masks):
+        return small_sum(
+            value, total_rows, [functools.partial(swap_both, rep_mask=r, tab_mask=t) for r, t in masks]
+        )
+
     got = swap(send, "rep", 1)
-    small = small + swap(small, "rep", 1)
     ahead = [added((keep[at, 1, 1], got[at, 1, 1])).astype(BF) for at in range(2)]
     first = [swap(ahead[at], *HALVES[at][0]) for at in range(2)]
+    small = small_step(small + zero_of(ahead[0][0, 0, 0, 0, 0]) + zero_of(ahead[1][0, 0, 0, 0, 0]), [(1, 0)])
+    small = small_step(small, [(2, 0), (0, 1), (2, 1)])
     keep, got, _ = lax.optimization_barrier((keep, got, ahead))
     behind = [added((keep[at, 1, 0], got[at, 1, 0])).astype(BF) for at in range(2)]
     later = [swap(behind[at], *HALVES[at][0]) for at in range(2)]
     keep, got, _ = lax.optimization_barrier((keep, got, behind))
     kept = [added((keep[at, 0], got[at, 0])) for at in range(2)]
-    sends = [added((kept[at][1], first[at])).astype(BF) for at in range(2)]
+    ready = zero_of(small[0, 0])
+    sends = [added((kept[at][1], first[at]), ready).astype(BF) for at in range(2)]
     sent = [swap(sends[at], *HALVES[at][1]) for at in range(2)]
-    small = small + zero_of(sends[0][0, 0, 0, 0, 0])
-    small = added([small] + [swap(small, "tab", mask) for mask in (2, 4, 6)])
     returned = gate(returned, sends[0][0, 0, 0, 0, 0] + sends[1][0, 0, 0, 0, 0])
     near_grads = near_parts(returned)
     add_next(True, 1, behind + sends)
     bases = far_bases(gate(returned, token))
     add_next(True, NEAR_FIRST - 1, sends)
     sources = [[kept[at][0], later[at], sent[at]] for at in range(2)]
-
-    token = token + zero_of(small[0, 0])
 
     def take_far(high, low):
         both = [added([part[high, low] for part in sources[at]], token) for at in range(2)]
@@ -719,25 +753,24 @@
     parts = [piece, swap(piece, "tab", 2), swap(piece, "tab", 4), swap(piece, "tab", 6)]
     far_grads = far_parts([gate(part, piece[0, 0, 0, 0]) for part in bases])
     add_next(False, FAR_FIRST, [piece])
-    values = [joined([part[at : at + 1] for part in parts], token) for at in range(2)]
-    near = [swap(values[at], *HALVES[at][1]) for at in range(2)]
-    across = [swap(values[at], *HALVES[at][0]) for at in range(2)]
-    add_next(False, 1, values)
-    both = [swap(near[at], *HALVES[at][0]) for at in range(2)]
-    add_next(False, 1, near)
-    small = small + zero_of(token)
-    small = added([small, swap(small, "rep", 2), swap(small, "tab", 1), swap_both(small, 2, 1)])
-    for axis, known in (("rep", 2), ("tab", 3)):
-        for mask in masks_of(axis)[known:]:
-            small = small + swap(small, axis, mask)
-    other = []
-    for at in range(2):
-        other.append([swap(part, "rep", 1) for part in (values[at], near[at], across[at])])
-    add_next(False, slot_count, other[0] + other[1])
-    blocks = []
-    for at in range(2):
-        last = gate(both[at], token)
-        blocks += [values[at], near[at], across[at], last] + other[at] + [swap(last, "rep", 1)]
+    values = joined(parts, token)
+    from_y = swap(values, "tab", 1)
+    from_x = swap(values, "rep", 2)
+    small = small + zero_of(values[0, 0, 0, 0, 0])
+    small = small_step(small, [(0, 2), (0, 4), (0, 6)])
+    for rep_mask in masks_of("rep")[2:]:
+        small = small_step(small, [(rep_mask, 0)])
+    for tab_mask in masks_of("tab")[3:]:
+        small = small_step(small, [(0, tab_mask)])
+    add_next(False, 1, [values])
+    other = [swap(values, "rep", 1)]
+    add_next(False, 1, other)
+    token = token + zero_of(small[0, 0])
+    last = [swap(from_y[0], "rep", 2), swap(from_x[1], "tab", 1)]
+    other += [swap(from_y, "rep", 1), swap(from_x, "rep", 1)]
+    add_next(False, slot_count, other)
+    last = [gate(part, token) for part in last]
+    blocks = [values, from_y, from_x] + last + other + [swap(part, "rep", 1) for part in last]
 
     strips = small[:-8].reshape(matrix_count, 8, size)
     sums = small[-8:]

time: 379 us -> 372 us (0.982)
  waiting for transfers between devices: 62.5 us -> 51.1 us
  starting transfers between devices: 60.2 us -> 54.3 us
  local copies, waits for them, and re-layouts: 29.3 us -> 34.2 us
    ppermute x39 -> x28, waiting for transfers between devices: 55.7 us -> 32.7 us  [swap(): lax.ppermute(value, axis, [(at, at ^ mask) for at in range(lax.axis_size(...]
    ppermute x1 -> x7, waiting for transfers between devices: 0.01 us -> 12.4 us  [swap_both(): return lax.ppermute(value, ('tab', 'rep'), perm)]
    ppermute x39 -> x28, starting transfers between devices: 33.7 us -> 24.6 us  [swap(): lax.ppermute(value, axis, [(at, at ^ mask) for at in range(lax.axis_size(...]
    ppermute x1 -> x7, starting transfers between devices: 0.76 us -> 8.08 us  [swap_both(): return lax.ppermute(value, ('tab', 'rep'), perm)]
    all_to_all x2, starting transfers between devices: 12.6 us -> 7.93 us  [on_device(): lax.all_to_all(looked, 'tab', split_axis=0, concat_axis=0, tiled=True)]
  transfers between devices with their start and end apart: 44 -> 39, of which waited for: 18 -> 10; matrix products, arithmetic and copies ran while one was open for 12% -> 13% of each run, Pallas kernels for 31% -> 33%
where the time goes in v9:
time: 372 us; the launch traced here: 368 us
  Pallas kernels  189 us (51%)
  starting transfers between devices  54.3 us (15%)
  waiting for transfers between devices  51.1 us (14%)
  local copies, waits for them, and re-layouts  34.2 us (9%)
  other arithmetic  26.8 us (7%)
  between operations  12.4 us (3%)
    pallas_call x10, Pallas kernels, add_rows(): pl.pallas_call(functools.partial(add_kernel, part_count, accumulate), gri...  82.5 us
    pallas_call x2, Pallas kernels, lookup(): pl.pallas_call(functools.partial(lookup_kernel, first_slot), in_specs=[sm...  43.3 us
    ppermute x28, waiting for transfers between devices, swap(): lax.ppermute(value, axis, [(at, at ^ mask) for at in range(lax.axis_size(...  32.7 us
    pallas_call x1, Pallas kernels, dense_step(): pl.pallas_call(functools.partial(dense_kernel, dense_width, width, starts...  27.6 us
    ppermute x28, starting transfers between devices, swap(): lax.ppermute(value, axis, [(at, at ^ mask) for at in range(lax.axis_size(...  24.6 us
    pallas_call x2, Pallas kernels, weight_parts(): pl.pallas_call(functools.partial(weight_kernel, core), grid=(matrix_count...  22.2 us
    unnamed x93, local copies, waits for them, and re-layouts  14.2 us
    pallas_call x1, Pallas kernels, assemble(): pl.pallas_call(functools.partial(assemble_kernel, layer_count), grid=(mat...  13.3 us
  transfers between devices with their start and end apart: 39, of which 10 were waited for; matrix products, arithmetic and copies ran while one was open for 13% of the time, Pallas kernels for 33%

profile of v9, /device:TPU:0, one launch (start us, length us, event | category | flops | bytes accessed | tf_op | source)
XLA Modules:
  0.0 367.7 jit_solution(10942599324683069959)
XLA Ops:
  5.2 7.3 %all-to-all-start = ((s32[8,5,512]{2,1,0:T(8,128)}), s32[8,5,512]{2,1,0:T(8,128)S(1)}, u32[]{:S(2)}, u32[]{:S(2)}) async-start(s32[8,5,512]{2,1,0:T(8,128)} %reshape.524), calls=%async_computation | async-start | bytes 262144 | tf_op jit(solution)/shard_map/all_to_all | solution.py:621
  13.8 6.0 %all-to-all-done = s32[8,5,512]{2,1,0:T(8,128)S(1)} async-done(((s32[8,5,512]{2,1,0:T(8,128)}), s32[8,5,512]{2,1,0:T(8,128)S(1)}, u32[]{:S(2)}, u32[]{:S(2)}) %all-to-all-start) | async-done | bytes 81952 | tf_op jit(solution)/shard_map/all_to_all | solution.py:621
  20.5 18.7 %lookup.2 = bf16[8,2,40,512]{3,2,1,0:T(8,128)(2,1)} custom-call(s32[20480]{0:T(1024)} %bitcast.160, s32[5]{0:T(128)} %dynamic_slice.3.rows_ref, bf16[5,39,32768]{2,1,0:T(8,128)(2,1)} %table_hbm.3), custom_call_target="tpu_custom_call" | custom-call | flops 20132660 | bytes 5750 | tf_op jit(solution)/shard_map/lookup/pallas_call | solution.py:112
  39.3 3.6 all-to-all-start.1
  44.7 24.5 %lookup.3 = bf16[8,3,40,512]{3,2,1,0:T(8,128)(2,1)} custom-call(s32[20480]{0:T(1024)} %bitcast.161, s32[5]{0:T(128)} %dynamic_slice.3.rows_ref, bf16[5,39,32768]{2,1,0:T(8,128)(2,1)} %table_hbm.3), custom_call_target="tpu_custom_call" | custom-call | flops 30198988 | bytes 8626 | tf_op jit(solution)/shard_map/lookup/pallas_call | solution.py:112
  69.3 4.4 %all-to-all-start.2 = ((bf16[8,3,40,512]{3,2,1,0:T(8,128)(2,1)}), bf16[8,3,40,512]{3,2,1,0:T(8,128)(2,1)S(1)}, u32[]{:S(2)}, u32[]{:S(2)}) async-start(bf16[8,3,40,512]{3,2,1,0:T(8,128)(2,1)} %lookup.3), calls=%async_computation.2 | async-start | bytes 1966080 | tf_op jit(solution)/shard_map/all_to_all | solution.py:633
  77.2 3.5 multiply_bitcast_fusion
  97.9 27.6 %dense.1 = (f32[1,512]{1,0:T(1,128)}, f32[16,512]{1,0:T(8,128)}, bf16[40,40,512]{2,1,0:T(8,128)(2,1)}, bf16[5,1152,512]{2,1,0:T(8,128)(2,1)}, bf16[5,1152,512]{2,1,0:T(8,128)(2,1)}, /*index=5*/f32[8,1152]{1,0:T(8,128)}) custom-call(s32[26]{0:T(128)} %place_ref.1, f32[1]{0:T(128)S(6)} %convert.63.bias_ref, bf16[8,2,40,512]{3,2,1,0:T(8,128)(2,1)} %copy-done.20, ...), custom_call_target="tpu_custom_call" | custom-call | flops 13589544 | bytes 30965 | tf_op jit(solution)/shard_map/dense/pallas_call | solution.py:379
  125.5 9.7 %weight_parts.3 = bf16[2,16,5,32,512]{4,3,2,1,0:T(8,128)(2,1)} custom-call(s32[1]{0:T(128)} %bitcast.own_ref, bf16[5,1152,512]{2,1,0:T(8,128)(2,1)} %get-tuple-element.42.left_ref, bf16[5,1152,512]{2,1,0:T(8,128)(2,1)} %get-tuple-element.43.right_ref), custom_call_target="tpu_custom_call" | custom-call | flops 3397386 | bytes 33177 | tf_op jit(solution)/shard_map/weight_parts/pallas_call | solution.py:461
  135.5 6.4 %all-to-all-start.3 = ((bf16[8,5,40,512]{3,2,1,0:T(8,128)(2,1)}), bf16[8,5,40,512]{3,2,1,0:T(8,128)(2,1)S(1)}, u32[]{:S(2)}, u32[]{:S(2)}) async-start(bf16[8,5,40,512]{3,2,1,0:T(8,128)(2,1)} %bitcast.35), calls=%async_computation.3 | async-start | bytes 3276800 | tf_op jit(solution)/shard_map/all_to_all | solution.py:669
  142.0 12.5 %weight_parts.2 = (f32[2,16,5,32,512]{4,3,2,1,0:T(8,128)}, f32[5,8,1152]{2,1,0:T(8,128)}) custom-call(s32[1]{0:T(128)} %bitcast.own_ref, bf16[5,1152,512]{2,1,0:T(8,128)(2,1)} %get-tuple-element.42.left_ref, bf16[5,1152,512]{2,1,0:T(8,128)(2,1)} %get-tuple-element.43.right_ref), custom_call_target="tpu_custom_call" | custom-call | flops 3397386 | bytes 33177 | tf_op jit(solution)/shard_map/weight_parts/pallas_call | solution.py:461
  154.4 2.7 fusion.10
  163.2 3.6 fusion.8
  170.6 3.0 convert_add_fusion.1
  173.7 6.5 %collective-permute-done.7 = bf16[56,1152]{1,0:T(8,128)(2,1)S(1)} collective-permute-done((bf16[56,1152]{1,0:T(8,128)(2,1)S(1)}, bf16[56,1152]{1,0:T(8,128)(2,1)S(1)}, u32[]{:S(2)}, u32[]{:S(2)}) %collective-permute-start.7) | collective-permute-done | bytes 129056 | tf_op jit(solution)/shard_map/ppermute | solution.py:51
  180.2 5.8 %collective-permute-done.6 = bf16[56,1152]{1,0:T(8,128)(2,1)S(1)} collective-permute-done((bf16[56,1152]{1,0:T(8,128)(2,1)S(1)}, bf16[56,1152]{1,0:T(8,128)(2,1)S(1)}, u32[]{:S(2)}, u32[]{:S(2)}) %collective-permute-start.6) | collective-permute-done | bytes 129056 | tf_op jit(solution)/shard_map/ppermute | solution.py:51
  199.9 7.4 %add_rows.10 = (f32[5,39,8192]{2,1,0:T(8,128)}, f32[8,128]{1,0:T(8,128)S(1)}) custom-call(s32[1]{0:T(128)} %bitcast.34.base_ref, s32[8,5,1,512]{3,2,1,0:T(1,128)S(1)} %copy-done.6, s32[8,5,1,512]{3,2,1,0:T(1,128)S(1)} %copy-done.7, bf16[8,5,40,512]{3,2,1,0:T(8,128)(2,1)S(1)} %broadcast_multiply_fusion.3.refs_2_, ...), custom_call_target="tpu_custom_call" | custom-call | flops 5234491 | bytes 1916 | tf_op jit(solution)/shard_map/add_rows/pallas_call | solution.py:185
  207.3 7.5 %add_rows.11 = (f32[5,39,8192]{2,1,0:T(8,128)}, f32[8,128]{1,0:T(8,128)S(1)}) custom-call(s32[1]{0:T(128)} %bitcast.34.base_ref, s32[8,5,1,512]{3,2,1,0:T(1,128)S(1)} %copy-done.6, s32[8,5,1,512]{3,2,1,0:T(1,128)S(1)} %copy-done.7, bf16[8,5,40,512]{3,2,1,0:T(8,128)(2,1)S(1)} %broadcast_multiply_fusion.3.refs_2_, ...), custom_call_target="tpu_custom_call", output_to_operand_aliasing={{0}: (5, {})} | custom-call | flops 5234491 | bytes 1916 | tf_op jit(solution)/shard_map/add_rows/pallas_call | solution.py:185
  218.1 6.5 %collective-permute-done.8 = bf16[2,2,5,32,512]{4,3,2,1,0:T(8,128)(2,1)S(1)} collective-permute-done((bf16[2,2,5,32,512]{4,3,2,1,0:T(8,128)(2,1)S(1)}, bf16[2,2,5,32,512]{4,3,2,1,0:T(8,128)(2,1)S(1)}, u32[]{:S(2)}, u32[]{:S(2)}) %collective-permute-start.8) | collective-permute-done | bytes 655392 | tf_op jit(solution)/shard_map/ppermute | solution.py:42
  225.6 3.0 collective-permute-start.17
  232.0 7.4 %add_rows.12 = (f32[5,39,8192]{2,1,0:T(8,128)}, f32[8,128]{1,0:T(8,128)}) custom-call(s32[1]{0:T(128)} %bitcast.34.base_ref, s32[8,5,1,512]{3,2,1,0:T(1,128)S(1)} %copy-done.6, s32[8,5,1,512]{3,2,1,0:T(1,128)S(1)} %copy-done.7, bf16[8,5,40,512]{3,2,1,0:T(8,128)(2,1)S(1)} %broadcast_multiply_fusion.3.refs_2_, ...), custom_call_target="tpu_custom_call", output_to_operand_aliasing={{0}: (5, {})} | custom-call | flops 5234491 | bytes 1916 | tf_op jit(solution)/shard_map/add_rows/pallas_call | solution.py:185
  239.5 7.4 %add_rows.13 = (f32[5,39,8192]{2,1,0:T(8,128)}, f32[8,128]{1,0:T(8,128)}) custom-call(s32[1]{0:T(128)} %bitcast.34.base_ref, s32[8,5,1,512]{3,2,1,0:T(1,128)S(1)} %copy-done.6, s32[8,5,1,512]{3,2,1,0:T(1,128)S(1)} %copy-done.7, bf16[8,5,40,512]{3,2,1,0:T(8,128)(2,1)S(1)} %broadcast_multiply_fusion.3.refs_2_, ...), custom_call_target="tpu_custom_call", output_to_operand_aliasing={{0}: (5, {})} | custom-call | flops 5234491 | bytes 1916 | tf_op jit(solution)/shard_map/add_rows/pallas_call | solution.py:185
  246.9 7.4 %add_rows.14 = (f32[5,39,8192]{2,1,0:T(8,128)}, f32[8,128]{1,0:T(8,128)S(1)}) custom-call(s32[1]{0:T(128)} %bitcast.34.base_ref, s32[8,5,1,512]{3,2,1,0:T(1,128)S(1)} %copy-done.6, s32[8,5,1,512]{3,2,1,0:T(1,128)S(1)} %copy-done.7, bf16[8,5,40,512]{3,2,1,0:T(8,128)(2,1)S(1)} %broadcast_multiply_fusion.3.refs_2_, ...), custom_call_target="tpu_custom_call", output_to_operand_aliasing={{0}: (5, {})} | custom-call | flops 5234491 | bytes 1916 | tf_op jit(solution)/shard_map/add_rows/pallas_call | solution.py:185
  259.6 2.8 collective-permute-start.25
  265.6 9.0 %add_rows.15 = (f32[5,39,8192]{2,1,0:T(8,128)}, f32[8,128]{1,0:T(8,128)}) custom-call(s32[1]{0:T(128)} %bitcast.34.base_ref, s32[8,5,1,512]{3,2,1,0:T(1,128)S(1)} %copy-done.8, s32[8,5,1,512]{3,2,1,0:T(1,128)S(1)} %copy-done.9, bf16[8,5,40,512]{3,2,1,0:T(8,128)(2,1)S(1)} %broadcast_multiply_fusion.1.refs_2_, ...), custom_call_target="tpu_custom_call", output_to_operand_aliasing={{0}: (5, {})} | custom-call | flops 5234491 | bytes 1916 | tf_op jit(solution)/shard_map/add_rows/pallas_call | solution.py:185
  274.6 8.8 %add_rows.16 = (f32[5,39,8192]{2,1,0:T(8,128)}, f32[8,128]{1,0:T(8,128)S(1)}) custom-call(s32[1]{0:T(128)} %bitcast.34.base_ref, s32[8,5,1,512]{3,2,1,0:T(1,128)S(1)} %copy-done.8, s32[8,5,1,512]{3,2,1,0:T(1,128)S(1)} %copy-done.9, bf16[8,5,40,512]{3,2,1,0:T(8,128)(2,1)S(1)} %broadcast_multiply_fusion.1.refs_2_, ...), custom_call_target="tpu_custom_call", output_to_operand_aliasing={{0}: (5, {})} | custom-call | flops 5234491 | bytes 1916 | tf_op jit(solution)/shard_map/add_rows/pallas_call | solution.py:185
  284.6 8.0 %collective-permute-done.24 = bf16[2,5,32,512]{3,2,1,0:T(8,128)(2,1)S(1)} collective-permute-done((bf16[2,5,32,512]{3,2,1,0:T(8,128)(2,1)S(1)}, bf16[2,5,32,512]{3,2,1,0:T(8,128)(2,1)S(1)}, u32[]{:S(2)}, u32[]{:S(2)}) %collective-permute-start.24) | collective-permute-done | bytes 327712 | tf_op jit(solution)/shard_map/ppermute | solution.py:42
  301.4 8.8 %add_rows.17 = (f32[5,39,8192]{2,1,0:T(8,128)}, f32[8,128]{1,0:T(8,128)}) custom-call(s32[1]{0:T(128)} %bitcast.34.base_ref, s32[8,5,1,512]{3,2,1,0:T(1,128)S(1)} %copy-done.8, s32[8,5,1,512]{3,2,1,0:T(1,128)S(1)} %copy-done.9, bf16[8,5,40,512]{3,2,1,0:T(8,128)(2,1)S(1)} %broadcast_multiply_fusion.1.refs_2_, ...), custom_call_target="tpu_custom_call", output_to_operand_aliasing={{0}: (5, {})} | custom-call | flops 5234491 | bytes 1916 | tf_op jit(solution)/shard_map/add_rows/pallas_call | solution.py:185
  310.4 13.3 %collective-permute-done.26.refs_1_ = bf16[2,4,5,32,512]{4,3,2,1,0:T(8,128)(2,1)S(1)} collective-permute-done((bf16[2,4,5,32,512]{4,3,2,1,0:T(8,128)(2,1)S(1)}, bf16[2,4,5,32,512]{4,3,2,1,0:T(8,128)(2,1)S(1)}, u32[]{:S(2)}, u32[]{:S(2)}) %collective-permute-start.26) | collective-permute-done | bytes 1310752 | tf_op jit(solution)/shard_map/ppermute | solution.py:42
  329.0 9.2 %add_rows.18 = (f32[5,39,8192]{2,1,0:T(8,128)}, f32[8,128]{1,0:T(8,128)}) custom-call(s32[1]{0:T(128)} %bitcast.34.base_ref, s32[8,5,1,512]{3,2,1,0:T(1,128)S(1)} %copy-done.8, s32[8,5,1,512]{3,2,1,0:T(1,128)S(1)} %copy-done.9, bf16[8,5,40,512]{3,2,1,0:T(8,128)(2,1)S(1)} %broadcast_multiply_fusion.1.refs_2_, ...), custom_call_target="tpu_custom_call", output_to_operand_aliasing={{0}: (5, {})} | custom-call | flops 5234491 | bytes 1916 | tf_op jit(solution)/shard_map/add_rows/pallas_call | solution.py:185
  338.2 9.6 %add_rows.19 = (f32[5,39,8192]{2,1,0:T(8,128)}, f32[8,128]{1,0:T(8,128)S(1)}) custom-call(s32[1]{0:T(128)} %bitcast.34.base_ref, s32[8,5,1,512]{3,2,1,0:T(1,128)S(1)} %copy-done.8, s32[8,5,1,512]{3,2,1,0:T(1,128)S(1)} %copy-done.9, bf16[8,5,40,512]{3,2,1,0:T(8,128)(2,1)S(1)} %broadcast_multiply_fusion.1.refs_2_, ...), custom_call_target="tpu_custom_call", output_to_operand_aliasing={{0}: (5, {})} | custom-call | flops 5234491 | bytes 1916 | tf_op jit(solution)/shard_map/add_rows/pallas_call | solution.py:185
  353.0 13.3 %assemble.1 = (f32[3,1027,1027]{2,1,0:T(8,128)}, f32[1,1027,1024]{2,1,0:T(8,128)}, f32[1,1024,1024]{2,1,0:T(8,128)}) custom-call(s32[1]{0:T(128)} %bitcast.own_ref, bf16[2,4,5,32,512]{4,3,2,1,0:T(8,128)(2,1)} %copy-done, bf16[2,4,5,32,512]{4,3,2,1,0:T(8,128)(2,1)} %copy-done.18, bf16[2,4,5,32,512]{4,3,2,1,0:T(8,128)(2,1)} %copy-done.19, ...), custom_call_target="tpu_custom_call" | custom-call | bytes 39813 | tf_op jit(solution)/shard_map/assemble/pallas_call | solution.py:566
  (272 shorter events, 79.9 us)
Async XLA Ops:
  5.2 14.6 %all-to-all-start = ((s32[8,5,512]{2,1,0:T(8,128)}), s32[8,5,512]{2,1,0:T(8,128)S(1)}, u32[]{:S(2)}, u32[]{:S(2)}) async-start(s32[8,5,512]{2,1,0:T(8,128)} %reshape.524), calls=%async_computation | async-start | bytes 262144 | tf_op jit(solution)/shard_map/all_to_all | solution.py:621
  39.3 30.0 %all-to-all-start.1 = ((bf16[8,2,40,512]{3,2,1,0:T(8,128)(2,1)}), bf16[8,2,40,512]{3,2,1,0:T(8,128)(2,1)S(1)}, u32[]{:S(2)}, u32[]{:S(2)}) async-start(bf16[8,2,40,512]{3,2,1,0:T(8,128)(2,1)} %lookup.2), calls=%async_computation.1 | async-start | bytes 1310720 | tf_op jit(solution)/shard_map/all_to_all | solution.py:633
  69.3 27.7 %all-to-all-start.2 = ((bf16[8,3,40,512]{3,2,1,0:T(8,128)(2,1)}), bf16[8,3,40,512]{3,2,1,0:T(8,128)(2,1)S(1)}, u32[]{:S(2)}, u32[]{:S(2)}) async-start(bf16[8,3,40,512]{3,2,1,0:T(8,128)(2,1)} %lookup.3), calls=%async_computation.2 | async-start | bytes 1966080 | tf_op jit(solution)/shard_map/all_to_all | solution.py:633
  74.9 19.9 %collective-permute-start = (s32[8,5,512]{2,1,0:T(8,128)S(1)}, s32[8,5,512]{2,1,0:T(8,128)S(1)}, u32[]{:S(2)}, u32[]{:S(2)}) collective-permute-start(s32[8,5,512]{2,1,0:T(8,128)S(1)} %broadcast_add_fusion), channel_id=1, source_target_pairs={{0,1},{1,0},{2,3},{3,2},{4,5},{5,4},{6,7},{7,6},{8,9},{9,8},{10,11... | collective-permute-start | bytes 245768 | tf_op jit(solution)/shard_map/ppermute | solution.py:42
  74.9 17.8 %collective-permute-start.1 = (s32[8,5,512]{2,1,0:T(8,128)S(1)}, s32[8,5,512]{2,1,0:T(8,128)S(1)}, u32[]{:S(2)}, u32[]{:S(2)}) collective-permute-start(s32[8,5,512]{2,1,0:T(8,128)S(1)} %broadcast_add_fusion), channel_id=1, source_target_pairs={{0,2},{1,3},{2,0},{3,1},{4,6},{5,7},{6,4},{7,5},{8,10},{9,11},{10,... | collective-permute-start | bytes 245768 | tf_op jit(solution)/shard_map/ppermute | solution.py:42
  135.2 19.3 %collective-permute-start.3 = (bf16[2,2,2,2,2,5,32,512]{7,6,5,4,3,2,1,0:T(8,128)(2,1)}, bf16[2,2,2,2,2,5,32,512]{7,6,5,4,3,2,1,0:T(8,128)(2,1)}, u32[]{:S(2)}, u32[]{:S(2)}) collective-permute-start(bf16[2,2,2,2,2,5,32,512]{7,6,5,4,3,2,1,0:T(8,128)(2,1)} %bitcast.158), channel_id=1, source_target_pairs={{0,1},{1,0},{2,3},{3,2},{4,5},{5,4},{6,7},{7,6},{8,9},{9,8},{10,11... | collective-permute-start | bytes 15728648 | tf_op jit(solution)/shard_map/ppermute | solution.py:42
  135.5 55.8 %all-to-all-start.3 = ((bf16[8,5,40,512]{3,2,1,0:T(8,128)(2,1)}), bf16[8,5,40,512]{3,2,1,0:T(8,128)(2,1)S(1)}, u32[]{:S(2)}, u32[]{:S(2)}) async-start(bf16[8,5,40,512]{3,2,1,0:T(8,128)(2,1)} %bitcast.35), calls=%async_computation.3 | async-start | bytes 3276800 | tf_op jit(solution)/shard_map/all_to_all | solution.py:669
  157.1 30.3 %collective-permute-start.11 = (bf16[2,2,5,32,512]{4,3,2,1,0:T(8,128)(2,1)S(1)}, bf16[2,2,5,32,512]{4,3,2,1,0:T(8,128)(2,1)S(1)}, u32[]{:S(2)}, u32[]{:S(2)}) collective-permute-start(bf16[2,2,5,32,512]{4,3,2,1,0:T(8,128)(2,1)S(1)} %get-tuple-element.83), channel_id=1, source_target_pairs={{0,4},{4,0},{8,12},{12,8},{16,20},{20,16},{24,28},{28,24},{1,5},{5... | collective-permute-start | bytes 1966088 | tf_op jit(solution)/shard_map/ppermute | solution.py:42
  160.3 27.6 %collective-permute-start.9 = (bf16[2,2,5,32,512]{4,3,2,1,0:T(8,128)(2,1)S(1)}, bf16[2,2,5,32,512]{4,3,2,1,0:T(8,128)(2,1)S(1)}, u32[]{:S(2)}, u32[]{:S(2)}) collective-permute-start(bf16[2,2,5,32,512]{4,3,2,1,0:T(8,128)(2,1)S(1)} %get-tuple-element.84), channel_id=1, source_target_pairs={{0,2},{1,3},{2,0},{3,1},{4,6},{5,7},{6,4},{7,5},{8,10},{9,11},{10,... | collective-permute-start | bytes 1966088 | tf_op jit(solution)/shard_map/ppermute | solution.py:42
  167.0 13.2 %collective-permute-start.7 = (bf16[56,1152]{1,0:T(8,128)(2,1)S(1)}, bf16[56,1152]{1,0:T(8,128)(2,1)S(1)}, u32[]{:S(2)}, u32[]{:S(2)}) collective-permute-start(bf16[56,1152]{1,0:T(8,128)(2,1)S(1)} %pad_maximum_fusion.6), channel_id=1, source_target_pairs={{0,6},{1,7},{2,4},{3,5},{4,2},{5,3},{6,0},{7,1},{8,14},{9,15},{10,... | collective-permute-start | bytes 387080 | tf_op jit(solution)/shard_map/ppermute | solution.py:51
  168.0 18.0 %collective-permute-start.6 = (bf16[56,1152]{1,0:T(8,128)(2,1)S(1)}, bf16[56,1152]{1,0:T(8,128)(2,1)S(1)}, u32[]{:S(2)}, u32[]{:S(2)}) collective-permute-start(bf16[56,1152]{1,0:T(8,128)(2,1)S(1)} %pad_maximum_fusion.6), channel_id=1, source_target_pairs={{0,4},{1,5},{2,6},{3,7},{4,0},{5,1},{6,2},{7,3},{8,12},{9,13},{10,... | collective-permute-start | bytes 387080 | tf_op jit(solution)/shard_map/ppermute | solution.py:51
  170.0 16.1 %collective-permute-start.5 = (bf16[56,1152]{1,0:T(8,128)(2,1)S(1)}, bf16[56,1152]{1,0:T(8,128)(2,1)S(1)}, u32[]{:S(2)}, u32[]{:S(2)}) collective-permute-start(bf16[56,1152]{1,0:T(8,128)(2,1)S(1)} %pad_maximum_fusion.6), channel_id=1, source_target_pairs={{0,2},{1,3},{2,0},{3,1},{4,6},{5,7},{6,4},{7,5},{8,10},{9,11},{10,... | collective-permute-start | bytes 387080 | tf_op jit(solution)/shard_map/ppermute | solution.py:51
  192.7 24.7 %collective-permute-start.13 = (bf16[2,2,5,32,512]{4,3,2,1,0:T(8,128)(2,1)}, bf16[2,2,5,32,512]{4,3,2,1,0:T(8,128)(2,1)S(1)}, u32[]{:S(2)}, u32[]{:S(2)}) collective-permute-start(bf16[2,2,5,32,512]{4,3,2,1,0:T(8,128)(2,1)} %get-tuple-element.81.refs_5_), channel_id=1, source_target_pairs={{0,4},{4,0},{8,12},{12,8},{16,20},{20,16},{24,28},{28,24},{1,5},{5... | collective-permute-start | bytes 1966088 | tf_op jit(solution)/shard_map/ppermute | solution.py:42
  192.8 24.6 %collective-permute-start.14 = (bf16[2,2,5,32,512]{4,3,2,0,1:T(8,128)(2,1)}, bf16[2,2,5,32,512]{4,3,2,0,1:T(8,128)(2,1)S(1)}, u32[]{:S(2)}, u32[]{:S(2)}) collective-permute-start(bf16[2,2,5,32,512]{4,3,2,0,1:T(8,128)(2,1)} %copy-done.23), channel_id=1, source_target_pairs={{0,2},{1,3},{2,0},{3,1},{4,6},{5,7},{6,4},{7,5},{8,10},{9,11},{10,... | collective-permute-start | bytes 1966088 | tf_op jit(solution)/shard_map/ppermute | solution.py:42
  194.9 29.8 %collective-permute-start.8 = (bf16[2,2,5,32,512]{4,3,2,1,0:T(8,128)(2,1)S(1)}, bf16[2,2,5,32,512]{4,3,2,1,0:T(8,128)(2,1)S(1)}, u32[]{:S(2)}, u32[]{:S(2)}) collective-permute-start(bf16[2,2,5,32,512]{4,3,2,1,0:T(8,128)(2,1)S(1)} %copy-done.10), channel_id=1, source_target_pairs={{0,2},{1,3},{2,0},{3,1},{4,6},{5,7},{6,4},{7,5},{8,10},{9,11},{10,... | collective-permute-start | bytes 1966088 | tf_op jit(solution)/shard_map/ppermute | solution.py:42
  196.4 28.2 %collective-permute-start.10 = (bf16[2,2,5,32,512]{4,3,2,1,0:T(8,128)(2,1)S(1)}, bf16[2,2,5,32,512]{4,3,2,1,0:T(8,128)(2,1)S(1)}, u32[]{:S(2)}, u32[]{:S(2)}) collective-permute-start(bf16[2,2,5,32,512]{4,3,2,1,0:T(8,128)(2,1)S(1)} %copy-done.3), channel_id=1, source_target_pairs={{0,4},{4,0},{8,12},{12,8},{16,20},{20,16},{24,28},{28,24},{1,5},{5... | collective-permute-start | bytes 1966088 | tf_op jit(solution)/shard_map/ppermute | solution.py:42
  216.7 42.7 %collective-permute-start.18 = (bf16[8,5,40,512]{3,2,1,0:T(8,128)(2,1)S(1)}, bf16[8,5,40,512]{3,2,1,0:T(8,128)(2,1)S(1)}, u32[]{:S(2)}, u32[]{:S(2)}) collective-permute-start(bf16[8,5,40,512]{3,2,1,0:T(8,128)(2,1)S(1)} %broadcast_multiply_fusion.2), channel_id=1, source_target_pairs={{0,2},{1,3},{2,0},{3,1},{4,6},{5,7},{6,4},{7,5},{8,10},{9,11},{10,... | collective-permute-start | bytes 4915208 | tf_op jit(solution)/shard_map/ppermute | solution.py:42
  225.6 29.1 %collective-permute-start.17 = (bf16[2,5,32,512]{3,2,1,0:T(8,128)(2,1)S(1)}, bf16[2,5,32,512]{3,2,1,0:T(8,128)(2,1)S(1)}, u32[]{:S(2)}, u32[]{:S(2)}) collective-permute-start(bf16[2,5,32,512]{3,2,1,0:T(8,128)(2,1)S(1)} %pad_maximum_fusion.4.refs_8_), channel_id=1, source_target_pairs={{0,24},{4,28},{8,16},{12,20},{16,8},{20,12},{24,0},{28,4},{1,25},{... | collective-permute-start | bytes 983048 | tf_op jit(solution)/shard_map/ppermute | solution.py:42
  229.5 27.8 %collective-permute-start.16 = (bf16[2,5,32,512]{3,2,1,0:T(8,128)(2,1)S(1)}, bf16[2,5,32,512]{3,2,1,0:T(8,128)(2,1)S(1)}, u32[]{:S(2)}, u32[]{:S(2)}) collective-permute-start(bf16[2,5,32,512]{3,2,1,0:T(8,128)(2,1)S(1)} %pad_maximum_fusion.3.refs_7_), channel_id=1, source_target_pairs={{0,16},{4,20},{8,24},{12,28},{16,0},{20,4},{24,8},{28,12},{1,17},{... | collective-permute-start | bytes 983048 | tf_op jit(solution)/shard_map/ppermute | solution.py:42
  231.9 25.5 %collective-permute-start.15 = (bf16[2,5,32,512]{3,2,1,0:T(8,128)(2,1)S(1)}, bf16[2,5,32,512]{3,2,1,0:T(8,128)(2,1)S(1)}, u32[]{:S(2)}, u32[]{:S(2)}) collective-permute-start(bf16[2,5,32,512]{3,2,1,0:T(8,128)(2,1)S(1)} %pad_maximum_fusion.2.refs_6_), channel_id=1, source_target_pairs={{0,8},{4,12},{8,0},{12,4},{16,24},{20,28},{24,16},{28,20},{1,9},{5... | collective-permute-start | bytes 983048 | tf_op jit(solution)/shard_map/ppermute | solution.py:42
  259.6 25.0 %collective-permute-start.25 = (bf16[2,5,32,512]{3,2,1,0:T(8,128)(2,1)S(1)}, bf16[2,5,32,512]{3,2,1,0:T(8,128)(2,1)S(1)}, u32[]{:S(2)}, u32[]{:S(2)}) collective-permute-start(bf16[2,5,32,512]{3,2,1,0:T(8,128)(2,1)S(1)} %add_convert_fusion.2.refs_5_), channel_id=1, source_target_pairs={{0,24},{4,28},{8,16},{12,20},{16,8},{20,12},{24,0},{28,4},{1,25},{... | collective-permute-start | bytes 983048 | tf_op jit(solution)/shard_map/ppermute | solution.py:42
  262.4 30.2 %collective-permute-start.24 = (bf16[2,5,32,512]{3,2,1,0:T(8,128)(2,1)S(1)}, bf16[2,5,32,512]{3,2,1,0:T(8,128)(2,1)S(1)}, u32[]{:S(2)}, u32[]{:S(2)}) collective-permute-start(bf16[2,5,32,512]{3,2,1,0:T(8,128)(2,1)S(1)} %add_convert_fusion.2.refs_5_), channel_id=1, source_target_pairs={{0,16},{4,20},{8,24},{12,28},{16,0},{20,4},{24,8},{28,12},{1,17},{... | collective-permute-start | bytes 983048 | tf_op jit(solution)/shard_map/ppermute | solution.py:42
  265.5 27.2 %collective-permute-start.23 = (bf16[2,5,32,512]{3,2,1,0:T(8,128)(2,1)S(1)}, bf16[2,5,32,512]{3,2,1,0:T(8,128)(2,1)S(1)}, u32[]{:S(2)}, u32[]{:S(2)}) collective-permute-start(bf16[2,5,32,512]{3,2,1,0:T(8,128)(2,1)S(1)} %add_convert_fusion.2.refs_5_), channel_id=1, source_target_pairs={{0,8},{4,12},{8,0},{12,4},{16,24},{20,28},{24,16},{28,20},{1,9},{5... | collective-permute-start | bytes 983048 | tf_op jit(solution)/shard_map/ppermute | solution.py:42
  292.9 30.8 %collective-permute-start.26 = (bf16[2,4,5,32,512]{4,3,2,1,0:T(8,128)(2,1)S(1)}, bf16[2,4,5,32,512]{4,3,2,1,0:T(8,128)(2,1)S(1)}, u32[]{:S(2)}, u32[]{:S(2)}) collective-permute-start(bf16[2,4,5,32,512]{4,3,2,1,0:T(8,128)(2,1)S(1)} %pad_maximum_fusion.refs_5_.refs_0_), channel_id=1, source_target_pairs={{0,4},{4,0},{8,12},{12,8},{16,20},{20,16},{24,28},{28,24},{1,5},{5... | collective-permute-start | bytes 3932168 | tf_op jit(solution)/shard_map/ppermute | solution.py:42
  294.5 30.5 %collective-permute-start.27 = (bf16[2,4,5,32,512]{4,3,2,1,0:T(8,128)(2,1)S(1)}, bf16[2,4,5,32,512]{4,3,2,1,0:T(8,128)(2,1)S(1)}, u32[]{:S(2)}, u32[]{:S(2)}) collective-permute-start(bf16[2,4,5,32,512]{4,3,2,1,0:T(8,128)(2,1)S(1)} %pad_maximum_fusion.refs_5_.refs_0_), channel_id=1, source_target_pairs={{0,2},{1,3},{2,0},{3,1},{4,6},{5,7},{6,4},{7,5},{8,10},{9,11},{10,... | collective-permute-start | bytes 3932168 | tf_op jit(solution)/shard_map/ppermute | solution.py:42
  296.3 13.8 %collective-permute-start.22 = (bf16[56,1152]{1,0:T(8,128)(2,1)S(1)}, bf16[56,1152]{1,0:T(8,128)(2,1)S(1)}, u32[]{:S(2)}, u32[]{:S(2)}) collective-permute-start(bf16[56,1152]{1,0:T(8,128)(2,1)S(1)} %pad_maximum_fusion.7), channel_id=1, source_target_pairs={{0,24},{1,25},{2,26},{3,27},{4,28},{5,29},{6,30},{7,31},{8,16},{9,... | collective-permute-start | bytes 387080 | tf_op jit(solution)/shard_map/ppermute | solution.py:51
  298.9 11.4 %collective-permute-start.20 = (bf16[56,1152]{1,0:T(8,128)(2,1)S(1)}, bf16[56,1152]{1,0:T(8,128)(2,1)S(1)}, u32[]{:S(2)}, u32[]{:S(2)}) collective-permute-start(bf16[56,1152]{1,0:T(8,128)(2,1)S(1)} %pad_maximum_fusion.7), channel_id=1, source_target_pairs={{0,8},{1,9},{2,10},{3,11},{4,12},{5,13},{6,14},{7,15},{8,0},{9,1},... | collective-permute-start | bytes 387080 | tf_op jit(solution)/shard_map/ppermute | solution.py:51
  310.2 18.8 %collective-permute-start.29 = (bf16[2,4,5,32,512]{4,3,2,1,0:T(8,128)(2,1)S(1)}, bf16[2,4,5,32,512]{4,3,2,1,0:T(8,128)(2,1)S(1)}, u32[]{:S(2)}, u32[]{:S(2)}) collective-permute-start(bf16[2,4,5,32,512]{4,3,2,1,0:T(8,128)(2,1)S(1)} %pad_maximum_fusion.refs_5_.refs_0_), channel_id=1, source_target_pairs={{0,1},{1,0},{2,3},{3,2},{4,5},{5,4},{6,7},{7,6},{8,9},{9,8},{10,11... | collective-permute-start | bytes 3932168 | tf_op jit(solution)/shard_map/ppermute | solution.py:42
  323.8 14.4 %collective-permute-start.30 = (bf16[2,4,5,32,512]{4,3,2,1,0:T(8,128)(2,1)S(1)}, bf16[2,4,5,32,512]{4,3,2,1,0:T(8,128)(2,1)S(1)}, u32[]{:S(2)}, u32[]{:S(2)}) collective-permute-start(bf16[2,4,5,32,512]{4,3,2,1,0:T(8,128)(2,1)S(1)} %collective-permute-done.26.refs_1_), channel_id=1, source_target_pairs={{0,1},{1,0},{2,3},{3,2},{4,5},{5,4},{6,7},{7,6},{8,9},{9,8},{10,11... | collective-permute-start | bytes 3932168 | tf_op jit(solution)/shard_map/ppermute | solution.py:42
  325.0 13.2 %collective-permute-start.31 = (bf16[2,4,5,32,512]{4,3,2,1,0:T(8,128)(2,1)S(1)}, bf16[2,4,5,32,512]{4,3,2,1,0:T(8,128)(2,1)S(1)}, u32[]{:S(2)}, u32[]{:S(2)}) collective-permute-start(bf16[2,4,5,32,512]{4,3,2,1,0:T(8,128)(2,1)S(1)} %collective-permute-done.27.refs_2_), channel_id=1, source_target_pairs={{0,1},{1,0},{2,3},{3,2},{4,5},{5,4},{6,7},{7,6},{8,9},{9,8},{10,11... | collective-permute-start | bytes 3932168 | tf_op jit(solution)/shard_map/ppermute | solution.py:42
  325.0 24.0 %collective-permute-start.28 = (bf16[4,5,32,512]{3,2,1,0:T(8,128)(2,1)S(1)}, bf16[4,5,32,512]{3,2,1,0:T(8,128)(2,1)S(1)}, u32[]{:S(2)}, u32[]{:S(2)}) collective-permute-start(bf16[4,5,32,512]{3,2,1,0:T(8,128)(2,1)S(1)} %slice_bitcast_fusion.5), channel_id=1, source_target_pairs={{0,2},{1,3},{2,0},{3,1},{4,6},{5,7},{6,4},{7,5},{8,10},{9,11},{10,... | collective-permute-start | bytes 1966088 | tf_op jit(solution)/shard_map/ppermute | solution.py:42
  325.7 23.5 %collective-permute-start.32 = (bf16[4,5,32,512]{3,2,1,0:T(8,128)(2,1)S(1)}, bf16[4,5,32,512]{3,2,1,0:T(8,128)(2,1)S(1)}, u32[]{:S(2)}, u32[]{:S(2)}) collective-permute-start(bf16[4,5,32,512]{3,2,1,0:T(8,128)(2,1)S(1)} %slice_bitcast_fusion.4), channel_id=1, source_target_pairs={{0,4},{4,0},{8,12},{12,8},{16,20},{20,16},{24,28},{28,24},{1,5},{5... | collective-permute-start | bytes 1966088 | tf_op jit(solution)/shard_map/ppermute | solution.py:42
  (52 other events, 362.9 us)

commit v10 on v9

--- a/solution.py
+++ b/solution.py
@@ -623,12 +623,11 @@
     )
     listed = jnp.transpose(wanted, (1, 0, 2)).reshape(-1)
 
-    first_size = slot_count % LOOK_SLOTS
-    starts = ([0] if first_size else []) + list(range(first_size, slot_count, LOOK_SLOTS))
+    starts = list(range(0, slot_count, LOOK_SLOTS))
     arrived = []
     for begin in starts:
         looked = lookup(
-            tables, listed, own_rows, tab_count, begin, LOOK_SLOTS if begin or not first_size else first_size
+            tables, listed, own_rows, tab_count, begin, min(LOOK_SLOTS, slot_count - begin)
         )
         arrived.append(lax.all_to_all(looked, "tab", split_axis=0, concat_axis=0, tiled=True))
 
@@ -766,7 +765,7 @@
     other = [swap(values, "rep", 1)]
     add_next(False, 1, other)
     token = token + zero_of(small[0, 0])
-    last = [swap(from_y[0], "rep", 2), swap(from_x[1], "tab", 1)]
+    last = [swap(gate(from_y[0], token), "rep", 2), swap(gate(from_x[1], token), "tab", 1)]
     other += [swap(from_y, "rep", 1), swap(from_x, "rep", 1)]
     add_next(False, slot_count, other)
     last = [gate(part, token) for part in last]

time: 372 us -> 370 us (level)
  Pallas kernels: 189 us -> 185 us
    ppermute x28, waiting for transfers between devices: 32.7 us -> 21.1 us  [swap(): lax.ppermute(value, axis, [(at, at ^ mask) for at in range(lax.axis_size(...]
    ppermute x7, waiting for transfers between devices: 12.4 us -> 18 us  [swap_both(): return lax.ppermute(value, ('tab', 'rep'), perm)]
    all_to_all x2, waiting for transfers between devices: 0.01 us -> 4.14 us  [on_device(): lax.all_to_all(looked, 'tab', split_axis=0, concat_axis=0, tiled=True)]
  transfers between devices with their start and end apart: 39 -> 39, of which waited for: 10 -> 12; matrix products, arithmetic and copies ran while one was open for 13% -> 14% of each run, Pallas kernels for 33% -> 31%
where the time goes in v10:
time: 370 us; the launch traced here: 365 us
  Pallas kernels  185 us (50%)
  starting transfers between devices  54.9 us (15%)
  waiting for transfers between devices  49.3 us (13%)
  local copies, waits for them, and re-layouts  35.2 us (10%)
  other arithmetic  27 us (7%)
  between operations  13.7 us (4%)
    pallas_call x10, Pallas kernels, add_rows(): pl.pallas_call(functools.partial(add_kernel, part_count, accumulate), gri...  82.3 us
    pallas_call x2, Pallas kernels, lookup(): pl.pallas_call(functools.partial(lookup_kernel, first_slot), in_specs=[sm...  39.8 us
    pallas_call x1, Pallas kernels, dense_step(): pl.pallas_call(functools.partial(dense_kernel, dense_width, width, starts...  27.5 us
    ppermute x28, starting transfers between devices, swap(): lax.ppermute(value, axis, [(at, at ^ mask) for at in range(lax.axis_size(...  24.7 us
    pallas_call x2, Pallas kernels, weight_parts(): pl.pallas_call(functools.partial(weight_kernel, core), grid=(matrix_count...  22.2 us
    ppermute x28, waiting for transfers between devices, swap(): lax.ppermute(value, axis, [(at, at ^ mask) for at in range(lax.axis_size(...  21.1 us
    ppermute x7, waiting for transfers between devices, swap_both(): return lax.ppermute(value, ('tab', 'rep'), perm)  18 us
    unnamed x93, local copies, waits for them, and re-layouts  14.3 us
  transfers between devices with their start and end apart: 39, of which 12 were waited for; matrix products, arithmetic and copies ran while one was open for 14% of the time, Pallas kernels for 31%

profile of v10, /device:TPU:0, one launch (start us, length us, event | category | flops | bytes accessed | tf_op | source)
XLA Modules:
  0.0 365.1 jit_solution(2322727874360900538)
XLA Ops:
  5.2 7.3 %all-to-all-start = ((s32[8,5,512]{2,1,0:T(8,128)}), s32[8,5,512]{2,1,0:T(8,128)S(1)}, u32[]{:S(2)}, u32[]{:S(2)}) async-start(s32[8,5,512]{2,1,0:T(8,128)} %reshape.536), calls=%async_computation | async-start | bytes 262144 | tf_op jit(solution)/shard_map/all_to_all | solution.py:621
  13.8 6.0 %all-to-all-done = s32[8,5,512]{2,1,0:T(8,128)S(1)} async-done(((s32[8,5,512]{2,1,0:T(8,128)}), s32[8,5,512]{2,1,0:T(8,128)S(1)}, u32[]{:S(2)}, u32[]{:S(2)}) %all-to-all-start) | async-done | bytes 81952 | tf_op jit(solution)/shard_map/all_to_all | solution.py:621
  20.5 22.5 %lookup.2 = bf16[8,3,40,512]{3,2,1,0:T(8,128)(2,1)} custom-call(s32[20480]{0:T(1024)} %bitcast.161, s32[5]{0:T(128)} %dynamic_slice.3.rows_ref, bf16[5,39,32768]{2,1,0:T(8,128)(2,1)} %table_hbm.3), custom_call_target="tpu_custom_call" | custom-call | flops 30198988 | bytes 8626 | tf_op jit(solution)/shard_map/lookup/pallas_call | solution.py:112
  43.0 3.6 all-to-all-start.1
  48.4 17.3 %lookup.3 = bf16[8,2,40,512]{3,2,1,0:T(8,128)(2,1)} custom-call(s32[20480]{0:T(1024)} %bitcast.162, s32[5]{0:T(128)} %dynamic_slice.3.rows_ref, bf16[5,39,32768]{2,1,0:T(8,128)(2,1)} %table_hbm.3), custom_call_target="tpu_custom_call" | custom-call | flops 20132660 | bytes 5750 | tf_op jit(solution)/shard_map/lookup/pallas_call | solution.py:112
  65.8 4.1 %all-to-all-done.1.refs_0_ = bf16[8,3,40,512]{3,2,1,0:T(8,128)(2,1)S(1)} async-done(((bf16[8,3,40,512]{3,2,1,0:T(8,128)(2,1)}), bf16[8,3,40,512]{3,2,1,0:T(8,128)(2,1)S(1)}, u32[]{:S(2)}, u32[]{:S(2)}) %all-to-all-start.1) | async-done | bytes 983072 | tf_op jit(solution)/shard_map/all_to_all | solution.py:632
  69.9 3.7 %all-to-all-start.2 = ((bf16[8,2,40,512]{3,2,1,0:T(8,128)(2,1)}), bf16[8,2,40,512]{3,2,1,0:T(8,128)(2,1)S(1)}, u32[]{:S(2)}, u32[]{:S(2)}) async-start(bf16[8,2,40,512]{3,2,1,0:T(8,128)(2,1)} %lookup.3), calls=%async_computation.2 | async-start | bytes 1310720 | tf_op jit(solution)/shard_map/all_to_all | solution.py:632
  77.1 3.5 multiply_bitcast_fusion
  97.8 27.5 %dense.1 = (f32[1,512]{1,0:T(1,128)}, f32[16,512]{1,0:T(8,128)}, bf16[40,40,512]{2,1,0:T(8,128)(2,1)}, bf16[5,1152,512]{2,1,0:T(8,128)(2,1)}, bf16[5,1152,512]{2,1,0:T(8,128)(2,1)}, /*index=5*/f32[8,1152]{1,0:T(8,128)}) custom-call(s32[26]{0:T(128)} %place_ref.1, f32[1]{0:T(128)S(6)} %convert.67.bias_ref, bf16[8,3,40,512]{3,2,1,0:T(8,128)(2,1)} %copy-done.17, ...), custom_call_target="tpu_custom_call" | custom-call | flops 13589544 | bytes 30965 | tf_op jit(solution)/shard_map/dense/pallas_call | solution.py:379
  125.3 9.7 %weight_parts.3 = bf16[2,16,5,32,512]{4,3,2,1,0:T(8,128)(2,1)} custom-call(s32[1]{0:T(128)} %bitcast.own_ref, bf16[5,1152,512]{2,1,0:T(8,128)(2,1)} %get-tuple-element.43.left_ref, bf16[5,1152,512]{2,1,0:T(8,128)(2,1)} %get-tuple-element.44.right_ref), custom_call_target="tpu_custom_call" | custom-call | flops 3397386 | bytes 33177 | tf_op jit(solution)/shard_map/weight_parts/pallas_call | solution.py:461
  135.4 6.4 %all-to-all-start.3 = ((bf16[8,5,40,512]{3,2,1,0:T(8,128)(2,1)}), bf16[8,5,40,512]{3,2,1,0:T(8,128)(2,1)S(1)}, u32[]{:S(2)}, u32[]{:S(2)}) async-start(bf16[8,5,40,512]{3,2,1,0:T(8,128)(2,1)} %bitcast.35), calls=%async_computation.3 | async-start | bytes 3276800 | tf_op jit(solution)/shard_map/all_to_all | solution.py:668
  141.8 12.5 %weight_parts.2 = (f32[2,16,5,32,512]{4,3,2,1,0:T(8,128)}, f32[5,8,1152]{2,1,0:T(8,128)}) custom-call(s32[1]{0:T(128)} %bitcast.own_ref, bf16[5,1152,512]{2,1,0:T(8,128)(2,1)} %get-tuple-element.43.left_ref, bf16[5,1152,512]{2,1,0:T(8,128)(2,1)} %get-tuple-element.44.right_ref), custom_call_target="tpu_custom_call" | custom-call | flops 3397386 | bytes 33177 | tf_op jit(solution)/shard_map/weight_parts/pallas_call | solution.py:461
  163.1 3.6 fusion.8
  170.4 3.0 convert_add_fusion.1
  173.5 6.5 %collective-permute-done.7 = bf16[56,1152]{1,0:T(8,128)(2,1)S(1)} collective-permute-done((bf16[56,1152]{1,0:T(8,128)(2,1)S(1)}, bf16[56,1152]{1,0:T(8,128)(2,1)S(1)}, u32[]{:S(2)}, u32[]{:S(2)}) %collective-permute-start.7) | collective-permute-done | bytes 129056 | tf_op jit(solution)/shard_map/ppermute | solution.py:51
  180.1 5.8 %collective-permute-done.6 = bf16[56,1152]{1,0:T(8,128)(2,1)S(1)} collective-permute-done((bf16[56,1152]{1,0:T(8,128)(2,1)S(1)}, bf16[56,1152]{1,0:T(8,128)(2,1)S(1)}, u32[]{:S(2)}, u32[]{:S(2)}) %collective-permute-start.6) | collective-permute-done | bytes 129056 | tf_op jit(solution)/shard_map/ppermute | solution.py:51
  199.8 7.4 %add_rows.10 = (f32[5,39,8192]{2,1,0:T(8,128)}, f32[8,128]{1,0:T(8,128)S(1)}) custom-call(s32[1]{0:T(128)} %bitcast.34.base_ref, s32[8,5,1,512]{3,2,1,0:T(1,128)S(1)} %copy-done.6, s32[8,5,1,512]{3,2,1,0:T(1,128)S(1)} %copy-done.7, bf16[8,5,40,512]{3,2,1,0:T(8,128)(2,1)S(1)} %broadcast_multiply_fusion.3.refs_2_, ...), custom_call_target="tpu_custom_call" | custom-call | flops 5234491 | bytes 1916 | tf_op jit(solution)/shard_map/add_rows/pallas_call | solution.py:185
  207.2 7.5 %add_rows.11 = (f32[5,39,8192]{2,1,0:T(8,128)}, f32[8,128]{1,0:T(8,128)S(1)}) custom-call(s32[1]{0:T(128)} %bitcast.34.base_ref, s32[8,5,1,512]{3,2,1,0:T(1,128)S(1)} %copy-done.6, s32[8,5,1,512]{3,2,1,0:T(1,128)S(1)} %copy-done.7, bf16[8,5,40,512]{3,2,1,0:T(8,128)(2,1)S(1)} %broadcast_multiply_fusion.3.refs_2_, ...), custom_call_target="tpu_custom_call", output_to_operand_aliasing={{0}: (5, {})} | custom-call | flops 5234491 | bytes 1916 | tf_op jit(solution)/shard_map/add_rows/pallas_call | solution.py:185
  217.9 6.6 %collective-permute-done.8 = bf16[2,2,5,32,512]{4,3,2,1,0:T(8,128)(2,1)S(1)} collective-permute-done((bf16[2,2,5,32,512]{4,3,2,1,0:T(8,128)(2,1)S(1)}, bf16[2,2,5,32,512]{4,3,2,1,0:T(8,128)(2,1)S(1)}, u32[]{:S(2)}, u32[]{:S(2)}) %collective-permute-start.8) | collective-permute-done | bytes 655392 | tf_op jit(solution)/shard_map/ppermute | solution.py:42
  225.5 3.0 collective-permute-start.17
  231.9 7.4 %add_rows.12 = (f32[5,39,8192]{2,1,0:T(8,128)}, f32[8,128]{1,0:T(8,128)}) custom-call(s32[1]{0:T(128)} %bitcast.34.base_ref, s32[8,5,1,512]{3,2,1,0:T(1,128)S(1)} %copy-done.6, s32[8,5,1,512]{3,2,1,0:T(1,128)S(1)} %copy-done.7, bf16[8,5,40,512]{3,2,1,0:T(8,128)(2,1)S(1)} %broadcast_multiply_fusion.3.refs_2_, ...), custom_call_target="tpu_custom_call", output_to_operand_aliasing={{0}: (5, {})} | custom-call | flops 5234491 | bytes 1916 | tf_op jit(solution)/shard_map/add_rows/pallas_call | solution.py:185
  239.3 7.4 %add_rows.13 = (f32[5,39,8192]{2,1,0:T(8,128)}, f32[8,128]{1,0:T(8,128)}) custom-call(s32[1]{0:T(128)} %bitcast.34.base_ref, s32[8,5,1,512]{3,2,1,0:T(1,128)S(1)} %copy-done.6, s32[8,5,1,512]{3,2,1,0:T(1,128)S(1)} %copy-done.7, bf16[8,5,40,512]{3,2,1,0:T(8,128)(2,1)S(1)} %broadcast_multiply_fusion.3.refs_2_, ...), custom_call_target="tpu_custom_call", output_to_operand_aliasing={{0}: (5, {})} | custom-call | flops 5234491 | bytes 1916 | tf_op jit(solution)/shard_map/add_rows/pallas_call | solution.py:185
  246.7 7.4 %add_rows.14 = (f32[5,39,8192]{2,1,0:T(8,128)}, f32[8,128]{1,0:T(8,128)S(1)}) custom-call(s32[1]{0:T(128)} %bitcast.34.base_ref, s32[8,5,1,512]{3,2,1,0:T(1,128)S(1)} %copy-done.6, s32[8,5,1,512]{3,2,1,0:T(1,128)S(1)} %copy-done.7, bf16[8,5,40,512]{3,2,1,0:T(8,128)(2,1)S(1)} %broadcast_multiply_fusion.3.refs_2_, ...), custom_call_target="tpu_custom_call", output_to_operand_aliasing={{0}: (5, {})} | custom-call | flops 5234491 | bytes 1916 | tf_op jit(solution)/shard_map/add_rows/pallas_call | solution.py:185
  265.5 9.0 %add_rows.15 = (f32[5,39,8192]{2,1,0:T(8,128)}, f32[8,128]{1,0:T(8,128)}) custom-call(s32[1]{0:T(128)} %bitcast.34.base_ref, s32[8,5,1,512]{3,2,1,0:T(1,128)S(1)} %copy-done.8, s32[8,5,1,512]{3,2,1,0:T(1,128)S(1)} %copy-done.9, bf16[8,5,40,512]{3,2,1,0:T(8,128)(2,1)S(1)} %broadcast_multiply_fusion.1.refs_2_, ...), custom_call_target="tpu_custom_call", output_to_operand_aliasing={{0}: (5, {})} | custom-call | flops 5234491 | bytes 1916 | tf_op jit(solution)/shard_map/add_rows/pallas_call | solution.py:185
  274.5 8.8 %add_rows.16 = (f32[5,39,8192]{2,1,0:T(8,128)}, f32[8,128]{1,0:T(8,128)S(1)}) custom-call(s32[1]{0:T(128)} %bitcast.34.base_ref, s32[8,5,1,512]{3,2,1,0:T(1,128)S(1)} %copy-done.8, s32[8,5,1,512]{3,2,1,0:T(1,128)S(1)} %copy-done.9, bf16[8,5,40,512]{3,2,1,0:T(8,128)(2,1)S(1)} %broadcast_multiply_fusion.1.refs_2_, ...), custom_call_target="tpu_custom_call", output_to_operand_aliasing={{0}: (5, {})} | custom-call | flops 5234491 | bytes 1916 | tf_op jit(solution)/shard_map/add_rows/pallas_call | solution.py:185
  284.5 8.0 %collective-permute-done.24 = bf16[2,5,32,512]{3,2,1,0:T(8,128)(2,1)S(1)} collective-permute-done((bf16[2,5,32,512]{3,2,1,0:T(8,128)(2,1)S(1)}, bf16[2,5,32,512]{3,2,1,0:T(8,128)(2,1)S(1)}, u32[]{:S(2)}, u32[]{:S(2)}) %collective-permute-start.24) | collective-permute-done | bytes 327712 | tf_op jit(solution)/shard_map/ppermute | solution.py:42
  298.8 5.6 %collective-permute-done.22 = bf16[56,1152]{1,0:T(8,128)(2,1)S(1)} collective-permute-done((bf16[56,1152]{1,0:T(8,128)(2,1)S(1)}, bf16[56,1152]{1,0:T(8,128)(2,1)S(1)}, u32[]{:S(2)}, u32[]{:S(2)}) %collective-permute-start.22) | collective-permute-done | bytes 129056 | tf_op jit(solution)/shard_map/ppermute | solution.py:51
  304.4 3.0 collective-permute-start.20
  308.0 8.8 %add_rows.17 = (f32[5,39,8192]{2,1,0:T(8,128)}, f32[8,128]{1,0:T(8,128)}) custom-call(s32[1]{0:T(128)} %bitcast.34.base_ref, s32[8,5,1,512]{3,2,1,0:T(1,128)S(1)} %copy-done.8, s32[8,5,1,512]{3,2,1,0:T(1,128)S(1)} %copy-done.9, bf16[8,5,40,512]{3,2,1,0:T(8,128)(2,1)S(1)} %broadcast_multiply_fusion.1.refs_2_, ...), custom_call_target="tpu_custom_call", output_to_operand_aliasing={{0}: (5, {})} | custom-call | flops 5234491 | bytes 1916 | tf_op jit(solution)/shard_map/add_rows/pallas_call | solution.py:185
  318.1 9.2 %add_rows.18 = (f32[5,39,8192]{2,1,0:T(8,128)}, f32[8,128]{1,0:T(8,128)S(1)}) custom-call(s32[1]{0:T(128)} %bitcast.34.base_ref, s32[8,5,1,512]{3,2,1,0:T(1,128)S(1)} %copy-done.8, s32[8,5,1,512]{3,2,1,0:T(1,128)S(1)} %copy-done.9, bf16[8,5,40,512]{3,2,1,0:T(8,128)(2,1)S(1)} %broadcast_multiply_fusion.1.refs_2_, ...), custom_call_target="tpu_custom_call", output_to_operand_aliasing={{0}: (5, {})} | custom-call | flops 5234491 | bytes 1916 | tf_op jit(solution)/shard_map/add_rows/pallas_call | solution.py:185
  333.4 9.4 %add_rows.19 = (f32[5,39,8192]{2,1,0:T(8,128)}, f32[8,128]{1,0:T(8,128)S(1)}) custom-call(s32[1]{0:T(128)} %bitcast.34.base_ref, s32[8,5,1,512]{3,2,1,0:T(1,128)S(1)} %copy-done.8, s32[8,5,1,512]{3,2,1,0:T(1,128)S(1)} %copy-done.9, bf16[8,5,40,512]{3,2,1,0:T(8,128)(2,1)S(1)} %broadcast_multiply_fusion.1.refs_2_, ...), custom_call_target="tpu_custom_call", output_to_operand_aliasing={{0}: (5, {})} | custom-call | flops 5234491 | bytes 1916 | tf_op jit(solution)/shard_map/add_rows/pallas_call | solution.py:185
  350.4 13.3 %assemble.1 = (f32[3,1027,1027]{2,1,0:T(8,128)}, f32[1,1027,1024]{2,1,0:T(8,128)}, f32[1,1024,1024]{2,1,0:T(8,128)}) custom-call(s32[1]{0:T(128)} %bitcast.own_ref, bf16[2,4,5,32,512]{4,3,2,1,0:T(8,128)(2,1)} %copy-done, bf16[2,4,5,32,512]{4,3,2,1,0:T(8,128)(2,1)} %copy-done.18, bf16[2,4,5,32,512]{4,3,2,1,0:T(8,128)(2,1)} %copy-done.19, ...), custom_call_target="tpu_custom_call" | custom-call | bytes 39813 | tf_op jit(solution)/shard_map/assemble/pallas_call | solution.py:566
  (274 shorter events, 86.5 us)
Async XLA Ops:
  5.2 14.6 %all-to-all-start = ((s32[8,5,512]{2,1,0:T(8,128)}), s32[8,5,512]{2,1,0:T(8,128)S(1)}, u32[]{:S(2)}, u32[]{:S(2)}) async-start(s32[8,5,512]{2,1,0:T(8,128)} %reshape.536), calls=%async_computation | async-start | bytes 262144 | tf_op jit(solution)/shard_map/all_to_all | solution.py:621
  43.0 26.9 %all-to-all-start.1 = ((bf16[8,3,40,512]{3,2,1,0:T(8,128)(2,1)}), bf16[8,3,40,512]{3,2,1,0:T(8,128)(2,1)S(1)}, u32[]{:S(2)}, u32[]{:S(2)}) async-start(bf16[8,3,40,512]{3,2,1,0:T(8,128)(2,1)} %lookup.2), calls=%async_computation.1 | async-start | bytes 1966080 | tf_op jit(solution)/shard_map/all_to_all | solution.py:632
  69.9 27.0 %all-to-all-start.2 = ((bf16[8,2,40,512]{3,2,1,0:T(8,128)(2,1)}), bf16[8,2,40,512]{3,2,1,0:T(8,128)(2,1)S(1)}, u32[]{:S(2)}, u32[]{:S(2)}) async-start(bf16[8,2,40,512]{3,2,1,0:T(8,128)(2,1)} %lookup.3), calls=%async_computation.2 | async-start | bytes 1310720 | tf_op jit(solution)/shard_map/all_to_all | solution.py:632
  74.8 19.9 %collective-permute-start = (s32[8,5,512]{2,1,0:T(8,128)S(1)}, s32[8,5,512]{2,1,0:T(8,128)S(1)}, u32[]{:S(2)}, u32[]{:S(2)}) collective-permute-start(s32[8,5,512]{2,1,0:T(8,128)S(1)} %broadcast_add_fusion), channel_id=1, source_target_pairs={{0,1},{1,0},{2,3},{3,2},{4,5},{5,4},{6,7},{7,6},{8,9},{9,8},{10,11... | collective-permute-start | bytes 245768 | tf_op jit(solution)/shard_map/ppermute | solution.py:42
  74.9 17.8 %collective-permute-start.1 = (s32[8,5,512]{2,1,0:T(8,128)S(1)}, s32[8,5,512]{2,1,0:T(8,128)S(1)}, u32[]{:S(2)}, u32[]{:S(2)}) collective-permute-start(s32[8,5,512]{2,1,0:T(8,128)S(1)} %broadcast_add_fusion), channel_id=1, source_target_pairs={{0,2},{1,3},{2,0},{3,1},{4,6},{5,7},{6,4},{7,5},{8,10},{9,11},{10,... | collective-permute-start | bytes 245768 | tf_op jit(solution)/shard_map/ppermute | solution.py:42
  135.0 19.3 %collective-permute-start.3 = (bf16[2,2,2,2,2,5,32,512]{7,6,5,4,3,2,1,0:T(8,128)(2,1)}, bf16[2,2,2,2,2,5,32,512]{7,6,5,4,3,2,1,0:T(8,128)(2,1)}, u32[]{:S(2)}, u32[]{:S(2)}) collective-permute-start(bf16[2,2,2,2,2,5,32,512]{7,6,5,4,3,2,1,0:T(8,128)(2,1)} %bitcast.159), channel_id=1, source_target_pairs={{0,1},{1,0},{2,3},{3,2},{4,5},{5,4},{6,7},{7,6},{8,9},{9,8},{10,11... | collective-permute-start | bytes 15728648 | tf_op jit(solution)/shard_map/ppermute | solution.py:42
  135.4 55.8 %all-to-all-start.3 = ((bf16[8,5,40,512]{3,2,1,0:T(8,128)(2,1)}), bf16[8,5,40,512]{3,2,1,0:T(8,128)(2,1)S(1)}, u32[]{:S(2)}, u32[]{:S(2)}) async-start(bf16[8,5,40,512]{3,2,1,0:T(8,128)(2,1)} %bitcast.35), calls=%async_computation.3 | async-start | bytes 3276800 | tf_op jit(solution)/shard_map/all_to_all | solution.py:668
  157.0 30.4 %collective-permute-start.11 = (bf16[2,2,5,32,512]{4,3,2,1,0:T(8,128)(2,1)S(1)}, bf16[2,2,5,32,512]{4,3,2,1,0:T(8,128)(2,1)S(1)}, u32[]{:S(2)}, u32[]{:S(2)}) collective-permute-start(bf16[2,2,5,32,512]{4,3,2,1,0:T(8,128)(2,1)S(1)} %get-tuple-element.85), channel_id=1, source_target_pairs={{0,4},{4,0},{8,12},{12,8},{16,20},{20,16},{24,28},{28,24},{1,5},{5... | collective-permute-start | bytes 1966088 | tf_op jit(solution)/shard_map/ppermute | solution.py:42
  160.1 27.6 %collective-permute-start.9 = (bf16[2,2,5,32,512]{4,3,2,1,0:T(8,128)(2,1)S(1)}, bf16[2,2,5,32,512]{4,3,2,1,0:T(8,128)(2,1)S(1)}, u32[]{:S(2)}, u32[]{:S(2)}) collective-permute-start(bf16[2,2,5,32,512]{4,3,2,1,0:T(8,128)(2,1)S(1)} %get-tuple-element.86), channel_id=1, source_target_pairs={{0,2},{1,3},{2,0},{3,1},{4,6},{5,7},{6,4},{7,5},{8,10},{9,11},{10,... | collective-permute-start | bytes 1966088 | tf_op jit(solution)/shard_map/ppermute | solution.py:42
  166.9 13.2 %collective-permute-start.7 = (bf16[56,1152]{1,0:T(8,128)(2,1)S(1)}, bf16[56,1152]{1,0:T(8,128)(2,1)S(1)}, u32[]{:S(2)}, u32[]{:S(2)}) collective-permute-start(bf16[56,1152]{1,0:T(8,128)(2,1)S(1)} %pad_maximum_fusion.6), channel_id=1, source_target_pairs={{0,6},{1,7},{2,4},{3,5},{4,2},{5,3},{6,0},{7,1},{8,14},{9,15},{10,... | collective-permute-start | bytes 387080 | tf_op jit(solution)/shard_map/ppermute | solution.py:51
  167.9 18.1 %collective-permute-start.6 = (bf16[56,1152]{1,0:T(8,128)(2,1)S(1)}, bf16[56,1152]{1,0:T(8,128)(2,1)S(1)}, u32[]{:S(2)}, u32[]{:S(2)}) collective-permute-start(bf16[56,1152]{1,0:T(8,128)(2,1)S(1)} %pad_maximum_fusion.6), channel_id=1, source_target_pairs={{0,4},{1,5},{2,6},{3,7},{4,0},{5,1},{6,2},{7,3},{8,12},{9,13},{10,... | collective-permute-start | bytes 387080 | tf_op jit(solution)/shard_map/ppermute | solution.py:51
  169.9 16.1 %collective-permute-start.5 = (bf16[56,1152]{1,0:T(8,128)(2,1)S(1)}, bf16[56,1152]{1,0:T(8,128)(2,1)S(1)}, u32[]{:S(2)}, u32[]{:S(2)}) collective-permute-start(bf16[56,1152]{1,0:T(8,128)(2,1)S(1)} %pad_maximum_fusion.6), channel_id=1, source_target_pairs={{0,2},{1,3},{2,0},{3,1},{4,6},{5,7},{6,4},{7,5},{8,10},{9,11},{10,... | collective-permute-start | bytes 387080 | tf_op jit(solution)/shard_map/ppermute | solution.py:51
  192.4 7.3 %collective-permute-start.12 = (bf16[8,5,40,512]{3,2,1,0:T(8,128)(2,1)S(1)}, bf16[8,5,40,512]{3,2,1,0:T(8,128)(2,1)S(1)}, u32[]{:S(2)}, u32[]{:S(2)}) collective-permute-start(bf16[8,5,40,512]{3,2,1,0:T(8,128)(2,1)S(1)} %broadcast_multiply_fusion.3.refs_2_), channel_id=1, source_target_pairs={{0,1},{1,0},{2,3},{3,2},{4,5},{5,4},{6,7},{7,6},{8,9},{9,8},{10,11... | collective-permute-start | bytes 4915208 | tf_op jit(solution)/shard_map/ppermute | solution.py:42
  192.6 24.7 %collective-permute-start.13 = (bf16[2,2,5,32,512]{4,3,2,1,0:T(8,128)(2,1)}, bf16[2,2,5,32,512]{4,3,2,1,0:T(8,128)(2,1)S(1)}, u32[]{:S(2)}, u32[]{:S(2)}) collective-permute-start(bf16[2,2,5,32,512]{4,3,2,1,0:T(8,128)(2,1)} %get-tuple-element.83.refs_5_), channel_id=1, source_target_pairs={{0,4},{4,0},{8,12},{12,8},{16,20},{20,16},{24,28},{28,24},{1,5},{5... | collective-permute-start | bytes 1966088 | tf_op jit(solution)/shard_map/ppermute | solution.py:42
  192.6 24.6 %collective-permute-start.14 = (bf16[2,2,5,32,512]{4,3,2,0,1:T(8,128)(2,1)}, bf16[2,2,5,32,512]{4,3,2,0,1:T(8,128)(2,1)S(1)}, u32[]{:S(2)}, u32[]{:S(2)}) collective-permute-start(bf16[2,2,5,32,512]{4,3,2,0,1:T(8,128)(2,1)} %copy-done.23), channel_id=1, source_target_pairs={{0,2},{1,3},{2,0},{3,1},{4,6},{5,7},{6,4},{7,5},{8,10},{9,11},{10,... | collective-permute-start | bytes 1966088 | tf_op jit(solution)/shard_map/ppermute | solution.py:42
  194.7 29.8 %collective-permute-start.8 = (bf16[2,2,5,32,512]{4,3,2,1,0:T(8,128)(2,1)S(1)}, bf16[2,2,5,32,512]{4,3,2,1,0:T(8,128)(2,1)S(1)}, u32[]{:S(2)}, u32[]{:S(2)}) collective-permute-start(bf16[2,2,5,32,512]{4,3,2,1,0:T(8,128)(2,1)S(1)} %copy-done.10), channel_id=1, source_target_pairs={{0,2},{1,3},{2,0},{3,1},{4,6},{5,7},{6,4},{7,5},{8,10},{9,11},{10,... | collective-permute-start | bytes 1966088 | tf_op jit(solution)/shard_map/ppermute | solution.py:42
  196.3 28.2 %collective-permute-start.10 = (bf16[2,2,5,32,512]{4,3,2,1,0:T(8,128)(2,1)S(1)}, bf16[2,2,5,32,512]{4,3,2,1,0:T(8,128)(2,1)S(1)}, u32[]{:S(2)}, u32[]{:S(2)}) collective-permute-start(bf16[2,2,5,32,512]{4,3,2,1,0:T(8,128)(2,1)S(1)} %copy-done.3), channel_id=1, source_target_pairs={{0,4},{4,0},{8,12},{12,8},{16,20},{20,16},{24,28},{28,24},{1,5},{5... | collective-permute-start | bytes 1966088 | tf_op jit(solution)/shard_map/ppermute | solution.py:42
  216.6 42.7 %collective-permute-start.18 = (bf16[8,5,40,512]{3,2,1,0:T(8,128)(2,1)S(1)}, bf16[8,5,40,512]{3,2,1,0:T(8,128)(2,1)S(1)}, u32[]{:S(2)}, u32[]{:S(2)}) collective-permute-start(bf16[8,5,40,512]{3,2,1,0:T(8,128)(2,1)S(1)} %broadcast_multiply_fusion.2), channel_id=1, source_target_pairs={{0,2},{1,3},{2,0},{3,1},{4,6},{5,7},{6,4},{7,5},{8,10},{9,11},{10,... | collective-permute-start | bytes 4915208 | tf_op jit(solution)/shard_map/ppermute | solution.py:42
  225.5 29.1 %collective-permute-start.17 = (bf16[2,5,32,512]{3,2,1,0:T(8,128)(2,1)S(1)}, bf16[2,5,32,512]{3,2,1,0:T(8,128)(2,1)S(1)}, u32[]{:S(2)}, u32[]{:S(2)}) collective-permute-start(bf16[2,5,32,512]{3,2,1,0:T(8,128)(2,1)S(1)} %pad_maximum_fusion.4.refs_8_), channel_id=1, source_target_pairs={{0,24},{4,28},{8,16},{12,20},{16,8},{20,12},{24,0},{28,4},{1,25},{... | collective-permute-start | bytes 983048 | tf_op jit(solution)/shard_map/ppermute | solution.py:42
  229.4 27.8 %collective-permute-start.16 = (bf16[2,5,32,512]{3,2,1,0:T(8,128)(2,1)S(1)}, bf16[2,5,32,512]{3,2,1,0:T(8,128)(2,1)S(1)}, u32[]{:S(2)}, u32[]{:S(2)}) collective-permute-start(bf16[2,5,32,512]{3,2,1,0:T(8,128)(2,1)S(1)} %pad_maximum_fusion.3.refs_7_), channel_id=1, source_target_pairs={{0,16},{4,20},{8,24},{12,28},{16,0},{20,4},{24,8},{28,12},{1,17},{... | collective-permute-start | bytes 983048 | tf_op jit(solution)/shard_map/ppermute | solution.py:42
  231.8 25.5 %collective-permute-start.15 = (bf16[2,5,32,512]{3,2,1,0:T(8,128)(2,1)S(1)}, bf16[2,5,32,512]{3,2,1,0:T(8,128)(2,1)S(1)}, u32[]{:S(2)}, u32[]{:S(2)}) collective-permute-start(bf16[2,5,32,512]{3,2,1,0:T(8,128)(2,1)S(1)} %pad_maximum_fusion.2.refs_6_), channel_id=1, source_target_pairs={{0,8},{4,12},{8,0},{12,4},{16,24},{20,28},{24,16},{28,20},{1,9},{5... | collective-permute-start | bytes 983048 | tf_op jit(solution)/shard_map/ppermute | solution.py:42
  259.5 24.9 %collective-permute-start.25 = (bf16[2,5,32,512]{3,2,1,0:T(8,128)(2,1)S(1)}, bf16[2,5,32,512]{3,2,1,0:T(8,128)(2,1)S(1)}, u32[]{:S(2)}, u32[]{:S(2)}) collective-permute-start(bf16[2,5,32,512]{3,2,1,0:T(8,128)(2,1)S(1)} %add_convert_fusion.2.refs_5_), channel_id=1, source_target_pairs={{0,24},{4,28},{8,16},{12,20},{16,8},{20,12},{24,0},{28,4},{1,25},{... | collective-permute-start | bytes 983048 | tf_op jit(solution)/shard_map/ppermute | solution.py:42
  262.3 30.2 %collective-permute-start.24 = (bf16[2,5,32,512]{3,2,1,0:T(8,128)(2,1)S(1)}, bf16[2,5,32,512]{3,2,1,0:T(8,128)(2,1)S(1)}, u32[]{:S(2)}, u32[]{:S(2)}) collective-permute-start(bf16[2,5,32,512]{3,2,1,0:T(8,128)(2,1)S(1)} %add_convert_fusion.2.refs_5_), channel_id=1, source_target_pairs={{0,16},{4,20},{8,24},{12,28},{16,0},{20,4},{24,8},{28,12},{1,17},{... | collective-permute-start | bytes 983048 | tf_op jit(solution)/shard_map/ppermute | solution.py:42
  265.4 27.2 %collective-permute-start.23 = (bf16[2,5,32,512]{3,2,1,0:T(8,128)(2,1)S(1)}, bf16[2,5,32,512]{3,2,1,0:T(8,128)(2,1)S(1)}, u32[]{:S(2)}, u32[]{:S(2)}) collective-permute-start(bf16[2,5,32,512]{3,2,1,0:T(8,128)(2,1)S(1)} %add_convert_fusion.2.refs_5_), channel_id=1, source_target_pairs={{0,8},{4,12},{8,0},{12,4},{16,24},{20,28},{24,16},{28,20},{1,9},{5... | collective-permute-start | bytes 983048 | tf_op jit(solution)/shard_map/ppermute | solution.py:42
  292.8 35.6 %collective-permute-start.26 = (bf16[2,4,5,32,512]{4,3,2,1,0:T(8,128)(2,1)S(1)}, bf16[2,4,5,32,512]{4,3,2,1,0:T(8,128)(2,1)S(1)}, u32[]{:S(2)}, u32[]{:S(2)}) collective-permute-start(bf16[2,4,5,32,512]{4,3,2,1,0:T(8,128)(2,1)S(1)} %pad_maximum_fusion.refs_5_.refs_0_), channel_id=1, source_target_pairs={{0,4},{4,0},{8,12},{12,8},{16,20},{20,16},{24,28},{28,24},{1,5},{5... | collective-permute-start | bytes 3932168 | tf_op jit(solution)/shard_map/ppermute | solution.py:42
  294.4 34.2 %collective-permute-start.27 = (bf16[2,4,5,32,512]{4,3,2,1,0:T(8,128)(2,1)S(1)}, bf16[2,4,5,32,512]{4,3,2,1,0:T(8,128)(2,1)S(1)}, u32[]{:S(2)}, u32[]{:S(2)}) collective-permute-start(bf16[2,4,5,32,512]{4,3,2,1,0:T(8,128)(2,1)S(1)} %pad_maximum_fusion.refs_5_.refs_0_), channel_id=1, source_target_pairs={{0,2},{1,3},{2,0},{3,1},{4,6},{5,7},{6,4},{7,5},{8,10},{9,11},{10,... | collective-permute-start | bytes 3932168 | tf_op jit(solution)/shard_map/ppermute | solution.py:42
  294.9 23.2 %collective-permute-start.28 = (bf16[2,4,5,32,512]{4,3,2,1,0:T(8,128)(2,1)S(1)}, bf16[2,4,5,32,512]{4,3,2,1,0:T(8,128)(2,1)S(1)}, u32[]{:S(2)}, u32[]{:S(2)}) collective-permute-start(bf16[2,4,5,32,512]{4,3,2,1,0:T(8,128)(2,1)S(1)} %pad_maximum_fusion.refs_5_.refs_0_), channel_id=1, source_target_pairs={{0,1},{1,0},{2,3},{3,2},{4,5},{5,4},{6,7},{7,6},{8,9},{9,8},{10,11... | collective-permute-start | bytes 3932168 | tf_op jit(solution)/shard_map/ppermute | solution.py:42
  296.2 8.2 %collective-permute-start.22 = (bf16[56,1152]{1,0:T(8,128)(2,1)S(1)}, bf16[56,1152]{1,0:T(8,128)(2,1)S(1)}, u32[]{:S(2)}, u32[]{:S(2)}) collective-permute-start(bf16[56,1152]{1,0:T(8,128)(2,1)S(1)} %pad_maximum_fusion.7), channel_id=1, source_target_pairs={{0,24},{1,25},{2,26},{3,27},{4,28},{5,29},{6,30},{7,31},{8,16},{9,... | collective-permute-start | bytes 387080 | tf_op jit(solution)/shard_map/ppermute | solution.py:51
  298.8 18.0 %collective-permute-start.21 = (bf16[56,1152]{1,0:T(8,128)(2,1)S(1)}, bf16[56,1152]{1,0:T(8,128)(2,1)S(1)}, u32[]{:S(2)}, u32[]{:S(2)}) collective-permute-start(bf16[56,1152]{1,0:T(8,128)(2,1)S(1)} %pad_maximum_fusion.7), channel_id=1, source_target_pairs={{0,16},{1,17},{2,18},{3,19},{4,20},{5,21},{6,22},{7,23},{8,24},{9,... | collective-permute-start | bytes 387080 | tf_op jit(solution)/shard_map/ppermute | solution.py:51
  304.4 12.4 %collective-permute-start.20 = (bf16[56,1152]{1,0:T(8,128)(2,1)S(1)}, bf16[56,1152]{1,0:T(8,128)(2,1)S(1)}, u32[]{:S(2)}, u32[]{:S(2)}) collective-permute-start(bf16[56,1152]{1,0:T(8,128)(2,1)S(1)} %pad_maximum_fusion.7), channel_id=1, source_target_pairs={{0,8},{1,9},{2,10},{3,11},{4,12},{5,13},{6,14},{7,15},{8,0},{9,1},... | collective-permute-start | bytes 387080 | tf_op jit(solution)/shard_map/ppermute | solution.py:51
  329.1 16.8 %collective-permute-start.29 = (bf16[4,5,32,512]{3,2,1,0:T(8,128)(2,1)S(1)}, bf16[4,5,32,512]{3,2,1,0:T(8,128)(2,1)S(1)}, u32[]{:S(2)}, u32[]{:S(2)}) collective-permute-start(bf16[4,5,32,512]{3,2,1,0:T(8,128)(2,1)S(1)} %fusion.12), channel_id=1, source_target_pairs={{0,2},{1,3},{2,0},{3,1},{4,6},{5,7},{6,4},{7,5},{8,10},{9,11},{10,... | collective-permute-start | bytes 1966088 | tf_op jit(solution)/shard_map/ppermute | solution.py:42
  330.7 16.5 %collective-permute-start.32 = (bf16[4,5,32,512]{3,2,1,0:T(8,128)(2,1)S(1)}, bf16[4,5,32,512]{3,2,1,0:T(8,128)(2,1)S(1)}, u32[]{:S(2)}, u32[]{:S(2)}) collective-permute-start(bf16[4,5,32,512]{3,2,1,0:T(8,128)(2,1)S(1)} %fusion.11), channel_id=1, source_target_pairs={{0,4},{4,0},{8,12},{12,8},{16,20},{20,16},{24,28},{28,24},{1,5},{5... | collective-permute-start | bytes 1966088 | tf_op jit(solution)/shard_map/ppermute | solution.py:42
  (52 other events, 380.2 us)

commit v11 on v10

--- a/solution.py
+++ b/solution.py
@@ -15,7 +15,7 @@
 LOOK_BLOCKS = 8
 LOOK_ROWS = 32
 ADD_LOW = 512
-ADD_TABS = 4
+ADD_TABS = 8
 NEAR_FIRST = 2
 FAR_FIRST = 2
 MAIN = 1024
@@ -130,7 +130,7 @@
     )(wanted, own_rows, tables)
 
 
-def add_kernel(part_count, has_before, base_ref, *refs):
+def add_kernel(part_count, has_before, steps, base_ref, *refs):
     ids_refs = refs[:part_count]
     grad_refs = refs[part_count : 2 * part_count]
     before_ref = refs[2 * part_count] if has_before else None
@@ -142,7 +142,8 @@
 
     @pl.when(step == 0)
     def _():
-        total[...] = jnp.zeros_like(total)
+        if steps > 1:
+            total[...] = jnp.zeros_like(total)
         token_ref[...] = jnp.zeros_like(token_ref)
 
     high_iota = lax.broadcasted_iota(I32, (high_count, cols), 0)
@@ -161,7 +162,8 @@
             term = lax.dot_general(left, low_hot, NT, preferred_element_type=F32)
             product = term if product is None else product + term
     for lane in range(ADD_LOW // 128):
-        total[lane] += product[:, lane * 128 : (lane + 1) * 128]
+        part = product[:, lane * 128 : (lane + 1) * 128]
+        total[lane] = part if steps == 1 else total[lane] + part
 
     @pl.when(step == pl.num_programs(0) - 1)
     def _():
@@ -183,7 +185,7 @@
     block = pl.BlockSpec((1, embed_dim, share), lambda t: (slot, 0, 0))
     whole = [] if so_far is None else [so_far]
     table_grad, token = pl.pallas_call(
-        functools.partial(add_kernel, part_count, accumulate),
+        functools.partial(add_kernel, part_count, accumulate, tab_count // ADD_TABS),
         grid=(tab_count // ADD_TABS,),
         in_specs=[pl.BlockSpec(memory_space=pltpu.SMEM)]
         + [pl.BlockSpec((ADD_TABS, 1, 1, count), lambda t: (t, slot, 0, 0))] * part_count
@@ -755,19 +757,19 @@
     values = joined(parts, token)
     from_y = swap(values, "tab", 1)
     from_x = swap(values, "rep", 2)
-    small = small + zero_of(values[0, 0, 0, 0, 0])
+    add_next(False, 1, [values])
+    other = [swap(values, "rep", 1)]
+    add_next(False, 1, other)
+    last = [swap(gate(from_y[0], token), "rep", 2), swap(gate(from_x[1], token), "tab", 1)]
+    small = small + zero_of(token)
     small = small_step(small, [(0, 2), (0, 4), (0, 6)])
     for rep_mask in masks_of("rep")[2:]:
         small = small_step(small, [(rep_mask, 0)])
     for tab_mask in masks_of("tab")[3:]:
         small = small_step(small, [(0, tab_mask)])
-    add_next(False, 1, [values])
-    other = [swap(values, "rep", 1)]
-    add_next(False, 1, other)
-    token = token + zero_of(small[0, 0])
-    last = [swap(gate(from_y[0], token), "rep", 2), swap(gate(from_x[1], token), "tab", 1)]
     other += [swap(from_y, "rep", 1), swap(from_x, "rep", 1)]
     add_next(False, slot_count, other)
+    token = token + zero_of(small[0, 0])
     last = [gate(part, token) for part in last]
     blocks = [values, from_y, from_x] + last + other + [swap(part, "rep", 1) for part in last]
 

time: 370 us -> 376 us (1.016)
  other arithmetic: 27 us -> 34.2 us
  Pallas kernels: 185 us -> 181 us
    ppermute x28, waiting for transfers between devices: 21.1 us -> 25.5 us  [swap(): lax.ppermute(value, axis, [(at, at ^ mask) for at in range(lax.axis_size(...]
    ppermute x7, waiting for transfers between devices: 18 us -> 13.7 us  [swap_both(): return lax.ppermute(value, ('tab', 'rep'), perm)]
    unnamed x93 -> x95, local copies, waits for them, and re-layouts: 14.3 us -> 16.7 us
  transfers between devices with their start and end apart: 39 -> 39, of which waited for: 12 -> 12; matrix products, arithmetic and copies ran while one was open for 14% -> 14% of each run, Pallas kernels for 31% -> 29%
where the time goes in v11:
time: 376 us; the launch traced here: 372 us
  Pallas kernels  181 us (48%)
  starting transfers between devices  56.1 us (15%)
  waiting for transfers between devices  51.9 us (14%)
  local copies, waits for them, and re-layouts  35.7 us (9%)
  other arithmetic  34.2 us (9%)
  between operations  13.1 us (3%)
    pallas_call x10, Pallas kernels, add_rows(): pl.pallas_call(functools.partial(add_kernel, part_count, accumulate, tab_...  79 us
    pallas_call x2, Pallas kernels, lookup(): pl.pallas_call(functools.partial(lookup_kernel, first_slot), in_specs=[sm...  39.2 us
    pallas_call x1, Pallas kernels, dense_step(): pl.pallas_call(functools.partial(dense_kernel, dense_width, width, starts...  27.5 us
    ppermute x28, starting transfers between devices, swap(): lax.ppermute(value, axis, [(at, at ^ mask) for at in range(lax.axis_size(...  26.7 us
    ppermute x28, waiting for transfers between devices, swap(): lax.ppermute(value, axis, [(at, at ^ mask) for at in range(lax.axis_size(...  25.5 us
    pallas_call x2, Pallas kernels, weight_parts(): pl.pallas_call(functools.partial(weight_kernel, core), grid=(matrix_count...  22.4 us
    unnamed x95, local copies, waits for them, and re-layouts  16.7 us
    ppermute x7, waiting for transfers between devices, swap_both(): return lax.ppermute(value, ('tab', 'rep'), perm)  13.7 us
  transfers between devices with their start and end apart: 39, of which 12 were waited for; matrix products, arithmetic and copies ran while one was open for 14% of the time, Pallas kernels for 29%

profile of v11, /device:TPU:0, one launch (start us, length us, event | category | flops | bytes accessed | tf_op | source)
XLA Modules:
  0.0 372.3 jit_solution(4926050854506387139)
XLA Ops:
  5.2 7.3 %all-to-all-start = ((s32[8,5,512]{2,1,0:T(8,128)}), s32[8,5,512]{2,1,0:T(8,128)S(1)}, u32[]{:S(2)}, u32[]{:S(2)}) async-start(s32[8,5,512]{2,1,0:T(8,128)} %reshape.530), calls=%async_computation | async-start | bytes 262144 | tf_op jit(solution)/shard_map/all_to_all | solution.py:623
  13.8 6.0 %all-to-all-done = s32[8,5,512]{2,1,0:T(8,128)S(1)} async-done(((s32[8,5,512]{2,1,0:T(8,128)}), s32[8,5,512]{2,1,0:T(8,128)S(1)}, u32[]{:S(2)}, u32[]{:S(2)}) %all-to-all-start) | async-done | bytes 81952 | tf_op jit(solution)/shard_map/all_to_all | solution.py:623
  20.5 24.5 %lookup.2 = bf16[8,3,40,512]{3,2,1,0:T(8,128)(2,1)} custom-call(s32[20480]{0:T(1024)} %bitcast.136, s32[5]{0:T(128)} %dynamic_slice.3.rows_ref, bf16[5,39,32768]{2,1,0:T(8,128)(2,1)} %table_hbm.3), custom_call_target="tpu_custom_call" | custom-call | flops 30198988 | bytes 8626 | tf_op jit(solution)/shard_map/lookup/pallas_call | solution.py:112
  45.0 3.6 all-to-all-start.1
  50.4 14.7 %lookup.3 = bf16[8,2,40,512]{3,2,1,0:T(8,128)(2,1)} custom-call(s32[20480]{0:T(1024)} %bitcast.137, s32[5]{0:T(128)} %dynamic_slice.3.rows_ref, bf16[5,39,32768]{2,1,0:T(8,128)(2,1)} %table_hbm.3), custom_call_target="tpu_custom_call" | custom-call | flops 20132660 | bytes 5750 | tf_op jit(solution)/shard_map/lookup/pallas_call | solution.py:112
  65.2 6.7 %all-to-all-done.1.refs_0_ = bf16[8,3,40,512]{3,2,1,0:T(8,128)(2,1)S(1)} async-done(((bf16[8,3,40,512]{3,2,1,0:T(8,128)(2,1)}), bf16[8,3,40,512]{3,2,1,0:T(8,128)(2,1)S(1)}, u32[]{:S(2)}, u32[]{:S(2)}) %all-to-all-start.1) | async-done | bytes 983072 | tf_op jit(solution)/shard_map/all_to_all | solution.py:634
  71.9 4.6 %all-to-all-start.2 = ((bf16[8,2,40,512]{3,2,1,0:T(8,128)(2,1)}), bf16[8,2,40,512]{3,2,1,0:T(8,128)(2,1)S(1)}, u32[]{:S(2)}, u32[]{:S(2)}) async-start(bf16[8,2,40,512]{3,2,1,0:T(8,128)(2,1)} %lookup.3), calls=%async_computation.2 | async-start | bytes 1310720 | tf_op jit(solution)/shard_map/all_to_all | solution.py:634
  79.9 3.9 %multiply_bitcast_fusion = (bf16[1027,1027]{1,0:T(8,128)(2,1)S(1)}, bf16[1027,1027]{1,0:T(8,128)(2,1)S(1)}, bf16[1027,1027]{1,0:T(8,128)(2,1)S(1)}) fusion(bf16[3,1027,1027]{2,1,0:T(8,128)(2,1)} %param.20, bf16[]{:T(256)} %bitcast.6), kind=kLoop, calls=%fused_computation.7 | loop fusion | flops 3164187 | bytes 12656750 | tf_op jit(solution)/shard_map/mul | solution.py:639
  101.3 27.5 %dense.1 = (f32[1,512]{1,0:T(1,128)}, f32[16,512]{1,0:T(8,128)}, bf16[40,40,512]{2,1,0:T(8,128)(2,1)}, bf16[5,1152,512]{2,1,0:T(8,128)(2,1)}, bf16[5,1152,512]{2,1,0:T(8,128)(2,1)}, /*index=5*/f32[8,1152]{1,0:T(8,128)}) custom-call(s32[26]{0:T(128)} %place_ref.1, f32[1]{0:T(128)S(6)} %convert.67.bias_ref, bf16[8,3,40,512]{3,2,1,0:T(8,128)(2,1)} %copy-done.20, ...), custom_call_target="tpu_custom_call" | custom-call | flops 13589544 | bytes 30965 | tf_op jit(solution)/shard_map/dense/pallas_call | solution.py:381
  128.8 9.7 %weight_parts.3 = bf16[2,16,5,32,512]{4,3,2,1,0:T(8,128)(2,1)} custom-call(s32[1]{0:T(128)} %bitcast.own_ref, bf16[5,1152,512]{2,1,0:T(8,128)(2,1)} %get-tuple-element.43.left_ref, bf16[5,1152,512]{2,1,0:T(8,128)(2,1)} %get-tuple-element.44.right_ref), custom_call_target="tpu_custom_call" | custom-call | flops 3397386 | bytes 33177 | tf_op jit(solution)/shard_map/weight_parts/pallas_call | solution.py:463
  138.5 6.0 %all-to-all-start.3 = ((bf16[8,5,40,512]{3,2,1,0:T(8,128)(2,1)}), bf16[8,5,40,512]{3,2,1,0:T(8,128)(2,1)S(1)}, u32[]{:S(2)}, u32[]{:S(2)}) async-start(bf16[8,5,40,512]{3,2,1,0:T(8,128)(2,1)} %bitcast.29), calls=%async_computation.3 | async-start | bytes 3276800 | tf_op jit(solution)/shard_map/all_to_all | solution.py:670
  144.5 12.7 %weight_parts.2 = (f32[2,16,5,32,512]{4,3,2,1,0:T(8,128)}, f32[5,8,1152]{2,1,0:T(8,128)}) custom-call(s32[1]{0:T(128)} %bitcast.own_ref, bf16[5,1152,512]{2,1,0:T(8,128)(2,1)} %get-tuple-element.43.left_ref, bf16[5,1152,512]{2,1,0:T(8,128)(2,1)} %get-tuple-element.44.right_ref), custom_call_target="tpu_custom_call" | custom-call | flops 3397386 | bytes 33177 | tf_op jit(solution)/shard_map/weight_parts/pallas_call | solution.py:463
  166.0 3.6 fusion.9
  173.4 3.0 convert_add_fusion
  176.4 5.4 %collective-permute-done.7 = bf16[56,1152]{1,0:T(8,128)(2,1)S(1)} collective-permute-done((bf16[56,1152]{1,0:T(8,128)(2,1)S(1)}, bf16[56,1152]{1,0:T(8,128)(2,1)S(1)}, u32[]{:S(2)}, u32[]{:S(2)}) %collective-permute-start.7) | collective-permute-done | bytes 129056 | tf_op jit(solution)/shard_map/ppermute | solution.py:51
  181.9 8.0 %collective-permute-done.6 = bf16[56,1152]{1,0:T(8,128)(2,1)S(1)} collective-permute-done((bf16[56,1152]{1,0:T(8,128)(2,1)S(1)}, bf16[56,1152]{1,0:T(8,128)(2,1)S(1)}, u32[]{:S(2)}, u32[]{:S(2)}) %collective-permute-start.6) | collective-permute-done | bytes 129056 | tf_op jit(solution)/shard_map/ppermute | solution.py:51
  204.1 6.9 %add_rows.10 = (f32[5,39,8192]{2,1,0:T(8,128)}, f32[8,128]{1,0:T(8,128)S(1)}) custom-call(s32[1]{0:T(128)} %bitcast.28.base_ref, s32[8,5,1,512]{3,2,1,0:T(1,128)S(1)} %copy-done.8, s32[8,5,1,512]{3,2,1,0:T(1,128)S(1)} %copy-done.9, bf16[8,5,40,512]{3,2,1,0:T(8,128)(2,1)S(1)} %broadcast_multiply_fusion.3.refs_2_, ...), custom_call_target="tpu_custom_call" | custom-call | flops 5234491 | bytes 1916 | tf_op jit(solution)/shard_map/add_rows/pallas_call | solution.py:187
  213.3 7.3 %add_rows.11 = (f32[5,39,8192]{2,1,0:T(8,128)}, f32[8,128]{1,0:T(8,128)S(1)}) custom-call(s32[1]{0:T(128)} %bitcast.28.base_ref, s32[8,5,1,512]{3,2,1,0:T(1,128)S(1)} %copy-done.8, s32[8,5,1,512]{3,2,1,0:T(1,128)S(1)} %copy-done.9, bf16[8,5,40,512]{3,2,1,0:T(8,128)(2,1)S(1)} %broadcast_multiply_fusion.3.refs_2_, ...), custom_call_target="tpu_custom_call", output_to_operand_aliasing={{0}: (5, {})} | custom-call | flops 5234491 | bytes 1916 | tf_op jit(solution)/shard_map/add_rows/pallas_call | solution.py:187
  222.1 7.1 %collective-permute-done.12 = bf16[2,2,5,32,512]{4,3,2,1,0:T(8,128)(2,1)S(1)} collective-permute-done((bf16[2,2,5,32,512]{4,3,2,1,0:T(8,128)(2,1)S(1)}, bf16[2,2,5,32,512]{4,3,2,1,0:T(8,128)(2,1)S(1)}, u32[]{:S(2)}, u32[]{:S(2)}) %collective-permute-start.12) | collective-permute-done | bytes 655392 | tf_op jit(solution)/shard_map/ppermute | solution.py:42
  230.3 3.2 collective-permute-start.18
  236.4 6.9 %add_rows.12 = (f32[5,39,8192]{2,1,0:T(8,128)}, f32[8,128]{1,0:T(8,128)}) custom-call(s32[1]{0:T(128)} %bitcast.28.base_ref, s32[8,5,1,512]{3,2,1,0:T(1,128)S(1)} %copy-done.8, s32[8,5,1,512]{3,2,1,0:T(1,128)S(1)} %copy-done.9, bf16[8,5,40,512]{3,2,1,0:T(8,128)(2,1)S(1)} %broadcast_multiply_fusion.3.refs_2_, ...), custom_call_target="tpu_custom_call", output_to_operand_aliasing={{0}: (5, {})} | custom-call | flops 5234491 | bytes 1916 | tf_op jit(solution)/shard_map/add_rows/pallas_call | solution.py:187
  243.3 7.1 %add_rows.13 = (f32[5,39,8192]{2,1,0:T(8,128)}, f32[8,128]{1,0:T(8,128)}) custom-call(s32[1]{0:T(128)} %bitcast.28.base_ref, s32[8,5,1,512]{3,2,1,0:T(1,128)S(1)} %copy-done.8, s32[8,5,1,512]{3,2,1,0:T(1,128)S(1)} %copy-done.9, bf16[8,5,40,512]{3,2,1,0:T(8,128)(2,1)S(1)} %broadcast_multiply_fusion.3.refs_2_, ...), custom_call_target="tpu_custom_call", output_to_operand_aliasing={{0}: (5, {})} | custom-call | flops 5234491 | bytes 1916 | tf_op jit(solution)/shard_map/add_rows/pallas_call | solution.py:187
  250.4 6.9 %add_rows.14 = (f32[5,39,8192]{2,1,0:T(8,128)}, f32[8,128]{1,0:T(8,128)S(1)}) custom-call(s32[1]{0:T(128)} %bitcast.28.base_ref, s32[8,5,1,512]{3,2,1,0:T(1,128)S(1)} %copy-done.8, s32[8,5,1,512]{3,2,1,0:T(1,128)S(1)} %copy-done.9, bf16[8,5,40,512]{3,2,1,0:T(8,128)(2,1)S(1)} %broadcast_multiply_fusion.3.refs_2_, ...), custom_call_target="tpu_custom_call", output_to_operand_aliasing={{0}: (5, {})} | custom-call | flops 5234491 | bytes 1916 | tf_op jit(solution)/shard_map/add_rows/pallas_call | solution.py:187
  257.8 4.2 %collective-permute-done.17 = bf16[2,5,32,512]{3,2,1,0:T(8,128)(2,1)S(1)} collective-permute-done((bf16[2,5,32,512]{3,2,1,0:T(8,128)(2,1)S(1)}, bf16[2,5,32,512]{3,2,1,0:T(8,128)(2,1)S(1)}, u32[]{:S(2)}, u32[]{:S(2)}) %collective-permute-start.17) | collective-permute-done | bytes 327712 | tf_op jit(solution)/shard_map/ppermute | solution.py:42
  269.9 8.6 %add_rows.15 = (f32[5,39,8192]{2,1,0:T(8,128)}, f32[8,128]{1,0:T(8,128)}) custom-call(s32[1]{0:T(128)} %bitcast.28.base_ref, s32[8,5,1,512]{3,2,1,0:T(1,128)S(1)} %copy-done.10, s32[8,5,1,512]{3,2,1,0:T(1,128)S(1)} %copy-done.11, bf16[8,5,40,512]{3,2,1,0:T(8,128)(2,1)S(1)} %broadcast_multiply_fusion.1.refs_2_, ...), custom_call_target="tpu_custom_call", output_to_operand_aliasing={{0}: (5, {})} | custom-call | flops 5234491 | bytes 1916 | tf_op jit(solution)/shard_map/add_rows/pallas_call | solution.py:187
  278.5 8.3 %add_rows.16 = (f32[5,39,8192]{2,1,0:T(8,128)}, f32[8,128]{1,0:T(8,128)S(1)}) custom-call(s32[1]{0:T(128)} %bitcast.28.base_ref, s32[8,5,1,512]{3,2,1,0:T(1,128)S(1)} %copy-done.10, s32[8,5,1,512]{3,2,1,0:T(1,128)S(1)} %copy-done.11, bf16[8,5,40,512]{3,2,1,0:T(8,128)(2,1)S(1)} %broadcast_multiply_fusion.1.refs_2_, ...), custom_call_target="tpu_custom_call", output_to_operand_aliasing={{0}: (5, {})} | custom-call | flops 5234491 | bytes 1916 | tf_op jit(solution)/shard_map/add_rows/pallas_call | solution.py:187
  288.1 9.2 %collective-permute-done.21 = bf16[2,5,32,512]{3,2,1,0:T(8,128)(2,1)S(1)} collective-permute-done((bf16[2,5,32,512]{3,2,1,0:T(8,128)(2,1)S(1)}, bf16[2,5,32,512]{3,2,1,0:T(8,128)(2,1)S(1)}, u32[]{:S(2)}, u32[]{:S(2)}) %collective-permute-start.21) | collective-permute-done | bytes 327712 | tf_op jit(solution)/shard_map/ppermute | solution.py:42
  302.1 8.7 %add_rows.17 = (f32[5,39,8192]{2,1,0:T(8,128)}, f32[8,128]{1,0:T(8,128)}) custom-call(s32[1]{0:T(128)} %bitcast.28.base_ref, s32[8,5,1,512]{3,2,1,0:T(1,128)S(1)} %copy-done.10, s32[8,5,1,512]{3,2,1,0:T(1,128)S(1)} %copy-done.11, bf16[8,5,40,512]{3,2,1,0:T(8,128)(2,1)S(1)} %broadcast_multiply_fusion.1.refs_2_, ...), custom_call_target="tpu_custom_call", output_to_operand_aliasing={{0}: (5, {})} | custom-call | flops 5234491 | bytes 1916 | tf_op jit(solution)/shard_map/add_rows/pallas_call | solution.py:187
  310.9 8.8 %add_rows.18 = (f32[5,39,8192]{2,1,0:T(8,128)}, f32[8,128]{1,0:T(8,128)S(1)}) custom-call(s32[1]{0:T(128)} %bitcast.28.base_ref, s32[8,5,1,512]{3,2,1,0:T(1,128)S(1)} %copy-done.10, s32[8,5,1,512]{3,2,1,0:T(1,128)S(1)} %copy-done.11, bf16[8,5,40,512]{3,2,1,0:T(8,128)(2,1)S(1)} %broadcast_multiply_fusion.1.refs_2_, ...), custom_call_target="tpu_custom_call", output_to_operand_aliasing={{0}: (5, {})} | custom-call | flops 5234491 | bytes 1916 | tf_op jit(solution)/shard_map/add_rows/pallas_call | solution.py:187
  326.8 3.9 %collective-permute-done.27.refs_1_ = bf16[2,4,5,32,512]{4,3,2,1,0:T(8,128)(2,1)} collective-permute-done((bf16[2,4,5,32,512]{4,3,2,1,0:T(8,128)(2,1)}, bf16[2,4,5,32,512]{4,3,2,1,0:T(8,128)(2,1)}, u32[]{:S(2)}, u32[]{:S(2)}) %collective-permute-start.27) | collective-permute-done | bytes 1310752 | tf_op jit(solution)/shard_map/ppermute | solution.py:42
  343.1 9.4 %add_rows.19 = (f32[5,39,8192]{2,1,0:T(8,128)}, f32[8,128]{1,0:T(8,128)S(1)}) custom-call(s32[1]{0:T(128)} %bitcast.28.base_ref, s32[8,5,1,512]{3,2,1,0:T(1,128)S(1)} %copy-done.10, s32[8,5,1,512]{3,2,1,0:T(1,128)S(1)} %copy-done.11, bf16[8,5,40,512]{3,2,1,0:T(8,128)(2,1)S(1)} %broadcast_multiply_fusion.1.refs_2_, ...), custom_call_target="tpu_custom_call", output_to_operand_aliasing={{0}: (5, {})} | custom-call | flops 5234491 | bytes 1916 | tf_op jit(solution)/shard_map/add_rows/pallas_call | solution.py:187
  357.6 13.3 %assemble.1 = (f32[3,1027,1027]{2,1,0:T(8,128)}, f32[1,1027,1024]{2,1,0:T(8,128)}, f32[1,1024,1024]{2,1,0:T(8,128)}) custom-call(s32[1]{0:T(128)} %bitcast.own_ref, bf16[2,4,5,32,512]{4,3,2,1,0:T(8,128)(2,1)} %pad_maximum_fusion.refs_5_.refs_0_, bf16[2,4,5,32,512]{4,3,2,1,0:T(8,128)(2,1)} %collective-permute-done.27.refs_1_, ...), custom_call_target="tpu_custom_call" | custom-call | bytes 39813 | tf_op jit(solution)/shard_map/assemble/pallas_call | solution.py:568
  (272 shorter events, 92.2 us)
Async XLA Ops:
  5.2 14.6 %all-to-all-start = ((s32[8,5,512]{2,1,0:T(8,128)}), s32[8,5,512]{2,1,0:T(8,128)S(1)}, u32[]{:S(2)}, u32[]{:S(2)}) async-start(s32[8,5,512]{2,1,0:T(8,128)} %reshape.530), calls=%async_computation | async-start | bytes 262144 | tf_op jit(solution)/shard_map/all_to_all | solution.py:623
  45.0 26.9 %all-to-all-start.1 = ((bf16[8,3,40,512]{3,2,1,0:T(8,128)(2,1)}), bf16[8,3,40,512]{3,2,1,0:T(8,128)(2,1)S(1)}, u32[]{:S(2)}, u32[]{:S(2)}) async-start(bf16[8,3,40,512]{3,2,1,0:T(8,128)(2,1)} %lookup.2), calls=%async_computation.1 | async-start | bytes 1966080 | tf_op jit(solution)/shard_map/all_to_all | solution.py:634
  71.9 28.5 %all-to-all-start.2 = ((bf16[8,2,40,512]{3,2,1,0:T(8,128)(2,1)}), bf16[8,2,40,512]{3,2,1,0:T(8,128)(2,1)S(1)}, u32[]{:S(2)}, u32[]{:S(2)}) async-start(bf16[8,2,40,512]{3,2,1,0:T(8,128)(2,1)} %lookup.3), calls=%async_computation.2 | async-start | bytes 1310720 | tf_op jit(solution)/shard_map/all_to_all | solution.py:634
  77.7 18.8 %collective-permute-start.1 = (s32[8,5,512]{2,1,0:T(8,128)S(1)}, s32[8,5,512]{2,1,0:T(8,128)S(1)}, u32[]{:S(2)}, u32[]{:S(2)}) collective-permute-start(s32[8,5,512]{2,1,0:T(8,128)S(1)} %broadcast_add_fusion), channel_id=1, source_target_pairs={{0,2},{1,3},{2,0},{3,1},{4,6},{5,7},{6,4},{7,5},{8,10},{9,11},{10,... | collective-permute-start | bytes 245768 | tf_op jit(solution)/shard_map/ppermute | solution.py:42
  79.3 19.7 %collective-permute-start = (s32[8,5,512]{2,1,0:T(8,128)S(1)}, s32[8,5,512]{2,1,0:T(8,128)S(1)}, u32[]{:S(2)}, u32[]{:S(2)}) collective-permute-start(s32[8,5,512]{2,1,0:T(8,128)S(1)} %broadcast_add_fusion), channel_id=1, source_target_pairs={{0,1},{1,0},{2,3},{3,2},{4,5},{5,4},{6,7},{7,6},{8,9},{9,8},{10,11... | collective-permute-start | bytes 245768 | tf_op jit(solution)/shard_map/ppermute | solution.py:42
  138.5 18.7 %collective-permute-start.3 = (bf16[2,2,2,2,2,5,32,512]{7,6,5,4,3,2,1,0:T(8,128)(2,1)}, bf16[2,2,2,2,2,5,32,512]{7,6,5,4,3,2,1,0:T(8,128)(2,1)}, u32[]{:S(2)}, u32[]{:S(2)}) collective-permute-start(bf16[2,2,2,2,2,5,32,512]{7,6,5,4,3,2,1,0:T(8,128)(2,1)} %bitcast.134), channel_id=1, source_target_pairs={{0,1},{1,0},{2,3},{3,2},{4,5},{5,4},{6,7},{7,6},{8,9},{9,8},{10,11... | collective-permute-start | bytes 15728648 | tf_op jit(solution)/shard_map/ppermute | solution.py:42
  138.5 57.3 %all-to-all-start.3 = ((bf16[8,5,40,512]{3,2,1,0:T(8,128)(2,1)}), bf16[8,5,40,512]{3,2,1,0:T(8,128)(2,1)S(1)}, u32[]{:S(2)}, u32[]{:S(2)}) async-start(bf16[8,5,40,512]{3,2,1,0:T(8,128)(2,1)} %bitcast.29), calls=%async_computation.3 | async-start | bytes 3276800 | tf_op jit(solution)/shard_map/all_to_all | solution.py:670
  159.9 31.4 %collective-permute-start.8 = (bf16[2,2,5,32,512]{4,3,2,1,0:T(8,128)(2,1)S(1)}, bf16[2,2,5,32,512]{4,3,2,1,0:T(8,128)(2,1)S(1)}, u32[]{:S(2)}, u32[]{:S(2)}) collective-permute-start(bf16[2,2,5,32,512]{4,3,2,1,0:T(8,128)(2,1)S(1)} %get-tuple-element.86), channel_id=1, source_target_pairs={{0,2},{1,3},{2,0},{3,1},{4,6},{5,7},{6,4},{7,5},{8,10},{9,11},{10,... | collective-permute-start | bytes 1966088 | tf_op jit(solution)/shard_map/ppermute | solution.py:42
  161.6 31.3 %collective-permute-start.9 = (bf16[2,2,5,32,512]{4,3,2,1,0:T(8,128)(2,1)S(1)}, bf16[2,2,5,32,512]{4,3,2,1,0:T(8,128)(2,1)S(1)}, u32[]{:S(2)}, u32[]{:S(2)}) collective-permute-start(bf16[2,2,5,32,512]{4,3,2,1,0:T(8,128)(2,1)S(1)} %get-tuple-element.85), channel_id=1, source_target_pairs={{0,4},{4,0},{8,12},{12,8},{16,20},{20,16},{24,28},{28,24},{1,5},{5... | collective-permute-start | bytes 1966088 | tf_op jit(solution)/shard_map/ppermute | solution.py:42
  169.8 12.0 %collective-permute-start.7 = (bf16[56,1152]{1,0:T(8,128)(2,1)S(1)}, bf16[56,1152]{1,0:T(8,128)(2,1)S(1)}, u32[]{:S(2)}, u32[]{:S(2)}) collective-permute-start(bf16[56,1152]{1,0:T(8,128)(2,1)S(1)} %pad_maximum_fusion.6), channel_id=1, source_target_pairs={{0,6},{1,7},{2,4},{3,5},{4,2},{5,3},{6,0},{7,1},{8,14},{9,15},{10,... | collective-permute-start | bytes 387080 | tf_op jit(solution)/shard_map/ppermute | solution.py:51
  170.8 19.1 %collective-permute-start.6 = (bf16[56,1152]{1,0:T(8,128)(2,1)S(1)}, bf16[56,1152]{1,0:T(8,128)(2,1)S(1)}, u32[]{:S(2)}, u32[]{:S(2)}) collective-permute-start(bf16[56,1152]{1,0:T(8,128)(2,1)S(1)} %pad_maximum_fusion.6), channel_id=1, source_target_pairs={{0,4},{1,5},{2,6},{3,7},{4,0},{5,1},{6,2},{7,3},{8,12},{9,13},{10,... | collective-permute-start | bytes 387080 | tf_op jit(solution)/shard_map/ppermute | solution.py:51
  172.8 17.1 %collective-permute-start.5 = (bf16[56,1152]{1,0:T(8,128)(2,1)S(1)}, bf16[56,1152]{1,0:T(8,128)(2,1)S(1)}, u32[]{:S(2)}, u32[]{:S(2)}) collective-permute-start(bf16[56,1152]{1,0:T(8,128)(2,1)S(1)} %pad_maximum_fusion.6), channel_id=1, source_target_pairs={{0,2},{1,3},{2,0},{3,1},{4,6},{5,7},{6,4},{7,5},{8,10},{9,11},{10,... | collective-permute-start | bytes 387080 | tf_op jit(solution)/shard_map/ppermute | solution.py:51
  197.3 23.9 %collective-permute-start.14 = (bf16[2,2,5,32,512]{4,3,2,1,0:T(8,128)(2,1)}, bf16[2,2,5,32,512]{4,3,2,1,0:T(8,128)(2,1)S(1)}, u32[]{:S(2)}, u32[]{:S(2)}) collective-permute-start(bf16[2,2,5,32,512]{4,3,2,1,0:T(8,128)(2,1)} %get-tuple-element.83.refs_5_), channel_id=1, source_target_pairs={{0,4},{4,0},{8,12},{12,8},{16,20},{20,16},{24,28},{28,24},{1,5},{5... | collective-permute-start | bytes 1966088 | tf_op jit(solution)/shard_map/ppermute | solution.py:42
  197.4 23.8 %collective-permute-start.15 = (bf16[2,2,5,32,512]{4,3,2,1,0:T(8,128)(2,1)}, bf16[2,2,5,32,512]{4,3,2,1,0:T(8,128)(2,1)S(1)}, u32[]{:S(2)}, u32[]{:S(2)}) collective-permute-start(bf16[2,2,5,32,512]{4,3,2,1,0:T(8,128)(2,1)} %copy-done.4), channel_id=1, source_target_pairs={{0,2},{1,3},{2,0},{3,1},{4,6},{5,7},{6,4},{7,5},{8,10},{9,11},{10,... | collective-permute-start | bytes 1966088 | tf_op jit(solution)/shard_map/ppermute | solution.py:42
  199.5 29.8 %collective-permute-start.12 = (bf16[2,2,5,32,512]{4,3,2,1,0:T(8,128)(2,1)S(1)}, bf16[2,2,5,32,512]{4,3,2,1,0:T(8,128)(2,1)S(1)}, u32[]{:S(2)}, u32[]{:S(2)}) collective-permute-start(bf16[2,2,5,32,512]{4,3,2,1,0:T(8,128)(2,1)S(1)} %copy-done.12), channel_id=1, source_target_pairs={{0,2},{1,3},{2,0},{3,1},{4,6},{5,7},{6,4},{7,5},{8,10},{9,11},{10,... | collective-permute-start | bytes 1966088 | tf_op jit(solution)/shard_map/ppermute | solution.py:42
  201.0 28.2 %collective-permute-start.13 = (bf16[2,2,5,32,512]{4,3,2,1,0:T(8,128)(2,1)S(1)}, bf16[2,2,5,32,512]{4,3,2,1,0:T(8,128)(2,1)S(1)}, u32[]{:S(2)}, u32[]{:S(2)}) collective-permute-start(bf16[2,2,5,32,512]{4,3,2,1,0:T(8,128)(2,1)S(1)} %copy-done.3), channel_id=1, source_target_pairs={{0,4},{4,0},{8,12},{12,8},{16,20},{20,16},{24,28},{28,24},{1,5},{5... | collective-permute-start | bytes 1966088 | tf_op jit(solution)/shard_map/ppermute | solution.py:42
  212.5 51.5 %collective-permute-start.11 = (bf16[8,5,40,512]{3,2,1,0:T(8,128)(2,1)S(1)}, bf16[8,5,40,512]{3,2,1,0:T(8,128)(2,1)S(1)}, u32[]{:S(2)}, u32[]{:S(2)}) collective-permute-start(bf16[8,5,40,512]{3,2,1,0:T(8,128)(2,1)S(1)} %broadcast_multiply_fusion.2), channel_id=1, source_target_pairs={{0,2},{1,3},{2,0},{3,1},{4,6},{5,7},{6,4},{7,5},{8,10},{9,11},{10,... | collective-permute-start | bytes 4915208 | tf_op jit(solution)/shard_map/ppermute | solution.py:42
  230.3 27.5 %collective-permute-start.18 = (bf16[2,5,32,512]{3,2,1,0:T(8,128)(2,1)S(1)}, bf16[2,5,32,512]{3,2,1,0:T(8,128)(2,1)S(1)}, u32[]{:S(2)}, u32[]{:S(2)}) collective-permute-start(bf16[2,5,32,512]{3,2,1,0:T(8,128)(2,1)S(1)} %pad_maximum_fusion.4.refs_8_), channel_id=1, source_target_pairs={{0,24},{4,28},{8,16},{12,20},{16,8},{20,12},{24,0},{28,4},{1,25},{... | collective-permute-start | bytes 983048 | tf_op jit(solution)/shard_map/ppermute | solution.py:42
  233.5 28.5 %collective-permute-start.17 = (bf16[2,5,32,512]{3,2,1,0:T(8,128)(2,1)S(1)}, bf16[2,5,32,512]{3,2,1,0:T(8,128)(2,1)S(1)}, u32[]{:S(2)}, u32[]{:S(2)}) collective-permute-start(bf16[2,5,32,512]{3,2,1,0:T(8,128)(2,1)S(1)} %pad_maximum_fusion.3.refs_7_), channel_id=1, source_target_pairs={{0,16},{4,20},{8,24},{12,28},{16,0},{20,4},{24,8},{28,12},{1,17},{... | collective-permute-start | bytes 983048 | tf_op jit(solution)/shard_map/ppermute | solution.py:42
  236.2 25.8 %collective-permute-start.16 = (bf16[2,5,32,512]{3,2,1,0:T(8,128)(2,1)S(1)}, bf16[2,5,32,512]{3,2,1,0:T(8,128)(2,1)S(1)}, u32[]{:S(2)}, u32[]{:S(2)}) collective-permute-start(bf16[2,5,32,512]{3,2,1,0:T(8,128)(2,1)S(1)} %pad_maximum_fusion.2.refs_6_), channel_id=1, source_target_pairs={{0,8},{4,12},{8,0},{12,4},{16,24},{20,28},{24,16},{28,20},{1,9},{5... | collective-permute-start | bytes 983048 | tf_op jit(solution)/shard_map/ppermute | solution.py:42
  264.3 23.7 %collective-permute-start.22 = (bf16[2,5,32,512]{3,2,1,0:T(8,128)(2,1)S(1)}, bf16[2,5,32,512]{3,2,1,0:T(8,128)(2,1)S(1)}, u32[]{:S(2)}, u32[]{:S(2)}) collective-permute-start(bf16[2,5,32,512]{3,2,1,0:T(8,128)(2,1)S(1)} %add_convert_fusion.2.refs_5_), channel_id=1, source_target_pairs={{0,24},{4,28},{8,16},{12,20},{16,8},{20,12},{24,0},{28,4},{1,25},{... | collective-permute-start | bytes 983048 | tf_op jit(solution)/shard_map/ppermute | solution.py:42
  266.9 30.3 %collective-permute-start.21 = (bf16[2,5,32,512]{3,2,1,0:T(8,128)(2,1)S(1)}, bf16[2,5,32,512]{3,2,1,0:T(8,128)(2,1)S(1)}, u32[]{:S(2)}, u32[]{:S(2)}) collective-permute-start(bf16[2,5,32,512]{3,2,1,0:T(8,128)(2,1)S(1)} %add_convert_fusion.2.refs_5_), channel_id=1, source_target_pairs={{0,16},{4,20},{8,24},{12,28},{16,0},{20,4},{24,8},{28,12},{1,17},{... | collective-permute-start | bytes 983048 | tf_op jit(solution)/shard_map/ppermute | solution.py:42
  269.9 27.4 %collective-permute-start.20 = (bf16[2,5,32,512]{3,2,1,0:T(8,128)(2,1)S(1)}, bf16[2,5,32,512]{3,2,1,0:T(8,128)(2,1)S(1)}, u32[]{:S(2)}, u32[]{:S(2)}) collective-permute-start(bf16[2,5,32,512]{3,2,1,0:T(8,128)(2,1)S(1)} %add_convert_fusion.2.refs_5_), channel_id=1, source_target_pairs={{0,8},{4,12},{8,0},{12,4},{16,24},{20,28},{24,16},{28,20},{1,9},{5... | collective-permute-start | bytes 983048 | tf_op jit(solution)/shard_map/ppermute | solution.py:42
  298.5 12.3 %collective-permute-start.23 = (bf16[2,4,5,32,512]{4,3,2,1,0:T(8,128)(2,1)}, bf16[2,4,5,32,512]{4,3,2,1,0:T(8,128)(2,1)S(1)}, u32[]{:S(2)}, u32[]{:S(2)}) collective-permute-start(bf16[2,4,5,32,512]{4,3,2,1,0:T(8,128)(2,1)} %pad_maximum_fusion.refs_5_.refs_0_), channel_id=1, source_target_pairs={{0,1},{1,0},{2,3},{3,2},{4,5},{5,4},{6,7},{7,6},{8,9},{9,8},{10,11... | collective-permute-start | bytes 3932168 | tf_op jit(solution)/shard_map/ppermute | solution.py:42
  299.2 31.4 %collective-permute-start.27 = (bf16[2,4,5,32,512]{4,3,2,1,0:T(8,128)(2,1)}, bf16[2,4,5,32,512]{4,3,2,1,0:T(8,128)(2,1)}, u32[]{:S(2)}, u32[]{:S(2)}) collective-permute-start(bf16[2,4,5,32,512]{4,3,2,1,0:T(8,128)(2,1)} %pad_maximum_fusion.refs_5_.refs_0_), channel_id=1, source_target_pairs={{0,4},{4,0},{8,12},{12,8},{16,20},{20,16},{24,28},{28,24},{1,5},{5... | collective-permute-start | bytes 3932168 | tf_op jit(solution)/shard_map/ppermute | solution.py:42
  300.7 31.2 %collective-permute-start.28 = (bf16[2,4,5,32,512]{4,3,2,1,0:T(8,128)(2,1)}, bf16[2,4,5,32,512]{4,3,2,1,0:T(8,128)(2,1)}, u32[]{:S(2)}, u32[]{:S(2)}) collective-permute-start(bf16[2,4,5,32,512]{4,3,2,1,0:T(8,128)(2,1)} %pad_maximum_fusion.refs_5_.refs_0_), channel_id=1, source_target_pairs={{0,2},{1,3},{2,0},{3,1},{4,6},{5,7},{6,4},{7,5},{8,10},{9,11},{10,... | collective-permute-start | bytes 3932168 | tf_op jit(solution)/shard_map/ppermute | solution.py:42
  322.4 11.2 %collective-permute-start.26 = (bf16[56,1152]{1,0:T(8,128)(2,1)}, bf16[56,1152]{1,0:T(8,128)(2,1)}, u32[]{:S(2)}, u32[]{:S(2)}) collective-permute-start(bf16[56,1152]{1,0:T(8,128)(2,1)} %pad_maximum_fusion.7), channel_id=1, source_target_pairs={{0,24},{1,25},{2,26},{3,27},{4,28},{5,29},{6,30},{7,31},{8,16},{9,... | collective-permute-start | bytes 387080 | tf_op jit(solution)/shard_map/ppermute | solution.py:51
  324.9 12.8 %collective-permute-start.24 = (bf16[56,1152]{1,0:T(8,128)(2,1)}, bf16[56,1152]{1,0:T(8,128)(2,1)}, u32[]{:S(2)}, u32[]{:S(2)}) collective-permute-start(bf16[56,1152]{1,0:T(8,128)(2,1)} %pad_maximum_fusion.7), channel_id=1, source_target_pairs={{0,8},{1,9},{2,10},{3,11},{4,12},{5,13},{6,14},{7,15},{8,0},{9,1},... | collective-permute-start | bytes 387080 | tf_op jit(solution)/shard_map/ppermute | solution.py:51
  330.7 12.4 %collective-permute-start.30 = (bf16[2,4,5,32,512]{4,3,2,1,0:T(8,128)(2,1)}, bf16[2,4,5,32,512]{4,3,2,1,0:T(8,128)(2,1)S(1)}, u32[]{:S(2)}, u32[]{:S(2)}) collective-permute-start(bf16[2,4,5,32,512]{4,3,2,1,0:T(8,128)(2,1)} %collective-permute-done.27.refs_1_), channel_id=1, source_target_pairs={{0,1},{1,0},{2,3},{3,2},{4,5},{5,4},{6,7},{7,6},{8,9},{9,8},{10,11... | collective-permute-start | bytes 3932168 | tf_op jit(solution)/shard_map/ppermute | solution.py:42
  331.9 11.2 %collective-permute-start.31 = (bf16[2,4,5,32,512]{4,3,2,1,0:T(8,128)(2,1)}, bf16[2,4,5,32,512]{4,3,2,1,0:T(8,128)(2,1)S(1)}, u32[]{:S(2)}, u32[]{:S(2)}) collective-permute-start(bf16[2,4,5,32,512]{4,3,2,1,0:T(8,128)(2,1)} %collective-permute-done.28.refs_2_), channel_id=1, source_target_pairs={{0,1},{1,0},{2,3},{3,2},{4,5},{5,4},{6,7},{7,6},{8,9},{9,8},{10,11... | collective-permute-start | bytes 3932168 | tf_op jit(solution)/shard_map/ppermute | solution.py:42
  333.6 20.1 %collective-permute-start.29 = (bf16[4,5,32,512]{3,2,1,0:T(8,128)(2,1)S(1)}, bf16[4,5,32,512]{3,2,1,0:T(8,128)(2,1)S(1)}, u32[]{:S(2)}, u32[]{:S(2)}) collective-permute-start(bf16[4,5,32,512]{3,2,1,0:T(8,128)(2,1)S(1)} %fusion.13), channel_id=1, source_target_pairs={{0,2},{1,3},{2,0},{3,1},{4,6},{5,7},{6,4},{7,5},{8,10},{9,11},{10,... | collective-permute-start | bytes 1966088 | tf_op jit(solution)/shard_map/ppermute | solution.py:42
  335.4 18.4 %collective-permute-start.32 = (bf16[4,5,32,512]{3,2,1,0:T(8,128)(2,1)S(1)}, bf16[4,5,32,512]{3,2,1,0:T(8,128)(2,1)S(1)}, u32[]{:S(2)}, u32[]{:S(2)}) collective-permute-start(bf16[4,5,32,512]{3,2,1,0:T(8,128)(2,1)S(1)} %fusion.12), channel_id=1, source_target_pairs={{0,4},{4,0},{8,12},{12,8},{16,20},{20,16},{24,28},{28,24},{1,5},{5... | collective-permute-start | bytes 1966088 | tf_op jit(solution)/shard_map/ppermute | solution.py:42
  (53 other events, 356.3 us)

commit v12 on v11

--- a/solution.py
+++ b/solution.py
@@ -757,19 +757,19 @@
     values = joined(parts, token)
     from_y = swap(values, "tab", 1)
     from_x = swap(values, "rep", 2)
-    add_next(False, 1, [values])
-    other = [swap(values, "rep", 1)]
-    add_next(False, 1, other)
-    last = [swap(gate(from_y[0], token), "rep", 2), swap(gate(from_x[1], token), "tab", 1)]
-    small = small + zero_of(token)
+    small = small + zero_of(values[0, 0, 0, 0, 0])
     small = small_step(small, [(0, 2), (0, 4), (0, 6)])
     for rep_mask in masks_of("rep")[2:]:
         small = small_step(small, [(rep_mask, 0)])
     for tab_mask in masks_of("tab")[3:]:
         small = small_step(small, [(0, tab_mask)])
+    add_next(False, 1, [values])
+    other = [swap(values, "rep", 1)]
+    add_next(False, 1, other)
+    token = token + zero_of(small[0, 0])
+    last = [swap(gate(from_y[0], token), "rep", 2), swap(gate(from_x[1], token), "tab", 1)]
     other += [swap(from_y, "rep", 1), swap(from_x, "rep", 1)]
     add_next(False, slot_count, other)
-    token = token + zero_of(small[0, 0])
     last = [gate(part, token) for part in last]
     blocks = [values, from_y, from_x] + last + other + [swap(part, "rep", 1) for part in last]
 

time: 376 us -> 370 us (0.984)
  other arithmetic: 34.2 us -> 27.3 us
    ppermute x7, waiting for transfers between devices: 13.7 us -> 17.8 us  [swap_both(): return lax.ppermute(value, ('tab', 'rep'), perm)]
    unnamed x95 -> x93, local copies, waits for them, and re-layouts: 16.7 us -> 14.3 us
where the time goes in v12:
time: 370 us; the launch traced here: 365 us
  Pallas kernels  181 us (49%)
  starting transfers between devices  54.6 us (15%)
  waiting for transfers between devices  53.4 us (14%)
  local copies, waits for them, and re-layouts  35.2 us (10%)
  other arithmetic  27.3 us (7%)
  between operations  13.7 us (4%)
    pallas_call x10, Pallas kernels, add_rows(): pl.pallas_call(functools.partial(add_kernel, part_count, accumulate, tab_...  78.7 us
    pallas_call x2, Pallas kernels, lookup(): pl.pallas_call(functools.partial(lookup_kernel, first_slot), in_specs=[sm...  39.1 us
    pallas_call x1, Pallas kernels, dense_step(): pl.pallas_call(functools.partial(dense_kernel, dense_width, width, starts...  27.5 us
    ppermute x28, starting transfers between devices, swap(): lax.ppermute(value, axis, [(at, at ^ mask) for at in range(lax.axis_size(...  24.9 us
    ppermute x28, waiting for transfers between devices, swap(): lax.ppermute(value, axis, [(at, at ^ mask) for at in range(lax.axis_size(...  24.1 us
    pallas_call x2, Pallas kernels, weight_parts(): pl.pallas_call(functools.partial(weight_kernel, core), grid=(matrix_count...  22.4 us
    ppermute x7, waiting for transfers between devices, swap_both(): return lax.ppermute(value, ('tab', 'rep'), perm)  17.8 us
    unnamed x93, local copies, waits for them, and re-layouts  14.3 us
  transfers between devices with their start and end apart: 39, of which 12 were waited for; matrix products, arithmetic and copies ran while one was open for 14% of the time, Pallas kernels for 29%

profile of v12, /device:TPU:0, one launch (start us, length us, event | category | flops | bytes accessed | tf_op | source)
XLA Modules:
  0.0 365.1 jit_solution(1721431614631943554)
XLA Ops:
  5.2 7.3 %all-to-all-start = ((s32[8,5,512]{2,1,0:T(8,128)}), s32[8,5,512]{2,1,0:T(8,128)S(1)}, u32[]{:S(2)}, u32[]{:S(2)}) async-start(s32[8,5,512]{2,1,0:T(8,128)} %reshape.536), calls=%async_computation | async-start | bytes 262144 | tf_op jit(solution)/shard_map/all_to_all | solution.py:623
  13.8 6.0 %all-to-all-done = s32[8,5,512]{2,1,0:T(8,128)S(1)} async-done(((s32[8,5,512]{2,1,0:T(8,128)}), s32[8,5,512]{2,1,0:T(8,128)S(1)}, u32[]{:S(2)}, u32[]{:S(2)}) %all-to-all-start) | async-done | bytes 81952 | tf_op jit(solution)/shard_map/all_to_all | solution.py:623
  20.5 23.1 %lookup.2 = bf16[8,3,40,512]{3,2,1,0:T(8,128)(2,1)} custom-call(s32[20480]{0:T(1024)} %bitcast.161, s32[5]{0:T(128)} %dynamic_slice.3.rows_ref, bf16[5,39,32768]{2,1,0:T(8,128)(2,1)} %table_hbm.3), custom_call_target="tpu_custom_call" | custom-call | flops 30198988 | bytes 8626 | tf_op jit(solution)/shard_map/lookup/pallas_call | solution.py:112
  43.6 3.6 all-to-all-start.1
  49.1 16.0 %lookup.3 = bf16[8,2,40,512]{3,2,1,0:T(8,128)(2,1)} custom-call(s32[20480]{0:T(1024)} %bitcast.162, s32[5]{0:T(128)} %dynamic_slice.3.rows_ref, bf16[5,39,32768]{2,1,0:T(8,128)(2,1)} %table_hbm.3), custom_call_target="tpu_custom_call" | custom-call | flops 20132660 | bytes 5750 | tf_op jit(solution)/shard_map/lookup/pallas_call | solution.py:112
  65.1 5.4 %all-to-all-done.1.refs_0_ = bf16[8,3,40,512]{3,2,1,0:T(8,128)(2,1)S(1)} async-done(((bf16[8,3,40,512]{3,2,1,0:T(8,128)(2,1)}), bf16[8,3,40,512]{3,2,1,0:T(8,128)(2,1)S(1)}, u32[]{:S(2)}, u32[]{:S(2)}) %all-to-all-start.1) | async-done | bytes 983072 | tf_op jit(solution)/shard_map/all_to_all | solution.py:634
  70.6 3.5 all-to-all-start.2
  77.6 3.9 %multiply_bitcast_fusion = (bf16[1027,1027]{1,0:T(8,128)(2,1)S(1)}, bf16[1027,1027]{1,0:T(8,128)(2,1)S(1)}, bf16[1027,1027]{1,0:T(8,128)(2,1)S(1)}) fusion(bf16[3,1027,1027]{2,1,0:T(8,128)(2,1)} %param.20, bf16[]{:T(256)} %bitcast.6), kind=kLoop, calls=%fused_computation.7 | loop fusion | flops 3164187 | bytes 12656750 | tf_op jit(solution)/shard_map/mul | solution.py:639
  98.6 27.5 %dense.1 = (f32[1,512]{1,0:T(1,128)}, f32[16,512]{1,0:T(8,128)}, bf16[40,40,512]{2,1,0:T(8,128)(2,1)}, bf16[5,1152,512]{2,1,0:T(8,128)(2,1)}, bf16[5,1152,512]{2,1,0:T(8,128)(2,1)}, /*index=5*/f32[8,1152]{1,0:T(8,128)}) custom-call(s32[26]{0:T(128)} %place_ref.1, f32[1]{0:T(128)S(6)} %convert.67.bias_ref, bf16[8,3,40,512]{3,2,1,0:T(8,128)(2,1)} %copy-done.17, ...), custom_call_target="tpu_custom_call" | custom-call | flops 13589544 | bytes 30965 | tf_op jit(solution)/shard_map/dense/pallas_call | solution.py:381
  126.1 9.7 %weight_parts.3 = bf16[2,16,5,32,512]{4,3,2,1,0:T(8,128)(2,1)} custom-call(s32[1]{0:T(128)} %bitcast.own_ref, bf16[5,1152,512]{2,1,0:T(8,128)(2,1)} %get-tuple-element.43.left_ref, bf16[5,1152,512]{2,1,0:T(8,128)(2,1)} %get-tuple-element.44.right_ref), custom_call_target="tpu_custom_call" | custom-call | flops 3397386 | bytes 33177 | tf_op jit(solution)/shard_map/weight_parts/pallas_call | solution.py:463
  136.2 5.9 %all-to-all-start.3 = ((bf16[8,5,40,512]{3,2,1,0:T(8,128)(2,1)}), bf16[8,5,40,512]{3,2,1,0:T(8,128)(2,1)S(1)}, u32[]{:S(2)}, u32[]{:S(2)}) async-start(bf16[8,5,40,512]{3,2,1,0:T(8,128)(2,1)} %bitcast.35), calls=%async_computation.3 | async-start | bytes 3276800 | tf_op jit(solution)/shard_map/all_to_all | solution.py:670
  142.1 12.7 %weight_parts.2 = (f32[2,16,5,32,512]{4,3,2,1,0:T(8,128)}, f32[5,8,1152]{2,1,0:T(8,128)}) custom-call(s32[1]{0:T(128)} %bitcast.own_ref, bf16[5,1152,512]{2,1,0:T(8,128)(2,1)} %get-tuple-element.43.left_ref, bf16[5,1152,512]{2,1,0:T(8,128)(2,1)} %get-tuple-element.44.right_ref), custom_call_target="tpu_custom_call" | custom-call | flops 3397386 | bytes 33177 | tf_op jit(solution)/shard_map/weight_parts/pallas_call | solution.py:463
  163.5 3.6 fusion.8
  170.9 3.0 convert_add_fusion.1
  174.0 6.5 %collective-permute-done.7 = bf16[56,1152]{1,0:T(8,128)(2,1)S(1)} collective-permute-done((bf16[56,1152]{1,0:T(8,128)(2,1)S(1)}, bf16[56,1152]{1,0:T(8,128)(2,1)S(1)}, u32[]{:S(2)}, u32[]{:S(2)}) %collective-permute-start.7) | collective-permute-done | bytes 129056 | tf_op jit(solution)/shard_map/ppermute | solution.py:51
  180.6 5.8 %collective-permute-done.6 = bf16[56,1152]{1,0:T(8,128)(2,1)S(1)} collective-permute-done((bf16[56,1152]{1,0:T(8,128)(2,1)S(1)}, bf16[56,1152]{1,0:T(8,128)(2,1)S(1)}, u32[]{:S(2)}, u32[]{:S(2)}) %collective-permute-start.6) | collective-permute-done | bytes 129056 | tf_op jit(solution)/shard_map/ppermute | solution.py:51
  200.2 6.9 %add_rows.10 = (f32[5,39,8192]{2,1,0:T(8,128)}, f32[8,128]{1,0:T(8,128)S(1)}) custom-call(s32[1]{0:T(128)} %bitcast.34.base_ref, s32[8,5,1,512]{3,2,1,0:T(1,128)S(1)} %copy-done.6, s32[8,5,1,512]{3,2,1,0:T(1,128)S(1)} %copy-done.7, bf16[8,5,40,512]{3,2,1,0:T(8,128)(2,1)S(1)} %broadcast_multiply_fusion.3.refs_2_, ...), custom_call_target="tpu_custom_call" | custom-call | flops 5234491 | bytes 1916 | tf_op jit(solution)/shard_map/add_rows/pallas_call | solution.py:187
  207.1 7.3 %add_rows.11 = (f32[5,39,8192]{2,1,0:T(8,128)}, f32[8,128]{1,0:T(8,128)S(1)}) custom-call(s32[1]{0:T(128)} %bitcast.34.base_ref, s32[8,5,1,512]{3,2,1,0:T(1,128)S(1)} %copy-done.6, s32[8,5,1,512]{3,2,1,0:T(1,128)S(1)} %copy-done.7, bf16[8,5,40,512]{3,2,1,0:T(8,128)(2,1)S(1)} %broadcast_multiply_fusion.3.refs_2_, ...), custom_call_target="tpu_custom_call", output_to_operand_aliasing={{0}: (5, {})} | custom-call | flops 5234491 | bytes 1916 | tf_op jit(solution)/shard_map/add_rows/pallas_call | solution.py:187
  217.6 7.3 %collective-permute-done.8 = bf16[2,2,5,32,512]{4,3,2,1,0:T(8,128)(2,1)S(1)} collective-permute-done((bf16[2,2,5,32,512]{4,3,2,1,0:T(8,128)(2,1)S(1)}, bf16[2,2,5,32,512]{4,3,2,1,0:T(8,128)(2,1)S(1)}, u32[]{:S(2)}, u32[]{:S(2)}) %collective-permute-start.8) | collective-permute-done | bytes 655392 | tf_op jit(solution)/shard_map/ppermute | solution.py:42
  232.4 6.9 %add_rows.12 = (f32[5,39,8192]{2,1,0:T(8,128)}, f32[8,128]{1,0:T(8,128)}) custom-call(s32[1]{0:T(128)} %bitcast.34.base_ref, s32[8,5,1,512]{3,2,1,0:T(1,128)S(1)} %copy-done.6, s32[8,5,1,512]{3,2,1,0:T(1,128)S(1)} %copy-done.7, bf16[8,5,40,512]{3,2,1,0:T(8,128)(2,1)S(1)} %broadcast_multiply_fusion.3.refs_2_, ...), custom_call_target="tpu_custom_call", output_to_operand_aliasing={{0}: (5, {})} | custom-call | flops 5234491 | bytes 1916 | tf_op jit(solution)/shard_map/add_rows/pallas_call | solution.py:187
  239.3 7.1 %add_rows.13 = (f32[5,39,8192]{2,1,0:T(8,128)}, f32[8,128]{1,0:T(8,128)}) custom-call(s32[1]{0:T(128)} %bitcast.34.base_ref, s32[8,5,1,512]{3,2,1,0:T(1,128)S(1)} %copy-done.6, s32[8,5,1,512]{3,2,1,0:T(1,128)S(1)} %copy-done.7, bf16[8,5,40,512]{3,2,1,0:T(8,128)(2,1)S(1)} %broadcast_multiply_fusion.3.refs_2_, ...), custom_call_target="tpu_custom_call", output_to_operand_aliasing={{0}: (5, {})} | custom-call | flops 5234491 | bytes 1916 | tf_op jit(solution)/shard_map/add_rows/pallas_call | solution.py:187
  246.4 6.9 %add_rows.14 = (f32[5,39,8192]{2,1,0:T(8,128)}, f32[8,128]{1,0:T(8,128)S(1)}) custom-call(s32[1]{0:T(128)} %bitcast.34.base_ref, s32[8,5,1,512]{3,2,1,0:T(1,128)S(1)} %copy-done.6, s32[8,5,1,512]{3,2,1,0:T(1,128)S(1)} %copy-done.7, bf16[8,5,40,512]{3,2,1,0:T(8,128)(2,1)S(1)} %broadcast_multiply_fusion.3.refs_2_, ...), custom_call_target="tpu_custom_call", output_to_operand_aliasing={{0}: (5, {})} | custom-call | flops 5234491 | bytes 1916 | tf_op jit(solution)/shard_map/add_rows/pallas_call | solution.py:187
  253.8 3.8 %collective-permute-done.16 = bf16[2,5,32,512]{3,2,1,0:T(8,128)(2,1)S(1)} collective-permute-done((bf16[2,5,32,512]{3,2,1,0:T(8,128)(2,1)S(1)}, bf16[2,5,32,512]{3,2,1,0:T(8,128)(2,1)S(1)}, u32[]{:S(2)}, u32[]{:S(2)}) %collective-permute-start.16) | collective-permute-done | bytes 327712 | tf_op jit(solution)/shard_map/ppermute | solution.py:42
  266.0 8.6 %add_rows.15 = (f32[5,39,8192]{2,1,0:T(8,128)}, f32[8,128]{1,0:T(8,128)}) custom-call(s32[1]{0:T(128)} %bitcast.34.base_ref, s32[8,5,1,512]{3,2,1,0:T(1,128)S(1)} %copy-done.8, s32[8,5,1,512]{3,2,1,0:T(1,128)S(1)} %copy-done.9, bf16[8,5,40,512]{3,2,1,0:T(8,128)(2,1)S(1)} %broadcast_multiply_fusion.1.refs_2_, ...), custom_call_target="tpu_custom_call", output_to_operand_aliasing={{0}: (5, {})} | custom-call | flops 5234491 | bytes 1916 | tf_op jit(solution)/shard_map/add_rows/pallas_call | solution.py:187
  274.6 8.3 %add_rows.16 = (f32[5,39,8192]{2,1,0:T(8,128)}, f32[8,128]{1,0:T(8,128)S(1)}) custom-call(s32[1]{0:T(128)} %bitcast.34.base_ref, s32[8,5,1,512]{3,2,1,0:T(1,128)S(1)} %copy-done.8, s32[8,5,1,512]{3,2,1,0:T(1,128)S(1)} %copy-done.9, bf16[8,5,40,512]{3,2,1,0:T(8,128)(2,1)S(1)} %broadcast_multiply_fusion.1.refs_2_, ...), custom_call_target="tpu_custom_call", output_to_operand_aliasing={{0}: (5, {})} | custom-call | flops 5234491 | bytes 1916 | tf_op jit(solution)/shard_map/add_rows/pallas_call | solution.py:187
  284.1 8.8 %collective-permute-done.24 = bf16[2,5,32,512]{3,2,1,0:T(8,128)(2,1)S(1)} collective-permute-done((bf16[2,5,32,512]{3,2,1,0:T(8,128)(2,1)S(1)}, bf16[2,5,32,512]{3,2,1,0:T(8,128)(2,1)S(1)}, u32[]{:S(2)}, u32[]{:S(2)}) %collective-permute-start.24) | collective-permute-done | bytes 327712 | tf_op jit(solution)/shard_map/ppermute | solution.py:42
  299.3 5.5 %collective-permute-done.22 = bf16[56,1152]{1,0:T(8,128)(2,1)S(1)} collective-permute-done((bf16[56,1152]{1,0:T(8,128)(2,1)S(1)}, bf16[56,1152]{1,0:T(8,128)(2,1)S(1)}, u32[]{:S(2)}, u32[]{:S(2)}) %collective-permute-start.22) | collective-permute-done | bytes 129056 | tf_op jit(solution)/shard_map/ppermute | solution.py:51
  304.8 3.1 collective-permute-start.20
  308.5 8.7 %add_rows.17 = (f32[5,39,8192]{2,1,0:T(8,128)}, f32[8,128]{1,0:T(8,128)}) custom-call(s32[1]{0:T(128)} %bitcast.34.base_ref, s32[8,5,1,512]{3,2,1,0:T(1,128)S(1)} %copy-done.8, s32[8,5,1,512]{3,2,1,0:T(1,128)S(1)} %copy-done.9, bf16[8,5,40,512]{3,2,1,0:T(8,128)(2,1)S(1)} %broadcast_multiply_fusion.1.refs_2_, ...), custom_call_target="tpu_custom_call", output_to_operand_aliasing={{0}: (5, {})} | custom-call | flops 5234491 | bytes 1916 | tf_op jit(solution)/shard_map/add_rows/pallas_call | solution.py:187
  318.6 8.8 %add_rows.18 = (f32[5,39,8192]{2,1,0:T(8,128)}, f32[8,128]{1,0:T(8,128)S(1)}) custom-call(s32[1]{0:T(128)} %bitcast.34.base_ref, s32[8,5,1,512]{3,2,1,0:T(1,128)S(1)} %copy-done.8, s32[8,5,1,512]{3,2,1,0:T(1,128)S(1)} %copy-done.9, bf16[8,5,40,512]{3,2,1,0:T(8,128)(2,1)S(1)} %broadcast_multiply_fusion.1.refs_2_, ...), custom_call_target="tpu_custom_call", output_to_operand_aliasing={{0}: (5, {})} | custom-call | flops 5234491 | bytes 1916 | tf_op jit(solution)/shard_map/add_rows/pallas_call | solution.py:187
  333.5 9.2 %add_rows.19 = (f32[5,39,8192]{2,1,0:T(8,128)}, f32[8,128]{1,0:T(8,128)S(1)}) custom-call(s32[1]{0:T(128)} %bitcast.34.base_ref, s32[8,5,1,512]{3,2,1,0:T(1,128)S(1)} %copy-done.8, s32[8,5,1,512]{3,2,1,0:T(1,128)S(1)} %copy-done.9, bf16[8,5,40,512]{3,2,1,0:T(8,128)(2,1)S(1)} %broadcast_multiply_fusion.1.refs_2_, ...), custom_call_target="tpu_custom_call", output_to_operand_aliasing={{0}: (5, {})} | custom-call | flops 5234491 | bytes 1916 | tf_op jit(solution)/shard_map/add_rows/pallas_call | solution.py:187
  350.5 13.3 %assemble.1 = (f32[3,1027,1027]{2,1,0:T(8,128)}, f32[1,1027,1024]{2,1,0:T(8,128)}, f32[1,1024,1024]{2,1,0:T(8,128)}) custom-call(s32[1]{0:T(128)} %bitcast.own_ref, bf16[2,4,5,32,512]{4,3,2,1,0:T(8,128)(2,1)} %copy-done, bf16[2,4,5,32,512]{4,3,2,1,0:T(8,128)(2,1)} %copy-done.18, bf16[2,4,5,32,512]{4,3,2,1,0:T(8,128)(2,1)} %copy-done.19, ...), custom_call_target="tpu_custom_call" | custom-call | bytes 39813 | tf_op jit(solution)/shard_map/assemble/pallas_call | solution.py:568
  (274 shorter events, 87.4 us)
Async XLA Ops:
  5.2 14.6 %all-to-all-start = ((s32[8,5,512]{2,1,0:T(8,128)}), s32[8,5,512]{2,1,0:T(8,128)S(1)}, u32[]{:S(2)}, u32[]{:S(2)}) async-start(s32[8,5,512]{2,1,0:T(8,128)} %reshape.536), calls=%async_computation | async-start | bytes 262144 | tf_op jit(solution)/shard_map/all_to_all | solution.py:623
  43.6 26.9 %all-to-all-start.1 = ((bf16[8,3,40,512]{3,2,1,0:T(8,128)(2,1)}), bf16[8,3,40,512]{3,2,1,0:T(8,128)(2,1)S(1)}, u32[]{:S(2)}, u32[]{:S(2)}) async-start(bf16[8,3,40,512]{3,2,1,0:T(8,128)(2,1)} %lookup.2), calls=%async_computation.1 | async-start | bytes 1966080 | tf_op jit(solution)/shard_map/all_to_all | solution.py:634
  70.6 27.2 %all-to-all-start.2 = ((bf16[8,2,40,512]{3,2,1,0:T(8,128)(2,1)}), bf16[8,2,40,512]{3,2,1,0:T(8,128)(2,1)S(1)}, u32[]{:S(2)}, u32[]{:S(2)}) async-start(bf16[8,2,40,512]{3,2,1,0:T(8,128)(2,1)} %lookup.3), calls=%async_computation.2 | async-start | bytes 1310720 | tf_op jit(solution)/shard_map/all_to_all | solution.py:634
  75.3 20.3 %collective-permute-start = (s32[8,5,512]{2,1,0:T(8,128)S(1)}, s32[8,5,512]{2,1,0:T(8,128)S(1)}, u32[]{:S(2)}, u32[]{:S(2)}) collective-permute-start(s32[8,5,512]{2,1,0:T(8,128)S(1)} %broadcast_add_fusion), channel_id=1, source_target_pairs={{0,1},{1,0},{2,3},{3,2},{4,5},{5,4},{6,7},{7,6},{8,9},{9,8},{10,11... | collective-permute-start | bytes 245768 | tf_op jit(solution)/shard_map/ppermute | solution.py:42
  75.4 18.1 %collective-permute-start.1 = (s32[8,5,512]{2,1,0:T(8,128)S(1)}, s32[8,5,512]{2,1,0:T(8,128)S(1)}, u32[]{:S(2)}, u32[]{:S(2)}) collective-permute-start(s32[8,5,512]{2,1,0:T(8,128)S(1)} %broadcast_add_fusion), channel_id=1, source_target_pairs={{0,2},{1,3},{2,0},{3,1},{4,6},{5,7},{6,4},{7,5},{8,10},{9,11},{10,... | collective-permute-start | bytes 245768 | tf_op jit(solution)/shard_map/ppermute | solution.py:42
  135.8 19.0 %collective-permute-start.3 = (bf16[2,2,2,2,2,5,32,512]{7,6,5,4,3,2,1,0:T(8,128)(2,1)}, bf16[2,2,2,2,2,5,32,512]{7,6,5,4,3,2,1,0:T(8,128)(2,1)}, u32[]{:S(2)}, u32[]{:S(2)}) collective-permute-start(bf16[2,2,2,2,2,5,32,512]{7,6,5,4,3,2,1,0:T(8,128)(2,1)} %bitcast.159), channel_id=1, source_target_pairs={{0,1},{1,0},{2,3},{3,2},{4,5},{5,4},{6,7},{7,6},{8,9},{9,8},{10,11... | collective-permute-start | bytes 15728648 | tf_op jit(solution)/shard_map/ppermute | solution.py:42
  136.2 55.4 %all-to-all-start.3 = ((bf16[8,5,40,512]{3,2,1,0:T(8,128)(2,1)}), bf16[8,5,40,512]{3,2,1,0:T(8,128)(2,1)S(1)}, u32[]{:S(2)}, u32[]{:S(2)}) async-start(bf16[8,5,40,512]{3,2,1,0:T(8,128)(2,1)} %bitcast.35), calls=%async_computation.3 | async-start | bytes 3276800 | tf_op jit(solution)/shard_map/all_to_all | solution.py:670
  157.5 30.2 %collective-permute-start.11 = (bf16[2,2,5,32,512]{4,3,2,1,0:T(8,128)(2,1)S(1)}, bf16[2,2,5,32,512]{4,3,2,1,0:T(8,128)(2,1)S(1)}, u32[]{:S(2)}, u32[]{:S(2)}) collective-permute-start(bf16[2,2,5,32,512]{4,3,2,1,0:T(8,128)(2,1)S(1)} %get-tuple-element.85), channel_id=1, source_target_pairs={{0,4},{4,0},{8,12},{12,8},{16,20},{20,16},{24,28},{28,24},{1,5},{5... | collective-permute-start | bytes 1966088 | tf_op jit(solution)/shard_map/ppermute | solution.py:42
  160.6 27.5 %collective-permute-start.9 = (bf16[2,2,5,32,512]{4,3,2,1,0:T(8,128)(2,1)S(1)}, bf16[2,2,5,32,512]{4,3,2,1,0:T(8,128)(2,1)S(1)}, u32[]{:S(2)}, u32[]{:S(2)}) collective-permute-start(bf16[2,2,5,32,512]{4,3,2,1,0:T(8,128)(2,1)S(1)} %get-tuple-element.86), channel_id=1, source_target_pairs={{0,2},{1,3},{2,0},{3,1},{4,6},{5,7},{6,4},{7,5},{8,10},{9,11},{10,... | collective-permute-start | bytes 1966088 | tf_op jit(solution)/shard_map/ppermute | solution.py:42
  167.4 13.2 %collective-permute-start.7 = (bf16[56,1152]{1,0:T(8,128)(2,1)S(1)}, bf16[56,1152]{1,0:T(8,128)(2,1)S(1)}, u32[]{:S(2)}, u32[]{:S(2)}) collective-permute-start(bf16[56,1152]{1,0:T(8,128)(2,1)S(1)} %pad_maximum_fusion.6), channel_id=1, source_target_pairs={{0,6},{1,7},{2,4},{3,5},{4,2},{5,3},{6,0},{7,1},{8,14},{9,15},{10,... | collective-permute-start | bytes 387080 | tf_op jit(solution)/shard_map/ppermute | solution.py:51
  168.4 17.9 %collective-permute-start.6 = (bf16[56,1152]{1,0:T(8,128)(2,1)S(1)}, bf16[56,1152]{1,0:T(8,128)(2,1)S(1)}, u32[]{:S(2)}, u32[]{:S(2)}) collective-permute-start(bf16[56,1152]{1,0:T(8,128)(2,1)S(1)} %pad_maximum_fusion.6), channel_id=1, source_target_pairs={{0,4},{1,5},{2,6},{3,7},{4,0},{5,1},{6,2},{7,3},{8,12},{9,13},{10,... | collective-permute-start | bytes 387080 | tf_op jit(solution)/shard_map/ppermute | solution.py:51
  170.4 16.0 %collective-permute-start.5 = (bf16[56,1152]{1,0:T(8,128)(2,1)S(1)}, bf16[56,1152]{1,0:T(8,128)(2,1)S(1)}, u32[]{:S(2)}, u32[]{:S(2)}) collective-permute-start(bf16[56,1152]{1,0:T(8,128)(2,1)S(1)} %pad_maximum_fusion.6), channel_id=1, source_target_pairs={{0,2},{1,3},{2,0},{3,1},{4,6},{5,7},{6,4},{7,5},{8,10},{9,11},{10,... | collective-permute-start | bytes 387080 | tf_op jit(solution)/shard_map/ppermute | solution.py:51
  192.8 7.3 %collective-permute-start.12 = (bf16[8,5,40,512]{3,2,1,0:T(8,128)(2,1)S(1)}, bf16[8,5,40,512]{3,2,1,0:T(8,128)(2,1)S(1)}, u32[]{:S(2)}, u32[]{:S(2)}) collective-permute-start(bf16[8,5,40,512]{3,2,1,0:T(8,128)(2,1)S(1)} %broadcast_multiply_fusion.3.refs_2_), channel_id=1, source_target_pairs={{0,1},{1,0},{2,3},{3,2},{4,5},{5,4},{6,7},{7,6},{8,9},{9,8},{10,11... | collective-permute-start | bytes 4915208 | tf_op jit(solution)/shard_map/ppermute | solution.py:42
  192.9 23.9 %collective-permute-start.13 = (bf16[2,2,5,32,512]{4,3,2,1,0:T(8,128)(2,1)}, bf16[2,2,5,32,512]{4,3,2,1,0:T(8,128)(2,1)S(1)}, u32[]{:S(2)}, u32[]{:S(2)}) collective-permute-start(bf16[2,2,5,32,512]{4,3,2,1,0:T(8,128)(2,1)} %get-tuple-element.83.refs_5_), channel_id=1, source_target_pairs={{0,4},{4,0},{8,12},{12,8},{16,20},{20,16},{24,28},{28,24},{1,5},{5... | collective-permute-start | bytes 1966088 | tf_op jit(solution)/shard_map/ppermute | solution.py:42
  193.0 23.9 %collective-permute-start.14 = (bf16[2,2,5,32,512]{4,3,2,0,1:T(8,128)(2,1)}, bf16[2,2,5,32,512]{4,3,2,0,1:T(8,128)(2,1)S(1)}, u32[]{:S(2)}, u32[]{:S(2)}) collective-permute-start(bf16[2,2,5,32,512]{4,3,2,0,1:T(8,128)(2,1)} %copy-done.23), channel_id=1, source_target_pairs={{0,2},{1,3},{2,0},{3,1},{4,6},{5,7},{6,4},{7,5},{8,10},{9,11},{10,... | collective-permute-start | bytes 1966088 | tf_op jit(solution)/shard_map/ppermute | solution.py:42
  195.1 29.7 %collective-permute-start.8 = (bf16[2,2,5,32,512]{4,3,2,1,0:T(8,128)(2,1)S(1)}, bf16[2,2,5,32,512]{4,3,2,1,0:T(8,128)(2,1)S(1)}, u32[]{:S(2)}, u32[]{:S(2)}) collective-permute-start(bf16[2,2,5,32,512]{4,3,2,1,0:T(8,128)(2,1)S(1)} %copy-done.10), channel_id=1, source_target_pairs={{0,2},{1,3},{2,0},{3,1},{4,6},{5,7},{6,4},{7,5},{8,10},{9,11},{10,... | collective-permute-start | bytes 1966088 | tf_op jit(solution)/shard_map/ppermute | solution.py:42
  196.7 28.2 %collective-permute-start.10 = (bf16[2,2,5,32,512]{4,3,2,1,0:T(8,128)(2,1)S(1)}, bf16[2,2,5,32,512]{4,3,2,1,0:T(8,128)(2,1)S(1)}, u32[]{:S(2)}, u32[]{:S(2)}) collective-permute-start(bf16[2,2,5,32,512]{4,3,2,1,0:T(8,128)(2,1)S(1)} %copy-done.3), channel_id=1, source_target_pairs={{0,4},{4,0},{8,12},{12,8},{16,20},{20,16},{24,28},{28,24},{1,5},{5... | collective-permute-start | bytes 1966088 | tf_op jit(solution)/shard_map/ppermute | solution.py:42
  216.3 43.4 %collective-permute-start.18 = (bf16[8,5,40,512]{3,2,1,0:T(8,128)(2,1)S(1)}, bf16[8,5,40,512]{3,2,1,0:T(8,128)(2,1)S(1)}, u32[]{:S(2)}, u32[]{:S(2)}) collective-permute-start(bf16[8,5,40,512]{3,2,1,0:T(8,128)(2,1)S(1)} %broadcast_multiply_fusion.2), channel_id=1, source_target_pairs={{0,2},{1,3},{2,0},{3,1},{4,6},{5,7},{6,4},{7,5},{8,10},{9,11},{10,... | collective-permute-start | bytes 4915208 | tf_op jit(solution)/shard_map/ppermute | solution.py:42
  225.9 27.9 %collective-permute-start.17 = (bf16[2,5,32,512]{3,2,1,0:T(8,128)(2,1)S(1)}, bf16[2,5,32,512]{3,2,1,0:T(8,128)(2,1)S(1)}, u32[]{:S(2)}, u32[]{:S(2)}) collective-permute-start(bf16[2,5,32,512]{3,2,1,0:T(8,128)(2,1)S(1)} %pad_maximum_fusion.4.refs_8_), channel_id=1, source_target_pairs={{0,24},{4,28},{8,16},{12,20},{16,8},{20,12},{24,0},{28,4},{1,25},{... | collective-permute-start | bytes 983048 | tf_op jit(solution)/shard_map/ppermute | solution.py:42
  229.7 27.9 %collective-permute-start.16 = (bf16[2,5,32,512]{3,2,1,0:T(8,128)(2,1)S(1)}, bf16[2,5,32,512]{3,2,1,0:T(8,128)(2,1)S(1)}, u32[]{:S(2)}, u32[]{:S(2)}) collective-permute-start(bf16[2,5,32,512]{3,2,1,0:T(8,128)(2,1)S(1)} %pad_maximum_fusion.3.refs_7_), channel_id=1, source_target_pairs={{0,16},{4,20},{8,24},{12,28},{16,0},{20,4},{24,8},{28,12},{1,17},{... | collective-permute-start | bytes 983048 | tf_op jit(solution)/shard_map/ppermute | solution.py:42
  232.2 25.4 %collective-permute-start.15 = (bf16[2,5,32,512]{3,2,1,0:T(8,128)(2,1)S(1)}, bf16[2,5,32,512]{3,2,1,0:T(8,128)(2,1)S(1)}, u32[]{:S(2)}, u32[]{:S(2)}) collective-permute-start(bf16[2,5,32,512]{3,2,1,0:T(8,128)(2,1)S(1)} %pad_maximum_fusion.2.refs_6_), channel_id=1, source_target_pairs={{0,8},{4,12},{8,0},{12,4},{16,24},{20,28},{24,16},{28,20},{1,9},{5... | collective-permute-start | bytes 983048 | tf_op jit(solution)/shard_map/ppermute | solution.py:42
  259.9 24.2 %collective-permute-start.25 = (bf16[2,5,32,512]{3,2,1,0:T(8,128)(2,1)S(1)}, bf16[2,5,32,512]{3,2,1,0:T(8,128)(2,1)S(1)}, u32[]{:S(2)}, u32[]{:S(2)}) collective-permute-start(bf16[2,5,32,512]{3,2,1,0:T(8,128)(2,1)S(1)} %add_convert_fusion.2.refs_5_), channel_id=1, source_target_pairs={{0,24},{4,28},{8,16},{12,20},{16,8},{20,12},{24,0},{28,4},{1,25},{... | collective-permute-start | bytes 983048 | tf_op jit(solution)/shard_map/ppermute | solution.py:42
  262.6 30.3 %collective-permute-start.24 = (bf16[2,5,32,512]{3,2,1,0:T(8,128)(2,1)S(1)}, bf16[2,5,32,512]{3,2,1,0:T(8,128)(2,1)S(1)}, u32[]{:S(2)}, u32[]{:S(2)}) collective-permute-start(bf16[2,5,32,512]{3,2,1,0:T(8,128)(2,1)S(1)} %add_convert_fusion.2.refs_5_), channel_id=1, source_target_pairs={{0,16},{4,20},{8,24},{12,28},{16,0},{20,4},{24,8},{28,12},{1,17},{... | collective-permute-start | bytes 983048 | tf_op jit(solution)/shard_map/ppermute | solution.py:42
  265.9 27.1 %collective-permute-start.23 = (bf16[2,5,32,512]{3,2,1,0:T(8,128)(2,1)S(1)}, bf16[2,5,32,512]{3,2,1,0:T(8,128)(2,1)S(1)}, u32[]{:S(2)}, u32[]{:S(2)}) collective-permute-start(bf16[2,5,32,512]{3,2,1,0:T(8,128)(2,1)S(1)} %add_convert_fusion.2.refs_5_), channel_id=1, source_target_pairs={{0,8},{4,12},{8,0},{12,4},{16,24},{20,28},{24,16},{28,20},{1,9},{5... | collective-permute-start | bytes 983048 | tf_op jit(solution)/shard_map/ppermute | solution.py:42
  293.2 35.3 %collective-permute-start.26 = (bf16[2,4,5,32,512]{4,3,2,1,0:T(8,128)(2,1)S(1)}, bf16[2,4,5,32,512]{4,3,2,1,0:T(8,128)(2,1)S(1)}, u32[]{:S(2)}, u32[]{:S(2)}) collective-permute-start(bf16[2,4,5,32,512]{4,3,2,1,0:T(8,128)(2,1)S(1)} %pad_maximum_fusion.refs_5_.refs_0_), channel_id=1, source_target_pairs={{0,4},{4,0},{8,12},{12,8},{16,20},{20,16},{24,28},{28,24},{1,5},{5... | collective-permute-start | bytes 3932168 | tf_op jit(solution)/shard_map/ppermute | solution.py:42
  294.8 33.8 %collective-permute-start.27 = (bf16[2,4,5,32,512]{4,3,2,1,0:T(8,128)(2,1)S(1)}, bf16[2,4,5,32,512]{4,3,2,1,0:T(8,128)(2,1)S(1)}, u32[]{:S(2)}, u32[]{:S(2)}) collective-permute-start(bf16[2,4,5,32,512]{4,3,2,1,0:T(8,128)(2,1)S(1)} %pad_maximum_fusion.refs_5_.refs_0_), channel_id=1, source_target_pairs={{0,2},{1,3},{2,0},{3,1},{4,6},{5,7},{6,4},{7,5},{8,10},{9,11},{10,... | collective-permute-start | bytes 3932168 | tf_op jit(solution)/shard_map/ppermute | solution.py:42
  295.3 23.2 %collective-permute-start.28 = (bf16[2,4,5,32,512]{4,3,2,1,0:T(8,128)(2,1)S(1)}, bf16[2,4,5,32,512]{4,3,2,1,0:T(8,128)(2,1)S(1)}, u32[]{:S(2)}, u32[]{:S(2)}) collective-permute-start(bf16[2,4,5,32,512]{4,3,2,1,0:T(8,128)(2,1)S(1)} %pad_maximum_fusion.refs_5_.refs_0_), channel_id=1, source_target_pairs={{0,1},{1,0},{2,3},{3,2},{4,5},{5,4},{6,7},{7,6},{8,9},{9,8},{10,11... | collective-permute-start | bytes 3932168 | tf_op jit(solution)/shard_map/ppermute | solution.py:42
  296.6 8.2 %collective-permute-start.22 = (bf16[56,1152]{1,0:T(8,128)(2,1)S(1)}, bf16[56,1152]{1,0:T(8,128)(2,1)S(1)}, u32[]{:S(2)}, u32[]{:S(2)}) collective-permute-start(bf16[56,1152]{1,0:T(8,128)(2,1)S(1)} %pad_maximum_fusion.7), channel_id=1, source_target_pairs={{0,24},{1,25},{2,26},{3,27},{4,28},{5,29},{6,30},{7,31},{8,16},{9,... | collective-permute-start | bytes 387080 | tf_op jit(solution)/shard_map/ppermute | solution.py:51
  299.3 18.0 %collective-permute-start.21 = (bf16[56,1152]{1,0:T(8,128)(2,1)S(1)}, bf16[56,1152]{1,0:T(8,128)(2,1)S(1)}, u32[]{:S(2)}, u32[]{:S(2)}) collective-permute-start(bf16[56,1152]{1,0:T(8,128)(2,1)S(1)} %pad_maximum_fusion.7), channel_id=1, source_target_pairs={{0,16},{1,17},{2,18},{3,19},{4,20},{5,21},{6,22},{7,23},{8,24},{9,... | collective-permute-start | bytes 387080 | tf_op jit(solution)/shard_map/ppermute | solution.py:51
  304.8 12.5 %collective-permute-start.20 = (bf16[56,1152]{1,0:T(8,128)(2,1)S(1)}, bf16[56,1152]{1,0:T(8,128)(2,1)S(1)}, u32[]{:S(2)}, u32[]{:S(2)}) collective-permute-start(bf16[56,1152]{1,0:T(8,128)(2,1)S(1)} %pad_maximum_fusion.7), channel_id=1, source_target_pairs={{0,8},{1,9},{2,10},{3,11},{4,12},{5,13},{6,14},{7,15},{8,0},{9,1},... | collective-permute-start | bytes 387080 | tf_op jit(solution)/shard_map/ppermute | solution.py:51
  329.2 16.8 %collective-permute-start.29 = (bf16[4,5,32,512]{3,2,1,0:T(8,128)(2,1)S(1)}, bf16[4,5,32,512]{3,2,1,0:T(8,128)(2,1)S(1)}, u32[]{:S(2)}, u32[]{:S(2)}) collective-permute-start(bf16[4,5,32,512]{3,2,1,0:T(8,128)(2,1)S(1)} %fusion.12), channel_id=1, source_target_pairs={{0,2},{1,3},{2,0},{3,1},{4,6},{5,7},{6,4},{7,5},{8,10},{9,11},{10,... | collective-permute-start | bytes 1966088 | tf_op jit(solution)/shard_map/ppermute | solution.py:42
  330.8 16.5 %collective-permute-start.32 = (bf16[4,5,32,512]{3,2,1,0:T(8,128)(2,1)S(1)}, bf16[4,5,32,512]{3,2,1,0:T(8,128)(2,1)S(1)}, u32[]{:S(2)}, u32[]{:S(2)}) collective-permute-start(bf16[4,5,32,512]{3,2,1,0:T(8,128)(2,1)S(1)} %fusion.11), channel_id=1, source_target_pairs={{0,4},{4,0},{8,12},{12,8},{16,20},{20,16},{24,28},{28,24},{1,5},{5... | collective-permute-start | bytes 1966088 | tf_op jit(solution)/shard_map/ppermute | solution.py:42
  (52 other events, 380.5 us)
